TPU v7x, 32 devices: a whole 2x2x4 slice. The times are simulated.
32 devices in a mesh: gx: 4 (over y, x), gy: 8 (over z, core).
Axes of the slice: x: 2, y: 2, z: 4, core: 2. Of those that a mesh axis runs over, the one named last changes fastest.
Arguments:
- adjoint_source: float32 [2, 64, 64, 128], P(None, 'gx', 'gy'), may hold values from -16 to 16
- storage: float32 [4, 64, 64, 128], P(None, 'gx', 'gy'), may hold values from -0.2 to 2, as said below
- soil_ids: int32 [64, 64, 128], P('gx', 'gy'), may hold values from 0 to 15
- bc_mask: int32 [64, 64], P('gx', 'gy'), may hold values 0 or 1
- soil_props: float32 [3, 16], replicated, may hold values from 0.1 to 1
Outputs:
- adjoint: float32 [2, 64, 64, 128], P(None, 'gx', 'gy')
- residual: float32 [2, 64, 64, 128], P(None, 'gx', 'gy')
- next_basis: float32 [2, 64, 64, 128], P(None, 'gx', 'gy')
Inputs may be any that keep to these rules, and one draw needn't show every extreme that they name: `storage`: sp and St lie in 0.2 to 2, Spt within -0.04 to 0.04, Stp within -0.2 to 0.2.
All inputs are finite; a program needn't handle non-finite values. No bound on the sum of `bc_mask` on one device may be relied on, other than what follows from the above.
Results may differ from a plain program's by a relative error of at most 0.0008.
Values sent between devices are 32-bit elements; how exact they have to be, the bound alone decides.
No kernel may reach another device: no remote copies, remote signals or barrier semaphores. Data moves between devices by JAX's collectives and lax.ppermute only.
A program may use at most 64 MiB of HBM per device.

v0:
```python
import math

import jax
import jax.numpy as jnp
from jax import lax
from jax.sharding import PartitionSpec as P

NMAT = 16
MARGIN = 4
SWEEPS = 6
ITERS = 2


epsilon = 1e-06


def padded_2(block, sides, width):
    for axis, dim in sides:
        count = lax.axis_size(axis)
        forward = [(i, i + 1) for i in range(count - 1)]
        backward = [(target, source) for source, target in forward]
        low = lax.ppermute(
            lax.slice_in_dim(block, block.shape[dim] - width, None, axis=dim), axis, forward
        )
        high = lax.ppermute(lax.slice_in_dim(block, 0, width, axis=dim), axis, backward)
        block = jnp.concatenate([low, block, high], axis=dim)
    return block


def neighbour_list(field):
    middle = field[1:-1, 1:-1]
    below = jnp.pad(middle[:, :, :-1], ((0, 0), (0, 0), (1, 0)))
    above = jnp.pad(middle[:, :, 1:], ((0, 0), (0, 0), (0, 1)))
    return [field[:-2, 1:-1], field[2:, 1:-1], field[1:-1, :-2], field[1:-1, 2:], below, above]


def face_parts(coefficients):
    centre = coefficients[:, 1:-1, 1:-1]
    press_faces = jnp.stack(
        [jnp.sqrt(centre[0] * other) for other in neighbour_list(coefficients[0])]
    )
    heat_faces = jnp.stack(
        [jnp.sqrt(centre[1] * other) for other in neighbour_list(coefficients[1])]
    )
    return (press_faces, heat_faces, centre)


def laplace(field, faces, diagonal):
    total = diagonal * field[1:-1, 1:-1]
    for index, other in enumerate(neighbour_list(field)):
        total = total - faces[index] * other
    return total


def apply_adjoint(padded, spread_e, press_faces, heat_faces, centre):
    press_part = padded[0]
    heat_part = padded[1]
    mixed = press_part + spread_e * heat_part
    press_diag = jnp.sum(press_faces, axis=0) + centre[7]
    heat_diag = jnp.sum(heat_faces, axis=0)
    press_mid = press_part[1:-1, 1:-1]
    heat_mid = heat_part[1:-1, 1:-1]
    press_out = (
        centre[3] * press_mid + laplace(mixed, press_faces, press_diag) + centre[5] * heat_mid
    )
    heat_out = (
        centre[4] * press_mid + centre[6] * heat_mid + laplace(heat_part, heat_faces, heat_diag)
    )
    return jnp.stack([press_out, heat_out])


def block_inverse(press_faces, heat_faces, centre, outside):
    press_diag = jnp.sum(press_faces, axis=0) + centre[7]
    heat_diag = jnp.sum(heat_faces, axis=0)
    first = centre[3] + press_diag + outside
    cross = centre[5] + centre[2] * press_diag
    lower = centre[4]
    last = centre[6] + heat_diag + outside
    determinant = first * last - cross * lower
    return (last / determinant, -cross / determinant, -lower / determinant, first / determinant)


def subdomain_solve(rhs, press_faces, heat_faces, centre, inverse, spread_e):
    solution = jnp.zeros_like(rhs)
    for sweep in range(SWEEPS):
        padded = jnp.pad(solution, ((0, 0), (1, 1), (1, 1), (0, 0)))
        remain = rhs - apply_adjoint(padded, spread_e, press_faces, heat_faces, centre)
        step_p = inverse[0] * remain[0] + inverse[1] * remain[1]
        step_t = inverse[2] * remain[0] + inverse[3] * remain[1]
        solution = solution + jnp.stack([step_p, step_t])
    return solution


def assemble(material, storage, bc_mask):
    depth = material.shape[3]
    top = lax.broadcasted_iota(jnp.int32, (1, 1, depth), 2) == depth - 1
    boundary = jnp.where(top, 2.0 * material[0] * bc_mask[:, :, None].astype(jnp.float32), 0.0)
    return jnp.concatenate([material, storage, boundary[None]], axis=0)


def lookup(soil_props, ident):
    levels = jnp.arange(NMAT, dtype=jnp.float32)[:, None, None, None]
    onehot = (ident[None] == levels).astype(jnp.float32)
    return jnp.einsum("km,mxyz->kxyz", soil_props, onehot, precision=lax.Precision.HIGHEST)


def least_squares(columns, beta):
    count = len(columns)
    target = [beta] + [0.0 * beta for index in range(count)]
    rotations = []
    upper = []
    for column_index, column in enumerate(columns):
        values = list(column)
        for index, pair in enumerate(rotations):
            high = pair[0] * values[index] + pair[1] * values[index + 1]
            low = -pair[1] * values[index] + pair[0] * values[index + 1]
            values[index] = high
            values[index + 1] = low
        radius = jnp.sqrt(
            values[column_index] * values[column_index]
            + values[column_index + 1] * values[column_index + 1]
        )
        cosine = values[column_index] / radius
        sine = values[column_index + 1] / radius
        values[column_index] = radius
        rotations.append((cosine, sine))
        high = cosine * target[column_index] + sine * target[column_index + 1]
        low = -sine * target[column_index] + cosine * target[column_index + 1]
        target[column_index] = high
        target[column_index + 1] = low
        upper.append(values[: column_index + 1])
    weights = [None] * count
    for index in reversed(range(count)):
        accum = target[index]
        for later in range(index + 1, count):
            accum = accum - upper[later][index] * weights[later]
        weights[index] = accum / upper[index][index]
    return weights


def fold_axis(padded, count, axis):
    width = MARGIN
    total = lax.slice_in_dim(padded, 2 * width, 2 * width + count, axis=axis)
    lower = lax.slice_in_dim(padded, 0, width, axis=axis)
    upper = lax.slice_in_dim(padded, count + 3 * width, count + 4 * width, axis=axis)
    spread_low = [(0, 0)] * padded.ndim
    spread_low[axis] = (0, count - width)
    spread_high = [(0, 0)] * padded.ndim
    spread_high[axis] = (count - width, 0)
    return total + jnp.pad(lower, spread_low) + jnp.pad(upper, spread_high)


def global_length(vector):
    return jnp.sqrt(lax.psum(jnp.sum(vector * vector), ("gx", "gy")) + epsilon)


def shards(adjoint_source, storage, soil_ids, bc_mask, soil_props):
    rows_x = soil_ids.shape[0]
    rows_y = soil_ids.shape[1]
    depth = soil_ids.shape[2]
    cycle = MARGIN + 1
    material = lookup(soil_props, soil_ids.astype(jnp.float32))
    fields = assemble(material, storage, bc_mask)
    widened = padded_2(fields, (("gx", 1), ("gy", 2)), cycle)
    start_x = lax.axis_index("gx") * rows_x - MARGIN
    start_y = lax.axis_index("gy") * rows_y - MARGIN
    along_x = start_x + jnp.arange(rows_x + 2 * MARGIN, dtype=jnp.int32)
    along_y = start_y + jnp.arange(rows_y + 2 * MARGIN, dtype=jnp.int32)
    inside_x = (along_x >= 0) & (along_x < rows_x * lax.axis_size("gx"))
    inside_y = (along_y >= 0) & (along_y < rows_y * lax.axis_size("gy"))
    outside = (1.0 - (inside_x[:, None] & inside_y[None, :]).astype(jnp.float32))[:, :, None]
    sub_press, sub_heat, sub_centre = face_parts(widened)
    sub_inverse = block_inverse(sub_press, sub_heat, sub_centre, outside)
    own_coeffs = widened[:, MARGIN:-MARGIN, MARGIN:-MARGIN]
    own_press, own_heat, own_centre = face_parts(own_coeffs)
    beta = global_length(adjoint_source)
    basis = [adjoint_source / beta]
    directions = []
    columns = []
    for column_index in range(ITERS):
        rhs = jnp.pad(basis[-1], ((0, 0), (MARGIN, MARGIN), (MARGIN, MARGIN), (0, 0)))
        solved = subdomain_solve(rhs, sub_press, sub_heat, sub_centre, sub_inverse, widened[2])
        gathered = padded_2(solved, (("gx", 1), ("gy", 2)), MARGIN)
        direction = fold_axis(fold_axis(gathered, rows_x, 1), rows_y, 2)
        directions.append(direction)
        padded = padded_2(direction, (("gx", 1), ("gy", 2)), 1)
        image = apply_adjoint(padded, own_coeffs[2], own_press, own_heat, own_centre)
        heights = []
        for prior in basis:
            height = lax.psum(jnp.sum(image * prior), ("gx", "gy"))
            image = image - height * prior
            heights.append(height)
        length = global_length(image)
        heights.append(length)
        columns.append(heights)
        basis.append(image / length)
    weights = least_squares(columns, beta)
    adjoint = weights[0] * directions[0]
    adjoint = adjoint + weights[1] * directions[1]
    residual = jnp.zeros_like(adjoint_source)
    for row in range(ITERS + 1):
        factor = beta if row == 0 else 0.0 * beta
        for column_index in range(ITERS):
            if row <= column_index + 1:
                factor = factor - columns[column_index][row] * weights[column_index]
        residual = residual + factor * basis[row]
    cell_count = 2.0 * rows_x * lax.axis_size("gx") * rows_y * lax.axis_size("gy") * depth
    next_basis = basis[-1] * math.sqrt(cell_count)
    return (adjoint, residual, next_basis)


def solution(mesh):
    in_specs = (
        P(None, "gx", "gy", None),
        P(None, "gx", "gy", None),
        P("gx", "gy", None),
        P("gx", "gy"),
        P(),
    )
    out_specs = (P(None, "gx", "gy", None), P(None, "gx", "gy", None), P(None, "gx", "gy", None))
    return jax.shard_map(shards, mesh=mesh, in_specs=in_specs, out_specs=out_specs, check_vma=False)
```

profile of v0, /device:TPU:0, one launch (start us, length us, event | category | flops | bytes accessed | tf_op | source)
XLA Modules:
  0.0 383.5 jit_solution(14675182615680498154)
XLA Ops:
  3.9 1.3 collective-permute-start.1
  5.2 5.5 %collective-permute-start = (f32[8,5,8,128]{3,2,1,0:T(8,128)S(1)}, f32[8,5,8,128]{3,2,1,0:T(8,128)S(1)}, u32[]{:S(2)}, u32[]{:S(2)}) collective-permute-start(f32[8,5,8,128]{3,2,1,0:T(8,128)S(1)} %get-tuple-element.39), channel_id=1, source_target_pairs={{0,8},{8,16},{16,24},{1,9},{9,17},{17,25},{2,10},{10,18},{18,26},{... | collective-permute-start | bytes 491528 | tf_op jit(solution)/shard_map/ppermute | solution.py:22
  10.7 1.5 multiply_reduce_fusion.5
  12.8 40.7 %psum.42 = f32[]{:T(128)} all-reduce(f32[]{:T(128)} %multiply_reduce_fusion.5), channel_id=1, replica_groups=mesh['gx'=4,'gy'=8] {'gx','gy'}, use_global_device_ids=true, to_apply=%region_1.2 | all-reduce | flops 1 | bytes 8 | tf_op jit(solution)/shard_map/psum | solution.py:154
  55.8 1.4 collective-permute-start.3
  57.4 3.1 collective-permute-start.2
  72.3 1.3 collective-permute-start.5
  73.6 4.8 %collective-permute-start.4 = (f32[2,4,16,128]{3,2,1,0:T(8,128)S(1)}, f32[2,4,16,128]{3,2,1,0:T(8,128)S(1)}, u32[]{:S(2)}, u32[]{:S(2)}) collective-permute-start(f32[2,4,16,128]{3,2,1,0:T(8,128)S(1)} %get-tuple-element.65), channel_id=1, source_target_pairs={{0,8},{8,16},{16,24},{1,9},{9,17},{17,25},{2,10},{10,18},{18,26},{... | collective-permute-start | bytes 196616 | tf_op jit(solution)/shard_map/ppermute | solution.py:22
  78.7 1.6 collective-permute-done.4
  80.4 1.3 collective-permute-start.7
  81.7 7.7 %collective-permute-start.6 = (f32[2,32,4,128]{3,2,1,0:T(4,128)S(1)}, f32[2,32,4,128]{3,2,1,0:T(4,128)S(1)}, u32[]{:S(2)}, u32[]{:S(2)}) collective-permute-start(f32[2,32,4,128]{3,2,1,0:T(4,128)S(1)} %get-tuple-element.37), channel_id=1, source_target_pairs={{0,1},{1,2},{2,3},{3,4},{4,5},{5,6},{6,7},{8,9},{9,10},{10,11},{11... | collective-permute-start | bytes 393224 | tf_op jit(solution)/shard_map/ppermute | solution.py:22
  92.5 5.2 %collective-permute-start.8 = (f32[2,1,8,128]{3,2,1,0:T(8,128)S(1)}, f32[2,1,8,128]{3,2,1,0:T(8,128)S(1)}, u32[]{:S(2)}, u32[]{:S(2)}) collective-permute-start(f32[2,1,8,128]{3,2,1,0:T(8,128)S(1)} %get-tuple-element.157), channel_id=1, source_target_pairs={{0,8},{8,16},{16,24},{1,9},{9,17},{17,25},{2,10},{10,18},{18,26},{... | collective-permute-start | bytes 24584 | tf_op jit(solution)/shard_map/ppermute | solution.py:22
  99.1 1.3 collective-permute-start.11
  100.4 5.6 %collective-permute-start.10 = (f32[2,18,1,128]{3,2,1,0:T(1,128)S(1)}, f32[2,18,1,128]{3,2,1,0:T(1,128)S(1)}, u32[]{:S(2)}, u32[]{:S(2)}) collective-permute-start(f32[2,18,1,128]{3,2,1,0:T(1,128)S(1)} %get-tuple-element.153), channel_id=1, source_target_pairs={{0,1},{1,2},{2,3},{3,4},{4,5},{5,6},{6,7},{8,9},{9,10},{10,11},{11... | collective-permute-start | bytes 55304 | tf_op jit(solution)/shard_map/ppermute | solution.py:22
  110.0 47.6 %psum.43 = f32[]{:T(128)} all-reduce(f32[]{:T(128)} %multiply_reduce_fusion.4), channel_id=1, replica_groups=mesh['gx'=4,'gy'=8] {'gx','gy'}, use_global_device_ids=true, to_apply=%region_3.4 | all-reduce | flops 1 | bytes 8 | tf_op jit(solution)/shard_map/psum | solution.py:190
  157.6 2.3 multiply_reduce_fusion.3
  159.9 40.6 %psum.44 = f32[]{:T(128)} all-reduce(f32[]{:T(128)} %multiply_reduce_fusion.3), channel_id=1, replica_groups=mesh['gx'=4,'gy'=8] {'gx','gy'}, use_global_device_ids=true, to_apply=%region_5.6 | all-reduce | flops 1 | bytes 8 | tf_op jit(solution)/shard_map/psum | solution.py:154
  201.2 1.7 broadcast_divide_fusion.1
  213.4 1.3 collective-permute-start.13
  214.7 4.8 %collective-permute-start.12 = (f32[2,4,16,128]{3,2,1,0:T(8,128)S(1)}, f32[2,4,16,128]{3,2,1,0:T(8,128)S(1)}, u32[]{:S(2)}, u32[]{:S(2)}) collective-permute-start(f32[2,4,16,128]{3,2,1,0:T(8,128)S(1)} %get-tuple-element.41), channel_id=1, source_target_pairs={{0,8},{8,16},{16,24},{1,9},{9,17},{17,25},{2,10},{10,18},{18,26},{... | collective-permute-start | bytes 196616 | tf_op jit(solution)/shard_map/ppermute | solution.py:22
  219.9 1.6 collective-permute-done.12
  221.5 1.3 collective-permute-start.15
  222.8 3.2 collective-permute-start.14
  228.7 5.6 %collective-permute-start.16 = (f32[2,1,8,128]{3,2,1,0:T(8,128)S(1)}, f32[2,1,8,128]{3,2,1,0:T(8,128)S(1)}, u32[]{:S(2)}, u32[]{:S(2)}) collective-permute-start(f32[2,1,8,128]{3,2,1,0:T(8,128)S(1)} %get-tuple-element.155), channel_id=1, source_target_pairs={{0,8},{8,16},{16,24},{1,9},{9,17},{17,25},{2,10},{10,18},{18,26},{... | collective-permute-start | bytes 24584 | tf_op jit(solution)/shard_map/ppermute | solution.py:22
  234.3 1.3 collective-permute-done.16
  237.0 3.0 collective-permute-start.18
  244.6 46.0 %psum.45 = f32[]{:T(128)} all-reduce(f32[]{:T(128)} %multiply_reduce_fusion.2), channel_id=1, replica_groups=mesh['gx'=4,'gy'=8] {'gx','gy'}, use_global_device_ids=true, to_apply=%region_7.8 | all-reduce | flops 1 | bytes 8 | tf_op jit(solution)/shard_map/psum | solution.py:190
  291.3 1.9 multiply_reduce_fusion.1
  293.2 40.6 %psum.46 = f32[]{:T(128)} all-reduce(f32[]{:T(128)} %get-tuple-element.3), channel_id=1, replica_groups=mesh['gx'=4,'gy'=8] {'gx','gy'}, use_global_device_ids=true, to_apply=%region_9.10 | all-reduce | flops 1 | bytes 8 | tf_op jit(solution)/shard_map/psum | solution.py:190
  334.5 2.0 multiply_reduce_fusion
  336.4 40.2 %psum.47 = f32[]{:T(128)} all-reduce(f32[]{:T(128)} %multiply_reduce_fusion), channel_id=1, replica_groups=mesh['gx'=4,'gy'=8] {'gx','gy'}, use_global_device_ids=true, to_apply=%region_11.12 | all-reduce | flops 1 | bytes 8 | tf_op jit(solution)/shard_map/psum | solution.py:154
  381.4 2.1 broadcast_multiply_fusion
  (314 shorter events, 43.0 us)
Async XLA Ops:
  2.0 60.2 %copy-start.27 = (f32[3,16,8,128]{3,2,1,0:T(8,128)}, f32[3,16,8,128]{3,2,1,0:T(8,128)S(1)}, u32[]{:S(2)}) copy-start(f32[3,16,8,128]{3,2,1,0:T(8,128)S(1)} %copy.14) | copy-start | bytes 589828
  2.9 59.3 %copy-start.41 = (f32[1,16,8,128]{3,2,1,0:T(8,128)}, f32[1,16,8,128]{3,2,1,0:T(8,128)S(1)}, u32[]{:S(2)}) copy-start(f32[1,16,8,128]{3,2,1,0:T(8,128)S(1)} %multiply_select_fusion) | copy-start | bytes 196612
  3.9 50.5 %collective-permute-start.1 = (f32[8,5,8,128]{3,2,1,0:T(8,128)S(1)}, f32[8,5,8,128]{3,2,1,0:T(8,128)S(1)}, u32[]{:S(2)}, u32[]{:S(2)}) collective-permute-start(f32[8,5,8,128]{3,2,1,0:T(8,128)S(1)} %get-tuple-element.40), channel_id=1, source_target_pairs={{8,0},{16,8},{24,16},{9,1},{17,9},{25,17},{10,2},{18,10},{26,18},{... | collective-permute-start | bytes 491528 | tf_op jit(solution)/shard_map/ppermute | solution.py:25
  5.2 49.2 %collective-permute-start = (f32[8,5,8,128]{3,2,1,0:T(8,128)S(1)}, f32[8,5,8,128]{3,2,1,0:T(8,128)S(1)}, u32[]{:S(2)}, u32[]{:S(2)}) collective-permute-start(f32[8,5,8,128]{3,2,1,0:T(8,128)S(1)} %get-tuple-element.39), channel_id=1, source_target_pairs={{0,8},{8,16},{16,24},{1,9},{9,17},{17,25},{2,10},{10,18},{18,26},{... | collective-permute-start | bytes 491528 | tf_op jit(solution)/shard_map/ppermute | solution.py:22
  55.8 4.8 %collective-permute-start.3 = (f32[8,26,5,128]{3,0,2,1:T(8,128)S(1)}, f32[8,26,5,128]{3,0,2,1:T(8,128)S(1)}, u32[]{:S(2)}, u32[]{:S(2)}) collective-permute-start(f32[8,26,5,128]{3,0,2,1:T(8,128)S(1)} %copy.16), channel_id=1, source_target_pairs={{1,0},{2,1},{3,2},{4,3},{5,4},{6,5},{7,6},{9,8},{10,9},{11,10},{12... | collective-permute-start | bytes 1597448 | tf_op jit(solution)/shard_map/ppermute | solution.py:25
  57.4 4.6 %collective-permute-start.2 = (f32[8,26,5,128]{3,0,2,1:T(8,128)S(1)}, f32[8,26,5,128]{3,0,2,1:T(8,128)S(1)}, u32[]{:S(2)}, u32[]{:S(2)}) collective-permute-start(f32[8,26,5,128]{3,0,2,1:T(8,128)S(1)} %copy.15), channel_id=1, source_target_pairs={{0,1},{1,2},{2,3},{3,4},{4,5},{5,6},{6,7},{8,9},{9,10},{10,11},{11... | collective-permute-start | bytes 1597448 | tf_op jit(solution)/shard_map/ppermute | solution.py:22
  72.0 18.4 %copy-start.28 = (f32[3,16,8,128]{3,2,1,0:T(8,128)S(1)}, f32[3,16,8,128]{3,2,1,0:T(8,128)}, u32[]{:S(2)}) copy-start(f32[3,16,8,128]{3,2,1,0:T(8,128)} %copy-done.27) | copy-start | bytes 589828
  72.0 18.4 %copy-start.38 = (f32[8,5,8,128]{3,2,1,0:T(8,128)S(1)}, f32[8,5,8,128]{3,2,1,0:T(8,128)}, u32[]{:S(2)}) copy-start(f32[8,5,8,128]{3,2,1,0:T(8,128)} %copy-done.37) | copy-start | bytes 491524
  72.0 18.4 %copy-start.40 = (f32[8,5,8,128]{3,2,1,0:T(8,128)S(1)}, f32[8,5,8,128]{3,2,1,0:T(8,128)}, u32[]{:S(2)}) copy-start(f32[8,5,8,128]{3,2,1,0:T(8,128)} %copy-done.39) | copy-start | bytes 491524
  72.0 18.4 %copy-start.42 = (f32[1,16,8,128]{3,2,1,0:T(8,128)S(1)}, f32[1,16,8,128]{3,2,1,0:T(8,128)}, u32[]{:S(2)}) copy-start(f32[1,16,8,128]{3,2,1,0:T(8,128)} %copy-done.41) | copy-start | bytes 196612
  72.3 6.4 %collective-permute-start.5 = (f32[2,4,16,128]{3,2,1,0:T(8,128)S(1)}, f32[2,4,16,128]{3,2,1,0:T(8,128)S(1)}, u32[]{:S(2)}, u32[]{:S(2)}) collective-permute-start(f32[2,4,16,128]{3,2,1,0:T(8,128)S(1)} %get-tuple-element.66), channel_id=1, source_target_pairs={{8,0},{16,8},{24,16},{9,1},{17,9},{25,17},{10,2},{18,10},{26,18},{... | collective-permute-start | bytes 196616 | tf_op jit(solution)/shard_map/ppermute | solution.py:25
  73.6 6.7 %collective-permute-start.4 = (f32[2,4,16,128]{3,2,1,0:T(8,128)S(1)}, f32[2,4,16,128]{3,2,1,0:T(8,128)S(1)}, u32[]{:S(2)}, u32[]{:S(2)}) collective-permute-start(f32[2,4,16,128]{3,2,1,0:T(8,128)S(1)} %get-tuple-element.65), channel_id=1, source_target_pairs={{0,8},{8,16},{16,24},{1,9},{9,17},{17,25},{2,10},{10,18},{18,26},{... | collective-permute-start | bytes 196616 | tf_op jit(solution)/shard_map/ppermute | solution.py:22
  80.4 10.1 %collective-permute-start.7 = (f32[2,32,4,128]{3,2,1,0:T(4,128)S(1)}, f32[2,32,4,128]{3,2,1,0:T(4,128)S(1)}, u32[]{:S(2)}, u32[]{:S(2)}) collective-permute-start(f32[2,32,4,128]{3,2,1,0:T(4,128)S(1)} %get-tuple-element.38), channel_id=1, source_target_pairs={{1,0},{2,1},{3,2},{4,3},{5,4},{6,5},{7,6},{9,8},{10,9},{11,10},{12... | collective-permute-start | bytes 393224 | tf_op jit(solution)/shard_map/ppermute | solution.py:25
  81.7 8.9 %collective-permute-start.6 = (f32[2,32,4,128]{3,2,1,0:T(4,128)S(1)}, f32[2,32,4,128]{3,2,1,0:T(4,128)S(1)}, u32[]{:S(2)}, u32[]{:S(2)}) collective-permute-start(f32[2,32,4,128]{3,2,1,0:T(4,128)S(1)} %get-tuple-element.37), channel_id=1, source_target_pairs={{0,1},{1,2},{2,3},{3,4},{4,5},{5,6},{6,7},{8,9},{9,10},{10,11},{11... | collective-permute-start | bytes 393224 | tf_op jit(solution)/shard_map/ppermute | solution.py:22
  90.4 17.6 %copy-start.49 = (f32[1,16,8,128]{3,0,2,1:T(1,128)}, f32[1,16,8,128]{3,0,2,1:T(1,128)S(1)}, u32[]{:S(2)}) copy-start(f32[1,16,8,128]{3,0,2,1:T(1,128)S(1)} %slice.1689) | copy-start | bytes 196612
  90.5 17.5 %copy-start.31 = (f32[18,10,128]{2,1,0:T(8,128)}, f32[18,10,128]{2,1,0:T(8,128)S(1)}, u32[]{:S(2)}) copy-start(f32[18,10,128]{2,1,0:T(8,128)S(1)} %get-tuple-element.30) | copy-start | bytes 276484
  91.2 6.6 %collective-permute-start.9 = (f32[2,1,8,128]{3,2,1,0:T(8,128)S(1)}, f32[2,1,8,128]{3,2,1,0:T(8,128)S(1)}, u32[]{:S(2)}, u32[]{:S(2)}) collective-permute-start(f32[2,1,8,128]{3,2,1,0:T(8,128)S(1)} %get-tuple-element.158), channel_id=1, source_target_pairs={{8,0},{16,8},{24,16},{9,1},{17,9},{25,17},{10,2},{18,10},{26,18},{... | collective-permute-start | bytes 24584 | tf_op jit(solution)/shard_map/ppermute | solution.py:25
  92.5 6.5 %collective-permute-start.8 = (f32[2,1,8,128]{3,2,1,0:T(8,128)S(1)}, f32[2,1,8,128]{3,2,1,0:T(8,128)S(1)}, u32[]{:S(2)}, u32[]{:S(2)}) collective-permute-start(f32[2,1,8,128]{3,2,1,0:T(8,128)S(1)} %get-tuple-element.157), channel_id=1, source_target_pairs={{0,8},{8,16},{16,24},{1,9},{9,17},{17,25},{2,10},{10,18},{18,26},{... | collective-permute-start | bytes 24584 | tf_op jit(solution)/shard_map/ppermute | solution.py:22
  99.1 7.0 %collective-permute-start.11 = (f32[2,18,1,128]{3,2,1,0:T(1,128)S(1)}, f32[2,18,1,128]{3,2,1,0:T(1,128)S(1)}, u32[]{:S(2)}, u32[]{:S(2)}) collective-permute-start(f32[2,18,1,128]{3,2,1,0:T(1,128)S(1)} %get-tuple-element.154), channel_id=1, source_target_pairs={{1,0},{2,1},{3,2},{4,3},{5,4},{6,5},{7,6},{9,8},{10,9},{11,10},{12... | collective-permute-start | bytes 55304 | tf_op jit(solution)/shard_map/ppermute | solution.py:25
  100.4 6.4 %collective-permute-start.10 = (f32[2,18,1,128]{3,2,1,0:T(1,128)S(1)}, f32[2,18,1,128]{3,2,1,0:T(1,128)S(1)}, u32[]{:S(2)}, u32[]{:S(2)}) collective-permute-start(f32[2,18,1,128]{3,2,1,0:T(1,128)S(1)} %get-tuple-element.153), channel_id=1, source_target_pairs={{0,1},{1,2},{2,3},{3,4},{4,5},{5,6},{6,7},{8,9},{9,10},{10,11},{11... | collective-permute-start | bytes 55304 | tf_op jit(solution)/shard_map/ppermute | solution.py:22
  213.4 6.4 %collective-permute-start.13 = (f32[2,4,16,128]{3,2,1,0:T(8,128)S(1)}, f32[2,4,16,128]{3,2,1,0:T(8,128)S(1)}, u32[]{:S(2)}, u32[]{:S(2)}) collective-permute-start(f32[2,4,16,128]{3,2,1,0:T(8,128)S(1)} %get-tuple-element.42), channel_id=1, source_target_pairs={{8,0},{16,8},{24,16},{9,1},{17,9},{25,17},{10,2},{18,10},{26,18},{... | collective-permute-start | bytes 196616 | tf_op jit(solution)/shard_map/ppermute | solution.py:25
  214.7 6.7 %collective-permute-start.12 = (f32[2,4,16,128]{3,2,1,0:T(8,128)S(1)}, f32[2,4,16,128]{3,2,1,0:T(8,128)S(1)}, u32[]{:S(2)}, u32[]{:S(2)}) collective-permute-start(f32[2,4,16,128]{3,2,1,0:T(8,128)S(1)} %get-tuple-element.41), channel_id=1, source_target_pairs={{0,8},{8,16},{16,24},{1,9},{9,17},{17,25},{2,10},{10,18},{18,26},{... | collective-permute-start | bytes 196616 | tf_op jit(solution)/shard_map/ppermute | solution.py:22
  221.5 4.5 %collective-permute-start.15 = (f32[2,32,4,128]{3,2,1,0:T(4,128)S(1)}, f32[2,32,4,128]{3,2,1,0:T(4,128)S(1)}, u32[]{:S(2)}, u32[]{:S(2)}) collective-permute-start(f32[2,32,4,128]{3,2,1,0:T(4,128)S(1)} %get-tuple-element.36), channel_id=1, source_target_pairs={{1,0},{2,1},{3,2},{4,3},{5,4},{6,5},{7,6},{9,8},{10,9},{11,10},{12... | collective-permute-start | bytes 393224 | tf_op jit(solution)/shard_map/ppermute | solution.py:25
  222.8 19.6 %copy-start.48 = (f32[18,10,128]{2,1,0:T(8,128)S(1)}, f32[18,10,128]{2,1,0:T(8,128)}, u32[]{:S(2)}) copy-start(f32[18,10,128]{2,1,0:T(8,128)} %get-tuple-element.6) | copy-start | bytes 276484
  222.8 4.1 %collective-permute-start.14 = (f32[2,32,4,128]{3,2,1,0:T(4,128)S(1)}, f32[2,32,4,128]{3,2,1,0:T(4,128)S(1)}, u32[]{:S(2)}, u32[]{:S(2)}) collective-permute-start(f32[2,32,4,128]{3,2,1,0:T(4,128)S(1)} %get-tuple-element.35), channel_id=1, source_target_pairs={{0,1},{1,2},{2,3},{3,4},{4,5},{5,6},{6,7},{8,9},{9,10},{10,11},{11... | collective-permute-start | bytes 393224 | tf_op jit(solution)/shard_map/ppermute | solution.py:22
  227.4 6.9 %collective-permute-start.17 = (f32[2,1,8,128]{3,2,1,0:T(8,128)S(1)}, f32[2,1,8,128]{3,2,1,0:T(8,128)S(1)}, u32[]{:S(2)}, u32[]{:S(2)}) collective-permute-start(f32[2,1,8,128]{3,2,1,0:T(8,128)S(1)} %get-tuple-element.156), channel_id=1, source_target_pairs={{8,0},{16,8},{24,16},{9,1},{17,9},{25,17},{10,2},{18,10},{26,18},{... | collective-permute-start | bytes 24584 | tf_op jit(solution)/shard_map/ppermute | solution.py:25
  228.7 62.5 %copy-start.34 = (f32[1,16,8,128]{3,2,1,0:T(8,128)S(1)}, f32[1,16,8,128]{3,2,1,0:T(8,128)}, u32[]{:S(2)}) copy-start(f32[1,16,8,128]{3,2,1,0:T(8,128)} %copy-done.33) | copy-start | bytes 196612
  228.7 62.5 %copy-start.36 = (f32[1,16,8,128]{3,2,1,0:T(8,128)S(1)}, f32[1,16,8,128]{3,2,1,0:T(8,128)}, u32[]{:S(2)}) copy-start(f32[1,16,8,128]{3,2,1,0:T(8,128)} %copy-done.35) | copy-start | bytes 196612
  228.7 6.9 %collective-permute-start.16 = (f32[2,1,8,128]{3,2,1,0:T(8,128)S(1)}, f32[2,1,8,128]{3,2,1,0:T(8,128)S(1)}, u32[]{:S(2)}, u32[]{:S(2)}) collective-permute-start(f32[2,1,8,128]{3,2,1,0:T(8,128)S(1)} %get-tuple-element.155), channel_id=1, source_target_pairs={{0,8},{8,16},{16,24},{1,9},{9,17},{17,25},{2,10},{10,18},{18,26},{... | collective-permute-start | bytes 24584 | tf_op jit(solution)/shard_map/ppermute | solution.py:22
  235.7 6.5 %collective-permute-start.19 = (f32[2,18,1,128]{3,2,1,0:T(1,128)S(1)}, f32[2,18,1,128]{3,2,1,0:T(1,128)S(1)}, u32[]{:S(2)}, u32[]{:S(2)}) collective-permute-start(f32[2,18,1,128]{3,2,1,0:T(1,128)S(1)} %get-tuple-element.144), channel_id=1, source_target_pairs={{1,0},{2,1},{3,2},{4,3},{5,4},{6,5},{7,6},{9,8},{10,9},{11,10},{12... | collective-permute-start | bytes 55304 | tf_op jit(solution)/shard_map/ppermute | solution.py:25
  237.0 5.2 %collective-permute-start.18 = (f32[2,18,1,128]{3,2,1,0:T(1,128)S(1)}, f32[2,18,1,128]{3,2,1,0:T(1,128)S(1)}, u32[]{:S(2)}, u32[]{:S(2)}) collective-permute-start(f32[2,18,1,128]{3,2,1,0:T(1,128)S(1)} %get-tuple-element.143), channel_id=1, source_target_pairs={{0,1},{1,2},{2,3},{3,4},{4,5},{5,6},{6,7},{8,9},{9,10},{10,11},{11... | collective-permute-start | bytes 55304 | tf_op jit(solution)/shard_map/ppermute | solution.py:22
  242.3 136.5 %copy-start.44 = (f32[2,16,8,128]{3,2,1,0:T(8,128)S(1)}, f32[2,16,8,128]{3,2,1,0:T(8,128)}, u32[]{:S(2)}) copy-start(f32[2,16,8,128]{3,2,1,0:T(8,128)} %copy-done.43) | copy-start | bytes 393220
  (53 other events, 363.9 us)
where the time goes:
time: 385 us; the launch traced here: 384 us
  blocking collectives  256 us (66%)
  starting transfers between devices  61.4 us (16%)
  other arithmetic  35.3 us (9%)
  between operations  11.3 us (3%)
  local copies, waits for them, and re-layouts  10.2 us (3%)
  waiting for transfers between devices  9.22 us (2%)
    psum x3, blocking collectives, shards(): height = lax.psum(jnp.sum(image * prior), ('gx', 'gy'))  134 us
    psum x3, blocking collectives, global_length(): return jnp.sqrt(lax.psum(jnp.sum(vector * vector), ('gx', 'gy')) + epsilon)  121 us
    ppermute x10, starting transfers between devices, padded_2(): lax.ppermute(lax.slice_in_dim(block, block.shape[dim] - width, None, axis...  48.3 us
    ppermute x10, starting transfers between devices, padded_2(): lax.ppermute(lax.slice_in_dim(block, 0, width, axis=dim), axis, backward)  13.1 us
    another operation x26, other arithmetic, apply_adjoint(): return jnp.stack([press_out, heat_out])  9.29 us
    ppermute x10, waiting for transfers between devices, padded_2(): lax.ppermute(lax.slice_in_dim(block, block.shape[dim] - width, None, axis...  8.61 us
  transfers between devices with their start and end apart: 20, of which 9 were waited for; matrix products, arithmetic and copies ran while one was open for 1% of the time, Pallas kernels for 0%

commit v1 on v0

v1 whole, which is shorter than its diff:
```python
import functools
import math

import jax
import jax.numpy as jnp
from jax import lax
from jax.experimental import pallas as pl
from jax.experimental.pallas import tpu as pltpu
from jax.sharding import PartitionSpec as P

MARGIN = 4
SWEEPS = 6
SUB = 8
LANE = 128
TILE = (SUB, LANE)
RIM = MARGIN + 1
EPSILON = 1e-06
F32 = jnp.float32


def sublane():
    return lax.broadcasted_iota(jnp.int32, TILE, 0)


def lane():
    return lax.broadcasted_iota(jnp.int32, TILE, 1)


def up_y(tile):
    return pltpu.roll(tile, SUB - 1, 0)


def down_y(tile):
    return pltpu.roll(tile, 1, 0)


def half_turn(tile):
    return pltpu.roll(tile, SUB // 2, 0)


def along_z(tile, spot):
    above = jnp.where(spot == LANE - 1, 0.0, pltpu.roll(tile, LANE - 1, 1))
    below = jnp.where(spot == 0, 0.0, pltpu.roll(tile, 1, 1))
    return above + below


def along_y(own, side, row, last_up, last_down):
    own_up, own_down = up_y(own), down_y(own)
    side_up, side_down = up_y(side), down_y(side)
    own_sum = jnp.where(row == 7, side_up, own_up) + jnp.where(row == 0, side_down, own_down)
    side_sum = jnp.where(row == 7, own_up, jnp.where(row == 3, last_up, side_up))
    side_sum = side_sum + jnp.where(row == 0, own_down, jnp.where(row == 4, last_down, side_down))
    return own_sum, side_sum


def along_y_own(own, side, row):
    up = jnp.where(row == 7, up_y(side), up_y(own))
    down = jnp.where(row == 0, down_y(side), down_y(own))
    return up + down


def position(axis):
    place = lax.axis_index(axis)
    first = lax.rem(place, 2) == 0
    return first, place > 0, place < lax.axis_size(axis) - 1


def from_sides(first, even, odd):
    return jnp.where(first, odd, even), jnp.where(first, even, odd)


def lookup(table, wire):
    index = jnp.maximum(wire.astype(jnp.int32) - 1, 0)
    return jnp.where(wire > 0.0, jnp.take_along_axis(table, index, axis=1), 0.0)


def wide_tables(props_ref):
    pad = jnp.zeros((props_ref.shape[0], LANE - props_ref.shape[1]), F32)
    wide = jnp.concatenate([props_ref[...], pad], axis=1)
    return [jnp.broadcast_to(wide[k : k + 1], TILE) for k in range(3)]


def pack_x_kernel(props_ref, storage_ref, ids_ref, bc_ref, fields_ref, wire_ref, even_ref, odd_ref):
    rows = ids_ref.shape[0]
    tables = wide_tables(props_ref)
    row, spot = sublane(), lane()
    diagonal = row == spot
    for x in range(rows):
        wire = (ids_ref[x] + 1).astype(F32)
        wire_ref[x] = wire
        kp = lookup(tables[0], wire)
        carried = lookup(tables[2], wire)
        line = jnp.concatenate(
            [bc_ref[pl.ds(x, 1), :].astype(F32), jnp.zeros((1, LANE - SUB), F32)], axis=1
        )
        held = jnp.sum(jnp.where(diagonal, jnp.broadcast_to(line, TILE), 0.0), axis=1, keepdims=True)
        bound = jnp.where(spot == LANE - 1, 2.0 * kp * held, 0.0)
        press = storage_ref[0, x]
        lower = storage_ref[1, x]
        fields_ref[0, x] = press + bound
        fields_ref[1, x] = carried * press - storage_ref[2, x]
        fields_ref[2, x] = lower
        fields_ref[3, x] = storage_ref[3, x] - carried * lower
    first, _, _ = position("gx")
    high, low = rows - MARGIN, 0
    start_even = jnp.where(first, high, low)
    start_odd = jnp.where(first, low, high)
    wire_even = jnp.where(first, rows - RIM, 0)
    wire_odd = jnp.where(first, 0, rows - RIM)
    for k in range(4):
        even_ref[pl.ds(k * MARGIN, MARGIN)] = fields_ref[k, pl.ds(start_even, MARGIN)]
        odd_ref[pl.ds(k * MARGIN, MARGIN)] = fields_ref[k, pl.ds(start_odd, MARGIN)]
    even_ref[pl.ds(4 * MARGIN, RIM)] = wire_ref[pl.ds(wire_even, RIM)]
    odd_ref[pl.ds(4 * MARGIN, RIM)] = wire_ref[pl.ds(wire_odd, RIM)]


def widen_x(fields_ref, wire_ref, even_ref, odd_ref):
    rows = wire_ref.shape[0]
    first, has_low, has_high = position("gx")
    fields = []
    for k in range(4):
        low, high = from_sides(
            first, even_ref[pl.ds(k * MARGIN, MARGIN)], odd_ref[pl.ds(k * MARGIN, MARGIN)]
        )
        fields.append(
            [low[i] for i in range(MARGIN)]
            + [fields_ref[k, x] for x in range(rows)]
            + [high[i] for i in range(MARGIN)]
        )
    low, high = from_sides(
        first, even_ref[pl.ds(4 * MARGIN, RIM)], odd_ref[pl.ds(4 * MARGIN, RIM)]
    )
    low = jnp.where(has_low, low, 0.0)
    high = jnp.where(has_high, high, 0.0)
    wire = (
        [low[i] for i in range(RIM)] + [wire_ref[x] for x in range(rows)] + [high[i] for i in range(RIM)]
    )
    return fields, wire


def pack_y_kernel(fields_ref, wire_ref, xe_ref, xo_ref, even_ref, odd_ref):
    fields, wire = widen_x(fields_ref, wire_ref, xe_ref, xo_ref)
    wide = len(fields[0])
    first, _, _ = position("gy")
    even_low = (sublane() < 4) != first
    for pair in range(2):
        for i in range(wide):
            one = fields[2 * pair][i]
            other = half_turn(fields[2 * pair + 1][i])
            even_ref[pair * wide + i] = jnp.where(even_low, one, other)
            odd_ref[pair * wide + i] = jnp.where(even_low, other, one)
    for j in range(wide + 2):
        even_ref[2 * wide + j] = wire[j]
        odd_ref[2 * wide + j] = wire[j]


def sweep_row(q_ref, t_ref, coeff_ref, j, row, spot, rhs):
    sums = []
    for ref in (q_ref, t_ref):
        own, side = ref[j, 0], ref[j, 1]
        own_sum, side_sum = along_y(own, side, row, 0.0, 0.0)
        own_sum = own_sum + (along_z(own, spot) + (ref[j - 1, 0] + ref[j + 1, 0]))
        side_sum = side_sum + (along_z(side, spot) + (ref[j - 1, 1] + ref[j + 1, 1]))
        sums.append([own_sum, side_sum])
    if rhs is not None:
        sums[0][0] = sums[0][0] + rhs[0]
        sums[1][0] = sums[1][0] + rhs[1]
    out = []
    for tile in range(2):
        flow, heat = sums[0][tile], sums[1][tile]
        out.append(
            (
                coeff_ref[0, j - 1, tile] * flow + coeff_ref[1, j - 1, tile] * heat,
                coeff_ref[2, j - 1, tile] * flow + coeff_ref[3, j - 1, tile] * heat,
            )
        )
    return out


def subdomain_sweeps(rhs_ref, coeff_ref, solved_ref, even_ref, odd_ref, buffers, rows):
    row, spot = sublane(), lane()
    wide = rows + 2 * MARGIN
    zero = jnp.zeros(TILE, F32)
    for buffer in buffers:
        for j in range(wide + 2):
            for tile in range(2):
                buffer[j, tile] = zero
    current, following = buffers[:2], buffers[2:]
    for x in range(rows):
        j = x + RIM
        flow, heat = rhs_ref[0, x], rhs_ref[1, x]
        current[0][j, 0] = coeff_ref[0, j - 1, 0] * flow + coeff_ref[1, j - 1, 0] * heat
        current[1][j, 0] = coeff_ref[2, j - 1, 0] * flow + coeff_ref[3, j - 1, 0] * heat
    first, _, _ = position("gy")
    even_low = (row < 4) != first
    for sweep in range(1, SWEEPS):
        reach = min(sweep, MARGIN)
        for x in range(-reach, rows + reach):
            j = x + RIM
            rhs = (rhs_ref[0, x], rhs_ref[1, x]) if 0 <= x < rows else None
            out = sweep_row(current[0], current[1], coeff_ref, j, row, spot, rhs)
            if sweep < SWEEPS - 1:
                for tile in range(2):
                    following[0][j, tile] = out[tile][0]
                    following[1][j, tile] = out[tile][1]
            else:
                for k in range(2):
                    own, side = out[0][k], out[1][k]
                    solved_ref[k, j - 1, 0] = own
                    solved_ref[k, j - 1, 1] = side
                    even_ref[k, j - 1] = jnp.where(even_low, own, side)
                    odd_ref[k, j - 1] = jnp.where(even_low, side, own)
        current, following = following, current


def coefficients_kernel(
    props_ref, fields_ref, wire_ref, xe_ref, xo_ref, ye_ref, yo_ref, source_ref,
    coeff_ref, image_ref, scale_ref, solved_ref, even_ref, odd_ref,
    gp_ref, gt_ref, rhs_ref, *buffers,
):
    rows = wire_ref.shape[0]
    wide = rows + 2 * MARGIN
    row, spot = sublane(), lane()
    tables = wide_tables(props_ref)
    roots = [jnp.sqrt(jnp.maximum(tables[0], 0.0)), jnp.sqrt(jnp.maximum(tables[1], 0.0))]
    fields, wire = widen_x(fields_ref, wire_ref, xe_ref, xo_ref)
    first, has_low, has_high = position("gy")
    out_wire = []
    for j in range(wide + 2):
        low, high = from_sides(first, ye_ref[2 * wide + j], yo_ref[2 * wide + j])
        low = jnp.where(has_low, low, 0.0)
        high = jnp.where(has_high, high, 0.0)
        own = wire[j]
        side = jnp.where(row < 4, high, low)
        beyond = jnp.where(row < 4, low, high)
        out_wire.append((own, side))
        for g, ref in enumerate((gp_ref, gt_ref)):
            ref[j, 0] = lookup(roots[g], own)
            ref[j, 1] = lookup(roots[g], side)
            ref[j, 2] = lookup(roots[g], beyond)
    for i in range(wide):
        j = i + 1
        stores = []
        for pair in range(2):
            low, high = from_sides(first, ye_ref[pair * wide + i], yo_ref[pair * wide + i])
            stores.append(jnp.where(row < 4, high, low))
            stores.append(half_turn(jnp.where(row < 4, low, high)))
        diagonals = []
        for ref in (gp_ref, gt_ref):
            beyond = ref[j, 2]
            own_sum, side_sum = along_y(ref[j, 0], ref[j, 1], row, up_y(beyond), down_y(beyond))
            own_sum = own_sum + along_z(ref[j, 0], spot) + (ref[j - 1, 0] + ref[j + 1, 0])
            side_sum = side_sum + along_z(ref[j, 1], spot) + (ref[j - 1, 1] + ref[j + 1, 1])
            diagonals.append((ref[j, 0] * own_sum, ref[j, 1] * side_sum))
        for tile in range(2):
            if tile == 0:
                press, cross, lower, heat = (fields[k][i] for k in range(4))
            else:
                press, cross, lower, heat = stores
            outside = jnp.where(out_wire[j][tile] > 0.0, 0.0, 1.0)
            gp, gt = gp_ref[j, tile], gt_ref[j, tile]
            a = press + diagonals[0][tile] + outside
            d = heat + diagonals[1][tile] + outside
            inverse = 1.0 / (a * d + cross * lower)
            pp, pt, tt = gp * gp, gp * gt, gt * gt
            coeff_ref[0, i, tile] = pp * d * inverse
            coeff_ref[1, i, tile] = pt * cross * inverse
            coeff_ref[2, i, tile] = -pt * lower * inverse
            coeff_ref[3, i, tile] = tt * a * inverse
            if tile == 0 and MARGIN <= i < wide - MARGIN:
                x = i - MARGIN
                over_p, over_t = 1.0 / gp, 1.0 / gt
                over = over_p * over_t
                image_ref[0, x] = a * (over_p * over_p)
                image_ref[1, x] = -cross * over
                image_ref[2, x] = lower * over
                image_ref[3, x] = d * (over_t * over_t)
                scale_ref[0, x] = gp
                scale_ref[1, x] = gt
                scale_ref[2, x] = over_p
                scale_ref[3, x] = over_t
                scale_ref[4, x] = lookup(tables[2], out_wire[j][0])
                rhs_ref[0, x] = source_ref[0, x] * over_p
                rhs_ref[1, x] = source_ref[1, x] * over_t
    subdomain_sweeps(rhs_ref, coeff_ref, solved_ref, even_ref, odd_ref, buffers, rows)


def fold_y_kernel(solved_ref, ye_ref, yo_ref, summed_ref, even_ref, odd_ref):
    wide = solved_ref.shape[1]
    row = sublane()
    first, has_low, has_high = position("gy")
    for k in range(2):
        for i in range(wide):
            low, high = from_sides(first, ye_ref[k, i], yo_ref[k, i])
            low = jnp.where(has_low, low, 0.0)
            high = jnp.where(has_high, high, 0.0)
            summed_ref[k, i, 0] = solved_ref[k, i, 0] + jnp.where(row < 4, low, high)
            summed_ref[k, i, 1] = solved_ref[k, i, 1] + jnp.where(row < 4, high, low)
    first, _, _ = position("gx")
    margin_even = jnp.where(first, wide - MARGIN, 0)
    margin_odd = jnp.where(first, 0, wide - MARGIN)
    rim_even = jnp.where(first, wide - MARGIN - 1, MARGIN)
    rim_odd = jnp.where(first, MARGIN, wide - MARGIN - 1)
    for k in range(2):
        for ref, margin, rim in ((even_ref, margin_even, rim_even), (odd_ref, margin_odd, rim_odd)):
            for tile in range(2):
                ref[k, pl.ds(tile * MARGIN, MARGIN)] = summed_ref[k, pl.ds(margin, MARGIN), tile]
            ref[k, 2 * MARGIN] = summed_ref[k, rim, 0]


def fold_x(summed_ref, xe_ref, xo_ref, field_refs):
    wide = summed_ref.shape[1]
    rows = wide - 2 * MARGIN
    first, has_low, has_high = position("gx")
    for k in range(2):
        low, high = from_sides(first, xe_ref[k], xo_ref[k])
        low = jnp.where(has_low, low, 0.0)
        high = jnp.where(has_high, high, 0.0)
        for x in range(-1, rows + 1):
            for tile in range(2):
                value = summed_ref[k, x + MARGIN, tile]
                if 0 <= x < MARGIN:
                    value = value + low[tile * MARGIN + x]
                if rows - MARGIN <= x < rows:
                    value = value + high[tile * MARGIN + x - (rows - MARGIN)]
                if tile == 0 and x == -1:
                    value = value + low[2 * MARGIN]
                if tile == 0 and x == rows:
                    value = value + high[2 * MARGIN]
                field_refs[k][x + 1, tile] = value


def image_row(field_refs, image_ref, x, row, spot):
    sums = []
    for ref in field_refs:
        own = ref[x + 1, 0]
        total = along_y_own(own, ref[x + 1, 1], row) + along_z(own, spot)
        sums.append(total + (ref[x, 0] + ref[x + 2, 0]))
    flow, heat = field_refs[0][x + 1, 0], field_refs[1][x + 1, 0]
    return (
        image_ref[0, x] * flow + image_ref[1, x] * heat - sums[0],
        image_ref[2, x] * flow + image_ref[3, x] * heat - sums[1],
    )


def keep_direction(direction_ref, scale_ref, field_refs, x):
    heat = field_refs[1][x + 1, 0] * scale_ref[3, x]
    direction_ref[1, x] = heat
    direction_ref[0, x] = field_refs[0][x + 1, 0] * scale_ref[2, x] - scale_ref[4, x] * heat


def gram_rows(pairs, row, offset):
    total = jnp.zeros(TILE, F32)
    for index, value in enumerate(pairs):
        line = jnp.broadcast_to(jnp.sum(value, axis=0, keepdims=True), TILE)
        total = total + jnp.where(row == index + offset, line, 0.0)
    return total


def step_kernel(
    summed_ref, xe_ref, xo_ref, coeff_ref, image_ref, scale_ref, source_ref,
    direction_ref, power_ref, gram_ref, solved_ref, even_ref, odd_ref,
    rhs_ref, q_ref, t_ref, *buffers,
):
    rows = source_ref.shape[1]
    row, spot = sublane(), lane()
    fields = (q_ref, t_ref)
    fold_x(summed_ref, xe_ref, xo_ref, fields)
    products = [jnp.zeros(TILE, F32) for _ in range(3)]
    for x in range(rows):
        keep_direction(direction_ref, scale_ref, fields, x)
        for k, part in enumerate(image_row(fields, image_ref, x, row, spot)):
            source = source_ref[k, x]
            scaled = part - source * scale_ref[2 + k, x]
            power = scaled * scale_ref[k, x]
            rhs_ref[k, x] = scaled
            power_ref[k, x] = power
            products[0] = products[0] + source * source
            products[1] = products[1] + source * power
            products[2] = products[2] + power * power
    gram_ref[...] = gram_rows(products, row, 0)
    subdomain_sweeps(rhs_ref, coeff_ref, solved_ref, even_ref, odd_ref, buffers, rows)


def last_kernel(
    summed_ref, xe_ref, xo_ref, image_ref, scale_ref, source_ref, power_ref, gram_in_ref,
    direction_ref, second_ref, gram_ref, q_ref, t_ref,
):
    rows = source_ref.shape[1]
    row, spot = sublane(), lane()
    fields = (q_ref, t_ref)
    fold_x(summed_ref, xe_ref, xo_ref, fields)
    products = [jnp.zeros(TILE, F32) for _ in range(3)]
    for x in range(rows):
        keep_direction(direction_ref, scale_ref, fields, x)
        for k, part in enumerate(image_row(fields, image_ref, x, row, spot)):
            power = power_ref[k, x]
            second = part * scale_ref[k, x] - power
            second_ref[k, x] = second
            products[0] = products[0] + source_ref[k, x] * second
            products[1] = products[1] + power * second
            products[2] = products[2] + second * second
    total = gram_in_ref[...] + gram_rows(products, row, 3)
    for device in range(gram_ref.shape[0]):
        gram_ref[device] = total


def combine_kernel(
    gram_ref, source_ref, power_ref, second_ref, one_ref, two_ref,
    adjoint_ref, residual_ref, basis_ref, *, scale,
):
    parts = [gram_ref[device] for device in range(gram_ref.shape[0])]
    while len(parts) > 1:
        parts = [parts[i] + parts[i + 1] if i + 1 < len(parts) else parts[i] for i in range(0, len(parts), 2)]
    sums = jnp.broadcast_to(jnp.sum(parts[0], axis=1, keepdims=True), TILE)
    g00, g01, g11, g02, g12, g22 = (sums[k : k + 1] for k in range(6))
    beta2 = g00 + EPSILON
    beta = jnp.sqrt(beta2)
    less = (EPSILON - g01) / beta2
    h11 = (g00 + g01) / beta2
    square = (less * less * g00 + 2.0 * less * g01 + g11) / beta2
    square = jnp.maximum(square, 0.0)
    h21 = jnp.sqrt(square + EPSILON)
    b = 1.0 / (beta * h21)
    a = less * b
    h12 = EPSILON * h11 / (beta2 * h21) + (a * g01 + b * g02) / beta
    short = EPSILON / (square + EPSILON) - (a * a * g01 + a * b * (g11 + g02) + b * b * g12)
    h22 = 1.0 - short
    c0 = a * short - h12 / beta
    c1 = a + b * short
    c2 = b
    square = c0 * (c0 * g00 + 2.0 * (c1 * g01 + c2 * g02)) + c1 * (c1 * g11 + 2.0 * c2 * g12) + c2 * c2 * g22
    h32 = jnp.sqrt(jnp.maximum(square, 0.0) + EPSILON)
    n0, n1, n2 = h21 * h32, -h11 * h32, h11 * h22 - h12 * h21
    factor = beta * n0 / (n0 * n0 + n1 * n1 + n2 * n2)
    f0, f1, f2 = factor * n0, factor * n1, factor * n2
    y2 = -f2 / h32
    y1 = (h11 * (beta - f0 - h12 * y2) - h21 * (f1 + h22 * y2)) / (h11 * h11 + h21 * h21)
    over = 1.0 / h32
    v0, v1, v2 = c0 * over, c1 * over, c2 * over
    wide = lambda value: jnp.broadcast_to(value, TILE)
    z_one, z_two = wide(y1 / beta + y2 * a), wide(y2 * b)
    r0, r1, r2 = wide(f0 / beta + f1 * a + f2 * v0), wide(f1 * b + f2 * v1), wide(f2 * v2)
    s0, s1, s2 = wide(scale * v0), wide(scale * v1), wide(scale * v2)
    for k in range(2):
        for x in range(source_ref.shape[1]):
            source, power, second = source_ref[k, x], power_ref[k, x], second_ref[k, x]
            adjoint_ref[k, x] = z_one * one_ref[k, x] + z_two * two_ref[k, x]
            residual_ref[k, x] = r0 * source + r1 * power + r2 * second
            basis_ref[k, x] = s0 * source + s1 * power + s2 * second


def call(kernel, outs, scratch=(), name=None):
    def run(*args):
        return pl.pallas_call(
            kernel,
            out_shape=[jax.ShapeDtypeStruct(shape, F32) for shape in outs],
            in_specs=[pl.BlockSpec(memory_space=pltpu.VMEM)] * len(args),
            out_specs=[pl.BlockSpec(memory_space=pltpu.VMEM)] * len(outs),
            scratch_shapes=[pltpu.VMEM(shape, F32) for shape in scratch],
            compiler_params=pltpu.CompilerParams(vmem_limit_bytes=32 * 1024 * 1024),
            name=name,
        )(*args)

    return run


def exchange(axis, even, odd):
    count = lax.axis_size(axis)
    pairs = [(i, i ^ 1) for i in range(count)]
    others = [(i, (((i - 1) % count) ^ 1) + 1) for i in range(count)]
    others = [(i, j % count) for i, j in others]
    return lax.ppermute(even, axis, pairs), lax.ppermute(odd, axis, others)


def shards(adjoint_source, storage, soil_ids, bc_mask, soil_props):
    rows, _, depth = soil_ids.shape
    wide = rows + 2 * MARGIN
    devices = lax.axis_size("gx") * lax.axis_size("gy")
    cells = 2.0 * rows * soil_ids.shape[1] * depth * devices
    own = (rows, *TILE)
    slab = (4 * MARGIN + RIM, *TILE)
    fields, wire, even, odd = call(pack_x_kernel, [(4, *own), own, slab, slab], name="pack_x")(
        soil_props, storage, soil_ids, bc_mask
    )
    xe, xo = exchange("gx", even, odd)
    slab = (3 * wide + 2, *TILE)
    even, odd = call(pack_y_kernel, [slab, slab], name="pack_y")(fields, wire, xe, xo)
    ye, yo = exchange("gy", even, odd)
    buffers = [(wide + 2, 2, *TILE)] * 4
    solved_shapes = [(2, wide, 2, *TILE), (2, wide, *TILE), (2, wide, *TILE)]
    coeff, image, scales, solved, even, odd = call(
        coefficients_kernel,
        [(4, wide, 2, *TILE), (4, *own), (5, *own)] + solved_shapes,
        [(wide + 2, 3, *TILE)] * 2 + [(2, *own)] + buffers,
        name="first_solve",
    )(soil_props, fields, wire, xe, xo, ye, yo, adjoint_source)

    fold_shapes = [(2, wide, 2, *TILE)] + [(2, 2 * MARGIN + 1, *TILE)] * 2
    ye, yo = exchange("gy", even, odd)
    summed, even, odd = call(fold_y_kernel, fold_shapes, name="fold_y")(solved, ye, yo)
    xe, xo = exchange("gx", even, odd)
    halo = [(rows + 2, 2, *TILE)] * 2
    one, power, gram, solved, even, odd = call(
        step_kernel,
        [(2, *own), (2, *own), TILE] + solved_shapes,
        [(2, *own)] + halo + buffers,
        name="second_solve",
    )(summed, xe, xo, coeff, image, scales, adjoint_source)

    ye, yo = exchange("gy", even, odd)
    summed, even, odd = call(fold_y_kernel, fold_shapes, name="fold_y")(solved, ye, yo)
    xe, xo = exchange("gx", even, odd)
    two, second, gram = call(
        last_kernel, [(2, *own), (2, *own), (devices, *TILE)], halo, name="last_image"
    )(summed, xe, xo, image, scales, adjoint_source, power, gram)
    gram = lax.all_to_all(gram, ("gx", "gy"), 0, 0)
    return tuple(
        call(
            functools.partial(combine_kernel, scale=math.sqrt(cells)), [(2, *own)] * 3, name="combine"
        )(gram, adjoint_source, power, second, one, two)
    )


def solution(mesh):
    in_specs = (
        P(None, "gx", "gy", None),
        P(None, "gx", "gy", None),
        P("gx", "gy", None),
        P("gx", "gy"),
        P(),
    )
    out_specs = (P(None, "gx", "gy", None), P(None, "gx", "gy", None), P(None, "gx", "gy", None))
    return jax.shard_map(shards, mesh=mesh, in_specs=in_specs, out_specs=out_specs, check_vma=False)
```

time: 385 us -> 66.8 us (0.17)
  blocking collectives: 256 us -> 9.88 us
  starting transfers between devices: 61.4 us -> 15.9 us
  other arithmetic: 35.3 us -> 0 us
  waiting for transfers between devices: 9.22 us -> 32.8 us
  between operations: 11.3 us -> 0.71 us
  local copies, waits for them, and re-layouts: 10.2 us -> 2.56 us
  Pallas kernels: 0 us -> 4.67 us
    psum x6 -> x0, blocking collectives: 256 us -> none  [the longest x3 134 us: shards(): height = lax.psum(jnp.sum(image * prior), ('gx', 'gy'))]
    ppermute x20 -> x12, starting transfers between devices: 61.4 us -> 15.9 us  [exchange(): return (lax.ppermute(even, axis, pairs), lax.ppermute(odd, axis, others))]
    ppermute x20 -> x12, waiting for transfers between devices: 9.22 us -> 32.8 us  [exchange(): return (lax.ppermute(even, axis, pairs), lax.ppermute(odd, axis, others))]
    all_to_all x0 -> x1, blocking collectives: none -> 9.88 us  [shards(): gram = lax.all_to_all(gram, ('gx', 'gy'), 0, 0)]
    another operation x28 -> x0, other arithmetic: 9.34 us -> none  [the longest x26 9.29 us: apply_adjoint(): return jnp.stack([press_out, heat_out])]
    reduce_sum x6 -> x0, other arithmetic: 9.15 us -> none  [the longest x3 5.82 us: global_length(): return jnp.sqrt(lax.psum(jnp.sum(vector * vector), ('gx', 'gy')) + epsilon)]
    add x41 -> x0, other arithmetic: 6.58 us -> none  [the longest x12 2.58 us: subdomain_solve(): step_p = inverse[0] * remain[0] + inverse[1] * remain[1]]
    slice x41 -> x0, local copies, waits for them, and re-layouts: 4.81 us -> none  [the longest x27 2.92 us: neighbour_list(): below = jnp.pad(middle[:, :, :-1], ((0, 0), (0, 0), (1, 0)))]
  transfers between devices with their start and end apart: 20 -> 12, of which waited for: 9 -> 10; matrix products, arithmetic and copies ran while one was open for 1% -> 0% of each run, Pallas kernels for 0% -> 0%
where the time goes in v1:
time: 66.8 us; the launch traced here: 66.5 us
  waiting for transfers between devices  32.8 us (49%)
  starting transfers between devices  15.9 us (24%)
  blocking collectives  9.88 us (15%)
  Pallas kernels  4.67 us (7%)
  local copies, waits for them, and re-layouts  2.56 us (4%)
  between operations  0.71 us (1%)
    ppermute x12, waiting for transfers between devices, exchange(): return (lax.ppermute(even, axis, pairs), lax.ppermute(odd, axis, others))  32.8 us
    ppermute x12, starting transfers between devices, exchange(): return (lax.ppermute(even, axis, pairs), lax.ppermute(odd, axis, others))  15.9 us
    all_to_all x1, blocking collectives, shards(): gram = lax.all_to_all(gram, ('gx', 'gy'), 0, 0)  9.88 us
    pallas_call x8, Pallas kernels, run(): pl.pallas_call(kernel, out_shape=[jax.ShapeDtypeStruct(shape, F32) for sh...  4.67 us
    unnamed x9, local copies, waits for them, and re-layouts  2.56 us
  transfers between devices with their start and end apart: 12, of which 10 were waited for; matrix products, arithmetic and copies ran while one was open for 0% of the time, Pallas kernels for 0%

profile of v1, /device:TPU:0, one launch (start us, length us, event | category | flops | bytes accessed | tf_op | source)
XLA Modules:
  0.0 66.5 jit_solution(11367710056577584561)
XLA Ops:
  0.6 0.8 %copy.8.bc_ref = s32[16,8]{1,0:T(8,128)S(1)} copy(s32[16,8]{0,1:T(8,128)} %param.8) | data formatting | bytes 1024 | tf_op args[3]
  1.4 0.9 %copy-done.1 = f32[4,16,8,128]{3,2,1,0:T(8,128)S(1)} copy-done((f32[4,16,8,128]{3,2,1,0:T(8,128)S(1)}, f32[4,16,8,128]{3,2,1,0:T(8,128)}, u32[]{:S(2)}) %copy-start.1) | copy-done | bytes 262168
  2.4 0.8 %copy-done.2 = s32[16,8,128]{2,1,0:T(8,128)S(1)} copy-done((s32[16,8,128]{2,1,0:T(8,128)S(1)}, s32[16,8,128]{2,1,0:T(8,128)}, u32[]{:S(2)}) %copy-start.2) | copy-done | bytes 65560
  3.2 0.3 pack_x.1
  3.5 3.0 %collective-permute-start = (f32[21,8,128]{2,1,0:T(8,128)S(1)}, f32[21,8,128]{2,1,0:T(8,128)S(1)}, u32[]{:S(2)}, u32[]{:S(2)}) collective-permute-start(f32[21,8,128]{2,1,0:T(8,128)S(1)} %get-tuple-element.32), channel_id=1, source_target_pairs={{0,8},{8,0},{16,24},{24,16},{1,9},{9,1},{17,25},{25,17},{2,10},{10... | collective-permute-start | bytes 258056 | tf_op jit(solution)/shard_map/ppermute | solution.py:473
  6.5 1.5 %collective-permute-start.1 = (f32[21,8,128]{2,1,0:T(8,128)S(1)}, f32[21,8,128]{2,1,0:T(8,128)S(1)}, u32[]{:S(2)}, u32[]{:S(2)}) collective-permute-start(f32[21,8,128]{2,1,0:T(8,128)S(1)} %get-tuple-element.33), channel_id=1, source_target_pairs={{0,24},{8,16},{16,8},{24,0},{1,25},{9,17},{17,9},{25,1},{2,26},{10... | collective-permute-start | bytes 258056 | tf_op jit(solution)/shard_map/ppermute | solution.py:473
  8.0 1.3 %collective-permute-done.xe_ref = f32[21,8,128]{2,1,0:T(8,128)S(1)} collective-permute-done((f32[21,8,128]{2,1,0:T(8,128)S(1)}, f32[21,8,128]{2,1,0:T(8,128)S(1)}, u32[]{:S(2)}, u32[]{:S(2)}) %collective-permute-start) | collective-permute-done | bytes 86048 | tf_op jit(solution)/shard_map/ppermute | solution.py:473
  9.4 3.0 %collective-permute-done.1.xo_ref = f32[21,8,128]{2,1,0:T(8,128)S(1)} collective-permute-done((f32[21,8,128]{2,1,0:T(8,128)S(1)}, f32[21,8,128]{2,1,0:T(8,128)S(1)}, u32[]{:S(2)}, u32[]{:S(2)}) %collective-permute-start.1) | collective-permute-done | bytes 86048 | tf_op jit(solution)/shard_map/ppermute | solution.py:473
  12.4 0.1 collective-permute-start.2
  12.5 3.7 %collective-permute-start.3 = (f32[74,8,128]{2,1,0:T(8,128)S(1)}, f32[74,8,128]{2,1,0:T(8,128)S(1)}, u32[]{:S(2)}, u32[]{:S(2)}) collective-permute-start(f32[74,8,128]{2,1,0:T(8,128)S(1)} %get-tuple-element.35), channel_id=1, source_target_pairs={{0,7},{1,2},{2,1},{3,4},{4,3},{5,6},{6,5},{7,0},{8,15},{9,10},{10,... | collective-permute-start | bytes 909320 | tf_op jit(solution)/shard_map/ppermute | solution.py:473
  16.2 7.0 %collective-permute-done.3.yo_ref = f32[74,8,128]{2,1,0:T(8,128)S(1)} collective-permute-done((f32[74,8,128]{2,1,0:T(8,128)S(1)}, f32[74,8,128]{2,1,0:T(8,128)S(1)}, u32[]{:S(2)}, u32[]{:S(2)}) %collective-permute-start.3) | collective-permute-done | bytes 303136 | tf_op jit(solution)/shard_map/ppermute | solution.py:473
  23.2 1.9 %first_solve.1 = (f32[4,24,2,8,128]{4,3,2,1,0:T(8,128)S(1)}, f32[4,16,8,128]{3,2,1,0:T(8,128)S(1)}, f32[5,16,8,128]{3,2,1,0:T(8,128)S(1)}, f32[2,24,2,8,128]{4,3...) custom-call(f32[3,16]{1,0:T(4,128)S(1)} %copy-done.3, ...), custom_call_target="tpu_custom_call" | custom-call | tf_op jit(solution)/shard_map/first_solve/pallas_call | solution.py:455
  25.1 0.1 collective-permute-start.4
  25.2 2.5 %collective-permute-start.5 = (f32[2,24,8,128]{3,2,1,0:T(8,128)S(1)}, f32[2,24,8,128]{3,2,1,0:T(8,128)S(1)}, u32[]{:S(2)}, u32[]{:S(2)}) collective-permute-start(f32[2,24,8,128]{3,2,1,0:T(8,128)S(1)} %get-tuple-element.38), channel_id=1, source_target_pairs={{0,7},{1,2},{2,1},{3,4},{4,3},{5,6},{6,5},{7,0},{8,15},{9,10},{10,... | collective-permute-start | bytes 589832 | tf_op jit(solution)/shard_map/ppermute | solution.py:473
  27.7 6.2 %collective-permute-done.5.yo_ref = f32[2,24,8,128]{3,2,1,0:T(8,128)S(1)} collective-permute-done((f32[2,24,8,128]{3,2,1,0:T(8,128)S(1)}, f32[2,24,8,128]{3,2,1,0:T(8,128)S(1)}, u32[]{:S(2)}, u32[]{:S(2)}) %collective-permute-start.5) | collective-permute-done | bytes 196640 | tf_op jit(solution)/shard_map/ppermute | solution.py:473
  33.9 0.1 fold_y.2
  34.0 1.3 %collective-permute-start.6 = (f32[2,9,8,128]{3,2,1,0:T(8,128)S(1)}, f32[2,9,8,128]{3,2,1,0:T(8,128)S(1)}, u32[]{:S(2)}, u32[]{:S(2)}) collective-permute-start(f32[2,9,8,128]{3,2,1,0:T(8,128)S(1)} %get-tuple-element.40), channel_id=1, source_target_pairs={{0,8},{8,0},{16,24},{24,16},{1,9},{9,1},{17,25},{25,17},{2,10},{10... | collective-permute-start | bytes 221192 | tf_op jit(solution)/shard_map/ppermute | solution.py:473
  35.3 1.3 %collective-permute-start.7 = (f32[2,9,8,128]{3,2,1,0:T(8,128)S(1)}, f32[2,9,8,128]{3,2,1,0:T(8,128)S(1)}, u32[]{:S(2)}, u32[]{:S(2)}) collective-permute-start(f32[2,9,8,128]{3,2,1,0:T(8,128)S(1)} %get-tuple-element.41), channel_id=1, source_target_pairs={{0,24},{8,16},{16,8},{24,0},{1,25},{9,17},{17,9},{25,1},{2,26},{10... | collective-permute-start | bytes 221192 | tf_op jit(solution)/shard_map/ppermute | solution.py:473
  36.6 1.8 %collective-permute-done.6.xe_ref = f32[2,9,8,128]{3,2,1,0:T(8,128)S(1)} collective-permute-done((f32[2,9,8,128]{3,2,1,0:T(8,128)S(1)}, f32[2,9,8,128]{3,2,1,0:T(8,128)S(1)}, u32[]{:S(2)}, u32[]{:S(2)}) %collective-permute-start.6) | collective-permute-done | bytes 73760 | tf_op jit(solution)/shard_map/ppermute | solution.py:473
  38.4 2.2 %collective-permute-done.7.xo_ref = f32[2,9,8,128]{3,2,1,0:T(8,128)S(1)} collective-permute-done((f32[2,9,8,128]{3,2,1,0:T(8,128)S(1)}, f32[2,9,8,128]{3,2,1,0:T(8,128)S(1)}, u32[]{:S(2)}, u32[]{:S(2)}) %collective-permute-start.7) | collective-permute-done | bytes 73760 | tf_op jit(solution)/shard_map/ppermute | solution.py:473
  40.6 1.1 %second_solve.1 = (f32[2,16,8,128]{3,2,1,0:T(8,128)S(1)}, f32[2,16,8,128]{3,2,1,0:T(8,128)S(1)}, f32[8,128]{1,0:T(8,128)S(1)}, f32[2,24,2,8,128]{4,3,2,1,0:T(8,1...) custom-call(f32[2,24,2,8,128]{4,3,2,1,0:T(8,128)S(1)} %get-tuple-element.39.summed_ref, ...), custom_call_target="tpu_custom_call" | custom-call | tf_op jit(solution)/shard_map/second_solve/pallas_call | solution.py:455
  41.7 0.1 collective-permute-start.8
  41.8 1.3 %collective-permute-done.8.ye_ref = f32[2,24,8,128]{3,2,1,0:T(8,128)S(1)} collective-permute-done((f32[2,24,8,128]{3,2,1,0:T(8,128)S(1)}, f32[2,24,8,128]{3,2,1,0:T(8,128)S(1)}, u32[]{:S(2)}, u32[]{:S(2)}) %collective-permute-start.8) | collective-permute-done | bytes 196640 | tf_op jit(solution)/shard_map/ppermute | solution.py:473
  43.2 5.6 %collective-permute-done.9.yo_ref = f32[2,24,8,128]{3,2,1,0:T(8,128)S(1)} collective-permute-done((f32[2,24,8,128]{3,2,1,0:T(8,128)S(1)}, f32[2,24,8,128]{3,2,1,0:T(8,128)S(1)}, u32[]{:S(2)}, u32[]{:S(2)}) %collective-permute-start.9) | collective-permute-done | bytes 196640 | tf_op jit(solution)/shard_map/ppermute | solution.py:473
  48.8 0.1 fold_y.3
  48.9 0.8 %collective-permute-start.10 = (f32[2,9,8,128]{3,2,1,0:T(8,128)S(1)}, f32[2,9,8,128]{3,2,1,0:T(8,128)S(1)}, u32[]{:S(2)}, u32[]{:S(2)}) collective-permute-start(f32[2,9,8,128]{3,2,1,0:T(8,128)S(1)} %get-tuple-element.49), channel_id=1, source_target_pairs={{0,8},{8,0},{16,24},{24,16},{1,9},{9,1},{17,25},{25,17},{2,10},{10... | collective-permute-start | bytes 221192 | tf_op jit(solution)/shard_map/ppermute | solution.py:473
  49.7 1.4 %collective-permute-start.11 = (f32[2,9,8,128]{3,2,1,0:T(8,128)S(1)}, f32[2,9,8,128]{3,2,1,0:T(8,128)S(1)}, u32[]{:S(2)}, u32[]{:S(2)}) collective-permute-start(f32[2,9,8,128]{3,2,1,0:T(8,128)S(1)} %get-tuple-element.50), channel_id=1, source_target_pairs={{0,24},{8,16},{16,8},{24,0},{1,25},{9,17},{17,9},{25,1},{2,26},{10... | collective-permute-start | bytes 221192 | tf_op jit(solution)/shard_map/ppermute | solution.py:473
  51.1 3.0 %collective-permute-done.10.xe_ref = f32[2,9,8,128]{3,2,1,0:T(8,128)S(1)} collective-permute-done((f32[2,9,8,128]{3,2,1,0:T(8,128)S(1)}, f32[2,9,8,128]{3,2,1,0:T(8,128)S(1)}, u32[]{:S(2)}, u32[]{:S(2)}) %collective-permute-start.10) | collective-permute-done | bytes 73760 | tf_op jit(solution)/shard_map/ppermute | solution.py:473
  54.1 1.4 %collective-permute-done.11.xo_ref = f32[2,9,8,128]{3,2,1,0:T(8,128)S(1)} collective-permute-done((f32[2,9,8,128]{3,2,1,0:T(8,128)S(1)}, f32[2,9,8,128]{3,2,1,0:T(8,128)S(1)}, u32[]{:S(2)}, u32[]{:S(2)}) %collective-permute-start.11) | collective-permute-done | bytes 73760 | tf_op jit(solution)/shard_map/ppermute | solution.py:473
  55.5 0.2 last_image.1
  55.7 9.9 %all_to_all.5.gram_ref = f32[32,8,128]{2,1,0:T(8,128)S(1)} all-to-all(f32[32,8,128]{2,1,0:T(8,128)S(1)} %get-tuple-element.53), channel_id=1, replica_groups=mesh['gx'=4,'gy'=8] {'gx','gy'}, dimensions={0} | all-to-all | bytes 262144 | tf_op jit(solution)/shard_map/all_to_all | solution.py:517
  65.6 0.9 %combine.1 = (f32[2,16,8,128]{3,2,1,0:T(8,128)}, f32[2,16,8,128]{3,2,1,0:T(8,128)}, f32[2,16,8,128]{3,2,1,0:T(8,128)}) custom-call(f32[32,8,128]{2,1,0:T(8,128)S(1)} %all_to_all.5.gram_ref, f32[2,16,8,128]{3,2,1,0:T(8,128)S(1)} %copy-done, f32[2,16,8,128]{3,2,1,0:T(8,128)S(1)} %get-tuple-element.51.power_ref, ...), custom_call_target="tpu_custom_call" | custom-call | tf_op jit(solution)/shard_map/combine/pallas_call | solution.py:455
  (10 shorter events, 0.1 us)
Async XLA Ops:
  0.6 0.8 %copy-start.3 = (f32[3,16]{1,0:T(4,128)S(1)}, f32[3,16]{1,0:T(4,128)}, u32[]{:S(2)}) copy-start(f32[3,16]{1,0:T(4,128)} %props_ref.3) | copy-start | bytes 580
  1.4 1.0 %copy-start.1 = (f32[4,16,8,128]{3,2,1,0:T(8,128)S(1)}, f32[4,16,8,128]{3,2,1,0:T(8,128)}, u32[]{:S(2)}) copy-start(f32[4,16,8,128]{3,2,1,0:T(8,128)} %storage_ref.1) | copy-start | bytes 786436
  2.4 0.8 %copy-start.2 = (s32[16,8,128]{2,1,0:T(8,128)S(1)}, s32[16,8,128]{2,1,0:T(8,128)}, u32[]{:S(2)}) copy-start(s32[16,8,128]{2,1,0:T(8,128)} %ids_ref.1) | copy-start | bytes 196612
  3.5 5.8 %collective-permute-start = (f32[21,8,128]{2,1,0:T(8,128)S(1)}, f32[21,8,128]{2,1,0:T(8,128)S(1)}, u32[]{:S(2)}, u32[]{:S(2)}) collective-permute-start(f32[21,8,128]{2,1,0:T(8,128)S(1)} %get-tuple-element.32), channel_id=1, source_target_pairs={{0,8},{8,0},{16,24},{24,16},{1,9},{9,1},{17,25},{25,17},{2,10},{10... | collective-permute-start | bytes 258056 | tf_op jit(solution)/shard_map/ppermute | solution.py:473
  6.5 5.8 %collective-permute-start.1 = (f32[21,8,128]{2,1,0:T(8,128)S(1)}, f32[21,8,128]{2,1,0:T(8,128)S(1)}, u32[]{:S(2)}, u32[]{:S(2)}) collective-permute-start(f32[21,8,128]{2,1,0:T(8,128)S(1)} %get-tuple-element.33), channel_id=1, source_target_pairs={{0,24},{8,16},{16,8},{24,0},{1,25},{9,17},{17,9},{25,1},{2,26},{10... | collective-permute-start | bytes 258056 | tf_op jit(solution)/shard_map/ppermute | solution.py:473
  12.3 10.9 %copy-start = (f32[2,16,8,128]{3,2,1,0:T(8,128)S(1)}, f32[2,16,8,128]{3,2,1,0:T(8,128)}, u32[]{:S(2)}) copy-start(f32[2,16,8,128]{3,2,1,0:T(8,128)} %source_ref.7) | copy-start | bytes 393220
  12.4 3.8 %collective-permute-start.2 = (f32[74,8,128]{2,1,0:T(8,128)S(1)}, f32[74,8,128]{2,1,0:T(8,128)S(1)}, u32[]{:S(2)}, u32[]{:S(2)}) collective-permute-start(f32[74,8,128]{2,1,0:T(8,128)S(1)} %get-tuple-element.34), channel_id=1, source_target_pairs={{0,1},{1,0},{2,3},{3,2},{4,5},{5,4},{6,7},{7,6},{8,9},{9,8},{10,11... | collective-permute-start | bytes 909320 | tf_op jit(solution)/shard_map/ppermute | solution.py:473
  12.5 10.7 %collective-permute-start.3 = (f32[74,8,128]{2,1,0:T(8,128)S(1)}, f32[74,8,128]{2,1,0:T(8,128)S(1)}, u32[]{:S(2)}, u32[]{:S(2)}) collective-permute-start(f32[74,8,128]{2,1,0:T(8,128)S(1)} %get-tuple-element.35), channel_id=1, source_target_pairs={{0,7},{1,2},{2,1},{3,4},{4,3},{5,6},{6,5},{7,0},{8,15},{9,10},{10,... | collective-permute-start | bytes 909320 | tf_op jit(solution)/shard_map/ppermute | solution.py:473
  25.1 2.6 %collective-permute-start.4 = (f32[2,24,8,128]{3,2,1,0:T(8,128)S(1)}, f32[2,24,8,128]{3,2,1,0:T(8,128)S(1)}, u32[]{:S(2)}, u32[]{:S(2)}) collective-permute-start(f32[2,24,8,128]{3,2,1,0:T(8,128)S(1)} %get-tuple-element.37), channel_id=1, source_target_pairs={{0,1},{1,0},{2,3},{3,2},{4,5},{5,4},{6,7},{7,6},{8,9},{9,8},{10,11... | collective-permute-start | bytes 589832 | tf_op jit(solution)/shard_map/ppermute | solution.py:473
  25.2 8.7 %collective-permute-start.5 = (f32[2,24,8,128]{3,2,1,0:T(8,128)S(1)}, f32[2,24,8,128]{3,2,1,0:T(8,128)S(1)}, u32[]{:S(2)}, u32[]{:S(2)}) collective-permute-start(f32[2,24,8,128]{3,2,1,0:T(8,128)S(1)} %get-tuple-element.38), channel_id=1, source_target_pairs={{0,7},{1,2},{2,1},{3,4},{4,3},{5,6},{6,5},{7,0},{8,15},{9,10},{10,... | collective-permute-start | bytes 589832 | tf_op jit(solution)/shard_map/ppermute | solution.py:473
  34.0 4.4 %collective-permute-start.6 = (f32[2,9,8,128]{3,2,1,0:T(8,128)S(1)}, f32[2,9,8,128]{3,2,1,0:T(8,128)S(1)}, u32[]{:S(2)}, u32[]{:S(2)}) collective-permute-start(f32[2,9,8,128]{3,2,1,0:T(8,128)S(1)} %get-tuple-element.40), channel_id=1, source_target_pairs={{0,8},{8,0},{16,24},{24,16},{1,9},{9,1},{17,25},{25,17},{2,10},{10... | collective-permute-start | bytes 221192 | tf_op jit(solution)/shard_map/ppermute | solution.py:473
  35.3 5.3 %collective-permute-start.7 = (f32[2,9,8,128]{3,2,1,0:T(8,128)S(1)}, f32[2,9,8,128]{3,2,1,0:T(8,128)S(1)}, u32[]{:S(2)}, u32[]{:S(2)}) collective-permute-start(f32[2,9,8,128]{3,2,1,0:T(8,128)S(1)} %get-tuple-element.41), channel_id=1, source_target_pairs={{0,24},{8,16},{16,8},{24,0},{1,25},{9,17},{17,9},{25,1},{2,26},{10... | collective-permute-start | bytes 221192 | tf_op jit(solution)/shard_map/ppermute | solution.py:473
  41.7 1.5 %collective-permute-start.8 = (f32[2,24,8,128]{3,2,1,0:T(8,128)S(1)}, f32[2,24,8,128]{3,2,1,0:T(8,128)S(1)}, u32[]{:S(2)}, u32[]{:S(2)}) collective-permute-start(f32[2,24,8,128]{3,2,1,0:T(8,128)S(1)} %get-tuple-element.46), channel_id=1, source_target_pairs={{0,1},{1,0},{2,3},{3,2},{4,5},{5,4},{6,7},{7,6},{8,9},{9,8},{10,11... | collective-permute-start | bytes 589832 | tf_op jit(solution)/shard_map/ppermute | solution.py:473
  41.8 7.1 %collective-permute-start.9 = (f32[2,24,8,128]{3,2,1,0:T(8,128)S(1)}, f32[2,24,8,128]{3,2,1,0:T(8,128)S(1)}, u32[]{:S(2)}, u32[]{:S(2)}) collective-permute-start(f32[2,24,8,128]{3,2,1,0:T(8,128)S(1)} %get-tuple-element.47), channel_id=1, source_target_pairs={{0,7},{1,2},{2,1},{3,4},{4,3},{5,6},{6,5},{7,0},{8,15},{9,10},{10,... | collective-permute-start | bytes 589832 | tf_op jit(solution)/shard_map/ppermute | solution.py:473
  48.9 5.2 %collective-permute-start.10 = (f32[2,9,8,128]{3,2,1,0:T(8,128)S(1)}, f32[2,9,8,128]{3,2,1,0:T(8,128)S(1)}, u32[]{:S(2)}, u32[]{:S(2)}) collective-permute-start(f32[2,9,8,128]{3,2,1,0:T(8,128)S(1)} %get-tuple-element.49), channel_id=1, source_target_pairs={{0,8},{8,0},{16,24},{24,16},{1,9},{9,1},{17,25},{25,17},{2,10},{10... | collective-permute-start | bytes 221192 | tf_op jit(solution)/shard_map/ppermute | solution.py:473
  49.7 5.8 %collective-permute-start.11 = (f32[2,9,8,128]{3,2,1,0:T(8,128)S(1)}, f32[2,9,8,128]{3,2,1,0:T(8,128)S(1)}, u32[]{:S(2)}, u32[]{:S(2)}) collective-permute-start(f32[2,9,8,128]{3,2,1,0:T(8,128)S(1)} %get-tuple-element.50), channel_id=1, source_target_pairs={{0,24},{8,16},{16,8},{24,0},{1,25},{9,17},{17,9},{25,1},{2,26},{10... | collective-permute-start | bytes 221192 | tf_op jit(solution)/shard_map/ppermute | solution.py:473

commit v2 on v1

--- a/solution.py
+++ b/solution.py
@@ -466,11 +466,20 @@
 
 
 def exchange(axis, even, odd):
+    n_x, n_y = lax.axis_size("gx"), lax.axis_size("gy")
     count = lax.axis_size(axis)
     pairs = [(i, i ^ 1) for i in range(count)]
-    others = [(i, (((i - 1) % count) ^ 1) + 1) for i in range(count)]
-    others = [(i, j % count) for i, j in others]
-    return lax.ppermute(even, axis, pairs), lax.ppermute(odd, axis, others)
+    others = []
+    for x in range(n_x):
+        for y in range(n_y):
+            place = x if axis == "gx" else y
+            if 0 < place < count - 1:
+                partner = ((place - 1) ^ 1) + 1
+                target = (partner, y) if axis == "gx" else (x, partner)
+            else:
+                target = (x, y ^ 1) if axis == "gx" else (x ^ 1, y)
+            others.append((x * n_y + y, target[0] * n_y + target[1]))
+    return lax.ppermute(even, axis, pairs), lax.ppermute(odd, ("gx", "gy"), others)
 
 
 def shards(adjoint_source, storage, soil_ids, bc_mask, soil_props):

time: 66.8 us -> 57.8 us (0.87)
  waiting for transfers between devices: 32.8 us -> 20.4 us
  blocking collectives: 9.88 us -> 12.7 us
  starting transfers between devices: 15.9 us -> 16.6 us
    ppermute x12, waiting for transfers between devices: 32.8 us -> 20.4 us  [the longest x6 12.1 us: exchange(): lax.ppermute(odd, ('gx', 'gy'), others)]
    all_to_all x1, blocking collectives: 9.88 us -> 12.7 us  [shards(): gram = lax.all_to_all(gram, ('gx', 'gy'), 0, 0)]
    ppermute x12, starting transfers between devices: 15.9 us -> 16.6 us  [the longest x6 9.18 us: exchange(): lax.ppermute(odd, ('gx', 'gy'), others)]
  transfers between devices with their start and end apart: 12 -> 12, of which waited for: 10 -> 6; matrix products, arithmetic and copies ran while one was open for 0% -> 0% of each run, Pallas kernels for 0% -> 0%
where the time goes in v2:
time: 57.8 us; the launch traced here: 57.6 us
  waiting for transfers between devices  20.4 us (35%)
  starting transfers between devices  16.6 us (29%)
  blocking collectives  12.7 us (22%)
  Pallas kernels  4.67 us (8%)
  local copies, waits for them, and re-layouts  2.56 us (4%)
  between operations  0.7 us (1%)
    all_to_all x1, blocking collectives, shards(): gram = lax.all_to_all(gram, ('gx', 'gy'), 0, 0)  12.7 us
    ppermute x6, waiting for transfers between devices, exchange(): lax.ppermute(odd, ('gx', 'gy'), others)  12.1 us
    ppermute x6, starting transfers between devices, exchange(): lax.ppermute(odd, ('gx', 'gy'), others)  9.18 us
    ppermute x6, waiting for transfers between devices, exchange(): lax.ppermute(even, axis, pairs)  8.29 us
    ppermute x6, starting transfers between devices, exchange(): lax.ppermute(even, axis, pairs)  7.39 us
    pallas_call x8, Pallas kernels, run(): pl.pallas_call(kernel, out_shape=[jax.ShapeDtypeStruct(shape, F32) for sh...  4.67 us
    unnamed x9, local copies, waits for them, and re-layouts  2.56 us
  transfers between devices with their start and end apart: 12, of which 6 were waited for; matrix products, arithmetic and copies ran while one was open for 0% of the time, Pallas kernels for 0%

profile of v2, /device:TPU:0, one launch (start us, length us, event | category | flops | bytes accessed | tf_op | source)
XLA Modules:
  0.0 57.6 jit_solution(6474859994173793523)
XLA Ops:
  0.6 0.8 %copy.8.bc_ref = s32[16,8]{1,0:T(8,128)S(1)} copy(s32[16,8]{0,1:T(8,128)} %param.8) | data formatting | bytes 1024 | tf_op args[3]
  1.4 0.9 %copy-done.1 = f32[4,16,8,128]{3,2,1,0:T(8,128)S(1)} copy-done((f32[4,16,8,128]{3,2,1,0:T(8,128)S(1)}, f32[4,16,8,128]{3,2,1,0:T(8,128)}, u32[]{:S(2)}) %copy-start.1) | copy-done | bytes 262168
  2.4 0.8 %copy-done.2 = s32[16,8,128]{2,1,0:T(8,128)S(1)} copy-done((s32[16,8,128]{2,1,0:T(8,128)S(1)}, s32[16,8,128]{2,1,0:T(8,128)}, u32[]{:S(2)}) %copy-start.2) | copy-done | bytes 65560
  3.2 0.3 pack_x.1
  3.5 3.0 %collective-permute-start = (f32[21,8,128]{2,1,0:T(8,128)S(1)}, f32[21,8,128]{2,1,0:T(8,128)S(1)}, u32[]{:S(2)}, u32[]{:S(2)}) collective-permute-start(f32[21,8,128]{2,1,0:T(8,128)S(1)} %get-tuple-element.32), channel_id=1, source_target_pairs={{0,8},{8,0},{16,24},{24,16},{1,9},{9,1},{17,25},{25,17},{2,10},{10... | collective-permute-start | bytes 258056 | tf_op jit(solution)/shard_map/ppermute | solution.py:482
  6.5 0.0 collective-permute-start.1
  6.5 2.5 %collective-permute-done.xe_ref = f32[21,8,128]{2,1,0:T(8,128)S(1)} collective-permute-done((f32[21,8,128]{2,1,0:T(8,128)S(1)}, f32[21,8,128]{2,1,0:T(8,128)S(1)}, u32[]{:S(2)}, u32[]{:S(2)}) %collective-permute-start) | collective-permute-done | bytes 86048 | tf_op jit(solution)/shard_map/ppermute | solution.py:482
  9.1 0.0 collective-permute-done.1.xo_ref
  9.1 0.1 pack_y.1
  9.1 0.1 collective-permute-start.2
  9.2 4.6 %collective-permute-start.3 = (f32[74,8,128]{2,1,0:T(8,128)S(1)}, f32[74,8,128]{2,1,0:T(8,128)S(1)}, u32[]{:S(2)}, u32[]{:S(2)}) collective-permute-start(f32[74,8,128]{2,1,0:T(8,128)S(1)} %get-tuple-element.35), channel_id=1, source_target_pairs={{0,8},{1,2},{2,1},{3,4},{4,3},{5,6},{6,5},{7,15},{8,0},{9,10},{10,... | collective-permute-start | bytes 909320 | tf_op jit(solution)/shard_map/ppermute | solution.py:482
  13.8 4.8 %collective-permute-done.3.yo_ref = f32[74,8,128]{2,1,0:T(8,128)S(1)} collective-permute-done((f32[74,8,128]{2,1,0:T(8,128)S(1)}, f32[74,8,128]{2,1,0:T(8,128)S(1)}, u32[]{:S(2)}, u32[]{:S(2)}) %collective-permute-start.3) | collective-permute-done | bytes 303136 | tf_op jit(solution)/shard_map/ppermute | solution.py:482
  18.6 1.9 %first_solve.1 = (f32[4,24,2,8,128]{4,3,2,1,0:T(8,128)S(1)}, f32[4,16,8,128]{3,2,1,0:T(8,128)S(1)}, f32[5,16,8,128]{3,2,1,0:T(8,128)S(1)}, f32[2,24,2,8,128]{4,3...) custom-call(f32[3,16]{1,0:T(4,128)S(1)} %copy-done.3, ...), custom_call_target="tpu_custom_call" | custom-call | tf_op jit(solution)/shard_map/first_solve/pallas_call | solution.py:455
  20.5 0.1 collective-permute-start.4
  20.6 2.1 %collective-permute-start.5 = (f32[2,24,8,128]{3,2,1,0:T(8,128)S(1)}, f32[2,24,8,128]{3,2,1,0:T(8,128)S(1)}, u32[]{:S(2)}, u32[]{:S(2)}) collective-permute-start(f32[2,24,8,128]{3,2,1,0:T(8,128)S(1)} %get-tuple-element.38), channel_id=1, source_target_pairs={{0,8},{1,2},{2,1},{3,4},{4,3},{5,6},{6,5},{7,15},{8,0},{9,10},{10,... | collective-permute-start | bytes 589832 | tf_op jit(solution)/shard_map/ppermute | solution.py:482
  22.7 0.0 collective-permute-done.4.ye_ref
  22.7 3.6 %collective-permute-done.5.yo_ref = f32[2,24,8,128]{3,2,1,0:T(8,128)S(1)} collective-permute-done((f32[2,24,8,128]{3,2,1,0:T(8,128)S(1)}, f32[2,24,8,128]{3,2,1,0:T(8,128)S(1)}, u32[]{:S(2)}, u32[]{:S(2)}) %collective-permute-start.5) | collective-permute-done | bytes 196640 | tf_op jit(solution)/shard_map/ppermute | solution.py:482
  26.3 0.1 fold_y.2
  26.4 2.1 %collective-permute-start.6 = (f32[2,9,8,128]{3,2,1,0:T(8,128)S(1)}, f32[2,9,8,128]{3,2,1,0:T(8,128)S(1)}, u32[]{:S(2)}, u32[]{:S(2)}) collective-permute-start(f32[2,9,8,128]{3,2,1,0:T(8,128)S(1)} %get-tuple-element.40), channel_id=1, source_target_pairs={{0,8},{8,0},{16,24},{24,16},{1,9},{9,1},{17,25},{25,17},{2,10},{10... | collective-permute-start | bytes 221192 | tf_op jit(solution)/shard_map/ppermute | solution.py:482
  28.5 0.0 collective-permute-start.7
  28.5 3.0 %collective-permute-done.6.xe_ref = f32[2,9,8,128]{3,2,1,0:T(8,128)S(1)} collective-permute-done((f32[2,9,8,128]{3,2,1,0:T(8,128)S(1)}, f32[2,9,8,128]{3,2,1,0:T(8,128)S(1)}, u32[]{:S(2)}, u32[]{:S(2)}) %collective-permute-start.6) | collective-permute-done | bytes 73760 | tf_op jit(solution)/shard_map/ppermute | solution.py:482
  31.5 1.1 %second_solve.1 = (f32[2,16,8,128]{3,2,1,0:T(8,128)S(1)}, f32[2,16,8,128]{3,2,1,0:T(8,128)S(1)}, f32[8,128]{1,0:T(8,128)S(1)}, f32[2,24,2,8,128]{4,3,2,1,0:T(8,1...) custom-call(f32[2,24,2,8,128]{4,3,2,1,0:T(8,128)S(1)} %get-tuple-element.39.summed_ref, ...), custom_call_target="tpu_custom_call" | custom-call | tf_op jit(solution)/shard_map/second_solve/pallas_call | solution.py:455
  32.7 0.1 collective-permute-start.8
  32.7 2.4 %collective-permute-start.9 = (f32[2,24,8,128]{3,2,1,0:T(8,128)S(1)}, f32[2,24,8,128]{3,2,1,0:T(8,128)S(1)}, u32[]{:S(2)}, u32[]{:S(2)}) collective-permute-start(f32[2,24,8,128]{3,2,1,0:T(8,128)S(1)} %get-tuple-element.47), channel_id=1, source_target_pairs={{0,8},{1,2},{2,1},{3,4},{4,3},{5,6},{6,5},{7,15},{8,0},{9,10},{10,... | collective-permute-start | bytes 589832 | tf_op jit(solution)/shard_map/ppermute | solution.py:482
  35.2 0.0 collective-permute-done.8.ye_ref
  35.2 3.6 %collective-permute-done.9.yo_ref = f32[2,24,8,128]{3,2,1,0:T(8,128)S(1)} collective-permute-done((f32[2,24,8,128]{3,2,1,0:T(8,128)S(1)}, f32[2,24,8,128]{3,2,1,0:T(8,128)S(1)}, u32[]{:S(2)}, u32[]{:S(2)}) %collective-permute-start.9) | collective-permute-done | bytes 196640 | tf_op jit(solution)/shard_map/ppermute | solution.py:482
  38.8 0.1 fold_y.3
  38.9 2.1 %collective-permute-start.10 = (f32[2,9,8,128]{3,2,1,0:T(8,128)S(1)}, f32[2,9,8,128]{3,2,1,0:T(8,128)S(1)}, u32[]{:S(2)}, u32[]{:S(2)}) collective-permute-start(f32[2,9,8,128]{3,2,1,0:T(8,128)S(1)} %get-tuple-element.49), channel_id=1, source_target_pairs={{0,8},{8,0},{16,24},{24,16},{1,9},{9,1},{17,25},{25,17},{2,10},{10... | collective-permute-start | bytes 221192 | tf_op jit(solution)/shard_map/ppermute | solution.py:482
  41.0 2.7 %collective-permute-done.10.xe_ref = f32[2,9,8,128]{3,2,1,0:T(8,128)S(1)} collective-permute-done((f32[2,9,8,128]{3,2,1,0:T(8,128)S(1)}, f32[2,9,8,128]{3,2,1,0:T(8,128)S(1)}, u32[]{:S(2)}, u32[]{:S(2)}) %collective-permute-start.10) | collective-permute-done | bytes 73760 | tf_op jit(solution)/shard_map/ppermute | solution.py:482
  43.7 0.2 last_image.1
  43.9 12.7 %all_to_all.5.gram_ref = f32[32,8,128]{2,1,0:T(8,128)S(1)} all-to-all(f32[32,8,128]{2,1,0:T(8,128)S(1)} %get-tuple-element.53), channel_id=1, replica_groups=mesh['gx'=4,'gy'=8] {'gx','gy'}, dimensions={0} | all-to-all | bytes 262144 | tf_op jit(solution)/shard_map/all_to_all | solution.py:526
  56.6 0.9 %combine.1 = (f32[2,16,8,128]{3,2,1,0:T(8,128)}, f32[2,16,8,128]{3,2,1,0:T(8,128)}, f32[2,16,8,128]{3,2,1,0:T(8,128)}) custom-call(f32[32,8,128]{2,1,0:T(8,128)S(1)} %all_to_all.5.gram_ref, f32[2,16,8,128]{3,2,1,0:T(8,128)S(1)} %copy-done, f32[2,16,8,128]{3,2,1,0:T(8,128)S(1)} %get-tuple-element.51.power_ref, ...), custom_call_target="tpu_custom_call" | custom-call | tf_op jit(solution)/shard_map/combine/pallas_call | solution.py:455
  (10 shorter events, 0.0 us)
Async XLA Ops:
  0.6 0.8 %copy-start.3 = (f32[3,16]{1,0:T(4,128)S(1)}, f32[3,16]{1,0:T(4,128)}, u32[]{:S(2)}) copy-start(f32[3,16]{1,0:T(4,128)} %props_ref.3) | copy-start | bytes 580
  1.4 1.0 %copy-start.1 = (f32[4,16,8,128]{3,2,1,0:T(8,128)S(1)}, f32[4,16,8,128]{3,2,1,0:T(8,128)}, u32[]{:S(2)}) copy-start(f32[4,16,8,128]{3,2,1,0:T(8,128)} %storage_ref.1) | copy-start | bytes 786436
  2.4 0.8 %copy-start.2 = (s32[16,8,128]{2,1,0:T(8,128)S(1)}, s32[16,8,128]{2,1,0:T(8,128)}, u32[]{:S(2)}) copy-start(s32[16,8,128]{2,1,0:T(8,128)} %ids_ref.1) | copy-start | bytes 196612
  3.5 5.5 %collective-permute-start = (f32[21,8,128]{2,1,0:T(8,128)S(1)}, f32[21,8,128]{2,1,0:T(8,128)S(1)}, u32[]{:S(2)}, u32[]{:S(2)}) collective-permute-start(f32[21,8,128]{2,1,0:T(8,128)S(1)} %get-tuple-element.32), channel_id=1, source_target_pairs={{0,8},{8,0},{16,24},{24,16},{1,9},{9,1},{17,25},{25,17},{2,10},{10... | collective-permute-start | bytes 258056 | tf_op jit(solution)/shard_map/ppermute | solution.py:482
  6.5 2.5 %collective-permute-start.1 = (f32[21,8,128]{2,1,0:T(8,128)S(1)}, f32[21,8,128]{2,1,0:T(8,128)S(1)}, u32[]{:S(2)}, u32[]{:S(2)}) collective-permute-start(f32[21,8,128]{2,1,0:T(8,128)S(1)} %get-tuple-element.33), channel_id=1, source_target_pairs={{0,1},{1,0},{2,3},{3,2},{4,5},{5,4},{6,7},{7,6},{8,16},{9,17},{10,... | collective-permute-start | bytes 258056 | tf_op jit(solution)/shard_map/ppermute | solution.py:482
  9.1 9.5 %copy-start = (f32[2,16,8,128]{3,2,1,0:T(8,128)S(1)}, f32[2,16,8,128]{3,2,1,0:T(8,128)}, u32[]{:S(2)}) copy-start(f32[2,16,8,128]{3,2,1,0:T(8,128)} %source_ref.7) | copy-start | bytes 393220
  9.1 4.7 %collective-permute-start.2 = (f32[74,8,128]{2,1,0:T(8,128)S(1)}, f32[74,8,128]{2,1,0:T(8,128)S(1)}, u32[]{:S(2)}, u32[]{:S(2)}) collective-permute-start(f32[74,8,128]{2,1,0:T(8,128)S(1)} %get-tuple-element.34), channel_id=1, source_target_pairs={{0,1},{1,0},{2,3},{3,2},{4,5},{5,4},{6,7},{7,6},{8,9},{9,8},{10,11... | collective-permute-start | bytes 909320 | tf_op jit(solution)/shard_map/ppermute | solution.py:482
  9.2 9.4 %collective-permute-start.3 = (f32[74,8,128]{2,1,0:T(8,128)S(1)}, f32[74,8,128]{2,1,0:T(8,128)S(1)}, u32[]{:S(2)}, u32[]{:S(2)}) collective-permute-start(f32[74,8,128]{2,1,0:T(8,128)S(1)} %get-tuple-element.35), channel_id=1, source_target_pairs={{0,8},{1,2},{2,1},{3,4},{4,3},{5,6},{6,5},{7,15},{8,0},{9,10},{10,... | collective-permute-start | bytes 909320 | tf_op jit(solution)/shard_map/ppermute | solution.py:482
  20.5 2.2 %collective-permute-start.4 = (f32[2,24,8,128]{3,2,1,0:T(8,128)S(1)}, f32[2,24,8,128]{3,2,1,0:T(8,128)S(1)}, u32[]{:S(2)}, u32[]{:S(2)}) collective-permute-start(f32[2,24,8,128]{3,2,1,0:T(8,128)S(1)} %get-tuple-element.37), channel_id=1, source_target_pairs={{0,1},{1,0},{2,3},{3,2},{4,5},{5,4},{6,7},{7,6},{8,9},{9,8},{10,11... | collective-permute-start | bytes 589832 | tf_op jit(solution)/shard_map/ppermute | solution.py:482
  20.6 5.8 %collective-permute-start.5 = (f32[2,24,8,128]{3,2,1,0:T(8,128)S(1)}, f32[2,24,8,128]{3,2,1,0:T(8,128)S(1)}, u32[]{:S(2)}, u32[]{:S(2)}) collective-permute-start(f32[2,24,8,128]{3,2,1,0:T(8,128)S(1)} %get-tuple-element.38), channel_id=1, source_target_pairs={{0,8},{1,2},{2,1},{3,4},{4,3},{5,6},{6,5},{7,15},{8,0},{9,10},{10,... | collective-permute-start | bytes 589832 | tf_op jit(solution)/shard_map/ppermute | solution.py:482
  26.4 5.1 %collective-permute-start.6 = (f32[2,9,8,128]{3,2,1,0:T(8,128)S(1)}, f32[2,9,8,128]{3,2,1,0:T(8,128)S(1)}, u32[]{:S(2)}, u32[]{:S(2)}) collective-permute-start(f32[2,9,8,128]{3,2,1,0:T(8,128)S(1)} %get-tuple-element.40), channel_id=1, source_target_pairs={{0,8},{8,0},{16,24},{24,16},{1,9},{9,1},{17,25},{25,17},{2,10},{10... | collective-permute-start | bytes 221192 | tf_op jit(solution)/shard_map/ppermute | solution.py:482
  28.5 3.0 %collective-permute-start.7 = (f32[2,9,8,128]{3,2,1,0:T(8,128)S(1)}, f32[2,9,8,128]{3,2,1,0:T(8,128)S(1)}, u32[]{:S(2)}, u32[]{:S(2)}) collective-permute-start(f32[2,9,8,128]{3,2,1,0:T(8,128)S(1)} %get-tuple-element.41), channel_id=1, source_target_pairs={{0,1},{1,0},{2,3},{3,2},{4,5},{5,4},{6,7},{7,6},{8,16},{9,17},{10,... | collective-permute-start | bytes 221192 | tf_op jit(solution)/shard_map/ppermute | solution.py:482
  32.7 2.5 %collective-permute-start.8 = (f32[2,24,8,128]{3,2,1,0:T(8,128)S(1)}, f32[2,24,8,128]{3,2,1,0:T(8,128)S(1)}, u32[]{:S(2)}, u32[]{:S(2)}) collective-permute-start(f32[2,24,8,128]{3,2,1,0:T(8,128)S(1)} %get-tuple-element.46), channel_id=1, source_target_pairs={{0,1},{1,0},{2,3},{3,2},{4,5},{5,4},{6,7},{7,6},{8,9},{9,8},{10,11... | collective-permute-start | bytes 589832 | tf_op jit(solution)/shard_map/ppermute | solution.py:482
  32.7 6.1 %collective-permute-start.9 = (f32[2,24,8,128]{3,2,1,0:T(8,128)S(1)}, f32[2,24,8,128]{3,2,1,0:T(8,128)S(1)}, u32[]{:S(2)}, u32[]{:S(2)}) collective-permute-start(f32[2,24,8,128]{3,2,1,0:T(8,128)S(1)} %get-tuple-element.47), channel_id=1, source_target_pairs={{0,8},{1,2},{2,1},{3,4},{4,3},{5,6},{6,5},{7,15},{8,0},{9,10},{10,... | collective-permute-start | bytes 589832 | tf_op jit(solution)/shard_map/ppermute | solution.py:482
  38.9 4.8 %collective-permute-start.10 = (f32[2,9,8,128]{3,2,1,0:T(8,128)S(1)}, f32[2,9,8,128]{3,2,1,0:T(8,128)S(1)}, u32[]{:S(2)}, u32[]{:S(2)}) collective-permute-start(f32[2,9,8,128]{3,2,1,0:T(8,128)S(1)} %get-tuple-element.49), channel_id=1, source_target_pairs={{0,8},{8,0},{16,24},{24,16},{1,9},{9,1},{17,25},{25,17},{2,10},{10... | collective-permute-start | bytes 221192 | tf_op jit(solution)/shard_map/ppermute | solution.py:482
  41.0 2.7 %collective-permute-start.11 = (f32[2,9,8,128]{3,2,1,0:T(8,128)S(1)}, f32[2,9,8,128]{3,2,1,0:T(8,128)S(1)}, u32[]{:S(2)}, u32[]{:S(2)}) collective-permute-start(f32[2,9,8,128]{3,2,1,0:T(8,128)S(1)} %get-tuple-element.50), channel_id=1, source_target_pairs={{0,1},{1,0},{2,3},{3,2},{4,5},{5,4},{6,7},{7,6},{8,16},{9,17},{10,... | collective-permute-start | bytes 221192 | tf_op jit(solution)/shard_map/ppermute | solution.py:482

commit v3 on v2

--- a/solution.py
+++ b/solution.py
@@ -53,12 +53,6 @@
     return own_sum, side_sum
 
 
-def along_y_own(own, side, row):
-    up = jnp.where(row == 7, up_y(side), up_y(own))
-    down = jnp.where(row == 0, down_y(side), down_y(own))
-    return up + down
-
-
 def position(axis):
     place = lax.axis_index(axis)
     first = lax.rem(place, 2) == 0
@@ -80,20 +74,25 @@
     return [jnp.broadcast_to(wide[k : k + 1], TILE) for k in range(3)]
 
 
-def pack_x_kernel(props_ref, storage_ref, ids_ref, bc_ref, fields_ref, wire_ref, even_ref, odd_ref):
+def pack_x_kernel(
+    props_hbm, storage_hbm, ids_hbm, bc_hbm, fields_ref, wire_ref, even_ref, odd_ref,
+    props_ref, storage_ref, ids_ref, bc_ref, sems,
+):
+    places = ((ids_hbm, ids_ref), (storage_hbm, storage_ref), (props_hbm, props_ref), (bc_hbm, bc_ref))
+    copies = [pltpu.make_async_copy(src, dst, sems.at[k]) for k, (src, dst) in enumerate(places)]
+    for copy in copies:
+        copy.start()
     rows = ids_ref.shape[0]
+    spot = lane()
+    for copy in copies:
+        copy.wait()
     tables = wide_tables(props_ref)
-    row, spot = sublane(), lane()
-    diagonal = row == spot
     for x in range(rows):
         wire = (ids_ref[x] + 1).astype(F32)
         wire_ref[x] = wire
         kp = lookup(tables[0], wire)
         carried = lookup(tables[2], wire)
-        line = jnp.concatenate(
-            [bc_ref[pl.ds(x, 1), :].astype(F32), jnp.zeros((1, LANE - SUB), F32)], axis=1
-        )
-        held = jnp.sum(jnp.where(diagonal, jnp.broadcast_to(line, TILE), 0.0), axis=1, keepdims=True)
+        held = jnp.broadcast_to(bc_ref[:, x : x + 1].astype(F32), TILE)
         bound = jnp.where(spot == LANE - 1, 2.0 * kp * held, 0.0)
         press = storage_ref[0, x]
         lower = storage_ref[1, x]
@@ -138,20 +137,37 @@
     return fields, wire
 
 
-def pack_y_kernel(fields_ref, wire_ref, xe_ref, xo_ref, even_ref, odd_ref):
+def rim_rows(even_ref, odd_ref, base, tiles, rows_even, rows_odd):
+    for j, (tile_ref, index) in enumerate(tiles):
+        line = (base + j // SUB, pl.ds(j % SUB, 1))
+        even_ref[line] = tile_ref[(*index, pl.ds(rows_even, 1))]
+        odd_ref[line] = tile_ref[(*index, pl.ds(rows_odd, 1))]
+
+
+def pack_y_kernel(fields_ref, wire_ref, xe_ref, xo_ref, even_ref, odd_ref, all_wire_ref):
     fields, wire = widen_x(fields_ref, wire_ref, xe_ref, xo_ref)
     wide = len(fields[0])
     first, _, _ = position("gy")
     even_low = (sublane() < 4) != first
+
+    def put(spot, one, other):
+        other = half_turn(other)
+        even_ref[spot] = jnp.where(even_low, one, other)
+        odd_ref[spot] = jnp.where(even_low, other, one)
+
     for pair in range(2):
         for i in range(wide):
-            one = fields[2 * pair][i]
-            other = half_turn(fields[2 * pair + 1][i])
-            even_ref[pair * wide + i] = jnp.where(even_low, one, other)
-            odd_ref[pair * wide + i] = jnp.where(even_low, other, one)
-    for j in range(wide + 2):
-        even_ref[2 * wide + j] = wire[j]
-        odd_ref[2 * wide + j] = wire[j]
+            put(pair * wide + i, fields[2 * pair][i], fields[2 * pair + 1][i])
+    half = wide // 2 + 1
+    for j in range(half):
+        put(2 * wide + j, wire[j], wire[j + half])
+    for j in range(2 * half):
+        all_wire_ref[j] = wire[j]
+    rows_even, rows_odd = jnp.where(first, 3, 4), jnp.where(first, 4, 3)
+    spots = [(all_wire_ref, (j,)) for j in range(2 * half)]
+    last = even_ref.shape[0] - 1
+    even_ref[last] = odd_ref[last] = jnp.zeros(TILE, F32)
+    rim_rows(even_ref, odd_ref, 2 * wide + half, spots, rows_even, rows_odd)
 
 
 def sweep_row(q_ref, t_ref, coeff_ref, j, row, spot, rhs):
@@ -177,7 +193,7 @@
     return out
 
 
-def subdomain_sweeps(rhs_ref, coeff_ref, solved_ref, even_ref, odd_ref, buffers, rows):
+def subdomain_sweeps(rhs_ref, coeff_ref, solved_ref, rims_ref, even_ref, odd_ref, buffers, rows):
     row, spot = sublane(), lane()
     wide = rows + 2 * MARGIN
     zero = jnp.zeros(TILE, F32)
@@ -204,19 +220,27 @@
                     following[0][j, tile] = out[tile][0]
                     following[1][j, tile] = out[tile][1]
             else:
-                for k in range(2):
-                    own, side = out[0][k], out[1][k]
-                    solved_ref[k, j - 1, 0] = own
-                    solved_ref[k, j - 1, 1] = side
-                    even_ref[k, j - 1] = jnp.where(even_low, own, side)
-                    odd_ref[k, j - 1] = jnp.where(even_low, side, own)
+                i = j - 1
+                (own_q, own_t), (side_q, side_t) = out
+                solved_ref[0, i], solved_ref[1, i] = own_q, own_t
+                turned = half_turn(side_t)
+                even_ref[i] = jnp.where(even_low, turned, side_q)
+                odd_ref[i] = jnp.where(even_low, side_q, turned)
+                for k, side in enumerate((side_q, side_t)):
+                    line = (i // SUB, pl.ds(i % SUB, 1))
+                    rims_ref[(2 * k, *line)] = side[7:8]
+                    rims_ref[(2 * k + 1, *line)] = side[0:1]
         current, following = following, current
+    rows_even, rows_odd = jnp.where(first, 7, 0), jnp.where(first, 0, 7)
+    for k in range(2):
+        spots = [(solved_ref, (k, i)) for i in range(wide)]
+        rim_rows(even_ref, odd_ref, wide + k * (wide // SUB), spots, rows_even, rows_odd)
 
 
 def coefficients_kernel(
     props_ref, fields_ref, wire_ref, xe_ref, xo_ref, ye_ref, yo_ref, source_ref,
-    coeff_ref, image_ref, scale_ref, solved_ref, even_ref, odd_ref,
-    gp_ref, gt_ref, rhs_ref, *buffers,
+    coeff_ref, image_ref, scale_ref, solved_ref, rims_ref, even_ref, odd_ref,
+    gp_ref, gt_ref, beyond_ref, rhs_ref, *buffers,
 ):
     rows = wire_ref.shape[0]
     wide = rows + 2 * MARGIN
@@ -225,19 +249,25 @@
     roots = [jnp.sqrt(jnp.maximum(tables[0], 0.0)), jnp.sqrt(jnp.maximum(tables[1], 0.0))]
     fields, wire = widen_x(fields_ref, wire_ref, xe_ref, xo_ref)
     first, has_low, has_high = position("gy")
-    out_wire = []
-    for j in range(wide + 2):
+    half = wide // 2 + 1
+    sides = []
+    for j in range(half):
         low, high = from_sides(first, ye_ref[2 * wide + j], yo_ref[2 * wide + j])
         low = jnp.where(has_low, low, 0.0)
         high = jnp.where(has_high, high, 0.0)
-        own = wire[j]
-        side = jnp.where(row < 4, high, low)
-        beyond = jnp.where(row < 4, low, high)
-        out_wire.append((own, side))
+        sides.append((jnp.where(row < 4, high, low), half_turn(jnp.where(row < 4, low, high))))
+    sides = [side[0] for side in sides] + [side[1] for side in sides]
+    for tile in range(beyond_ref.shape[2]):
+        ends = from_sides(first, ye_ref[2 * wide + half + tile], yo_ref[2 * wide + half + tile])
+        for end, (there, value) in enumerate(zip((has_low, has_high), ends)):
+            value = jnp.where(there, value, 0.0)
+            for g in range(2):
+                beyond_ref[g, end, tile] = lookup(roots[g], value)
+    out_wire = list(zip(wire, sides))
+    for j in range(wide + 2):
         for g, ref in enumerate((gp_ref, gt_ref)):
-            ref[j, 0] = lookup(roots[g], own)
-            ref[j, 1] = lookup(roots[g], side)
-            ref[j, 2] = lookup(roots[g], beyond)
+            ref[j, 0] = lookup(roots[g], wire[j])
+            ref[j, 1] = lookup(roots[g], sides[j])
     for i in range(wide):
         j = i + 1
         stores = []
@@ -246,9 +276,11 @@
             stores.append(jnp.where(row < 4, high, low))
             stores.append(half_turn(jnp.where(row < 4, low, high)))
         diagonals = []
-        for ref in (gp_ref, gt_ref):
-            beyond = ref[j, 2]
-            own_sum, side_sum = along_y(ref[j, 0], ref[j, 1], row, up_y(beyond), down_y(beyond))
+        for g, ref in enumerate((gp_ref, gt_ref)):
+            last_down, last_up = (
+                jnp.broadcast_to(beyond_ref[g, end, j // SUB, pl.ds(j % SUB, 1)], TILE) for end in range(2)
+            )
+            own_sum, side_sum = along_y(ref[j, 0], ref[j, 1], row, last_up, last_down)
             own_sum = own_sum + along_z(ref[j, 0], spot) + (ref[j - 1, 0] + ref[j + 1, 0])
             side_sum = side_sum + along_z(ref[j, 1], spot) + (ref[j - 1, 1] + ref[j + 1, 1])
             diagonals.append((ref[j, 0] * own_sum, ref[j, 1] * side_sum))
@@ -282,61 +314,89 @@
                 scale_ref[4, x] = lookup(tables[2], out_wire[j][0])
                 rhs_ref[0, x] = source_ref[0, x] * over_p
                 rhs_ref[1, x] = source_ref[1, x] * over_t
-    subdomain_sweeps(rhs_ref, coeff_ref, solved_ref, even_ref, odd_ref, buffers, rows)
-
-
-def fold_y_kernel(solved_ref, ye_ref, yo_ref, summed_ref, even_ref, odd_ref):
+    subdomain_sweeps(rhs_ref, coeff_ref, solved_ref, rims_ref, even_ref, odd_ref, buffers, rows)
+
+
+def fold_y_kernel(solved_ref, rims_ref, ye_ref, yo_ref, summed_ref, edges_ref, even_ref, odd_ref):
     wide = solved_ref.shape[1]
     row = sublane()
     first, has_low, has_high = position("gy")
+    for i in range(wide):
+        low, high = from_sides(first, ye_ref[i], yo_ref[i])
+        low = jnp.where(has_low, low, 0.0)
+        high = jnp.where(has_high, high, 0.0)
+        summed_ref[0, i] = solved_ref[0, i] + jnp.where(row < 4, low, high)
+        summed_ref[1, i] = solved_ref[1, i] + half_turn(jnp.where(row < 4, high, low))
+    count = wide // SUB
     for k in range(2):
-        for i in range(wide):
-            low, high = from_sides(first, ye_ref[k, i], yo_ref[k, i])
-            low = jnp.where(has_low, low, 0.0)
-            high = jnp.where(has_high, high, 0.0)
-            summed_ref[k, i, 0] = solved_ref[k, i, 0] + jnp.where(row < 4, low, high)
-            summed_ref[k, i, 1] = solved_ref[k, i, 1] + jnp.where(row < 4, high, low)
+        for tile in range(count):
+            spot = wide + k * count + tile
+            low, high = from_sides(first, ye_ref[spot], yo_ref[spot])
+            edges_ref[2 * k, tile] = rims_ref[2 * k, tile] + jnp.where(has_low, low, 0.0)
+            edges_ref[2 * k + 1, tile] = rims_ref[2 * k + 1, tile] + jnp.where(has_high, high, 0.0)
     first, _, _ = position("gx")
     margin_even = jnp.where(first, wide - MARGIN, 0)
     margin_odd = jnp.where(first, 0, wide - MARGIN)
     rim_even = jnp.where(first, wide - MARGIN - 1, MARGIN)
     rim_odd = jnp.where(first, MARGIN, wide - MARGIN - 1)
     for k in range(2):
+        base = k * (MARGIN + 2)
         for ref, margin, rim in ((even_ref, margin_even, rim_even), (odd_ref, margin_odd, rim_odd)):
-            for tile in range(2):
-                ref[k, pl.ds(tile * MARGIN, MARGIN)] = summed_ref[k, pl.ds(margin, MARGIN), tile]
-            ref[k, 2 * MARGIN] = summed_ref[k, rim, 0]
-
-
-def fold_x(summed_ref, xe_ref, xo_ref, field_refs):
+            ref[pl.ds(base, MARGIN)] = summed_ref[k, pl.ds(margin, MARGIN)]
+            ref[base + MARGIN] = summed_ref[k, rim]
+        to_low = jnp.where(row < 4, edges_ref[2 * k, 0], half_turn(edges_ref[2 * k + 1, 0]))
+        last = count - 1
+        to_high = jnp.where(row < 4, half_turn(edges_ref[2 * k + 1, last]), edges_ref[2 * k, last])
+        even_ref[base + MARGIN + 1] = jnp.where(first, to_high, to_low)
+        odd_ref[base + MARGIN + 1] = jnp.where(first, to_low, to_high)
+
+
+def fold_x(summed_ref, edges_ref, xe_ref, xo_ref, field_refs, edge_ref):
     wide = summed_ref.shape[1]
     rows = wide - 2 * MARGIN
+    row = sublane()
     first, has_low, has_high = position("gx")
     for k in range(2):
-        low, high = from_sides(first, xe_ref[k], xo_ref[k])
+        base = k * (MARGIN + 2)
+        low, high = from_sides(first, xe_ref[pl.ds(base, MARGIN + 2)], xo_ref[pl.ds(base, MARGIN + 2)])
         low = jnp.where(has_low, low, 0.0)
         high = jnp.where(has_high, high, 0.0)
         for x in range(-1, rows + 1):
-            for tile in range(2):
-                value = summed_ref[k, x + MARGIN, tile]
-                if 0 <= x < MARGIN:
-                    value = value + low[tile * MARGIN + x]
-                if rows - MARGIN <= x < rows:
-                    value = value + high[tile * MARGIN + x - (rows - MARGIN)]
-                if tile == 0 and x == -1:
-                    value = value + low[2 * MARGIN]
-                if tile == 0 and x == rows:
-                    value = value + high[2 * MARGIN]
-                field_refs[k][x + 1, tile] = value
-
-
-def image_row(field_refs, image_ref, x, row, spot):
+            value = summed_ref[k, x + MARGIN]
+            if 0 <= x < MARGIN:
+                value = value + low[x]
+            if rows - MARGIN <= x < rows:
+                value = value + high[x - (rows - MARGIN)]
+            if x == -1:
+                value = value + low[MARGIN]
+            if x == rows:
+                value = value + high[MARGIN]
+            field_refs[k][x + 1] = value
+        from_low, from_high = low[MARGIN + 1], high[MARGIN + 1]
+        last = edge_ref.shape[1] - 1
+        for end in range(2):
+            for tile in range(last + 1):
+                value = edges_ref[2 * k + end, tile]
+                if tile == 0:
+                    part = half_turn(from_low) if end == 1 else from_low
+                    value = value + jnp.where(row < 4, 0.0, part)
+                if tile == last:
+                    part = half_turn(from_high) if end == 1 else from_high
+                    value = value + jnp.where(row < 4, part, 0.0)
+                edge_ref[2 * k + end, tile] = value
+
+
+def image_row(field_refs, edge_ref, image_ref, x, row, spot):
     sums = []
-    for ref in field_refs:
-        own = ref[x + 1, 0]
-        total = along_y_own(own, ref[x + 1, 1], row) + along_z(own, spot)
-        sums.append(total + (ref[x, 0] + ref[x + 2, 0]))
-    flow, heat = field_refs[0][x + 1, 0], field_refs[1][x + 1, 0]
+    i = x + MARGIN
+    for k, ref in enumerate(field_refs):
+        own = ref[x + 1]
+        down, up = (
+            jnp.broadcast_to(edge_ref[2 * k + end, i // SUB, pl.ds(i % SUB, 1)], TILE) for end in range(2)
+        )
+        total = jnp.where(row == 7, up, up_y(own)) + jnp.where(row == 0, down, down_y(own))
+        sums.append(total + along_z(own, spot) + (ref[x] + ref[x + 2]))
+    flow, heat = field_refs[0][x + 1], field_refs[1][x + 1]
     return (
         image_ref[0, x] * flow + image_ref[1, x] * heat - sums[0],
         image_ref[2, x] * flow + image_ref[3, x] * heat - sums[1],
@@ -344,9 +404,9 @@
 
 
 def keep_direction(direction_ref, scale_ref, field_refs, x):
-    heat = field_refs[1][x + 1, 0] * scale_ref[3, x]
+    heat = field_refs[1][x + 1] * scale_ref[3, x]
     direction_ref[1, x] = heat
-    direction_ref[0, x] = field_refs[0][x + 1, 0] * scale_ref[2, x] - scale_ref[4, x] * heat
+    direction_ref[0, x] = field_refs[0][x + 1] * scale_ref[2, x] - scale_ref[4, x] * heat
 
 
 def gram_rows(pairs, row, offset):
@@ -358,18 +418,18 @@
 
 
 def step_kernel(
-    summed_ref, xe_ref, xo_ref, coeff_ref, image_ref, scale_ref, source_ref,
-    direction_ref, power_ref, gram_ref, solved_ref, even_ref, odd_ref,
-    rhs_ref, q_ref, t_ref, *buffers,
+    summed_ref, edges_ref, xe_ref, xo_ref, coeff_ref, image_ref, scale_ref, source_ref,
+    direction_ref, power_ref, gram_ref, solved_ref, rims_ref, even_ref, odd_ref,
+    rhs_ref, q_ref, t_ref, edge_ref, *buffers,
 ):
     rows = source_ref.shape[1]
     row, spot = sublane(), lane()
     fields = (q_ref, t_ref)
-    fold_x(summed_ref, xe_ref, xo_ref, fields)
+    fold_x(summed_ref, edges_ref, xe_ref, xo_ref, fields, edge_ref)
     products = [jnp.zeros(TILE, F32) for _ in range(3)]
     for x in range(rows):
         keep_direction(direction_ref, scale_ref, fields, x)
-        for k, part in enumerate(image_row(fields, image_ref, x, row, spot)):
+        for k, part in enumerate(image_row(fields, edge_ref, image_ref, x, row, spot)):
             source = source_ref[k, x]
             scaled = part - source * scale_ref[2 + k, x]
             power = scaled * scale_ref[k, x]
@@ -379,41 +439,41 @@
             products[1] = products[1] + source * power
             products[2] = products[2] + power * power
     gram_ref[...] = gram_rows(products, row, 0)
-    subdomain_sweeps(rhs_ref, coeff_ref, solved_ref, even_ref, odd_ref, buffers, rows)
+    subdomain_sweeps(rhs_ref, coeff_ref, solved_ref, rims_ref, even_ref, odd_ref, buffers, rows)
 
 
 def last_kernel(
-    summed_ref, xe_ref, xo_ref, image_ref, scale_ref, source_ref, power_ref, gram_in_ref,
-    direction_ref, second_ref, gram_ref, q_ref, t_ref,
+    summed_ref, edges_ref, xe_ref, xo_ref, image_ref, scale_ref, source_ref, power_ref, gram_in_ref,
+    direction_ref, second_ref, gram_ref, q_ref, t_ref, edge_ref,
 ):
     rows = source_ref.shape[1]
     row, spot = sublane(), lane()
     fields = (q_ref, t_ref)
-    fold_x(summed_ref, xe_ref, xo_ref, fields)
+    fold_x(summed_ref, edges_ref, xe_ref, xo_ref, fields, edge_ref)
     products = [jnp.zeros(TILE, F32) for _ in range(3)]
     for x in range(rows):
         keep_direction(direction_ref, scale_ref, fields, x)
-        for k, part in enumerate(image_row(fields, image_ref, x, row, spot)):
+        for k, part in enumerate(image_row(fields, edge_ref, image_ref, x, row, spot)):
             power = power_ref[k, x]
             second = part * scale_ref[k, x] - power
             second_ref[k, x] = second
             products[0] = products[0] + source_ref[k, x] * second
             products[1] = products[1] + power * second
             products[2] = products[2] + second * second
-    total = gram_in_ref[...] + gram_rows(products, row, 3)
-    for device in range(gram_ref.shape[0]):
-        gram_ref[device] = total
+    total = jnp.sum(gram_in_ref[...] + gram_rows(products, row, 3), axis=1, keepdims=True)
+    line = jnp.sum(jnp.where(row == spot, jnp.broadcast_to(total, TILE), 0.0), axis=0, keepdims=True)
+    gram_ref[...] = jnp.broadcast_to(line, gram_ref.shape)
 
 
 def combine_kernel(
     gram_ref, source_ref, power_ref, second_ref, one_ref, two_ref,
-    adjoint_ref, residual_ref, basis_ref, *, scale,
+    adjoint_hbm, residual_hbm, basis_hbm, adjoint_ref, residual_ref, basis_ref, sems, *, scale,
 ):
-    parts = [gram_ref[device] for device in range(gram_ref.shape[0])]
-    while len(parts) > 1:
-        parts = [parts[i] + parts[i + 1] if i + 1 < len(parts) else parts[i] for i in range(0, len(parts), 2)]
-    sums = jnp.broadcast_to(jnp.sum(parts[0], axis=1, keepdims=True), TILE)
-    g00, g01, g11, g02, g12, g22 = (sums[k : k + 1] for k in range(6))
+    sums = jnp.sum(gram_ref[...], axis=0, keepdims=True)
+    spot = lax.broadcasted_iota(jnp.int32, sums.shape, 1)
+    g00, g01, g11, g02, g12, g22 = (
+        jnp.sum(jnp.where(spot == k, sums, 0.0), axis=1, keepdims=True) for k in range(6)
+    )
     beta2 = g00 + EPSILON
     beta = jnp.sqrt(beta2)
     less = (EPSILON - g01) / beta2
@@ -442,22 +502,30 @@
     z_one, z_two = wide(y1 / beta + y2 * a), wide(y2 * b)
     r0, r1, r2 = wide(f0 / beta + f1 * a + f2 * v0), wide(f1 * b + f2 * v1), wide(f2 * v2)
     s0, s1, s2 = wide(scale * v0), wide(scale * v1), wide(scale * v2)
+    copies = []
     for k in range(2):
         for x in range(source_ref.shape[1]):
             source, power, second = source_ref[k, x], power_ref[k, x], second_ref[k, x]
             adjoint_ref[k, x] = z_one * one_ref[k, x] + z_two * two_ref[k, x]
             residual_ref[k, x] = r0 * source + r1 * power + r2 * second
             basis_ref[k, x] = s0 * source + s1 * power + s2 * second
-
-
-def call(kernel, outs, scratch=(), name=None):
+        pairs = ((adjoint_ref, adjoint_hbm), (residual_ref, residual_hbm), (basis_ref, basis_hbm))
+        for index, (src, dst) in enumerate(pairs):
+            copy = pltpu.make_async_copy(src.at[k], dst.at[k], sems.at[k, index])
+            copy.start()
+            copies.append(copy)
+    for copy in copies:
+        copy.wait()
+
+
+def call(kernel, outs, scratch=(), name=None, inside=pltpu.VMEM, outside=pltpu.VMEM):
     def run(*args):
         return pl.pallas_call(
             kernel,
             out_shape=[jax.ShapeDtypeStruct(shape, F32) for shape in outs],
-            in_specs=[pl.BlockSpec(memory_space=pltpu.VMEM)] * len(args),
-            out_specs=[pl.BlockSpec(memory_space=pltpu.VMEM)] * len(outs),
-            scratch_shapes=[pltpu.VMEM(shape, F32) for shape in scratch],
+            in_specs=[pl.BlockSpec(memory_space=inside)] * len(args),
+            out_specs=[pl.BlockSpec(memory_space=outside)] * len(outs),
+            scratch_shapes=[pltpu.VMEM(spec, F32) if isinstance(spec, tuple) else spec for spec in scratch],
             compiler_params=pltpu.CompilerParams(vmem_limit_bytes=32 * 1024 * 1024),
             name=name,
         )(*args)
@@ -489,44 +557,58 @@
     cells = 2.0 * rows * soil_ids.shape[1] * depth * devices
     own = (rows, *TILE)
     slab = (4 * MARGIN + RIM, *TILE)
-    fields, wire, even, odd = call(pack_x_kernel, [(4, *own), own, slab, slab], name="pack_x")(
-        soil_props, storage, soil_ids, bc_mask
-    )
+    fields, wire, even, odd = call(
+        pack_x_kernel,
+        [(4, *own), own, slab, slab],
+        [soil_props.shape, (4, *own), pltpu.VMEM(own, jnp.int32), pltpu.VMEM((SUB, rows), jnp.int32)]
+        + [pltpu.SemaphoreType.DMA((4,))],
+        name="pack_x",
+        inside=pltpu.HBM,
+    )(*(pltpu.with_memory_space_constraint(x, pltpu.HBM) for x in (soil_props, storage, soil_ids, bc_mask.T)))
     xe, xo = exchange("gx", even, odd)
-    slab = (3 * wide + 2, *TILE)
-    even, odd = call(pack_y_kernel, [slab, slab], name="pack_y")(fields, wire, xe, xo)
+    half = wide // 2 + 1
+    rims = -(-2 * half // SUB)
+    slab = (2 * wide + half + rims, *TILE)
+    even, odd = call(pack_y_kernel, [slab, slab], [(2 * half, *TILE)], name="pack_y")(fields, wire, xe, xo)
     ye, yo = exchange("gy", even, odd)
     buffers = [(wide + 2, 2, *TILE)] * 4
-    solved_shapes = [(2, wide, 2, *TILE), (2, wide, *TILE), (2, wide, *TILE)]
-    coeff, image, scales, solved, even, odd = call(
+    count = wide // SUB
+    slab = (wide + 2 * count, *TILE)
+    solved_shapes = [(2, wide, *TILE), (4, count, *TILE), slab, slab]
+    coeff, image, scales, solved, edges, even, odd = call(
         coefficients_kernel,
         [(4, wide, 2, *TILE), (4, *own), (5, *own)] + solved_shapes,
-        [(wide + 2, 3, *TILE)] * 2 + [(2, *own)] + buffers,
+        [(wide + 2, 2, *TILE)] * 2 + [(2, 2, rims, *TILE), (2, *own)] + buffers,
         name="first_solve",
     )(soil_props, fields, wire, xe, xo, ye, yo, adjoint_source)
 
-    fold_shapes = [(2, wide, 2, *TILE)] + [(2, 2 * MARGIN + 1, *TILE)] * 2
+    slab = (2 * (MARGIN + 2), *TILE)
+    fold_shapes = [(2, wide, *TILE), (4, count, *TILE), slab, slab]
     ye, yo = exchange("gy", even, odd)
-    summed, even, odd = call(fold_y_kernel, fold_shapes, name="fold_y")(solved, ye, yo)
+    summed, edges, even, odd = call(fold_y_kernel, fold_shapes, name="fold_y")(solved, edges, ye, yo)
     xe, xo = exchange("gx", even, odd)
-    halo = [(rows + 2, 2, *TILE)] * 2
-    one, power, gram, solved, even, odd = call(
+    halo = [(rows + 2, *TILE)] * 2 + [(4, count, *TILE)]
+    one, power, gram, solved, rest, even, odd = call(
         step_kernel,
         [(2, *own), (2, *own), TILE] + solved_shapes,
         [(2, *own)] + halo + buffers,
         name="second_solve",
-    )(summed, xe, xo, coeff, image, scales, adjoint_source)
+    )(summed, edges, xe, xo, coeff, image, scales, adjoint_source)
 
     ye, yo = exchange("gy", even, odd)
-    summed, even, odd = call(fold_y_kernel, fold_shapes, name="fold_y")(solved, ye, yo)
+    summed, edges, even, odd = call(fold_y_kernel, fold_shapes, name="fold_y")(solved, rest, ye, yo)
     xe, xo = exchange("gx", even, odd)
     two, second, gram = call(
-        last_kernel, [(2, *own), (2, *own), (devices, *TILE)], halo, name="last_image"
-    )(summed, xe, xo, image, scales, adjoint_source, power, gram)
-    gram = lax.all_to_all(gram, ("gx", "gy"), 0, 0)
+        last_kernel, [(2, *own), (2, *own), (devices, LANE)], halo, name="last_image"
+    )(summed, edges, xe, xo, image, scales, adjoint_source, power, gram)
+    gram = lax.all_to_all(gram, ("gx", "gy"), 0, 0, tiled=True)
     return tuple(
         call(
-            functools.partial(combine_kernel, scale=math.sqrt(cells)), [(2, *own)] * 3, name="combine"
+            functools.partial(combine_kernel, scale=math.sqrt(cells)),
+            [(2, *own)] * 3,
+            [(2, *own)] * 3 + [pltpu.SemaphoreType.DMA((2, 3))],
+            name="combine",
+            outside=pltpu.HBM,
         )(gram, adjoint_source, power, second, one, two)
     )
 

time: 57.8 us -> 52.2 us (0.903)
  waiting for transfers between devices: 20.4 us -> 16.9 us
  local copies, waits for them, and re-layouts: 2.56 us -> 0.01 us
  blocking collectives: 12.7 us -> 11.5 us
  Pallas kernels: 4.67 us -> 5.72 us
    unnamed x9 -> x4, local copies, waits for them, and re-layouts: 2.56 us -> 0.01 us
    ppermute x6, waiting for transfers between devices: 12.1 us -> 10.1 us  [exchange(): lax.ppermute(odd, ('gx', 'gy'), others)]
    ppermute x6, waiting for transfers between devices: 8.29 us -> 6.83 us  [exchange(): lax.ppermute(even, axis, pairs)]
    all_to_all x1, blocking collectives: 12.7 us -> 11.5 us  [shards(): gram = lax.all_to_all(gram, ('gx', 'gy'), 0, 0, tiled=True)]
    pallas_call x8, Pallas kernels: 4.67 us -> 5.72 us  [run(): pl.pallas_call(kernel, out_shape=[jax.ShapeDtypeStruct(shape, F32) for sh...]
where the time goes in v3:
time: 52.2 us; the launch traced here: 52 us
  starting transfers between devices  17.1 us (33%)
  waiting for transfers between devices  16.9 us (32%)
  blocking collectives  11.5 us (22%)
  Pallas kernels  5.72 us (11%)
  between operations  0.7 us (1%)
    all_to_all x1, blocking collectives, shards(): gram = lax.all_to_all(gram, ('gx', 'gy'), 0, 0, tiled=True)  11.5 us
    ppermute x6, waiting for transfers between devices, exchange(): lax.ppermute(odd, ('gx', 'gy'), others)  10.1 us
    ppermute x6, starting transfers between devices, exchange(): lax.ppermute(odd, ('gx', 'gy'), others)  9.71 us
    ppermute x6, starting transfers between devices, exchange(): lax.ppermute(even, axis, pairs)  7.39 us
    ppermute x6, waiting for transfers between devices, exchange(): lax.ppermute(even, axis, pairs)  6.83 us
    pallas_call x8, Pallas kernels, run(): pl.pallas_call(kernel, out_shape=[jax.ShapeDtypeStruct(shape, F32) for sh...  5.72 us
  transfers between devices with their start and end apart: 12, of which 6 were waited for; matrix products, arithmetic and copies ran while one was open for 0% of the time, Pallas kernels for 0%

profile of v3, /device:TPU:0, one launch (start us, length us, event | category | flops | bytes accessed | tf_op | source)
XLA Modules:
  0.0 52.0 jit_solution(13483433503790255284)
XLA Ops:
  0.6 1.2 %pack_x.1 = (f32[4,16,8,128]{3,2,1,0:T(8,128)S(1)}, f32[16,8,128]{2,1,0:T(8,128)S(1)}, f32[21,8,128]{2,1,0:T(8,128)S(1)}, f32[21,8,128]{2,1,0:T(8,128)S(1)}) custom-call(f32[3,16]{1,0:T(4,128)} %props_ref.1, f32[4,16,8,128]{3,2,1,0:T(8,128)} %storage_hbm.1, s32[16,8,128]{2,1,0:T(8,128)} %ids_hbm.1, s32[8,16]{1,0:T(8,128)} %bitcast.7), custom_call_target="tpu_custom_call" | custom-call | tf_op jit(solution)/shard_map/pack_x/pallas_call | solution.py:523
  1.9 3.0 %collective-permute-start = (f32[21,8,128]{2,1,0:T(8,128)S(1)}, f32[21,8,128]{2,1,0:T(8,128)S(1)}, u32[]{:S(2)}, u32[]{:S(2)}) collective-permute-start(f32[21,8,128]{2,1,0:T(8,128)S(1)} %get-tuple-element.36), channel_id=1, source_target_pairs={{0,8},{8,0},{16,24},{24,16},{1,9},{9,1},{17,25},{25,17},{2,10},{10... | collective-permute-start | bytes 258056 | tf_op jit(solution)/shard_map/ppermute | solution.py:550
  4.9 0.0 collective-permute-start.1
  4.9 2.5 %collective-permute-done.xe_ref = f32[21,8,128]{2,1,0:T(8,128)S(1)} collective-permute-done((f32[21,8,128]{2,1,0:T(8,128)S(1)}, f32[21,8,128]{2,1,0:T(8,128)S(1)}, u32[]{:S(2)}, u32[]{:S(2)}) %collective-permute-start) | collective-permute-done | bytes 86048 | tf_op jit(solution)/shard_map/ppermute | solution.py:550
  7.4 0.0 collective-permute-done.1.xo_ref
  7.4 0.1 pack_y.1
  7.5 0.0 copy-start.1
  7.5 0.1 collective-permute-start.2
  7.6 4.6 %collective-permute-start.3 = (f32[65,8,128]{2,1,0:T(8,128)S(1)}, f32[65,8,128]{2,1,0:T(8,128)S(1)}, u32[]{:S(2)}, u32[]{:S(2)}) collective-permute-start(f32[65,8,128]{2,1,0:T(8,128)S(1)} %get-tuple-element.39), channel_id=1, source_target_pairs={{0,8},{1,2},{2,1},{3,4},{4,3},{5,6},{6,5},{7,15},{8,0},{9,10},{10,... | collective-permute-start | bytes 798728 | tf_op jit(solution)/shard_map/ppermute | solution.py:550
  12.2 0.0 collective-permute-done.2.ye_ref
  12.2 4.4 %collective-permute-done.3.yo_ref = f32[65,8,128]{2,1,0:T(8,128)S(1)} collective-permute-done((f32[65,8,128]{2,1,0:T(8,128)S(1)}, f32[65,8,128]{2,1,0:T(8,128)S(1)}, u32[]{:S(2)}, u32[]{:S(2)}) %collective-permute-start.3) | collective-permute-done | bytes 266272 | tf_op jit(solution)/shard_map/ppermute | solution.py:550
  16.6 1.9 %first_solve.1 = (f32[4,24,2,8,128]{4,3,2,1,0:T(8,128)S(1)}, f32[4,16,8,128]{3,2,1,0:T(8,128)S(1)}, f32[5,16,8,128]{3,2,1,0:T(8,128)S(1)}, f32[2,24,8,128]{3,2,1...) custom-call(f32[3,16]{1,0:T(4,128)S(1)} %copy-done.1, ...), custom_call_target="tpu_custom_call" | custom-call | tf_op jit(solution)/shard_map/first_solve/pallas_call | solution.py:523
  18.5 0.1 collective-permute-start.4
  18.5 2.1 %collective-permute-start.5 = (f32[30,8,128]{2,1,0:T(8,128)S(1)}, f32[30,8,128]{2,1,0:T(8,128)S(1)}, u32[]{:S(2)}, u32[]{:S(2)}) collective-permute-start(f32[30,8,128]{2,1,0:T(8,128)S(1)} %get-tuple-element.43), channel_id=1, source_target_pairs={{0,8},{1,2},{2,1},{3,4},{4,3},{5,6},{6,5},{7,15},{8,0},{9,10},{10,... | collective-permute-start | bytes 368648 | tf_op jit(solution)/shard_map/ppermute | solution.py:550
  20.7 0.0 collective-permute-done.4.ye_ref
  20.7 2.9 %collective-permute-done.5.yo_ref = f32[30,8,128]{2,1,0:T(8,128)S(1)} collective-permute-done((f32[30,8,128]{2,1,0:T(8,128)S(1)}, f32[30,8,128]{2,1,0:T(8,128)S(1)}, u32[]{:S(2)}, u32[]{:S(2)}) %collective-permute-start.5) | collective-permute-done | bytes 122912 | tf_op jit(solution)/shard_map/ppermute | solution.py:550
  23.5 0.1 fold_y.2
  23.6 2.1 %collective-permute-start.6 = (f32[12,8,128]{2,1,0:T(8,128)S(1)}, f32[12,8,128]{2,1,0:T(8,128)S(1)}, u32[]{:S(2)}, u32[]{:S(2)}) collective-permute-start(f32[12,8,128]{2,1,0:T(8,128)S(1)} %get-tuple-element.46), channel_id=1, source_target_pairs={{0,8},{8,0},{16,24},{24,16},{1,9},{9,1},{17,25},{25,17},{2,10},{10... | collective-permute-start | bytes 147464 | tf_op jit(solution)/shard_map/ppermute | solution.py:550
  25.7 0.0 collective-permute-start.7
  25.7 2.1 %collective-permute-done.6.xe_ref = f32[12,8,128]{2,1,0:T(8,128)S(1)} collective-permute-done((f32[12,8,128]{2,1,0:T(8,128)S(1)}, f32[12,8,128]{2,1,0:T(8,128)S(1)}, u32[]{:S(2)}, u32[]{:S(2)}) %collective-permute-start.6) | collective-permute-done | bytes 49184 | tf_op jit(solution)/shard_map/ppermute | solution.py:550
  27.8 1.2 %second_solve.1 = (f32[2,16,8,128]{3,2,1,0:T(8,128)S(1)}, f32[2,16,8,128]{3,2,1,0:T(8,128)S(1)}, f32[8,128]{1,0:T(8,128)S(1)}, f32[2,24,8,128]{3,2,1,0:T(8,128)S...) custom-call(f32[2,24,8,128]{3,2,1,0:T(8,128)S(1)} %get-tuple-element.44.summed_ref, ...), custom_call_target="tpu_custom_call" | custom-call | tf_op jit(solution)/shard_map/second_solve/pallas_call | solution.py:523
  29.0 0.1 collective-permute-start.8
  29.1 3.0 %collective-permute-start.9 = (f32[30,8,128]{2,1,0:T(8,128)S(1)}, f32[30,8,128]{2,1,0:T(8,128)S(1)}, u32[]{:S(2)}, u32[]{:S(2)}) collective-permute-start(f32[30,8,128]{2,1,0:T(8,128)S(1)} %get-tuple-element.54), channel_id=1, source_target_pairs={{0,8},{1,2},{2,1},{3,4},{4,3},{5,6},{6,5},{7,15},{8,0},{9,10},{10,... | collective-permute-start | bytes 368648 | tf_op jit(solution)/shard_map/ppermute | solution.py:550
  32.1 0.0 collective-permute-done.8.ye_ref
  32.1 2.9 %collective-permute-done.9.yo_ref = f32[30,8,128]{2,1,0:T(8,128)S(1)} collective-permute-done((f32[30,8,128]{2,1,0:T(8,128)S(1)}, f32[30,8,128]{2,1,0:T(8,128)S(1)}, u32[]{:S(2)}, u32[]{:S(2)}) %collective-permute-start.9) | collective-permute-done | bytes 122912 | tf_op jit(solution)/shard_map/ppermute | solution.py:550
  34.9 0.1 fold_y.3
  35.0 2.1 %collective-permute-start.10 = (f32[12,8,128]{2,1,0:T(8,128)S(1)}, f32[12,8,128]{2,1,0:T(8,128)S(1)}, u32[]{:S(2)}, u32[]{:S(2)}) collective-permute-start(f32[12,8,128]{2,1,0:T(8,128)S(1)} %get-tuple-element.57), channel_id=1, source_target_pairs={{0,8},{8,0},{16,24},{24,16},{1,9},{9,1},{17,25},{25,17},{2,10},{10... | collective-permute-start | bytes 147464 | tf_op jit(solution)/shard_map/ppermute | solution.py:550
  37.1 2.1 %collective-permute-done.10.xe_ref = f32[12,8,128]{2,1,0:T(8,128)S(1)} collective-permute-done((f32[12,8,128]{2,1,0:T(8,128)S(1)}, f32[12,8,128]{2,1,0:T(8,128)S(1)}, u32[]{:S(2)}, u32[]{:S(2)}) %collective-permute-start.10) | collective-permute-done | bytes 49184 | tf_op jit(solution)/shard_map/ppermute | solution.py:550
  39.2 0.0 collective-permute-done.11.xo_ref
  39.2 0.3 last_image.1
  39.5 11.5 %all_to_all.11 = f32[32,1,128]{2,1,0:T(1,128)S(1)} all-to-all(f32[32,1,128]{2,1,0:T(1,128)S(1)} %bitcast.6), channel_id=1, replica_groups=mesh['gx'=4,'gy'=8] {'gx','gy'}, dimensions={0} | all-to-all | bytes 32768 | tf_op jit(solution)/shard_map/all_to_all | solution.py:604
  51.0 1.0 %combine.1 = (f32[2,16,8,128]{3,2,1,0:T(8,128)}, f32[2,16,8,128]{3,2,1,0:T(8,128)}, f32[2,16,8,128]{3,2,1,0:T(8,128)}) custom-call(f32[32,128]{1,0:T(8,128)S(1)} %bitcast.5, f32[2,16,8,128]{3,2,1,0:T(8,128)S(1)} %copy-done, f32[2,16,8,128]{3,2,1,0:T(8,128)S(1)} %get-tuple-element.59.power_ref, f32[2,16,8,128]{3,2,1,0:T(8,128)S(1)} %get-tuple-element.62.second_ref, ...), custom_call_target="tpu_custom_call" | custom-call | tf_op jit(solution)/shard_map/combine/pallas_call | solution.py:523
  (5 shorter events, 0.0 us)
Async XLA Ops:
  1.9 5.5 %collective-permute-start = (f32[21,8,128]{2,1,0:T(8,128)S(1)}, f32[21,8,128]{2,1,0:T(8,128)S(1)}, u32[]{:S(2)}, u32[]{:S(2)}) collective-permute-start(f32[21,8,128]{2,1,0:T(8,128)S(1)} %get-tuple-element.36), channel_id=1, source_target_pairs={{0,8},{8,0},{16,24},{24,16},{1,9},{9,1},{17,25},{25,17},{2,10},{10... | collective-permute-start | bytes 258056 | tf_op jit(solution)/shard_map/ppermute | solution.py:550
  4.9 2.5 %collective-permute-start.1 = (f32[21,8,128]{2,1,0:T(8,128)S(1)}, f32[21,8,128]{2,1,0:T(8,128)S(1)}, u32[]{:S(2)}, u32[]{:S(2)}) collective-permute-start(f32[21,8,128]{2,1,0:T(8,128)S(1)} %get-tuple-element.37), channel_id=1, source_target_pairs={{0,1},{1,0},{2,3},{3,2},{4,5},{5,4},{6,7},{7,6},{8,16},{9,17},{10,... | collective-permute-start | bytes 258056 | tf_op jit(solution)/shard_map/ppermute | solution.py:550
  7.4 9.2 %copy-start = (f32[2,16,8,128]{3,2,1,0:T(8,128)S(1)}, f32[2,16,8,128]{3,2,1,0:T(8,128)}, u32[]{:S(2)}) copy-start(f32[2,16,8,128]{3,2,1,0:T(8,128)} %source_ref.7) | copy-start | bytes 393220
  7.5 9.1 %copy-start.1 = (f32[3,16]{1,0:T(4,128)S(1)}, f32[3,16]{1,0:T(4,128)}, u32[]{:S(2)}) copy-start(f32[3,16]{1,0:T(4,128)} %props_ref.1) | copy-start | bytes 580
  7.5 4.7 %collective-permute-start.2 = (f32[65,8,128]{2,1,0:T(8,128)S(1)}, f32[65,8,128]{2,1,0:T(8,128)S(1)}, u32[]{:S(2)}, u32[]{:S(2)}) collective-permute-start(f32[65,8,128]{2,1,0:T(8,128)S(1)} %get-tuple-element.38), channel_id=1, source_target_pairs={{0,1},{1,0},{2,3},{3,2},{4,5},{5,4},{6,7},{7,6},{8,9},{9,8},{10,11... | collective-permute-start | bytes 798728 | tf_op jit(solution)/shard_map/ppermute | solution.py:550
  7.6 9.0 %collective-permute-start.3 = (f32[65,8,128]{2,1,0:T(8,128)S(1)}, f32[65,8,128]{2,1,0:T(8,128)S(1)}, u32[]{:S(2)}, u32[]{:S(2)}) collective-permute-start(f32[65,8,128]{2,1,0:T(8,128)S(1)} %get-tuple-element.39), channel_id=1, source_target_pairs={{0,8},{1,2},{2,1},{3,4},{4,3},{5,6},{6,5},{7,15},{8,0},{9,10},{10,... | collective-permute-start | bytes 798728 | tf_op jit(solution)/shard_map/ppermute | solution.py:550
  18.5 2.2 %collective-permute-start.4 = (f32[30,8,128]{2,1,0:T(8,128)S(1)}, f32[30,8,128]{2,1,0:T(8,128)S(1)}, u32[]{:S(2)}, u32[]{:S(2)}) collective-permute-start(f32[30,8,128]{2,1,0:T(8,128)S(1)} %get-tuple-element.42), channel_id=1, source_target_pairs={{0,1},{1,0},{2,3},{3,2},{4,5},{5,4},{6,7},{7,6},{8,9},{9,8},{10,11... | collective-permute-start | bytes 368648 | tf_op jit(solution)/shard_map/ppermute | solution.py:550
  18.5 5.0 %collective-permute-start.5 = (f32[30,8,128]{2,1,0:T(8,128)S(1)}, f32[30,8,128]{2,1,0:T(8,128)S(1)}, u32[]{:S(2)}, u32[]{:S(2)}) collective-permute-start(f32[30,8,128]{2,1,0:T(8,128)S(1)} %get-tuple-element.43), channel_id=1, source_target_pairs={{0,8},{1,2},{2,1},{3,4},{4,3},{5,6},{6,5},{7,15},{8,0},{9,10},{10,... | collective-permute-start | bytes 368648 | tf_op jit(solution)/shard_map/ppermute | solution.py:550
  23.6 4.2 %collective-permute-start.6 = (f32[12,8,128]{2,1,0:T(8,128)S(1)}, f32[12,8,128]{2,1,0:T(8,128)S(1)}, u32[]{:S(2)}, u32[]{:S(2)}) collective-permute-start(f32[12,8,128]{2,1,0:T(8,128)S(1)} %get-tuple-element.46), channel_id=1, source_target_pairs={{0,8},{8,0},{16,24},{24,16},{1,9},{9,1},{17,25},{25,17},{2,10},{10... | collective-permute-start | bytes 147464 | tf_op jit(solution)/shard_map/ppermute | solution.py:550
  25.7 2.2 %collective-permute-start.7 = (f32[12,8,128]{2,1,0:T(8,128)S(1)}, f32[12,8,128]{2,1,0:T(8,128)S(1)}, u32[]{:S(2)}, u32[]{:S(2)}) collective-permute-start(f32[12,8,128]{2,1,0:T(8,128)S(1)} %get-tuple-element.47), channel_id=1, source_target_pairs={{0,1},{1,0},{2,3},{3,2},{4,5},{5,4},{6,7},{7,6},{8,16},{9,17},{10,... | collective-permute-start | bytes 147464 | tf_op jit(solution)/shard_map/ppermute | solution.py:550
  29.0 3.1 %collective-permute-start.8 = (f32[30,8,128]{2,1,0:T(8,128)S(1)}, f32[30,8,128]{2,1,0:T(8,128)S(1)}, u32[]{:S(2)}, u32[]{:S(2)}) collective-permute-start(f32[30,8,128]{2,1,0:T(8,128)S(1)} %get-tuple-element.53), channel_id=1, source_target_pairs={{0,1},{1,0},{2,3},{3,2},{4,5},{5,4},{6,7},{7,6},{8,9},{9,8},{10,11... | collective-permute-start | bytes 368648 | tf_op jit(solution)/shard_map/ppermute | solution.py:550
  29.1 5.8 %collective-permute-start.9 = (f32[30,8,128]{2,1,0:T(8,128)S(1)}, f32[30,8,128]{2,1,0:T(8,128)S(1)}, u32[]{:S(2)}, u32[]{:S(2)}) collective-permute-start(f32[30,8,128]{2,1,0:T(8,128)S(1)} %get-tuple-element.54), channel_id=1, source_target_pairs={{0,8},{1,2},{2,1},{3,4},{4,3},{5,6},{6,5},{7,15},{8,0},{9,10},{10,... | collective-permute-start | bytes 368648 | tf_op jit(solution)/shard_map/ppermute | solution.py:550
  35.0 4.2 %collective-permute-start.10 = (f32[12,8,128]{2,1,0:T(8,128)S(1)}, f32[12,8,128]{2,1,0:T(8,128)S(1)}, u32[]{:S(2)}, u32[]{:S(2)}) collective-permute-start(f32[12,8,128]{2,1,0:T(8,128)S(1)} %get-tuple-element.57), channel_id=1, source_target_pairs={{0,8},{8,0},{16,24},{24,16},{1,9},{9,1},{17,25},{25,17},{2,10},{10... | collective-permute-start | bytes 147464 | tf_op jit(solution)/shard_map/ppermute | solution.py:550
  37.1 2.2 %collective-permute-start.11 = (f32[12,8,128]{2,1,0:T(8,128)S(1)}, f32[12,8,128]{2,1,0:T(8,128)S(1)}, u32[]{:S(2)}, u32[]{:S(2)}) collective-permute-start(f32[12,8,128]{2,1,0:T(8,128)S(1)} %get-tuple-element.58), channel_id=1, source_target_pairs={{0,1},{1,0},{2,3},{3,2},{4,5},{5,4},{6,7},{7,6},{8,16},{9,17},{10,... | collective-permute-start | bytes 147464 | tf_op jit(solution)/shard_map/ppermute | solution.py:550

commit v4 on v3

--- a/solution.py
+++ b/solution.py
@@ -48,6 +48,8 @@
     own_up, own_down = up_y(own), down_y(own)
     side_up, side_down = up_y(side), down_y(side)
     own_sum = jnp.where(row == 7, side_up, own_up) + jnp.where(row == 0, side_down, own_down)
+    if last_up is None:
+        return own_sum, None
     side_sum = jnp.where(row == 7, own_up, jnp.where(row == 3, last_up, side_up))
     side_sum = side_sum + jnp.where(row == 0, own_down, jnp.where(row == 4, last_down, side_down))
     return own_sum, side_sum
@@ -74,8 +76,85 @@
     return [jnp.broadcast_to(wide[k : k + 1], TILE) for k in range(3)]
 
 
-def pack_x_kernel(
-    props_hbm, storage_hbm, ids_hbm, bc_hbm, fields_ref, wire_ref, even_ref, odd_ref,
+def rim_rows(even_ref, odd_ref, base, tiles, rows_even, rows_odd):
+    for j, (tile_ref, index) in enumerate(tiles):
+        line = (base + j // SUB, pl.ds(j % SUB, 1))
+        even_ref[line] = tile_ref[(*index, pl.ds(rows_even, 1))]
+        odd_ref[line] = tile_ref[(*index, pl.ds(rows_odd, 1))]
+
+
+def pack_y(fields, wire_ref, even_ref, odd_ref):
+    first, _, _ = position("gy")
+    even_low = (sublane() < 4) != first
+    count, half = len(fields[0]), wire_ref.shape[0] // 2
+
+    def put(spot, one, other):
+        other = half_turn(other)
+        even_ref[spot] = jnp.where(even_low, one, other)
+        odd_ref[spot] = jnp.where(even_low, other, one)
+
+    for pair in range(2):
+        for i in range(count):
+            put(pair * count + i, fields[2 * pair][i], fields[2 * pair + 1][i])
+    for j in range(half):
+        put(2 * count + j, wire_ref[j], wire_ref[j + half])
+    rows_even, rows_odd = jnp.where(first, 3, 4), jnp.where(first, 4, 3)
+    if 2 * half % SUB:
+        last = even_ref.shape[0] - 1
+        even_ref[last] = odd_ref[last] = jnp.zeros(TILE, F32)
+    spots = [(wire_ref, (j,)) for j in range(2 * half)]
+    rim_rows(even_ref, odd_ref, 2 * count + half, spots, rows_even, rows_odd)
+
+
+def y_slab(count, ids):
+    return (2 * count + ids // 2 + -(-ids // SUB), *TILE)
+
+
+def unpack_fields(even_ref, odd_ref, count, i):
+    first, _, _ = position("gy")
+    row = sublane()
+    out = []
+    for pair in range(2):
+        low, high = from_sides(first, even_ref[pair * count + i], odd_ref[pair * count + i])
+        out.append(jnp.where(row < 4, high, low))
+        out.append(half_turn(jnp.where(row < 4, low, high)))
+    return out
+
+
+def unpack_wire(even_ref, odd_ref, count, ids):
+    first, has_low, has_high = position("gy")
+    row = sublane()
+
+    def sides(spot):
+        low, high = from_sides(first, even_ref[spot], odd_ref[spot])
+        return jnp.where(has_low, low, 0.0), jnp.where(has_high, high, 0.0)
+
+    one, other = [], []
+    for j in range(ids // 2):
+        low, high = sides(2 * count + j)
+        one.append(jnp.where(row < 4, high, low))
+        other.append(half_turn(jnp.where(row < 4, low, high)))
+    beyond = [sides(2 * count + ids // 2 + tile) for tile in range(-(-ids // SUB))]
+    return one + other, beyond
+
+
+def halo_x(even_ref, odd_ref):
+    first, has_low, has_high = position("gx")
+    fields = []
+    for k in range(4):
+        spots = pl.ds(k * MARGIN, MARGIN)
+        low, high = from_sides(first, even_ref[spots], odd_ref[spots])
+        fields.append([low[i] for i in range(MARGIN)] + [high[i] for i in range(MARGIN)])
+    spots = pl.ds(4 * MARGIN, RIM)
+    low, high = from_sides(first, even_ref[spots], odd_ref[spots])
+    low = jnp.where(has_low, low, 0.0)
+    high = jnp.where(has_high, high, 0.0)
+    return fields, [low[i] for i in range(RIM)] + [high[i] for i in range(RIM)]
+
+
+def first_pack_kernel(
+    props_hbm, storage_hbm, ids_hbm, bc_hbm,
+    fields_ref, wire_ref, x_even_ref, x_odd_ref, y_even_ref, y_odd_ref,
     props_ref, storage_ref, ids_ref, bc_ref, sems,
 ):
     places = ((ids_hbm, ids_ref), (storage_hbm, storage_ref), (props_hbm, props_ref), (bc_hbm, bc_ref))
@@ -87,6 +166,7 @@
     for copy in copies:
         copy.wait()
     tables = wide_tables(props_ref)
+    fields = [[] for _ in range(4)]
     for x in range(rows):
         wire = (ids_ref[x] + 1).astype(F32)
         wire_ref[x] = wire
@@ -96,10 +176,12 @@
         bound = jnp.where(spot == LANE - 1, 2.0 * kp * held, 0.0)
         press = storage_ref[0, x]
         lower = storage_ref[1, x]
-        fields_ref[0, x] = press + bound
-        fields_ref[1, x] = carried * press - storage_ref[2, x]
-        fields_ref[2, x] = lower
-        fields_ref[3, x] = storage_ref[3, x] - carried * lower
+        fields[0].append(press + bound)
+        fields[1].append(carried * press - storage_ref[2, x])
+        fields[2].append(lower)
+        fields[3].append(storage_ref[3, x] - carried * lower)
+        for k in range(4):
+            fields_ref[k, x] = fields[k][x]
     first, _, _ = position("gx")
     high, low = rows - MARGIN, 0
     start_even = jnp.where(first, high, low)
@@ -107,70 +189,21 @@
     wire_even = jnp.where(first, rows - RIM, 0)
     wire_odd = jnp.where(first, 0, rows - RIM)
     for k in range(4):
-        even_ref[pl.ds(k * MARGIN, MARGIN)] = fields_ref[k, pl.ds(start_even, MARGIN)]
-        odd_ref[pl.ds(k * MARGIN, MARGIN)] = fields_ref[k, pl.ds(start_odd, MARGIN)]
-    even_ref[pl.ds(4 * MARGIN, RIM)] = wire_ref[pl.ds(wire_even, RIM)]
-    odd_ref[pl.ds(4 * MARGIN, RIM)] = wire_ref[pl.ds(wire_odd, RIM)]
-
-
-def widen_x(fields_ref, wire_ref, even_ref, odd_ref):
-    rows = wire_ref.shape[0]
-    first, has_low, has_high = position("gx")
-    fields = []
-    for k in range(4):
-        low, high = from_sides(
-            first, even_ref[pl.ds(k * MARGIN, MARGIN)], odd_ref[pl.ds(k * MARGIN, MARGIN)]
-        )
-        fields.append(
-            [low[i] for i in range(MARGIN)]
-            + [fields_ref[k, x] for x in range(rows)]
-            + [high[i] for i in range(MARGIN)]
-        )
-    low, high = from_sides(
-        first, even_ref[pl.ds(4 * MARGIN, RIM)], odd_ref[pl.ds(4 * MARGIN, RIM)]
-    )
-    low = jnp.where(has_low, low, 0.0)
-    high = jnp.where(has_high, high, 0.0)
-    wire = (
-        [low[i] for i in range(RIM)] + [wire_ref[x] for x in range(rows)] + [high[i] for i in range(RIM)]
-    )
-    return fields, wire
-
-
-def rim_rows(even_ref, odd_ref, base, tiles, rows_even, rows_odd):
-    for j, (tile_ref, index) in enumerate(tiles):
-        line = (base + j // SUB, pl.ds(j % SUB, 1))
-        even_ref[line] = tile_ref[(*index, pl.ds(rows_even, 1))]
-        odd_ref[line] = tile_ref[(*index, pl.ds(rows_odd, 1))]
-
-
-def pack_y_kernel(fields_ref, wire_ref, xe_ref, xo_ref, even_ref, odd_ref, all_wire_ref):
-    fields, wire = widen_x(fields_ref, wire_ref, xe_ref, xo_ref)
-    wide = len(fields[0])
-    first, _, _ = position("gy")
-    even_low = (sublane() < 4) != first
-
-    def put(spot, one, other):
-        other = half_turn(other)
-        even_ref[spot] = jnp.where(even_low, one, other)
-        odd_ref[spot] = jnp.where(even_low, other, one)
-
-    for pair in range(2):
-        for i in range(wide):
-            put(pair * wide + i, fields[2 * pair][i], fields[2 * pair + 1][i])
-    half = wide // 2 + 1
-    for j in range(half):
-        put(2 * wide + j, wire[j], wire[j + half])
-    for j in range(2 * half):
-        all_wire_ref[j] = wire[j]
-    rows_even, rows_odd = jnp.where(first, 3, 4), jnp.where(first, 4, 3)
-    spots = [(all_wire_ref, (j,)) for j in range(2 * half)]
-    last = even_ref.shape[0] - 1
-    even_ref[last] = odd_ref[last] = jnp.zeros(TILE, F32)
-    rim_rows(even_ref, odd_ref, 2 * wide + half, spots, rows_even, rows_odd)
-
-
-def sweep_row(q_ref, t_ref, coeff_ref, j, row, spot, rhs):
+        x_even_ref[pl.ds(k * MARGIN, MARGIN)] = fields_ref[k, pl.ds(start_even, MARGIN)]
+        x_odd_ref[pl.ds(k * MARGIN, MARGIN)] = fields_ref[k, pl.ds(start_odd, MARGIN)]
+    x_even_ref[pl.ds(4 * MARGIN, RIM)] = wire_ref[pl.ds(wire_even, RIM)]
+    x_odd_ref[pl.ds(4 * MARGIN, RIM)] = wire_ref[pl.ds(wire_odd, RIM)]
+    pack_y(fields, wire_ref, y_even_ref, y_odd_ref)
+
+
+def corner_pack_kernel(xe_ref, xo_ref, even_ref, odd_ref, wire_ref):
+    fields, wire = halo_x(xe_ref, xo_ref)
+    for j, value in enumerate(wire):
+        wire_ref[j] = value
+    pack_y(fields, wire_ref, even_ref, odd_ref)
+
+
+def sweep_row(q_ref, t_ref, coeff, j, row, spot, rhs):
     sums = []
     for ref in (q_ref, t_ref):
         own, side = ref[j, 0], ref[j, 1]
@@ -186,14 +219,14 @@
         flow, heat = sums[0][tile], sums[1][tile]
         out.append(
             (
-                coeff_ref[0, j - 1, tile] * flow + coeff_ref[1, j - 1, tile] * heat,
-                coeff_ref[2, j - 1, tile] * flow + coeff_ref[3, j - 1, tile] * heat,
+                coeff(0, j - 1, tile) * flow + coeff(1, j - 1, tile) * heat,
+                coeff(2, j - 1, tile) * flow + coeff(3, j - 1, tile) * heat,
             )
         )
     return out
 
 
-def subdomain_sweeps(rhs_ref, coeff_ref, solved_ref, rims_ref, even_ref, odd_ref, buffers, rows):
+def subdomain_sweeps(rhs_ref, coeff, solved_ref, rims_ref, even_ref, odd_ref, buffers, rows):
     row, spot = sublane(), lane()
     wide = rows + 2 * MARGIN
     zero = jnp.zeros(TILE, F32)
@@ -205,8 +238,8 @@
     for x in range(rows):
         j = x + RIM
         flow, heat = rhs_ref[0, x], rhs_ref[1, x]
-        current[0][j, 0] = coeff_ref[0, j - 1, 0] * flow + coeff_ref[1, j - 1, 0] * heat
-        current[1][j, 0] = coeff_ref[2, j - 1, 0] * flow + coeff_ref[3, j - 1, 0] * heat
+        current[0][j, 0] = coeff(0, j - 1, 0) * flow + coeff(1, j - 1, 0) * heat
+        current[1][j, 0] = coeff(2, j - 1, 0) * flow + coeff(3, j - 1, 0) * heat
     first, _, _ = position("gy")
     even_low = (row < 4) != first
     for sweep in range(1, SWEEPS):
@@ -214,7 +247,7 @@
         for x in range(-reach, rows + reach):
             j = x + RIM
             rhs = (rhs_ref[0, x], rhs_ref[1, x]) if 0 <= x < rows else None
-            out = sweep_row(current[0], current[1], coeff_ref, j, row, spot, rhs)
+            out = sweep_row(current[0], current[1], coeff, j, row, spot, rhs)
             if sweep < SWEEPS - 1:
                 for tile in range(2):
                     following[0][j, tile] = out[tile][0]
@@ -237,84 +270,159 @@
         rim_rows(even_ref, odd_ref, wide + k * (wide // SUB), spots, rows_even, rows_odd)
 
 
-def coefficients_kernel(
+def getter(own_ref, own_side_ref, rest_ref, rest_side_ref):
+    rows = own_ref.shape[1]
+
+    def coeff(k, i, tile):
+        ref, rest, start, count = (own_ref, rest_ref, MARGIN, rows)
+        if tile:
+            ref, rest, start, count = (own_side_ref, rest_side_ref, MARGIN + 1, rows - 2)
+        if start <= i < start + count:
+            return ref[k, i - start]
+        return rest[k, i if i < start else i - count]
+
+    return coeff
+
+
+def diagonal(tiles, index, spot):
+    j, last_up, last_down = index
+    own_sum, side_sum = along_y(tiles(j, 0), tiles(j, 1), sublane(), last_up, last_down)
+    out = []
+    for tile, total in ((0, own_sum), (1, side_sum)):
+        if tile == 1 and last_up is None:
+            break
+        centre = tiles(j, tile)
+        total = total + along_z(centre, spot) + (tiles(j - 1, tile) + tiles(j + 1, tile))
+        out.append(centre * total)
+    return out
+
+
+def block_tiles(stores, sums, scales, wire):
+    press, cross, lower, heat = stores
+    gp, gt = scales
+    outside = jnp.where(wire > 0.0, 0.0, 1.0)
+    a = press + sums[0] + outside
+    d = heat + sums[1] + outside
+    inverse = 1.0 / (a * d + cross * lower)
+    pp, pt, tt = gp * gp * inverse, gp * gt * inverse, gt * gt * inverse
+    return a, d, (pp * d, pt * cross, -(pt * lower), tt * a)
+
+
+def root_tables(props_ref):
+    tables = wide_tables(props_ref)
+    return [jnp.sqrt(jnp.maximum(table, 0.0)) for table in tables[:2]], tables[2]
+
+
+def beyond_lines(beyond_ref, g, j):
+    return tuple(
+        jnp.broadcast_to(beyond_ref[g, end, j // SUB, pl.ds(j % SUB, 1)], TILE) for end in (1, 0)
+    )
+
+
+def own_coefficients_kernel(
     props_ref, fields_ref, wire_ref, xe_ref, xo_ref, ye_ref, yo_ref, source_ref,
-    coeff_ref, image_ref, scale_ref, solved_ref, rims_ref, even_ref, odd_ref,
-    gp_ref, gt_ref, beyond_ref, rhs_ref, *buffers,
+    own_ref, own_side_ref, image_ref, scale_ref, rhs_ref, roots_ref, roots_side_ref, beyond_ref,
 ):
     rows = wire_ref.shape[0]
+    spot = lane()
+    roots, carried = root_tables(props_ref)
+    _, x_wire = halo_x(xe_ref, xo_ref)
+    sides, beyond = unpack_wire(ye_ref, yo_ref, rows, rows)
+    wire = x_wire[:RIM] + [wire_ref[x] for x in range(rows)] + x_wire[RIM:]
+    for g in range(2):
+        for j, value in enumerate(wire):
+            roots_ref[g, j] = lookup(roots[g], value)
+        for x in range(rows):
+            roots_side_ref[g, x] = lookup(roots[g], sides[x])
+        for tile, ends in enumerate(beyond):
+            for end in range(2):
+                beyond_ref[g, end, tile] = lookup(roots[g], ends[end])
+    for x in range(rows):
+        inner = 0 < x < rows - 1
+        sums = []
+        for g in range(2):
+            tiles = lambda j, tile: roots_side_ref[g, j - RIM] if tile else roots_ref[g, j]
+            lines = beyond_lines(beyond_ref, g, x) if inner else (None, None)
+            sums.append(diagonal(tiles, (x + RIM, *lines), spot))
+        stores = [fields_ref[k, x] for k in range(4)]
+        gp, gt = (roots_ref[g, x + RIM] for g in range(2))
+        a, d, coeffs = block_tiles(stores, (sums[0][0], sums[1][0]), (gp, gt), wire_ref[x])
+        for k in range(4):
+            own_ref[k, x] = coeffs[k]
+        over_p, over_t = 1.0 / gp, 1.0 / gt
+        over = over_p * over_t
+        image_ref[0, x] = a * (over_p * over_p)
+        image_ref[1, x] = -(stores[1] * over)
+        image_ref[2, x] = stores[2] * over
+        image_ref[3, x] = d * (over_t * over_t)
+        for k, value in enumerate((gp, gt, over_p, over_t, lookup(carried, wire_ref[x]))):
+            scale_ref[k, x] = value
+        rhs_ref[0, x] = source_ref[0, x] * over_p
+        rhs_ref[1, x] = source_ref[1, x] * over_t
+        if inner:
+            stores = unpack_fields(ye_ref, yo_ref, rows, x)
+            scales = [roots_side_ref[g, x] for g in range(2)]
+            _, _, coeffs = block_tiles(stores, (sums[0][1], sums[1][1]), scales, sides[x])
+            for k in range(4):
+                own_side_ref[k, x - 1] = coeffs[k]
+
+
+def first_solve_kernel(
+    props_ref, xe_ref, xo_ref, ye_ref, yo_ref, ce_ref, co_ref,
+    own_ref, own_side_ref, rhs_ref, roots_ref, roots_side_ref, beyond_ref,
+    rest_ref, rest_side_ref, solved_ref, rims_ref, even_ref, odd_ref,
+    corner_roots_ref, corner_beyond_ref, *buffers,
+):
+    rows = own_ref.shape[1]
     wide = rows + 2 * MARGIN
-    row, spot = sublane(), lane()
-    tables = wide_tables(props_ref)
-    roots = [jnp.sqrt(jnp.maximum(tables[0], 0.0)), jnp.sqrt(jnp.maximum(tables[1], 0.0))]
-    fields, wire = widen_x(fields_ref, wire_ref, xe_ref, xo_ref)
-    first, has_low, has_high = position("gy")
-    half = wide // 2 + 1
-    sides = []
-    for j in range(half):
-        low, high = from_sides(first, ye_ref[2 * wide + j], yo_ref[2 * wide + j])
-        low = jnp.where(has_low, low, 0.0)
-        high = jnp.where(has_high, high, 0.0)
-        sides.append((jnp.where(row < 4, high, low), half_turn(jnp.where(row < 4, low, high))))
-    sides = [side[0] for side in sides] + [side[1] for side in sides]
-    for tile in range(beyond_ref.shape[2]):
-        ends = from_sides(first, ye_ref[2 * wide + half + tile], yo_ref[2 * wide + half + tile])
-        for end, (there, value) in enumerate(zip((has_low, has_high), ends)):
-            value = jnp.where(there, value, 0.0)
-            for g in range(2):
-                beyond_ref[g, end, tile] = lookup(roots[g], value)
-    out_wire = list(zip(wire, sides))
-    for j in range(wide + 2):
-        for g, ref in enumerate((gp_ref, gt_ref)):
-            ref[j, 0] = lookup(roots[g], wire[j])
-            ref[j, 1] = lookup(roots[g], sides[j])
-    for i in range(wide):
-        j = i + 1
-        stores = []
-        for pair in range(2):
-            low, high = from_sides(first, ye_ref[pair * wide + i], yo_ref[pair * wide + i])
-            stores.append(jnp.where(row < 4, high, low))
-            stores.append(half_turn(jnp.where(row < 4, low, high)))
-        diagonals = []
-        for g, ref in enumerate((gp_ref, gt_ref)):
-            last_down, last_up = (
-                jnp.broadcast_to(beyond_ref[g, end, j // SUB, pl.ds(j % SUB, 1)], TILE) for end in range(2)
-            )
-            own_sum, side_sum = along_y(ref[j, 0], ref[j, 1], row, last_up, last_down)
-            own_sum = own_sum + along_z(ref[j, 0], spot) + (ref[j - 1, 0] + ref[j + 1, 0])
-            side_sum = side_sum + along_z(ref[j, 1], spot) + (ref[j - 1, 1] + ref[j + 1, 1])
-            diagonals.append((ref[j, 0] * own_sum, ref[j, 1] * side_sum))
-        for tile in range(2):
-            if tile == 0:
-                press, cross, lower, heat = (fields[k][i] for k in range(4))
+    spot = lane()
+    roots, _ = root_tables(props_ref)
+    x_fields, x_wire = halo_x(xe_ref, xo_ref)
+    sides, beyond = unpack_wire(ce_ref, co_ref, 2 * MARGIN, 2 * RIM)
+    own_sides, _ = unpack_wire(ye_ref, yo_ref, rows, rows)
+    for g in range(2):
+        for j, value in enumerate(sides):
+            corner_roots_ref[g, j] = lookup(roots[g], value)
+        for tile, ends in enumerate(beyond):
+            for end in range(2):
+                corner_beyond_ref[g, end, tile] = lookup(roots[g], ends[end])
+    for i in list(range(RIM)) + list(range(wide - RIM, wide)):
+        j, x = i + 1, i - MARGIN
+        own_row = 0 <= x < rows
+        sums = []
+        for g in range(2):
+
+            def tiles(j, tile):
+                if not tile:
+                    return roots_ref[g, j]
+                if RIM <= j < RIM + rows:
+                    return roots_side_ref[g, j - RIM]
+                return corner_roots_ref[g, j if j < RIM else j - rows]
+
+            if own_row:
+                lines = beyond_lines(beyond_ref, g, x)
             else:
-                press, cross, lower, heat = stores
-            outside = jnp.where(out_wire[j][tile] > 0.0, 0.0, 1.0)
-            gp, gt = gp_ref[j, tile], gt_ref[j, tile]
-            a = press + diagonals[0][tile] + outside
-            d = heat + diagonals[1][tile] + outside
-            inverse = 1.0 / (a * d + cross * lower)
-            pp, pt, tt = gp * gp, gp * gt, gt * gt
-            coeff_ref[0, i, tile] = pp * d * inverse
-            coeff_ref[1, i, tile] = pt * cross * inverse
-            coeff_ref[2, i, tile] = -pt * lower * inverse
-            coeff_ref[3, i, tile] = tt * a * inverse
-            if tile == 0 and MARGIN <= i < wide - MARGIN:
-                x = i - MARGIN
-                over_p, over_t = 1.0 / gp, 1.0 / gt
-                over = over_p * over_t
-                image_ref[0, x] = a * (over_p * over_p)
-                image_ref[1, x] = -cross * over
-                image_ref[2, x] = lower * over
-                image_ref[3, x] = d * (over_t * over_t)
-                scale_ref[0, x] = gp
-                scale_ref[1, x] = gt
-                scale_ref[2, x] = over_p
-                scale_ref[3, x] = over_t
-                scale_ref[4, x] = lookup(tables[2], out_wire[j][0])
-                rhs_ref[0, x] = source_ref[0, x] * over_p
-                rhs_ref[1, x] = source_ref[1, x] * over_t
-    subdomain_sweeps(rhs_ref, coeff_ref, solved_ref, rims_ref, even_ref, odd_ref, buffers, rows)
+                lines = beyond_lines(corner_beyond_ref, g, j if j < RIM else j - rows)
+            sums.append((diagonal(tiles, (j, *lines), spot), tiles(j, 0), tiles(j, 1)))
+        corner = i if i < MARGIN else i - rows
+        if not own_row:
+            stores = [x_fields[k][corner] for k in range(4)]
+            scales = (sums[0][1], sums[1][1])
+            spare = x_wire[j if j < RIM else j - rows]
+            _, _, coeffs = block_tiles(stores, (sums[0][0][0], sums[1][0][0]), scales, spare)
+            for k in range(4):
+                rest_ref[k, corner] = coeffs[k]
+            stores = unpack_fields(ce_ref, co_ref, 2 * MARGIN, corner)
+            spare = sides[j if j < RIM else j - rows]
+        else:
+            stores = unpack_fields(ye_ref, yo_ref, rows, x)
+            spare = own_sides[x]
+        scales = (sums[0][2], sums[1][2])
+        _, _, coeffs = block_tiles(stores, (sums[0][0][1], sums[1][0][1]), scales, spare)
+        for k in range(4):
+            rest_side_ref[k, i if i < RIM else i - (rows - 2)] = coeffs[k]
+    coeff = getter(own_ref, own_side_ref, rest_ref, rest_side_ref)
+    subdomain_sweeps(rhs_ref, coeff, solved_ref, rims_ref, even_ref, odd_ref, buffers, rows)
 
 
 def fold_y_kernel(solved_ref, rims_ref, ye_ref, yo_ref, summed_ref, edges_ref, even_ref, odd_ref):
@@ -418,7 +526,7 @@
 
 
 def step_kernel(
-    summed_ref, edges_ref, xe_ref, xo_ref, coeff_ref, image_ref, scale_ref, source_ref,
+    summed_ref, edges_ref, xe_ref, xo_ref, own_ref, own_side_ref, rest_ref, rest_side_ref, image_ref, scale_ref, source_ref,
     direction_ref, power_ref, gram_ref, solved_ref, rims_ref, even_ref, odd_ref,
     rhs_ref, q_ref, t_ref, edge_ref, *buffers,
 ):
@@ -439,7 +547,8 @@
             products[1] = products[1] + source * power
             products[2] = products[2] + power * power
     gram_ref[...] = gram_rows(products, row, 0)
-    subdomain_sweeps(rhs_ref, coeff_ref, solved_ref, rims_ref, even_ref, odd_ref, buffers, rows)
+    coeff = getter(own_ref, own_side_ref, rest_ref, rest_side_ref)
+    subdomain_sweeps(rhs_ref, coeff, solved_ref, rims_ref, even_ref, odd_ref, buffers, rows)
 
 
 def last_kernel(
@@ -556,31 +665,38 @@
     devices = lax.axis_size("gx") * lax.axis_size("gy")
     cells = 2.0 * rows * soil_ids.shape[1] * depth * devices
     own = (rows, *TILE)
-    slab = (4 * MARGIN + RIM, *TILE)
-    fields, wire, even, odd = call(
-        pack_x_kernel,
-        [(4, *own), own, slab, slab],
+    x_slab = (4 * MARGIN + RIM, *TILE)
+    slab = y_slab(rows, rows)
+    fields, wire, x_even, x_odd, y_even, y_odd = call(
+        first_pack_kernel,
+        [(4, *own), own, x_slab, x_slab, slab, slab],
         [soil_props.shape, (4, *own), pltpu.VMEM(own, jnp.int32), pltpu.VMEM((SUB, rows), jnp.int32)]
         + [pltpu.SemaphoreType.DMA((4,))],
-        name="pack_x",
+        name="first_pack",
         inside=pltpu.HBM,
     )(*(pltpu.with_memory_space_constraint(x, pltpu.HBM) for x in (soil_props, storage, soil_ids, bc_mask.T)))
-    xe, xo = exchange("gx", even, odd)
-    half = wide // 2 + 1
-    rims = -(-2 * half // SUB)
-    slab = (2 * wide + half + rims, *TILE)
-    even, odd = call(pack_y_kernel, [slab, slab], [(2 * half, *TILE)], name="pack_y")(fields, wire, xe, xo)
-    ye, yo = exchange("gy", even, odd)
+    xe, xo = exchange("gx", x_even, x_odd)
+    ye, yo = exchange("gy", y_even, y_odd)
+    slab = y_slab(2 * MARGIN, 2 * RIM)
+    even, odd = call(corner_pack_kernel, [slab, slab], [(2 * RIM, *TILE)], name="corner_pack")(xe, xo)
+    ce, co = exchange("gy", even, odd)
+    count = wide // SUB
+    own_coeff, own_side, image, scales, rhs, roots, roots_side, beyond = call(
+        own_coefficients_kernel,
+        [(4, *own), (4, rows - 2, *TILE), (4, *own), (5, *own), (2, *own)]
+        + [(2, rows + 2 * RIM, *TILE), (2, *own), (2, 2, -(-rows // SUB), *TILE)],
+        name="own_coefficients",
+    )(soil_props, fields, wire, xe, xo, ye, yo, adjoint_source)
     buffers = [(wide + 2, 2, *TILE)] * 4
-    count = wide // SUB
     slab = (wide + 2 * count, *TILE)
     solved_shapes = [(2, wide, *TILE), (4, count, *TILE), slab, slab]
-    coeff, image, scales, solved, edges, even, odd = call(
-        coefficients_kernel,
-        [(4, wide, 2, *TILE), (4, *own), (5, *own)] + solved_shapes,
-        [(wide + 2, 2, *TILE)] * 2 + [(2, 2, rims, *TILE), (2, *own)] + buffers,
+    rest, rest_side, solved, edges, even, odd = call(
+        first_solve_kernel,
+        [(4, 2 * MARGIN, *TILE), (4, 2 * RIM, *TILE)] + solved_shapes,
+        [(2, 2 * RIM, *TILE), (2, 2, -(-2 * RIM // SUB), *TILE)] + buffers,
         name="first_solve",
-    )(soil_props, fields, wire, xe, xo, ye, yo, adjoint_source)
+    )(soil_props, xe, xo, ye, yo, ce, co, own_coeff, own_side, rhs, roots, roots_side, beyond)
+    coeffs = (own_coeff, own_side, rest, rest_side)
 
     slab = (2 * (MARGIN + 2), *TILE)
     fold_shapes = [(2, wide, *TILE), (4, count, *TILE), slab, slab]
@@ -588,15 +704,15 @@
     summed, edges, even, odd = call(fold_y_kernel, fold_shapes, name="fold_y")(solved, edges, ye, yo)
     xe, xo = exchange("gx", even, odd)
     halo = [(rows + 2, *TILE)] * 2 + [(4, count, *TILE)]
-    one, power, gram, solved, rest, even, odd = call(
+    one, power, gram, solved, edges, even, odd = call(
         step_kernel,
         [(2, *own), (2, *own), TILE] + solved_shapes,
         [(2, *own)] + halo + buffers,
         name="second_solve",
-    )(summed, edges, xe, xo, coeff, image, scales, adjoint_source)
+    )(summed, edges, xe, xo, *coeffs, image, scales, adjoint_source)
 
     ye, yo = exchange("gy", even, odd)
-    summed, edges, even, odd = call(fold_y_kernel, fold_shapes, name="fold_y")(solved, rest, ye, yo)
+    summed, edges, even, odd = call(fold_y_kernel, fold_shapes, name="fold_y")(solved, edges, ye, yo)
     xe, xo = exchange("gx", even, odd)
     two, second, gram = call(
         last_kernel, [(2, *own), (2, *own), (devices, LANE)], halo, name="last_image"

time: 52.2 us -> 50.8 us (0.973)
  waiting for transfers between devices: 16.9 us -> 11.9 us
  starting transfers between devices: 17.1 us -> 19.6 us
  blocking collectives: 11.5 us -> 12.7 us
    ppermute x6 -> x7, waiting for transfers between devices: 6.83 us -> 4.31 us  [exchange(): lax.ppermute(even, axis, pairs)]
    ppermute x6 -> x7, waiting for transfers between devices: 10.1 us -> 7.63 us  [exchange(): lax.ppermute(odd, ('gx', 'gy'), others)]
    ppermute x6 -> x7, starting transfers between devices: 9.71 us -> 11.7 us  [exchange(): lax.ppermute(odd, ('gx', 'gy'), others)]
    all_to_all x1, blocking collectives: 11.5 us -> 12.7 us  [shards(): gram = lax.all_to_all(gram, ('gx', 'gy'), 0, 0, tiled=True)]
    ppermute x6 -> x7, starting transfers between devices: 7.39 us -> 7.9 us  [exchange(): lax.ppermute(even, axis, pairs)]
    pallas_call x8 -> x9, Pallas kernels: 5.72 us -> 5.66 us  [run(): pl.pallas_call(kernel, out_shape=[jax.ShapeDtypeStruct(shape, F32) for sh...]
  transfers between devices with their start and end apart: 12 -> 14, of which waited for: 6 -> 5; matrix products, arithmetic and copies ran while one was open for 0% -> 0% of each run, Pallas kernels for 0% -> 1%
where the time goes in v4:
time: 50.8 us; the launch traced here: 50.6 us
  starting transfers between devices  19.6 us (39%)
  blocking collectives  12.7 us (25%)
  waiting for transfers between devices  11.9 us (23%)
  Pallas kernels  5.66 us (11%)
  between operations  0.74 us (1%)
    all_to_all x1, blocking collectives, shards(): gram = lax.all_to_all(gram, ('gx', 'gy'), 0, 0, tiled=True)  12.7 us
    ppermute x7, starting transfers between devices, exchange(): lax.ppermute(odd, ('gx', 'gy'), others)  11.7 us
    ppermute x7, starting transfers between devices, exchange(): lax.ppermute(even, axis, pairs)  7.9 us
    ppermute x7, waiting for transfers between devices, exchange(): lax.ppermute(odd, ('gx', 'gy'), others)  7.63 us
    pallas_call x9, Pallas kernels, run(): pl.pallas_call(kernel, out_shape=[jax.ShapeDtypeStruct(shape, F32) for sh...  5.66 us
    ppermute x7, waiting for transfers between devices, exchange(): lax.ppermute(even, axis, pairs)  4.31 us
  transfers between devices with their start and end apart: 14, of which 5 were waited for; matrix products, arithmetic and copies ran while one was open for 0% of the time, Pallas kernels for 1%

profile of v4, /device:TPU:0, one launch (start us, length us, event | category | flops | bytes accessed | tf_op | source)
XLA Modules:
  0.0 50.6 jit_solution(9273666319544046455)
XLA Ops:
  0.6 1.2 %first_pack.1 = (f32[4,16,8,128]{3,2,1,0:T(8,128)S(1)}, f32[16,8,128]{2,1,0:T(8,128)S(1)}, f32[21,8,128]{2,1,0:T(8,128)S(1)}, f32[21,8,128]{2,1,0:T(8,128)S(1)},...) custom-call(f32[3,16]{1,0:T(4,128)} %props_ref.3, f32[4,16,8,128]{3,2,1,0:T(8,128)} %storage_hbm.1, ...), custom_call_target="tpu_custom_call" | custom-call | tf_op jit(solution)/shard_map/first_pack/pallas_call | solution.py:632
  1.9 0.0 copy-start
  1.9 3.0 %collective-permute-start = (f32[21,8,128]{2,1,0:T(8,128)S(1)}, f32[21,8,128]{2,1,0:T(8,128)S(1)}, u32[]{:S(2)}, u32[]{:S(2)}) collective-permute-start(f32[21,8,128]{2,1,0:T(8,128)S(1)} %get-tuple-element.43), channel_id=1, source_target_pairs={{0,8},{8,0},{16,24},{24,16},{1,9},{9,1},{17,25},{25,17},{2,10},{10... | collective-permute-start | bytes 258056 | tf_op jit(solution)/shard_map/ppermute | solution.py:659
  4.9 0.0 collective-permute-start.1
  4.9 0.5 %collective-permute-start.2 = (f32[42,8,128]{2,1,0:T(8,128)S(1)}, f32[42,8,128]{2,1,0:T(8,128)S(1)}, u32[]{:S(2)}, u32[]{:S(2)}) collective-permute-start(f32[42,8,128]{2,1,0:T(8,128)S(1)} %get-tuple-element.45), channel_id=1, source_target_pairs={{0,1},{1,0},{2,3},{3,2},{4,5},{5,4},{6,7},{7,6},{8,9},{9,8},{10,11... | collective-permute-start | bytes 516104 | tf_op jit(solution)/shard_map/ppermute | solution.py:659
  5.4 2.5 %collective-permute-start.3 = (f32[42,8,128]{2,1,0:T(8,128)S(1)}, f32[42,8,128]{2,1,0:T(8,128)S(1)}, u32[]{:S(2)}, u32[]{:S(2)}) collective-permute-start(f32[42,8,128]{2,1,0:T(8,128)S(1)} %get-tuple-element.46), channel_id=1, source_target_pairs={{0,8},{1,2},{2,1},{3,4},{4,3},{5,6},{6,5},{7,15},{8,0},{9,10},{10,... | collective-permute-start | bytes 516104 | tf_op jit(solution)/shard_map/ppermute | solution.py:659
  7.9 0.0 collective-permute-done.xe_ref
  7.9 0.0 collective-permute-done.1.xo_ref
  7.9 0.1 collective-permute-start.4
  8.0 0.0 copy-start.1
  8.0 4.1 %collective-permute-start.5 = (f32[23,8,128]{2,1,0:T(8,128)S(1)}, f32[23,8,128]{2,1,0:T(8,128)S(1)}, u32[]{:S(2)}, u32[]{:S(2)}) collective-permute-start(f32[23,8,128]{2,1,0:T(8,128)S(1)} %get-tuple-element.48), channel_id=1, source_target_pairs={{0,8},{1,2},{2,1},{3,4},{4,3},{5,6},{6,5},{7,15},{8,0},{9,10},{10,... | collective-permute-start | bytes 282632 | tf_op jit(solution)/shard_map/ppermute | solution.py:659
  12.2 0.0 collective-permute-done.3.yo_ref
  12.2 0.6 %own_coefficients.1 = (f32[4,16,8,128]{3,2,1,0:T(8,128)S(1)}, f32[4,14,8,128]{3,2,1,0:T(8,128)S(1)}, f32[4,16,8,128]{3,2,1,0:T(8,128)S(1)}, f32[5,16,8,128]{3,2,...) custom-call(f32[3,16]{1,0:T(4,128)S(1)} %copy-done.1, ...), custom_call_target="tpu_custom_call" | custom-call | tf_op jit(solution)/shard_map/own_coefficients/pallas_call | solution.py:632
  12.8 0.0 collective-permute-done.4.ce_ref
  12.8 1.9 %collective-permute-done.5.co_ref = f32[23,8,128]{2,1,0:T(8,128)S(1)} collective-permute-done((f32[23,8,128]{2,1,0:T(8,128)S(1)}, f32[23,8,128]{2,1,0:T(8,128)S(1)}, u32[]{:S(2)}, u32[]{:S(2)}) %collective-permute-start.5) | collective-permute-done | bytes 94240 | tf_op jit(solution)/shard_map/ppermute | solution.py:659
  14.7 1.3 %first_solve.1 = (f32[4,8,8,128]{3,2,1,0:T(8,128)S(1)}, f32[4,10,8,128]{3,2,1,0:T(8,128)S(1)}, f32[2,24,8,128]{3,2,1,0:T(8,128)S(1)}, f32[4,3,8,128]{3,2,1,0:T(8...) custom-call(f32[3,16]{1,0:T(4,128)S(1)} %copy-done.1, f32[21,8,128]{2,1,0:T(8,128)S(1)} %collective-permute-done.xe_ref, ...), custom_call_target="tpu_custom_call" | custom-call | tf_op jit(solution)/shard_map/first_solve/pallas_call | solution.py:632
  16.0 0.1 collective-permute-start.6
  16.1 2.1 %collective-permute-start.7 = (f32[30,8,128]{2,1,0:T(8,128)S(1)}, f32[30,8,128]{2,1,0:T(8,128)S(1)}, u32[]{:S(2)}, u32[]{:S(2)}) collective-permute-start(f32[30,8,128]{2,1,0:T(8,128)S(1)} %get-tuple-element.60), channel_id=1, source_target_pairs={{0,8},{1,2},{2,1},{3,4},{4,3},{5,6},{6,5},{7,15},{8,0},{9,10},{10,... | collective-permute-start | bytes 368648 | tf_op jit(solution)/shard_map/ppermute | solution.py:659
  18.2 2.9 %collective-permute-done.7.yo_ref = f32[30,8,128]{2,1,0:T(8,128)S(1)} collective-permute-done((f32[30,8,128]{2,1,0:T(8,128)S(1)}, f32[30,8,128]{2,1,0:T(8,128)S(1)}, u32[]{:S(2)}, u32[]{:S(2)}) %collective-permute-start.7) | collective-permute-done | bytes 122912 | tf_op jit(solution)/shard_map/ppermute | solution.py:659
  21.0 0.1 fold_y.2
  21.1 2.1 %collective-permute-start.8 = (f32[12,8,128]{2,1,0:T(8,128)S(1)}, f32[12,8,128]{2,1,0:T(8,128)S(1)}, u32[]{:S(2)}, u32[]{:S(2)}) collective-permute-start(f32[12,8,128]{2,1,0:T(8,128)S(1)} %get-tuple-element.63), channel_id=1, source_target_pairs={{0,8},{8,0},{16,24},{24,16},{1,9},{9,1},{17,25},{25,17},{2,10},{10... | collective-permute-start | bytes 147464 | tf_op jit(solution)/shard_map/ppermute | solution.py:659
  23.2 2.1 %collective-permute-done.8.xe_ref = f32[12,8,128]{2,1,0:T(8,128)S(1)} collective-permute-done((f32[12,8,128]{2,1,0:T(8,128)S(1)}, f32[12,8,128]{2,1,0:T(8,128)S(1)}, u32[]{:S(2)}, u32[]{:S(2)}) %collective-permute-start.8) | collective-permute-done | bytes 49184 | tf_op jit(solution)/shard_map/ppermute | solution.py:659
  25.3 1.2 %second_solve.1 = (f32[2,16,8,128]{3,2,1,0:T(8,128)S(1)}, f32[2,16,8,128]{3,2,1,0:T(8,128)S(1)}, f32[8,128]{1,0:T(8,128)S(1)}, f32[2,24,8,128]{3,2,1,0:T(8,128)S...) custom-call(f32[2,24,8,128]{3,2,1,0:T(8,128)S(1)} %get-tuple-element.61.summed_ref, ...), custom_call_target="tpu_custom_call" | custom-call | tf_op jit(solution)/shard_map/second_solve/pallas_call | solution.py:632
  26.5 0.1 collective-permute-start.10
  26.6 3.0 %collective-permute-start.11 = (f32[30,8,128]{2,1,0:T(8,128)S(1)}, f32[30,8,128]{2,1,0:T(8,128)S(1)}, u32[]{:S(2)}, u32[]{:S(2)}) collective-permute-start(f32[30,8,128]{2,1,0:T(8,128)S(1)} %get-tuple-element.72), channel_id=1, source_target_pairs={{0,8},{1,2},{2,1},{3,4},{4,3},{5,6},{6,5},{7,15},{8,0},{9,10},{10,... | collective-permute-start | bytes 368648 | tf_op jit(solution)/shard_map/ppermute | solution.py:659
  29.6 2.9 %collective-permute-done.11.yo_ref = f32[30,8,128]{2,1,0:T(8,128)S(1)} collective-permute-done((f32[30,8,128]{2,1,0:T(8,128)S(1)}, f32[30,8,128]{2,1,0:T(8,128)S(1)}, u32[]{:S(2)}, u32[]{:S(2)}) %collective-permute-start.11) | collective-permute-done | bytes 122912 | tf_op jit(solution)/shard_map/ppermute | solution.py:659
  32.4 0.1 fold_y.3
  32.5 2.1 %collective-permute-start.12 = (f32[12,8,128]{2,1,0:T(8,128)S(1)}, f32[12,8,128]{2,1,0:T(8,128)S(1)}, u32[]{:S(2)}, u32[]{:S(2)}) collective-permute-start(f32[12,8,128]{2,1,0:T(8,128)S(1)} %get-tuple-element.75), channel_id=1, source_target_pairs={{0,8},{8,0},{16,24},{24,16},{1,9},{9,1},{17,25},{25,17},{2,10},{10... | collective-permute-start | bytes 147464 | tf_op jit(solution)/shard_map/ppermute | solution.py:659
  34.6 2.1 %collective-permute-done.12.xe_ref = f32[12,8,128]{2,1,0:T(8,128)S(1)} collective-permute-done((f32[12,8,128]{2,1,0:T(8,128)S(1)}, f32[12,8,128]{2,1,0:T(8,128)S(1)}, u32[]{:S(2)}, u32[]{:S(2)}) %collective-permute-start.12) | collective-permute-done | bytes 49184 | tf_op jit(solution)/shard_map/ppermute | solution.py:659
  36.7 0.3 last_image.1
  37.0 12.7 %all_to_all.11 = f32[32,1,128]{2,1,0:T(1,128)S(1)} all-to-all(f32[32,1,128]{2,1,0:T(1,128)S(1)} %bitcast.6), channel_id=1, replica_groups=mesh['gx'=4,'gy'=8] {'gx','gy'}, dimensions={0} | all-to-all | bytes 32768 | tf_op jit(solution)/shard_map/all_to_all | solution.py:720
  49.7 1.0 %combine.1 = (f32[2,16,8,128]{3,2,1,0:T(8,128)}, f32[2,16,8,128]{3,2,1,0:T(8,128)}, f32[2,16,8,128]{3,2,1,0:T(8,128)}) custom-call(f32[32,128]{1,0:T(8,128)S(1)} %bitcast.5, f32[2,16,8,128]{3,2,1,0:T(8,128)S(1)} %copy-done, f32[2,16,8,128]{3,2,1,0:T(8,128)S(1)} %get-tuple-element.77.power_ref, f32[2,16,8,128]{3,2,1,0:T(8,128)S(1)} %get-tuple-element.80.second_ref, ...), custom_call_target="tpu_custom_call" | custom-call | tf_op jit(solution)/shard_map/combine/pallas_call | solution.py:632
  (10 shorter events, 0.1 us)
Async XLA Ops:
  1.9 10.3 %copy-start = (f32[2,16,8,128]{3,2,1,0:T(8,128)S(1)}, f32[2,16,8,128]{3,2,1,0:T(8,128)}, u32[]{:S(2)}) copy-start(f32[2,16,8,128]{3,2,1,0:T(8,128)} %source_ref.7) | copy-start | bytes 393220
  1.9 6.0 %collective-permute-start = (f32[21,8,128]{2,1,0:T(8,128)S(1)}, f32[21,8,128]{2,1,0:T(8,128)S(1)}, u32[]{:S(2)}, u32[]{:S(2)}) collective-permute-start(f32[21,8,128]{2,1,0:T(8,128)S(1)} %get-tuple-element.43), channel_id=1, source_target_pairs={{0,8},{8,0},{16,24},{24,16},{1,9},{9,1},{17,25},{25,17},{2,10},{10... | collective-permute-start | bytes 258056 | tf_op jit(solution)/shard_map/ppermute | solution.py:659
  4.9 3.0 %collective-permute-start.1 = (f32[21,8,128]{2,1,0:T(8,128)S(1)}, f32[21,8,128]{2,1,0:T(8,128)S(1)}, u32[]{:S(2)}, u32[]{:S(2)}) collective-permute-start(f32[21,8,128]{2,1,0:T(8,128)S(1)} %get-tuple-element.44), channel_id=1, source_target_pairs={{0,1},{1,0},{2,3},{3,2},{4,5},{5,4},{6,7},{7,6},{8,16},{9,17},{10,... | collective-permute-start | bytes 258056 | tf_op jit(solution)/shard_map/ppermute | solution.py:659
  4.9 7.3 %collective-permute-start.2 = (f32[42,8,128]{2,1,0:T(8,128)S(1)}, f32[42,8,128]{2,1,0:T(8,128)S(1)}, u32[]{:S(2)}, u32[]{:S(2)}) collective-permute-start(f32[42,8,128]{2,1,0:T(8,128)S(1)} %get-tuple-element.45), channel_id=1, source_target_pairs={{0,1},{1,0},{2,3},{3,2},{4,5},{5,4},{6,7},{7,6},{8,9},{9,8},{10,11... | collective-permute-start | bytes 516104 | tf_op jit(solution)/shard_map/ppermute | solution.py:659
  5.4 6.8 %collective-permute-start.3 = (f32[42,8,128]{2,1,0:T(8,128)S(1)}, f32[42,8,128]{2,1,0:T(8,128)S(1)}, u32[]{:S(2)}, u32[]{:S(2)}) collective-permute-start(f32[42,8,128]{2,1,0:T(8,128)S(1)} %get-tuple-element.46), channel_id=1, source_target_pairs={{0,8},{1,2},{2,1},{3,4},{4,3},{5,6},{6,5},{7,15},{8,0},{9,10},{10,... | collective-permute-start | bytes 516104 | tf_op jit(solution)/shard_map/ppermute | solution.py:659
  7.9 4.9 %collective-permute-start.4 = (f32[23,8,128]{2,1,0:T(8,128)S(1)}, f32[23,8,128]{2,1,0:T(8,128)S(1)}, u32[]{:S(2)}, u32[]{:S(2)}) collective-permute-start(f32[23,8,128]{2,1,0:T(8,128)S(1)} %get-tuple-element.47), channel_id=1, source_target_pairs={{0,1},{1,0},{2,3},{3,2},{4,5},{5,4},{6,7},{7,6},{8,9},{9,8},{10,11... | collective-permute-start | bytes 282632 | tf_op jit(solution)/shard_map/ppermute | solution.py:659
  8.0 4.2 %copy-start.1 = (f32[3,16]{1,0:T(4,128)S(1)}, f32[3,16]{1,0:T(4,128)}, u32[]{:S(2)}) copy-start(f32[3,16]{1,0:T(4,128)} %props_ref.3) | copy-start | bytes 580
  8.0 6.7 %collective-permute-start.5 = (f32[23,8,128]{2,1,0:T(8,128)S(1)}, f32[23,8,128]{2,1,0:T(8,128)S(1)}, u32[]{:S(2)}, u32[]{:S(2)}) collective-permute-start(f32[23,8,128]{2,1,0:T(8,128)S(1)} %get-tuple-element.48), channel_id=1, source_target_pairs={{0,8},{1,2},{2,1},{3,4},{4,3},{5,6},{6,5},{7,15},{8,0},{9,10},{10,... | collective-permute-start | bytes 282632 | tf_op jit(solution)/shard_map/ppermute | solution.py:659
  16.0 2.2 %collective-permute-start.6 = (f32[30,8,128]{2,1,0:T(8,128)S(1)}, f32[30,8,128]{2,1,0:T(8,128)S(1)}, u32[]{:S(2)}, u32[]{:S(2)}) collective-permute-start(f32[30,8,128]{2,1,0:T(8,128)S(1)} %get-tuple-element.59), channel_id=1, source_target_pairs={{0,1},{1,0},{2,3},{3,2},{4,5},{5,4},{6,7},{7,6},{8,9},{9,8},{10,11... | collective-permute-start | bytes 368648 | tf_op jit(solution)/shard_map/ppermute | solution.py:659
  16.1 5.0 %collective-permute-start.7 = (f32[30,8,128]{2,1,0:T(8,128)S(1)}, f32[30,8,128]{2,1,0:T(8,128)S(1)}, u32[]{:S(2)}, u32[]{:S(2)}) collective-permute-start(f32[30,8,128]{2,1,0:T(8,128)S(1)} %get-tuple-element.60), channel_id=1, source_target_pairs={{0,8},{1,2},{2,1},{3,4},{4,3},{5,6},{6,5},{7,15},{8,0},{9,10},{10,... | collective-permute-start | bytes 368648 | tf_op jit(solution)/shard_map/ppermute | solution.py:659
  21.1 4.2 %collective-permute-start.8 = (f32[12,8,128]{2,1,0:T(8,128)S(1)}, f32[12,8,128]{2,1,0:T(8,128)S(1)}, u32[]{:S(2)}, u32[]{:S(2)}) collective-permute-start(f32[12,8,128]{2,1,0:T(8,128)S(1)} %get-tuple-element.63), channel_id=1, source_target_pairs={{0,8},{8,0},{16,24},{24,16},{1,9},{9,1},{17,25},{25,17},{2,10},{10... | collective-permute-start | bytes 147464 | tf_op jit(solution)/shard_map/ppermute | solution.py:659
  23.2 2.2 %collective-permute-start.9 = (f32[12,8,128]{2,1,0:T(8,128)S(1)}, f32[12,8,128]{2,1,0:T(8,128)S(1)}, u32[]{:S(2)}, u32[]{:S(2)}) collective-permute-start(f32[12,8,128]{2,1,0:T(8,128)S(1)} %get-tuple-element.64), channel_id=1, source_target_pairs={{0,1},{1,0},{2,3},{3,2},{4,5},{5,4},{6,7},{7,6},{8,16},{9,17},{10,... | collective-permute-start | bytes 147464 | tf_op jit(solution)/shard_map/ppermute | solution.py:659
  26.5 3.1 %collective-permute-start.10 = (f32[30,8,128]{2,1,0:T(8,128)S(1)}, f32[30,8,128]{2,1,0:T(8,128)S(1)}, u32[]{:S(2)}, u32[]{:S(2)}) collective-permute-start(f32[30,8,128]{2,1,0:T(8,128)S(1)} %get-tuple-element.71), channel_id=1, source_target_pairs={{0,1},{1,0},{2,3},{3,2},{4,5},{5,4},{6,7},{7,6},{8,9},{9,8},{10,11... | collective-permute-start | bytes 368648 | tf_op jit(solution)/shard_map/ppermute | solution.py:659
  26.6 5.8 %collective-permute-start.11 = (f32[30,8,128]{2,1,0:T(8,128)S(1)}, f32[30,8,128]{2,1,0:T(8,128)S(1)}, u32[]{:S(2)}, u32[]{:S(2)}) collective-permute-start(f32[30,8,128]{2,1,0:T(8,128)S(1)} %get-tuple-element.72), channel_id=1, source_target_pairs={{0,8},{1,2},{2,1},{3,4},{4,3},{5,6},{6,5},{7,15},{8,0},{9,10},{10,... | collective-permute-start | bytes 368648 | tf_op jit(solution)/shard_map/ppermute | solution.py:659
  32.5 4.2 %collective-permute-start.12 = (f32[12,8,128]{2,1,0:T(8,128)S(1)}, f32[12,8,128]{2,1,0:T(8,128)S(1)}, u32[]{:S(2)}, u32[]{:S(2)}) collective-permute-start(f32[12,8,128]{2,1,0:T(8,128)S(1)} %get-tuple-element.75), channel_id=1, source_target_pairs={{0,8},{8,0},{16,24},{24,16},{1,9},{9,1},{17,25},{25,17},{2,10},{10... | collective-permute-start | bytes 147464 | tf_op jit(solution)/shard_map/ppermute | solution.py:659
  34.6 2.2 %collective-permute-start.13 = (f32[12,8,128]{2,1,0:T(8,128)S(1)}, f32[12,8,128]{2,1,0:T(8,128)S(1)}, u32[]{:S(2)}, u32[]{:S(2)}) collective-permute-start(f32[12,8,128]{2,1,0:T(8,128)S(1)} %get-tuple-element.76), channel_id=1, source_target_pairs={{0,1},{1,0},{2,3},{3,2},{4,5},{5,4},{6,7},{7,6},{8,16},{9,17},{10,... | collective-permute-start | bytes 147464 | tf_op jit(solution)/shard_map/ppermute | solution.py:659

commit v5 on v4

--- a/solution.py
+++ b/solution.py
@@ -654,7 +654,7 @@
                 partner = ((place - 1) ^ 1) + 1
                 target = (partner, y) if axis == "gx" else (x, partner)
             else:
-                target = (x, y ^ 1) if axis == "gx" else (x ^ 1, y)
+                target = (x, y ^ 1) if axis == "gx" else (x ^ (n_x // 2), y)
             others.append((x * n_y + y, target[0] * n_y + target[1]))
     return lax.ppermute(even, axis, pairs), lax.ppermute(odd, ("gx", "gy"), others)
 

time: 50.8 us -> 49.8 us (0.980)
  blocking collectives: 12.7 us -> 11.7 us
  waiting for transfers between devices: 11.9 us -> 12.8 us
  starting transfers between devices: 19.6 us -> 18.8 us
    ppermute x7, starting transfers between devices: 11.7 us -> 10.7 us  [exchange(): lax.ppermute(odd, ('gx', 'gy'), others)]
    all_to_all x1, blocking collectives: 12.7 us -> 11.7 us  [shards(): gram = lax.all_to_all(gram, ('gx', 'gy'), 0, 0, tiled=True)]
    ppermute x7, waiting for transfers between devices: 4.31 us -> 5.13 us  [exchange(): lax.ppermute(even, axis, pairs)]
  transfers between devices with their start and end apart: 14 -> 14, of which waited for: 5 -> 6; matrix products, arithmetic and copies ran while one was open for 0% -> 0% of each run, Pallas kernels for 1% -> 1%
where the time goes in v5:
time: 49.8 us; the launch traced here: 49.6 us
  starting transfers between devices  18.8 us (38%)
  waiting for transfers between devices  12.8 us (26%)
  blocking collectives  11.7 us (23%)
  Pallas kernels  5.66 us (11%)
  between operations  0.74 us (1%)
    all_to_all x1, blocking collectives, shards(): gram = lax.all_to_all(gram, ('gx', 'gy'), 0, 0, tiled=True)  11.7 us
    ppermute x7, starting transfers between devices, exchange(): lax.ppermute(odd, ('gx', 'gy'), others)  10.7 us
    ppermute x7, starting transfers between devices, exchange(): lax.ppermute(even, axis, pairs)  8.09 us
    ppermute x7, waiting for transfers between devices, exchange(): lax.ppermute(odd, ('gx', 'gy'), others)  7.62 us
    pallas_call x9, Pallas kernels, run(): pl.pallas_call(kernel, out_shape=[jax.ShapeDtypeStruct(shape, F32) for sh...  5.66 us
    ppermute x7, waiting for transfers between devices, exchange(): lax.ppermute(even, axis, pairs)  5.13 us
  transfers between devices with their start and end apart: 14, of which 6 were waited for; matrix products, arithmetic and copies ran while one was open for 0% of the time, Pallas kernels for 1%

profile of v5, /device:TPU:0, one launch (start us, length us, event | category | flops | bytes accessed | tf_op | source)
XLA Modules:
  0.0 49.6 jit_solution(4250393605201837220)
XLA Ops:
  0.6 1.2 %first_pack.1 = (f32[4,16,8,128]{3,2,1,0:T(8,128)S(1)}, f32[16,8,128]{2,1,0:T(8,128)S(1)}, f32[21,8,128]{2,1,0:T(8,128)S(1)}, f32[21,8,128]{2,1,0:T(8,128)S(1)},...) custom-call(f32[3,16]{1,0:T(4,128)} %props_ref.3, f32[4,16,8,128]{3,2,1,0:T(8,128)} %storage_hbm.1, ...), custom_call_target="tpu_custom_call" | custom-call | tf_op jit(solution)/shard_map/first_pack/pallas_call | solution.py:632
  1.9 0.0 copy-start
  1.9 3.0 %collective-permute-start = (f32[21,8,128]{2,1,0:T(8,128)S(1)}, f32[21,8,128]{2,1,0:T(8,128)S(1)}, u32[]{:S(2)}, u32[]{:S(2)}) collective-permute-start(f32[21,8,128]{2,1,0:T(8,128)S(1)} %get-tuple-element.43), channel_id=1, source_target_pairs={{0,8},{8,0},{16,24},{24,16},{1,9},{9,1},{17,25},{25,17},{2,10},{10... | collective-permute-start | bytes 258056 | tf_op jit(solution)/shard_map/ppermute | solution.py:659
  4.9 0.0 collective-permute-start.1
  4.9 0.5 %collective-permute-start.2 = (f32[42,8,128]{2,1,0:T(8,128)S(1)}, f32[42,8,128]{2,1,0:T(8,128)S(1)}, u32[]{:S(2)}, u32[]{:S(2)}) collective-permute-start(f32[42,8,128]{2,1,0:T(8,128)S(1)} %get-tuple-element.45), channel_id=1, source_target_pairs={{0,1},{1,0},{2,3},{3,2},{4,5},{5,4},{6,7},{7,6},{8,9},{9,8},{10,11... | collective-permute-start | bytes 516104 | tf_op jit(solution)/shard_map/ppermute | solution.py:659
  5.4 1.0 %collective-permute-start.3 = (f32[42,8,128]{2,1,0:T(8,128)S(1)}, f32[42,8,128]{2,1,0:T(8,128)S(1)}, u32[]{:S(2)}, u32[]{:S(2)}) collective-permute-start(f32[42,8,128]{2,1,0:T(8,128)S(1)} %get-tuple-element.46), channel_id=1, source_target_pairs={{0,16},{1,2},{2,1},{3,4},{4,3},{5,6},{6,5},{7,23},{8,24},{9,10},{1... | collective-permute-start | bytes 516104 | tf_op jit(solution)/shard_map/ppermute | solution.py:659
  6.4 1.0 %collective-permute-done.xe_ref = f32[21,8,128]{2,1,0:T(8,128)S(1)} collective-permute-done((f32[21,8,128]{2,1,0:T(8,128)S(1)}, f32[21,8,128]{2,1,0:T(8,128)S(1)}, u32[]{:S(2)}, u32[]{:S(2)}) %collective-permute-start) | collective-permute-done | bytes 86048 | tf_op jit(solution)/shard_map/ppermute | solution.py:659
  7.4 0.0 collective-permute-done.1.xo_ref
  7.5 0.1 collective-permute-start.4
  7.5 0.0 copy-start.1
  7.5 4.5 %collective-permute-start.5 = (f32[23,8,128]{2,1,0:T(8,128)S(1)}, f32[23,8,128]{2,1,0:T(8,128)S(1)}, u32[]{:S(2)}, u32[]{:S(2)}) collective-permute-start(f32[23,8,128]{2,1,0:T(8,128)S(1)} %get-tuple-element.48), channel_id=1, source_target_pairs={{0,16},{1,2},{2,1},{3,4},{4,3},{5,6},{6,5},{7,23},{8,24},{9,10},{1... | collective-permute-start | bytes 282632 | tf_op jit(solution)/shard_map/ppermute | solution.py:659
  12.1 0.0 collective-permute-done.2.ye_ref
  12.1 0.6 %own_coefficients.1 = (f32[4,16,8,128]{3,2,1,0:T(8,128)S(1)}, f32[4,14,8,128]{3,2,1,0:T(8,128)S(1)}, f32[4,16,8,128]{3,2,1,0:T(8,128)S(1)}, f32[5,16,8,128]{3,2,...) custom-call(f32[3,16]{1,0:T(4,128)S(1)} %copy-done.1, ...), custom_call_target="tpu_custom_call" | custom-call | tf_op jit(solution)/shard_map/own_coefficients/pallas_call | solution.py:632
  12.7 1.9 %collective-permute-done.5.co_ref = f32[23,8,128]{2,1,0:T(8,128)S(1)} collective-permute-done((f32[23,8,128]{2,1,0:T(8,128)S(1)}, f32[23,8,128]{2,1,0:T(8,128)S(1)}, u32[]{:S(2)}, u32[]{:S(2)}) %collective-permute-start.5) | collective-permute-done | bytes 94240 | tf_op jit(solution)/shard_map/ppermute | solution.py:659
  14.6 1.3 %first_solve.1 = (f32[4,8,8,128]{3,2,1,0:T(8,128)S(1)}, f32[4,10,8,128]{3,2,1,0:T(8,128)S(1)}, f32[2,24,8,128]{3,2,1,0:T(8,128)S(1)}, f32[4,3,8,128]{3,2,1,0:T(8...) custom-call(f32[3,16]{1,0:T(4,128)S(1)} %copy-done.1, f32[21,8,128]{2,1,0:T(8,128)S(1)} %collective-permute-done.xe_ref, ...), custom_call_target="tpu_custom_call" | custom-call | tf_op jit(solution)/shard_map/first_solve/pallas_call | solution.py:632
  15.9 0.1 collective-permute-start.6
  16.0 2.1 %collective-permute-start.7 = (f32[30,8,128]{2,1,0:T(8,128)S(1)}, f32[30,8,128]{2,1,0:T(8,128)S(1)}, u32[]{:S(2)}, u32[]{:S(2)}) collective-permute-start(f32[30,8,128]{2,1,0:T(8,128)S(1)} %get-tuple-element.60), channel_id=1, source_target_pairs={{0,16},{1,2},{2,1},{3,4},{4,3},{5,6},{6,5},{7,23},{8,24},{9,10},{1... | collective-permute-start | bytes 368648 | tf_op jit(solution)/shard_map/ppermute | solution.py:659
  18.1 2.9 %collective-permute-done.7.yo_ref = f32[30,8,128]{2,1,0:T(8,128)S(1)} collective-permute-done((f32[30,8,128]{2,1,0:T(8,128)S(1)}, f32[30,8,128]{2,1,0:T(8,128)S(1)}, u32[]{:S(2)}, u32[]{:S(2)}) %collective-permute-start.7) | collective-permute-done | bytes 122912 | tf_op jit(solution)/shard_map/ppermute | solution.py:659
  21.0 0.1 fold_y.2
  21.0 2.2 %collective-permute-start.8 = (f32[12,8,128]{2,1,0:T(8,128)S(1)}, f32[12,8,128]{2,1,0:T(8,128)S(1)}, u32[]{:S(2)}, u32[]{:S(2)}) collective-permute-start(f32[12,8,128]{2,1,0:T(8,128)S(1)} %get-tuple-element.63), channel_id=1, source_target_pairs={{0,8},{8,0},{16,24},{24,16},{1,9},{9,1},{17,25},{25,17},{2,10},{10... | collective-permute-start | bytes 147464 | tf_op jit(solution)/shard_map/ppermute | solution.py:659
  23.2 2.1 %collective-permute-done.8.xe_ref = f32[12,8,128]{2,1,0:T(8,128)S(1)} collective-permute-done((f32[12,8,128]{2,1,0:T(8,128)S(1)}, f32[12,8,128]{2,1,0:T(8,128)S(1)}, u32[]{:S(2)}, u32[]{:S(2)}) %collective-permute-start.8) | collective-permute-done | bytes 49184 | tf_op jit(solution)/shard_map/ppermute | solution.py:659
  25.3 1.2 %second_solve.1 = (f32[2,16,8,128]{3,2,1,0:T(8,128)S(1)}, f32[2,16,8,128]{3,2,1,0:T(8,128)S(1)}, f32[8,128]{1,0:T(8,128)S(1)}, f32[2,24,8,128]{3,2,1,0:T(8,128)S...) custom-call(f32[2,24,8,128]{3,2,1,0:T(8,128)S(1)} %get-tuple-element.61.summed_ref, ...), custom_call_target="tpu_custom_call" | custom-call | tf_op jit(solution)/shard_map/second_solve/pallas_call | solution.py:632
  26.5 0.1 collective-permute-start.10
  26.6 3.0 %collective-permute-start.11 = (f32[30,8,128]{2,1,0:T(8,128)S(1)}, f32[30,8,128]{2,1,0:T(8,128)S(1)}, u32[]{:S(2)}, u32[]{:S(2)}) collective-permute-start(f32[30,8,128]{2,1,0:T(8,128)S(1)} %get-tuple-element.72), channel_id=1, source_target_pairs={{0,16},{1,2},{2,1},{3,4},{4,3},{5,6},{6,5},{7,23},{8,24},{9,10},{1... | collective-permute-start | bytes 368648 | tf_op jit(solution)/shard_map/ppermute | solution.py:659
  29.6 2.9 %collective-permute-done.11.yo_ref = f32[30,8,128]{2,1,0:T(8,128)S(1)} collective-permute-done((f32[30,8,128]{2,1,0:T(8,128)S(1)}, f32[30,8,128]{2,1,0:T(8,128)S(1)}, u32[]{:S(2)}, u32[]{:S(2)}) %collective-permute-start.11) | collective-permute-done | bytes 122912 | tf_op jit(solution)/shard_map/ppermute | solution.py:659
  32.4 0.1 fold_y.3
  32.5 2.2 %collective-permute-start.12 = (f32[12,8,128]{2,1,0:T(8,128)S(1)}, f32[12,8,128]{2,1,0:T(8,128)S(1)}, u32[]{:S(2)}, u32[]{:S(2)}) collective-permute-start(f32[12,8,128]{2,1,0:T(8,128)S(1)} %get-tuple-element.75), channel_id=1, source_target_pairs={{0,8},{8,0},{16,24},{24,16},{1,9},{9,1},{17,25},{25,17},{2,10},{10... | collective-permute-start | bytes 147464 | tf_op jit(solution)/shard_map/ppermute | solution.py:659
  34.6 0.0 collective-permute-start.13
  34.6 2.1 %collective-permute-done.12.xe_ref = f32[12,8,128]{2,1,0:T(8,128)S(1)} collective-permute-done((f32[12,8,128]{2,1,0:T(8,128)S(1)}, f32[12,8,128]{2,1,0:T(8,128)S(1)}, u32[]{:S(2)}, u32[]{:S(2)}) %collective-permute-start.12) | collective-permute-done | bytes 49184 | tf_op jit(solution)/shard_map/ppermute | solution.py:659
  36.7 0.3 last_image.1
  37.0 11.7 %all_to_all.11 = f32[32,1,128]{2,1,0:T(1,128)S(1)} all-to-all(f32[32,1,128]{2,1,0:T(1,128)S(1)} %bitcast.6), channel_id=1, replica_groups=mesh['gx'=4,'gy'=8] {'gx','gy'}, dimensions={0} | all-to-all | bytes 32768 | tf_op jit(solution)/shard_map/all_to_all | solution.py:720
  48.6 1.0 %combine.1 = (f32[2,16,8,128]{3,2,1,0:T(8,128)}, f32[2,16,8,128]{3,2,1,0:T(8,128)}, f32[2,16,8,128]{3,2,1,0:T(8,128)}) custom-call(f32[32,128]{1,0:T(8,128)S(1)} %bitcast.5, f32[2,16,8,128]{3,2,1,0:T(8,128)S(1)} %copy-done, f32[2,16,8,128]{3,2,1,0:T(8,128)S(1)} %get-tuple-element.77.power_ref, f32[2,16,8,128]{3,2,1,0:T(8,128)S(1)} %get-tuple-element.80.second_ref, ...), custom_call_target="tpu_custom_call" | custom-call | tf_op jit(solution)/shard_map/combine/pallas_call | solution.py:632
  (10 shorter events, 0.1 us)
Async XLA Ops:
  1.9 10.2 %copy-start = (f32[2,16,8,128]{3,2,1,0:T(8,128)S(1)}, f32[2,16,8,128]{3,2,1,0:T(8,128)}, u32[]{:S(2)}) copy-start(f32[2,16,8,128]{3,2,1,0:T(8,128)} %source_ref.7) | copy-start | bytes 393220
  1.9 5.5 %collective-permute-start = (f32[21,8,128]{2,1,0:T(8,128)S(1)}, f32[21,8,128]{2,1,0:T(8,128)S(1)}, u32[]{:S(2)}, u32[]{:S(2)}) collective-permute-start(f32[21,8,128]{2,1,0:T(8,128)S(1)} %get-tuple-element.43), channel_id=1, source_target_pairs={{0,8},{8,0},{16,24},{24,16},{1,9},{9,1},{17,25},{25,17},{2,10},{10... | collective-permute-start | bytes 258056 | tf_op jit(solution)/shard_map/ppermute | solution.py:659
  4.9 2.5 %collective-permute-start.1 = (f32[21,8,128]{2,1,0:T(8,128)S(1)}, f32[21,8,128]{2,1,0:T(8,128)S(1)}, u32[]{:S(2)}, u32[]{:S(2)}) collective-permute-start(f32[21,8,128]{2,1,0:T(8,128)S(1)} %get-tuple-element.44), channel_id=1, source_target_pairs={{0,1},{1,0},{2,3},{3,2},{4,5},{5,4},{6,7},{7,6},{8,16},{9,17},{10,... | collective-permute-start | bytes 258056 | tf_op jit(solution)/shard_map/ppermute | solution.py:659
  4.9 7.2 %collective-permute-start.2 = (f32[42,8,128]{2,1,0:T(8,128)S(1)}, f32[42,8,128]{2,1,0:T(8,128)S(1)}, u32[]{:S(2)}, u32[]{:S(2)}) collective-permute-start(f32[42,8,128]{2,1,0:T(8,128)S(1)} %get-tuple-element.45), channel_id=1, source_target_pairs={{0,1},{1,0},{2,3},{3,2},{4,5},{5,4},{6,7},{7,6},{8,9},{9,8},{10,11... | collective-permute-start | bytes 516104 | tf_op jit(solution)/shard_map/ppermute | solution.py:659
  5.4 6.7 %collective-permute-start.3 = (f32[42,8,128]{2,1,0:T(8,128)S(1)}, f32[42,8,128]{2,1,0:T(8,128)S(1)}, u32[]{:S(2)}, u32[]{:S(2)}) collective-permute-start(f32[42,8,128]{2,1,0:T(8,128)S(1)} %get-tuple-element.46), channel_id=1, source_target_pairs={{0,16},{1,2},{2,1},{3,4},{4,3},{5,6},{6,5},{7,23},{8,24},{9,10},{1... | collective-permute-start | bytes 516104 | tf_op jit(solution)/shard_map/ppermute | solution.py:659
  7.5 5.3 %collective-permute-start.4 = (f32[23,8,128]{2,1,0:T(8,128)S(1)}, f32[23,8,128]{2,1,0:T(8,128)S(1)}, u32[]{:S(2)}, u32[]{:S(2)}) collective-permute-start(f32[23,8,128]{2,1,0:T(8,128)S(1)} %get-tuple-element.47), channel_id=1, source_target_pairs={{0,1},{1,0},{2,3},{3,2},{4,5},{5,4},{6,7},{7,6},{8,9},{9,8},{10,11... | collective-permute-start | bytes 282632 | tf_op jit(solution)/shard_map/ppermute | solution.py:659
  7.5 4.6 %copy-start.1 = (f32[3,16]{1,0:T(4,128)S(1)}, f32[3,16]{1,0:T(4,128)}, u32[]{:S(2)}) copy-start(f32[3,16]{1,0:T(4,128)} %props_ref.3) | copy-start | bytes 580
  7.5 7.1 %collective-permute-start.5 = (f32[23,8,128]{2,1,0:T(8,128)S(1)}, f32[23,8,128]{2,1,0:T(8,128)S(1)}, u32[]{:S(2)}, u32[]{:S(2)}) collective-permute-start(f32[23,8,128]{2,1,0:T(8,128)S(1)} %get-tuple-element.48), channel_id=1, source_target_pairs={{0,16},{1,2},{2,1},{3,4},{4,3},{5,6},{6,5},{7,23},{8,24},{9,10},{1... | collective-permute-start | bytes 282632 | tf_op jit(solution)/shard_map/ppermute | solution.py:659
  15.9 2.2 %collective-permute-start.6 = (f32[30,8,128]{2,1,0:T(8,128)S(1)}, f32[30,8,128]{2,1,0:T(8,128)S(1)}, u32[]{:S(2)}, u32[]{:S(2)}) collective-permute-start(f32[30,8,128]{2,1,0:T(8,128)S(1)} %get-tuple-element.59), channel_id=1, source_target_pairs={{0,1},{1,0},{2,3},{3,2},{4,5},{5,4},{6,7},{7,6},{8,9},{9,8},{10,11... | collective-permute-start | bytes 368648 | tf_op jit(solution)/shard_map/ppermute | solution.py:659
  16.0 5.0 %collective-permute-start.7 = (f32[30,8,128]{2,1,0:T(8,128)S(1)}, f32[30,8,128]{2,1,0:T(8,128)S(1)}, u32[]{:S(2)}, u32[]{:S(2)}) collective-permute-start(f32[30,8,128]{2,1,0:T(8,128)S(1)} %get-tuple-element.60), channel_id=1, source_target_pairs={{0,16},{1,2},{2,1},{3,4},{4,3},{5,6},{6,5},{7,23},{8,24},{9,10},{1... | collective-permute-start | bytes 368648 | tf_op jit(solution)/shard_map/ppermute | solution.py:659
  21.0 4.3 %collective-permute-start.8 = (f32[12,8,128]{2,1,0:T(8,128)S(1)}, f32[12,8,128]{2,1,0:T(8,128)S(1)}, u32[]{:S(2)}, u32[]{:S(2)}) collective-permute-start(f32[12,8,128]{2,1,0:T(8,128)S(1)} %get-tuple-element.63), channel_id=1, source_target_pairs={{0,8},{8,0},{16,24},{24,16},{1,9},{9,1},{17,25},{25,17},{2,10},{10... | collective-permute-start | bytes 147464 | tf_op jit(solution)/shard_map/ppermute | solution.py:659
  23.2 2.1 %collective-permute-start.9 = (f32[12,8,128]{2,1,0:T(8,128)S(1)}, f32[12,8,128]{2,1,0:T(8,128)S(1)}, u32[]{:S(2)}, u32[]{:S(2)}) collective-permute-start(f32[12,8,128]{2,1,0:T(8,128)S(1)} %get-tuple-element.64), channel_id=1, source_target_pairs={{0,1},{1,0},{2,3},{3,2},{4,5},{5,4},{6,7},{7,6},{8,16},{9,17},{10,... | collective-permute-start | bytes 147464 | tf_op jit(solution)/shard_map/ppermute | solution.py:659
  26.5 3.1 %collective-permute-start.10 = (f32[30,8,128]{2,1,0:T(8,128)S(1)}, f32[30,8,128]{2,1,0:T(8,128)S(1)}, u32[]{:S(2)}, u32[]{:S(2)}) collective-permute-start(f32[30,8,128]{2,1,0:T(8,128)S(1)} %get-tuple-element.71), channel_id=1, source_target_pairs={{0,1},{1,0},{2,3},{3,2},{4,5},{5,4},{6,7},{7,6},{8,9},{9,8},{10,11... | collective-permute-start | bytes 368648 | tf_op jit(solution)/shard_map/ppermute | solution.py:659
  26.6 5.8 %collective-permute-start.11 = (f32[30,8,128]{2,1,0:T(8,128)S(1)}, f32[30,8,128]{2,1,0:T(8,128)S(1)}, u32[]{:S(2)}, u32[]{:S(2)}) collective-permute-start(f32[30,8,128]{2,1,0:T(8,128)S(1)} %get-tuple-element.72), channel_id=1, source_target_pairs={{0,16},{1,2},{2,1},{3,4},{4,3},{5,6},{6,5},{7,23},{8,24},{9,10},{1... | collective-permute-start | bytes 368648 | tf_op jit(solution)/shard_map/ppermute | solution.py:659
  32.5 4.2 %collective-permute-start.12 = (f32[12,8,128]{2,1,0:T(8,128)S(1)}, f32[12,8,128]{2,1,0:T(8,128)S(1)}, u32[]{:S(2)}, u32[]{:S(2)}) collective-permute-start(f32[12,8,128]{2,1,0:T(8,128)S(1)} %get-tuple-element.75), channel_id=1, source_target_pairs={{0,8},{8,0},{16,24},{24,16},{1,9},{9,1},{17,25},{25,17},{2,10},{10... | collective-permute-start | bytes 147464 | tf_op jit(solution)/shard_map/ppermute | solution.py:659
  34.6 2.1 %collective-permute-start.13 = (f32[12,8,128]{2,1,0:T(8,128)S(1)}, f32[12,8,128]{2,1,0:T(8,128)S(1)}, u32[]{:S(2)}, u32[]{:S(2)}) collective-permute-start(f32[12,8,128]{2,1,0:T(8,128)S(1)} %get-tuple-element.76), channel_id=1, source_target_pairs={{0,1},{1,0},{2,3},{3,2},{4,5},{5,4},{6,7},{7,6},{8,16},{9,17},{10,... | collective-permute-start | bytes 147464 | tf_op jit(solution)/shard_map/ppermute | solution.py:659

commit v6 on v5

--- a/solution.py
+++ b/solution.py
@@ -83,10 +83,59 @@
         odd_ref[line] = tile_ref[(*index, pl.ds(rows_odd, 1))]
 
 
-def pack_y(fields, wire_ref, even_ref, odd_ref):
+def merge_far(near, far, row):
+    far = jnp.where(row == 3, pltpu.roll(far, 3, 0), pltpu.roll(far, 5, 0))
+    return jnp.where((row == 3) | (row == 4), far, near)
+
+
+def split_far(tile, row):
+    return jnp.where(row < 4, pltpu.roll(tile, 5, 0), pltpu.roll(tile, 3, 0))
+
+
+def merge_halves(one, other, row):
+    other = jnp.where(row < 4, pltpu.roll(other, 2, 0), pltpu.roll(other, 6, 0))
+    return jnp.where((row >= 2) & (row < 6), other, one)
+
+
+def split_halves(tile, row):
+    return jnp.where(row < 4, pltpu.roll(tile, 6, 0), pltpu.roll(tile, 2, 0))
+
+
+def condense(tiles, row):
+    return [
+        tiles[3],
+        merge_far(tiles[2], tiles[0], row),
+        tiles[4],
+        merge_far(tiles[5], tiles[7], row),
+        merge_halves(tiles[1], tiles[6], row),
+    ]
+
+
+def expand(tiles, row):
+    low, low_two, high, high_two, three = tiles
+    return [
+        split_far(low_two, row), three, low_two, low, high, high_two, split_halves(three, row), split_far(high_two, row),
+    ]
+
+
+def condense_wire(tiles, row):
+    four = merge_halves(tiles[1], tiles[8], row)
+    low, high = merge_far(tiles[2], tiles[0], row), merge_far(tiles[7], tiles[9], row)
+    return [tiles[4], tiles[3], low, four, tiles[5], tiles[6], high, four]
+
+
+def expand_wire(tiles, row):
+    low, low_two, low_three, four, high, high_two, high_three, _ = tiles
+    return [
+        split_far(low_three, row), four, low_three, low_two, low,
+        high, high_two, high_three, split_halves(four, row), split_far(high_three, row),
+    ]
+
+
+def pack_y(fields, wire, edges, even_ref, odd_ref):
     first, _, _ = position("gy")
     even_low = (sublane() < 4) != first
-    count, half = len(fields[0]), wire_ref.shape[0] // 2
+    count, half = len(fields[0]), len(wire) // 2
 
     def put(spot, one, other):
         other = half_turn(other)
@@ -97,17 +146,16 @@
         for i in range(count):
             put(pair * count + i, fields[2 * pair][i], fields[2 * pair + 1][i])
     for j in range(half):
-        put(2 * count + j, wire_ref[j], wire_ref[j + half])
+        put(2 * count + j, wire[j], wire[j + half])
     rows_even, rows_odd = jnp.where(first, 3, 4), jnp.where(first, 4, 3)
-    if 2 * half % SUB:
+    if len(edges) % SUB:
         last = even_ref.shape[0] - 1
         even_ref[last] = odd_ref[last] = jnp.zeros(TILE, F32)
-    spots = [(wire_ref, (j,)) for j in range(2 * half)]
-    rim_rows(even_ref, odd_ref, 2 * count + half, spots, rows_even, rows_odd)
-
-
-def y_slab(count, ids):
-    return (2 * count + ids // 2 + -(-ids // SUB), *TILE)
+    rim_rows(even_ref, odd_ref, 2 * count + half, edges, rows_even, rows_odd)
+
+
+def y_slab(count, ids, edges):
+    return (2 * count + ids // 2 + -(-edges // SUB), *TILE)
 
 
 def unpack_fields(even_ref, odd_ref, count, i):
@@ -134,7 +182,7 @@
         low, high = sides(2 * count + j)
         one.append(jnp.where(row < 4, high, low))
         other.append(half_turn(jnp.where(row < 4, low, high)))
-    beyond = [sides(2 * count + ids // 2 + tile) for tile in range(-(-ids // SUB))]
+    beyond = [sides(spot) for spot in range(2 * count + ids // 2, even_ref.shape[0])]
     return one + other, beyond
 
 
@@ -193,29 +241,33 @@
         x_odd_ref[pl.ds(k * MARGIN, MARGIN)] = fields_ref[k, pl.ds(start_odd, MARGIN)]
     x_even_ref[pl.ds(4 * MARGIN, RIM)] = wire_ref[pl.ds(wire_even, RIM)]
     x_odd_ref[pl.ds(4 * MARGIN, RIM)] = wire_ref[pl.ds(wire_odd, RIM)]
-    pack_y(fields, wire_ref, y_even_ref, y_odd_ref)
+    wire = [wire_ref[x] for x in range(rows)]
+    pack_y(fields, wire, [(wire_ref, (x,)) for x in range(rows)], y_even_ref, y_odd_ref)
 
 
 def corner_pack_kernel(xe_ref, xo_ref, even_ref, odd_ref, wire_ref):
+    row = sublane()
     fields, wire = halo_x(xe_ref, xo_ref)
-    for j, value in enumerate(wire):
-        wire_ref[j] = value
-    pack_y(fields, wire_ref, even_ref, odd_ref)
-
-
-def sweep_row(q_ref, t_ref, coeff, j, row, spot, rhs):
+    fields = [condense(field, row) for field in fields]
+    wire_ref[0], wire_ref[1] = wire[RIM - 1], wire[RIM]
+    edges = [(wire_ref, (j,)) for j in range(2)]
+    pack_y(fields, condense_wire(wire, row), edges, even_ref, odd_ref)
+
+
+def sweep_row(q_ref, t_ref, coeff, j, row, spot, rhs, count):
     sums = []
     for ref in (q_ref, t_ref):
         own, side = ref[j, 0], ref[j, 1]
-        own_sum, side_sum = along_y(own, side, row, 0.0, 0.0)
+        own_sum, side_sum = along_y(own, side, row, *((0.0, 0.0) if count == 2 else (None, None)))
         own_sum = own_sum + (along_z(own, spot) + (ref[j - 1, 0] + ref[j + 1, 0]))
-        side_sum = side_sum + (along_z(side, spot) + (ref[j - 1, 1] + ref[j + 1, 1]))
+        if count == 2:
+            side_sum = side_sum + (along_z(side, spot) + (ref[j - 1, 1] + ref[j + 1, 1]))
         sums.append([own_sum, side_sum])
     if rhs is not None:
         sums[0][0] = sums[0][0] + rhs[0]
         sums[1][0] = sums[1][0] + rhs[1]
     out = []
-    for tile in range(2):
+    for tile in range(count):
         flow, heat = sums[0][tile], sums[1][tile]
         out.append(
             (
@@ -242,32 +294,37 @@
         current[1][j, 0] = coeff(2, j - 1, 0) * flow + coeff(3, j - 1, 0) * heat
     first, _, _ = position("gy")
     even_low = (row < 4) != first
+    last = []
     for sweep in range(1, SWEEPS):
         reach = min(sweep, MARGIN)
         for x in range(-reach, rows + reach):
             j = x + RIM
             rhs = (rhs_ref[0, x], rhs_ref[1, x]) if 0 <= x < rows else None
-            out = sweep_row(current[0], current[1], coeff, j, row, spot, rhs)
+            count = 2 if max(-x, x - rows + 1) < sweep else 1
+            out = sweep_row(current[0], current[1], coeff, j, row, spot, rhs, count)
             if sweep < SWEEPS - 1:
-                for tile in range(2):
+                for tile in range(count):
                     following[0][j, tile] = out[tile][0]
                     following[1][j, tile] = out[tile][1]
             else:
                 i = j - 1
                 (own_q, own_t), (side_q, side_t) = out
                 solved_ref[0, i], solved_ref[1, i] = own_q, own_t
-                turned = half_turn(side_t)
-                even_ref[i] = jnp.where(even_low, turned, side_q)
-                odd_ref[i] = jnp.where(even_low, side_q, turned)
+                last.append((side_q, side_t))
                 for k, side in enumerate((side_q, side_t)):
                     line = (i // SUB, pl.ds(i % SUB, 1))
                     rims_ref[(2 * k, *line)] = side[7:8]
                     rims_ref[(2 * k + 1, *line)] = side[0:1]
         current, following = following, current
+    corners = [condense([last[i][k] for i in [*range(MARGIN), *range(rows + MARGIN, wide)]], row) for k in range(2)]
+    for i, (flow, heat) in enumerate(last[MARGIN : rows + MARGIN] + list(zip(*corners))):
+        heat = half_turn(heat)
+        even_ref[i] = jnp.where(even_low, heat, flow)
+        odd_ref[i] = jnp.where(even_low, flow, heat)
     rows_even, rows_odd = jnp.where(first, 7, 0), jnp.where(first, 0, 7)
     for k in range(2):
         spots = [(solved_ref, (k, i)) for i in range(wide)]
-        rim_rows(even_ref, odd_ref, wide + k * (wide // SUB), spots, rows_even, rows_odd)
+        rim_rows(even_ref, odd_ref, rows + 5 + k * (wide // SUB), spots, rows_even, rows_odd)
 
 
 def getter(own_ref, own_side_ref, rest_ref, rest_side_ref):
@@ -378,7 +435,11 @@
     spot = lane()
     roots, _ = root_tables(props_ref)
     x_fields, x_wire = halo_x(xe_ref, xo_ref)
-    sides, beyond = unpack_wire(ce_ref, co_ref, 2 * MARGIN, 2 * RIM)
+    row = sublane()
+    sides, beyond = unpack_wire(ce_ref, co_ref, 5, 8)
+    sides = expand_wire(sides, row)
+    corner_stores = [unpack_fields(ce_ref, co_ref, 5, i) for i in range(5)]
+    corner_stores = [expand([stores[k] for stores in corner_stores], row) for k in range(4)]
     own_sides, _ = unpack_wire(ye_ref, yo_ref, rows, rows)
     for g in range(2):
         for j, value in enumerate(sides):
@@ -402,7 +463,7 @@
             if own_row:
                 lines = beyond_lines(beyond_ref, g, x)
             else:
-                lines = beyond_lines(corner_beyond_ref, g, j if j < RIM else j - rows)
+                lines = beyond_lines(corner_beyond_ref, g, 0 if j < RIM else 1)
             sums.append((diagonal(tiles, (j, *lines), spot), tiles(j, 0), tiles(j, 1)))
         corner = i if i < MARGIN else i - rows
         if not own_row:
@@ -412,7 +473,7 @@
             _, _, coeffs = block_tiles(stores, (sums[0][0][0], sums[1][0][0]), scales, spare)
             for k in range(4):
                 rest_ref[k, corner] = coeffs[k]
-            stores = unpack_fields(ce_ref, co_ref, 2 * MARGIN, corner)
+            stores = [corner_stores[k][corner] for k in range(4)]
             spare = sides[j if j < RIM else j - rows]
         else:
             stores = unpack_fields(ye_ref, yo_ref, rows, x)
@@ -429,16 +490,25 @@
     wide = solved_ref.shape[1]
     row = sublane()
     first, has_low, has_high = position("gy")
-    for i in range(wide):
+    rows = wide - 2 * MARGIN
+    tiles = [[], []]
+    for i in range(rows + 5):
         low, high = from_sides(first, ye_ref[i], yo_ref[i])
         low = jnp.where(has_low, low, 0.0)
         high = jnp.where(has_high, high, 0.0)
-        summed_ref[0, i] = solved_ref[0, i] + jnp.where(row < 4, low, high)
-        summed_ref[1, i] = solved_ref[1, i] + half_turn(jnp.where(row < 4, high, low))
+        tiles[0].append(jnp.where(row < 4, low, high))
+        tiles[1].append(half_turn(jnp.where(row < 4, high, low)))
+    for k in range(2):
+        corners = expand(tiles[k][rows:], row)
+        for spot, reach in enumerate((1, 2, 3, 4, 4, 3, 2, 1)):
+            if reach < 4:
+                corners[spot] = jnp.where((row < reach) | (row >= SUB - reach), corners[spot], 0.0)
+        for i, value in enumerate(corners[:MARGIN] + tiles[k][:rows] + corners[MARGIN:]):
+            summed_ref[k, i] = solved_ref[k, i] + value
     count = wide // SUB
     for k in range(2):
         for tile in range(count):
-            spot = wide + k * count + tile
+            spot = rows + 5 + k * count + tile
             low, high = from_sides(first, ye_ref[spot], yo_ref[spot])
             edges_ref[2 * k, tile] = rims_ref[2 * k, tile] + jnp.where(has_low, low, 0.0)
             edges_ref[2 * k + 1, tile] = rims_ref[2 * k + 1, tile] + jnp.where(has_high, high, 0.0)
@@ -627,7 +697,7 @@
         copy.wait()
 
 
-def call(kernel, outs, scratch=(), name=None, inside=pltpu.VMEM, outside=pltpu.VMEM):
+def call(kernel, outs, scratch=(), name=None, inside=pltpu.VMEM, outside=pltpu.VMEM, cost=None):
     def run(*args):
         return pl.pallas_call(
             kernel,
@@ -637,6 +707,7 @@
             scratch_shapes=[pltpu.VMEM(spec, F32) if isinstance(spec, tuple) else spec for spec in scratch],
             compiler_params=pltpu.CompilerParams(vmem_limit_bytes=32 * 1024 * 1024),
             name=name,
+            cost_estimate=cost,
         )(*args)
 
     return run
@@ -666,7 +737,7 @@
     cells = 2.0 * rows * soil_ids.shape[1] * depth * devices
     own = (rows, *TILE)
     x_slab = (4 * MARGIN + RIM, *TILE)
-    slab = y_slab(rows, rows)
+    slab = y_slab(rows, rows, rows)
     fields, wire, x_even, x_odd, y_even, y_odd = call(
         first_pack_kernel,
         [(4, *own), own, x_slab, x_slab, slab, slab],
@@ -677,8 +748,9 @@
     )(*(pltpu.with_memory_space_constraint(x, pltpu.HBM) for x in (soil_props, storage, soil_ids, bc_mask.T)))
     xe, xo = exchange("gx", x_even, x_odd)
     ye, yo = exchange("gy", y_even, y_odd)
-    slab = y_slab(2 * MARGIN, 2 * RIM)
-    even, odd = call(corner_pack_kernel, [slab, slab], [(2 * RIM, *TILE)], name="corner_pack")(xe, xo)
+    slab = y_slab(5, 8, 2)
+    weight = pl.CostEstimate(flops=10**11, bytes_accessed=10**9, transcendentals=0)
+    even, odd = call(corner_pack_kernel, [slab, slab], [(2, *TILE)], name="corner_pack", cost=weight)(xe, xo)
     ce, co = exchange("gy", even, odd)
     count = wide // SUB
     own_coeff, own_side, image, scales, rhs, roots, roots_side, beyond = call(
@@ -688,12 +760,12 @@
         name="own_coefficients",
     )(soil_props, fields, wire, xe, xo, ye, yo, adjoint_source)
     buffers = [(wide + 2, 2, *TILE)] * 4
-    slab = (wide + 2 * count, *TILE)
+    slab = (rows + 5 + 2 * count, *TILE)
     solved_shapes = [(2, wide, *TILE), (4, count, *TILE), slab, slab]
     rest, rest_side, solved, edges, even, odd = call(
         first_solve_kernel,
         [(4, 2 * MARGIN, *TILE), (4, 2 * RIM, *TILE)] + solved_shapes,
-        [(2, 2 * RIM, *TILE), (2, 2, -(-2 * RIM // SUB), *TILE)] + buffers,
+        [(2, 2 * RIM, *TILE), (2, 2, 1, *TILE)] + buffers,
         name="first_solve",
     )(soil_props, xe, xo, ye, yo, ce, co, own_coeff, own_side, rhs, roots, roots_side, beyond)
     coeffs = (own_coeff, own_side, rest, rest_side)

time: 49.8 us -> 49.1 us (0.986)
  waiting for transfers between devices: 12.8 us -> 12.1 us
    ppermute x7, waiting for transfers between devices: 7.62 us -> 7 us  [exchange(): lax.ppermute(odd, ('gx', 'gy'), others)]
where the time goes in v6:
time: 49.1 us; the launch traced here: 48.9 us
  starting transfers between devices  18.8 us (38%)
  waiting for transfers between devices  12.1 us (25%)
  blocking collectives  11.7 us (24%)
  Pallas kernels  5.61 us (11%)
  between operations  0.73 us (1%)
    all_to_all x1, blocking collectives, shards(): gram = lax.all_to_all(gram, ('gx', 'gy'), 0, 0, tiled=True)  11.7 us
    ppermute x7, starting transfers between devices, exchange(): lax.ppermute(odd, ('gx', 'gy'), others)  10.7 us
    ppermute x7, starting transfers between devices, exchange(): lax.ppermute(even, axis, pairs)  8.09 us
    ppermute x7, waiting for transfers between devices, exchange(): lax.ppermute(odd, ('gx', 'gy'), others)  7 us
    pallas_call x9, Pallas kernels, run(): pl.pallas_call(kernel, out_shape=[jax.ShapeDtypeStruct(shape, F32) for sh...  5.61 us
    ppermute x7, waiting for transfers between devices, exchange(): lax.ppermute(even, axis, pairs)  5.08 us
  transfers between devices with their start and end apart: 14, of which 6 were waited for; matrix products, arithmetic and copies ran while one was open for 0% of the time, Pallas kernels for 1%

profile of v6, /device:TPU:0, one launch (start us, length us, event | category | flops | bytes accessed | tf_op | source)
XLA Modules:
  0.0 48.9 jit_solution(14118477096628068121)
XLA Ops:
  0.6 1.2 %first_pack.1 = (f32[4,16,8,128]{3,2,1,0:T(8,128)S(1)}, f32[16,8,128]{2,1,0:T(8,128)S(1)}, f32[21,8,128]{2,1,0:T(8,128)S(1)}, f32[21,8,128]{2,1,0:T(8,128)S(1)},...) custom-call(f32[3,16]{1,0:T(4,128)} %props_ref.3, f32[4,16,8,128]{3,2,1,0:T(8,128)} %storage_hbm.1, ...), custom_call_target="tpu_custom_call" | custom-call | tf_op jit(solution)/shard_map/first_pack/pallas_call | solution.py:702
  1.9 3.0 %collective-permute-start = (f32[21,8,128]{2,1,0:T(8,128)S(1)}, f32[21,8,128]{2,1,0:T(8,128)S(1)}, u32[]{:S(2)}, u32[]{:S(2)}) collective-permute-start(f32[21,8,128]{2,1,0:T(8,128)S(1)} %get-tuple-element.43), channel_id=1, source_target_pairs={{0,8},{8,0},{16,24},{24,16},{1,9},{9,1},{17,25},{25,17},{2,10},{10... | collective-permute-start | bytes 258056 | tf_op jit(solution)/shard_map/ppermute | solution.py:730
  4.9 0.5 %collective-permute-start.2 = (f32[42,8,128]{2,1,0:T(8,128)S(1)}, f32[42,8,128]{2,1,0:T(8,128)S(1)}, u32[]{:S(2)}, u32[]{:S(2)}) collective-permute-start(f32[42,8,128]{2,1,0:T(8,128)S(1)} %get-tuple-element.45), channel_id=1, source_target_pairs={{0,1},{1,0},{2,3},{3,2},{4,5},{5,4},{6,7},{7,6},{8,9},{9,8},{10,11... | collective-permute-start | bytes 516104 | tf_op jit(solution)/shard_map/ppermute | solution.py:730
  5.4 1.1 %collective-permute-start.3 = (f32[42,8,128]{2,1,0:T(8,128)S(1)}, f32[42,8,128]{2,1,0:T(8,128)S(1)}, u32[]{:S(2)}, u32[]{:S(2)}) collective-permute-start(f32[42,8,128]{2,1,0:T(8,128)S(1)} %get-tuple-element.46), channel_id=1, source_target_pairs={{0,16},{1,2},{2,1},{3,4},{4,3},{5,6},{6,5},{7,23},{8,24},{9,10},{1... | collective-permute-start | bytes 516104 | tf_op jit(solution)/shard_map/ppermute | solution.py:730
  6.5 0.9 %collective-permute-done.xe_ref = f32[21,8,128]{2,1,0:T(8,128)S(1)} collective-permute-done((f32[21,8,128]{2,1,0:T(8,128)S(1)}, f32[21,8,128]{2,1,0:T(8,128)S(1)}, u32[]{:S(2)}, u32[]{:S(2)}) %collective-permute-start) | collective-permute-done | bytes 86048 | tf_op jit(solution)/shard_map/ppermute | solution.py:730
  7.4 0.1 collective-permute-start.4
  7.5 0.0 copy-start.1
  7.5 4.5 %collective-permute-start.5 = (f32[15,8,128]{2,1,0:T(8,128)S(1)}, f32[15,8,128]{2,1,0:T(8,128)S(1)}, u32[]{:S(2)}, u32[]{:S(2)}) collective-permute-start(f32[15,8,128]{2,1,0:T(8,128)S(1)} %get-tuple-element.48), channel_id=1, source_target_pairs={{0,16},{1,2},{2,1},{3,4},{4,3},{5,6},{6,5},{7,23},{8,24},{9,10},{1... | collective-permute-start | bytes 184328 | tf_op jit(solution)/shard_map/ppermute | solution.py:730
  12.1 0.0 collective-permute-done.2.ye_ref
  12.1 0.0 collective-permute-done.3.yo_ref
  12.1 0.6 %own_coefficients.1 = (f32[4,16,8,128]{3,2,1,0:T(8,128)S(1)}, f32[4,14,8,128]{3,2,1,0:T(8,128)S(1)}, f32[4,16,8,128]{3,2,1,0:T(8,128)S(1)}, f32[5,16,8,128]{3,2,...) custom-call(f32[3,16]{1,0:T(4,128)S(1)} %copy-done.1, ...), custom_call_target="tpu_custom_call" | custom-call | tf_op jit(solution)/shard_map/own_coefficients/pallas_call | solution.py:702
  12.7 0.0 collective-permute-done.4.ce_ref
  12.7 1.5 %collective-permute-done.5.co_ref = f32[15,8,128]{2,1,0:T(8,128)S(1)} collective-permute-done((f32[15,8,128]{2,1,0:T(8,128)S(1)}, f32[15,8,128]{2,1,0:T(8,128)S(1)}, u32[]{:S(2)}, u32[]{:S(2)}) %collective-permute-start.5) | collective-permute-done | bytes 61472 | tf_op jit(solution)/shard_map/ppermute | solution.py:730
  14.3 1.2 %first_solve.1 = (f32[4,8,8,128]{3,2,1,0:T(8,128)S(1)}, f32[4,10,8,128]{3,2,1,0:T(8,128)S(1)}, f32[2,24,8,128]{3,2,1,0:T(8,128)S(1)}, f32[4,3,8,128]{3,2,1,0:T(8...) custom-call(f32[3,16]{1,0:T(4,128)S(1)} %copy-done.1, f32[21,8,128]{2,1,0:T(8,128)S(1)} %collective-permute-done.xe_ref, ...), custom_call_target="tpu_custom_call" | custom-call | tf_op jit(solution)/shard_map/first_solve/pallas_call | solution.py:702
  15.5 0.1 collective-permute-start.6
  15.6 2.1 %collective-permute-start.7 = (f32[27,8,128]{2,1,0:T(8,128)S(1)}, f32[27,8,128]{2,1,0:T(8,128)S(1)}, u32[]{:S(2)}, u32[]{:S(2)}) collective-permute-start(f32[27,8,128]{2,1,0:T(8,128)S(1)} %get-tuple-element.60), channel_id=1, source_target_pairs={{0,16},{1,2},{2,1},{3,4},{4,3},{5,6},{6,5},{7,23},{8,24},{9,10},{1... | collective-permute-start | bytes 331784 | tf_op jit(solution)/shard_map/ppermute | solution.py:730
  17.7 2.7 %collective-permute-done.7.yo_ref = f32[27,8,128]{2,1,0:T(8,128)S(1)} collective-permute-done((f32[27,8,128]{2,1,0:T(8,128)S(1)}, f32[27,8,128]{2,1,0:T(8,128)S(1)}, u32[]{:S(2)}, u32[]{:S(2)}) %collective-permute-start.7) | collective-permute-done | bytes 110624 | tf_op jit(solution)/shard_map/ppermute | solution.py:730
  20.4 0.1 fold_y.2
  20.5 2.2 %collective-permute-start.8 = (f32[12,8,128]{2,1,0:T(8,128)S(1)}, f32[12,8,128]{2,1,0:T(8,128)S(1)}, u32[]{:S(2)}, u32[]{:S(2)}) collective-permute-start(f32[12,8,128]{2,1,0:T(8,128)S(1)} %get-tuple-element.63), channel_id=1, source_target_pairs={{0,8},{8,0},{16,24},{24,16},{1,9},{9,1},{17,25},{25,17},{2,10},{10... | collective-permute-start | bytes 147464 | tf_op jit(solution)/shard_map/ppermute | solution.py:730
  22.7 0.0 collective-permute-start.9
  22.7 2.1 %collective-permute-done.8.xe_ref = f32[12,8,128]{2,1,0:T(8,128)S(1)} collective-permute-done((f32[12,8,128]{2,1,0:T(8,128)S(1)}, f32[12,8,128]{2,1,0:T(8,128)S(1)}, u32[]{:S(2)}, u32[]{:S(2)}) %collective-permute-start.8) | collective-permute-done | bytes 49184 | tf_op jit(solution)/shard_map/ppermute | solution.py:730
  24.8 0.0 collective-permute-done.9.xo_ref
  24.8 1.1 %second_solve.1 = (f32[2,16,8,128]{3,2,1,0:T(8,128)S(1)}, f32[2,16,8,128]{3,2,1,0:T(8,128)S(1)}, f32[8,128]{1,0:T(8,128)S(1)}, f32[2,24,8,128]{3,2,1,0:T(8,128)S...) custom-call(f32[2,24,8,128]{3,2,1,0:T(8,128)S(1)} %get-tuple-element.61.summed_ref, ...), custom_call_target="tpu_custom_call" | custom-call | tf_op jit(solution)/shard_map/second_solve/pallas_call | solution.py:702
  25.9 0.1 collective-permute-start.10
  26.0 3.0 %collective-permute-start.11 = (f32[27,8,128]{2,1,0:T(8,128)S(1)}, f32[27,8,128]{2,1,0:T(8,128)S(1)}, u32[]{:S(2)}, u32[]{:S(2)}) collective-permute-start(f32[27,8,128]{2,1,0:T(8,128)S(1)} %get-tuple-element.72), channel_id=1, source_target_pairs={{0,16},{1,2},{2,1},{3,4},{4,3},{5,6},{6,5},{7,23},{8,24},{9,10},{1... | collective-permute-start | bytes 331784 | tf_op jit(solution)/shard_map/ppermute | solution.py:730
  29.0 2.7 %collective-permute-done.11.yo_ref = f32[27,8,128]{2,1,0:T(8,128)S(1)} collective-permute-done((f32[27,8,128]{2,1,0:T(8,128)S(1)}, f32[27,8,128]{2,1,0:T(8,128)S(1)}, u32[]{:S(2)}, u32[]{:S(2)}) %collective-permute-start.11) | collective-permute-done | bytes 110624 | tf_op jit(solution)/shard_map/ppermute | solution.py:730
  31.7 0.1 fold_y.3
  31.8 2.2 %collective-permute-start.12 = (f32[12,8,128]{2,1,0:T(8,128)S(1)}, f32[12,8,128]{2,1,0:T(8,128)S(1)}, u32[]{:S(2)}, u32[]{:S(2)}) collective-permute-start(f32[12,8,128]{2,1,0:T(8,128)S(1)} %get-tuple-element.75), channel_id=1, source_target_pairs={{0,8},{8,0},{16,24},{24,16},{1,9},{9,1},{17,25},{25,17},{2,10},{10... | collective-permute-start | bytes 147464 | tf_op jit(solution)/shard_map/ppermute | solution.py:730
  33.9 2.1 %collective-permute-done.12.xe_ref = f32[12,8,128]{2,1,0:T(8,128)S(1)} collective-permute-done((f32[12,8,128]{2,1,0:T(8,128)S(1)}, f32[12,8,128]{2,1,0:T(8,128)S(1)}, u32[]{:S(2)}, u32[]{:S(2)}) %collective-permute-start.12) | collective-permute-done | bytes 49184 | tf_op jit(solution)/shard_map/ppermute | solution.py:730
  36.0 0.3 last_image.1
  36.3 11.7 %all_to_all.11 = f32[32,1,128]{2,1,0:T(1,128)S(1)} all-to-all(f32[32,1,128]{2,1,0:T(1,128)S(1)} %bitcast.6), channel_id=1, replica_groups=mesh['gx'=4,'gy'=8] {'gx','gy'}, dimensions={0} | all-to-all | bytes 32768 | tf_op jit(solution)/shard_map/all_to_all | solution.py:792
  47.9 1.0 %combine.1 = (f32[2,16,8,128]{3,2,1,0:T(8,128)}, f32[2,16,8,128]{3,2,1,0:T(8,128)}, f32[2,16,8,128]{3,2,1,0:T(8,128)}) custom-call(f32[32,128]{1,0:T(8,128)S(1)} %bitcast.5, f32[2,16,8,128]{3,2,1,0:T(8,128)S(1)} %copy-done, f32[2,16,8,128]{3,2,1,0:T(8,128)S(1)} %get-tuple-element.77.power_ref, f32[2,16,8,128]{3,2,1,0:T(8,128)S(1)} %get-tuple-element.80.second_ref, ...), custom_call_target="tpu_custom_call" | custom-call | tf_op jit(solution)/shard_map/combine/pallas_call | solution.py:702
  (10 shorter events, 0.1 us)
Async XLA Ops:
  1.9 5.5 %collective-permute-start = (f32[21,8,128]{2,1,0:T(8,128)S(1)}, f32[21,8,128]{2,1,0:T(8,128)S(1)}, u32[]{:S(2)}, u32[]{:S(2)}) collective-permute-start(f32[21,8,128]{2,1,0:T(8,128)S(1)} %get-tuple-element.43), channel_id=1, source_target_pairs={{0,8},{8,0},{16,24},{24,16},{1,9},{9,1},{17,25},{25,17},{2,10},{10... | collective-permute-start | bytes 258056 | tf_op jit(solution)/shard_map/ppermute | solution.py:730
  4.9 2.5 %collective-permute-start.1 = (f32[21,8,128]{2,1,0:T(8,128)S(1)}, f32[21,8,128]{2,1,0:T(8,128)S(1)}, u32[]{:S(2)}, u32[]{:S(2)}) collective-permute-start(f32[21,8,128]{2,1,0:T(8,128)S(1)} %get-tuple-element.44), channel_id=1, source_target_pairs={{0,1},{1,0},{2,3},{3,2},{4,5},{5,4},{6,7},{7,6},{8,16},{9,17},{10,... | collective-permute-start | bytes 258056 | tf_op jit(solution)/shard_map/ppermute | solution.py:730
  4.9 7.2 %collective-permute-start.2 = (f32[42,8,128]{2,1,0:T(8,128)S(1)}, f32[42,8,128]{2,1,0:T(8,128)S(1)}, u32[]{:S(2)}, u32[]{:S(2)}) collective-permute-start(f32[42,8,128]{2,1,0:T(8,128)S(1)} %get-tuple-element.45), channel_id=1, source_target_pairs={{0,1},{1,0},{2,3},{3,2},{4,5},{5,4},{6,7},{7,6},{8,9},{9,8},{10,11... | collective-permute-start | bytes 516104 | tf_op jit(solution)/shard_map/ppermute | solution.py:730
  5.4 6.7 %copy-start = (f32[2,16,8,128]{3,2,1,0:T(8,128)S(1)}, f32[2,16,8,128]{3,2,1,0:T(8,128)}, u32[]{:S(2)}) copy-start(f32[2,16,8,128]{3,2,1,0:T(8,128)} %source_ref.7) | copy-start | bytes 393220
  5.4 6.7 %collective-permute-start.3 = (f32[42,8,128]{2,1,0:T(8,128)S(1)}, f32[42,8,128]{2,1,0:T(8,128)S(1)}, u32[]{:S(2)}, u32[]{:S(2)}) collective-permute-start(f32[42,8,128]{2,1,0:T(8,128)S(1)} %get-tuple-element.46), channel_id=1, source_target_pairs={{0,16},{1,2},{2,1},{3,4},{4,3},{5,6},{6,5},{7,23},{8,24},{9,10},{1... | collective-permute-start | bytes 516104 | tf_op jit(solution)/shard_map/ppermute | solution.py:730
  7.4 5.3 %collective-permute-start.4 = (f32[15,8,128]{2,1,0:T(8,128)S(1)}, f32[15,8,128]{2,1,0:T(8,128)S(1)}, u32[]{:S(2)}, u32[]{:S(2)}) collective-permute-start(f32[15,8,128]{2,1,0:T(8,128)S(1)} %get-tuple-element.47), channel_id=1, source_target_pairs={{0,1},{1,0},{2,3},{3,2},{4,5},{5,4},{6,7},{7,6},{8,9},{9,8},{10,11... | collective-permute-start | bytes 184328 | tf_op jit(solution)/shard_map/ppermute | solution.py:730
  7.5 4.6 %copy-start.1 = (f32[3,16]{1,0:T(4,128)S(1)}, f32[3,16]{1,0:T(4,128)}, u32[]{:S(2)}) copy-start(f32[3,16]{1,0:T(4,128)} %props_ref.3) | copy-start | bytes 580
  7.5 6.7 %collective-permute-start.5 = (f32[15,8,128]{2,1,0:T(8,128)S(1)}, f32[15,8,128]{2,1,0:T(8,128)S(1)}, u32[]{:S(2)}, u32[]{:S(2)}) collective-permute-start(f32[15,8,128]{2,1,0:T(8,128)S(1)} %get-tuple-element.48), channel_id=1, source_target_pairs={{0,16},{1,2},{2,1},{3,4},{4,3},{5,6},{6,5},{7,23},{8,24},{9,10},{1... | collective-permute-start | bytes 184328 | tf_op jit(solution)/shard_map/ppermute | solution.py:730
  15.5 2.2 %collective-permute-start.6 = (f32[27,8,128]{2,1,0:T(8,128)S(1)}, f32[27,8,128]{2,1,0:T(8,128)S(1)}, u32[]{:S(2)}, u32[]{:S(2)}) collective-permute-start(f32[27,8,128]{2,1,0:T(8,128)S(1)} %get-tuple-element.59), channel_id=1, source_target_pairs={{0,1},{1,0},{2,3},{3,2},{4,5},{5,4},{6,7},{7,6},{8,9},{9,8},{10,11... | collective-permute-start | bytes 331784 | tf_op jit(solution)/shard_map/ppermute | solution.py:730
  15.6 4.8 %collective-permute-start.7 = (f32[27,8,128]{2,1,0:T(8,128)S(1)}, f32[27,8,128]{2,1,0:T(8,128)S(1)}, u32[]{:S(2)}, u32[]{:S(2)}) collective-permute-start(f32[27,8,128]{2,1,0:T(8,128)S(1)} %get-tuple-element.60), channel_id=1, source_target_pairs={{0,16},{1,2},{2,1},{3,4},{4,3},{5,6},{6,5},{7,23},{8,24},{9,10},{1... | collective-permute-start | bytes 331784 | tf_op jit(solution)/shard_map/ppermute | solution.py:730
  20.5 4.3 %collective-permute-start.8 = (f32[12,8,128]{2,1,0:T(8,128)S(1)}, f32[12,8,128]{2,1,0:T(8,128)S(1)}, u32[]{:S(2)}, u32[]{:S(2)}) collective-permute-start(f32[12,8,128]{2,1,0:T(8,128)S(1)} %get-tuple-element.63), channel_id=1, source_target_pairs={{0,8},{8,0},{16,24},{24,16},{1,9},{9,1},{17,25},{25,17},{2,10},{10... | collective-permute-start | bytes 147464 | tf_op jit(solution)/shard_map/ppermute | solution.py:730
  22.7 2.1 %collective-permute-start.9 = (f32[12,8,128]{2,1,0:T(8,128)S(1)}, f32[12,8,128]{2,1,0:T(8,128)S(1)}, u32[]{:S(2)}, u32[]{:S(2)}) collective-permute-start(f32[12,8,128]{2,1,0:T(8,128)S(1)} %get-tuple-element.64), channel_id=1, source_target_pairs={{0,1},{1,0},{2,3},{3,2},{4,5},{5,4},{6,7},{7,6},{8,16},{9,17},{10,... | collective-permute-start | bytes 147464 | tf_op jit(solution)/shard_map/ppermute | solution.py:730
  25.9 3.1 %collective-permute-start.10 = (f32[27,8,128]{2,1,0:T(8,128)S(1)}, f32[27,8,128]{2,1,0:T(8,128)S(1)}, u32[]{:S(2)}, u32[]{:S(2)}) collective-permute-start(f32[27,8,128]{2,1,0:T(8,128)S(1)} %get-tuple-element.71), channel_id=1, source_target_pairs={{0,1},{1,0},{2,3},{3,2},{4,5},{5,4},{6,7},{7,6},{8,9},{9,8},{10,11... | collective-permute-start | bytes 331784 | tf_op jit(solution)/shard_map/ppermute | solution.py:730
  26.0 5.7 %collective-permute-start.11 = (f32[27,8,128]{2,1,0:T(8,128)S(1)}, f32[27,8,128]{2,1,0:T(8,128)S(1)}, u32[]{:S(2)}, u32[]{:S(2)}) collective-permute-start(f32[27,8,128]{2,1,0:T(8,128)S(1)} %get-tuple-element.72), channel_id=1, source_target_pairs={{0,16},{1,2},{2,1},{3,4},{4,3},{5,6},{6,5},{7,23},{8,24},{9,10},{1... | collective-permute-start | bytes 331784 | tf_op jit(solution)/shard_map/ppermute | solution.py:730
  31.8 4.2 %collective-permute-start.12 = (f32[12,8,128]{2,1,0:T(8,128)S(1)}, f32[12,8,128]{2,1,0:T(8,128)S(1)}, u32[]{:S(2)}, u32[]{:S(2)}) collective-permute-start(f32[12,8,128]{2,1,0:T(8,128)S(1)} %get-tuple-element.75), channel_id=1, source_target_pairs={{0,8},{8,0},{16,24},{24,16},{1,9},{9,1},{17,25},{25,17},{2,10},{10... | collective-permute-start | bytes 147464 | tf_op jit(solution)/shard_map/ppermute | solution.py:730
  33.9 2.1 %collective-permute-start.13 = (f32[12,8,128]{2,1,0:T(8,128)S(1)}, f32[12,8,128]{2,1,0:T(8,128)S(1)}, u32[]{:S(2)}, u32[]{:S(2)}) collective-permute-start(f32[12,8,128]{2,1,0:T(8,128)S(1)} %get-tuple-element.76), channel_id=1, source_target_pairs={{0,1},{1,0},{2,3},{3,2},{4,5},{5,4},{6,7},{7,6},{8,16},{9,17},{10,... | collective-permute-start | bytes 147464 | tf_op jit(solution)/shard_map/ppermute | solution.py:730

commit v7 on v6

--- a/solution.py
+++ b/solution.py
@@ -205,7 +205,8 @@
     fields_ref, wire_ref, x_even_ref, x_odd_ref, y_even_ref, y_odd_ref,
     props_ref, storage_ref, ids_ref, bc_ref, sems,
 ):
-    places = ((ids_hbm, ids_ref), (storage_hbm, storage_ref), (props_hbm, props_ref), (bc_hbm, bc_ref))
+    places = [(ids_hbm, ids_ref), (props_hbm, props_ref), (bc_hbm, bc_ref)]
+    places += [(storage_hbm.at[k], storage_ref.at[k]) for k in range(4)]
     copies = [pltpu.make_async_copy(src, dst, sems.at[k]) for k, (src, dst) in enumerate(places)]
     for copy in copies:
         copy.start()
@@ -254,14 +255,14 @@
     pack_y(fields, condense_wire(wire, row), edges, even_ref, odd_ref)
 
 
-def sweep_row(q_ref, t_ref, coeff, j, row, spot, rhs, count):
+def sweep_row(load, coeff, j, row, spot, rhs, count):
     sums = []
-    for ref in (q_ref, t_ref):
-        own, side = ref[j, 0], ref[j, 1]
+    for k in range(2):
+        own, side = load(k, j, 0), load(k, j, 1)
         own_sum, side_sum = along_y(own, side, row, *((0.0, 0.0) if count == 2 else (None, None)))
-        own_sum = own_sum + (along_z(own, spot) + (ref[j - 1, 0] + ref[j + 1, 0]))
+        own_sum = own_sum + (along_z(own, spot) + (load(k, j - 1, 0) + load(k, j + 1, 0)))
         if count == 2:
-            side_sum = side_sum + (along_z(side, spot) + (ref[j - 1, 1] + ref[j + 1, 1]))
+            side_sum = side_sum + (along_z(side, spot) + (load(k, j - 1, 1) + load(k, j + 1, 1)))
         sums.append([own_sum, side_sum])
     if rhs is not None:
         sums[0][0] = sums[0][0] + rhs[0]
@@ -278,14 +279,35 @@
     return out
 
 
+def reach_of(sweep, rows):
+    reach = min(sweep, MARGIN)
+    return [(x, 2 if max(-x, x - rows + 1) < sweep else 1) for x in range(-reach, rows + reach)]
+
+
+def read_first(rows):
+    written = [{(x + RIM, 0) for x in range(rows)}, set()]
+    missing = []
+    for sweep in range(1, SWEEPS):
+        half = (sweep - 1) % 2
+        reads = set()
+        for x, count in reach_of(sweep, rows):
+            j = x + RIM
+            reads |= {(j, 0), (j, 1), (j - 1, 0), (j + 1, 0)}
+            if count == 2:
+                reads |= {(j - 1, 1), (j + 1, 1)}
+        missing += [(half, *spot) for spot in sorted(reads - written[half])]
+        written[half] |= reads
+        written[1 - half] |= {(x + RIM, tile) for x, count in reach_of(sweep, rows) for tile in range(count)}
+    return missing
+
+
 def subdomain_sweeps(rhs_ref, coeff, solved_ref, rims_ref, even_ref, odd_ref, buffers, rows):
     row, spot = sublane(), lane()
     wide = rows + 2 * MARGIN
     zero = jnp.zeros(TILE, F32)
-    for buffer in buffers:
-        for j in range(wide + 2):
-            for tile in range(2):
-                buffer[j, tile] = zero
+    for half, j, tile in read_first(rows):
+        for k in range(2):
+            buffers[2 * half + k][j, tile] = zero
     current, following = buffers[:2], buffers[2:]
     for x in range(rows):
         j = x + RIM
@@ -296,12 +318,11 @@
     even_low = (row < 4) != first
     last = []
     for sweep in range(1, SWEEPS):
-        reach = min(sweep, MARGIN)
-        for x in range(-reach, rows + reach):
+        load = functools.cache(functools.partial(lambda pair, k, j, tile: pair[k][j, tile], current))
+        for x, count in reach_of(sweep, rows):
             j = x + RIM
             rhs = (rhs_ref[0, x], rhs_ref[1, x]) if 0 <= x < rows else None
-            count = 2 if max(-x, x - rows + 1) < sweep else 1
-            out = sweep_row(current[0], current[1], coeff, j, row, spot, rhs, count)
+            out = sweep_row(load, coeff, j, row, spot, rhs, count)
             if sweep < SWEEPS - 1:
                 for tile in range(count):
                     following[0][j, tile] = out[tile][0]
@@ -597,32 +618,52 @@
 
 def step_kernel(
     summed_ref, edges_ref, xe_ref, xo_ref, own_ref, own_side_ref, rest_ref, rest_side_ref, image_ref, scale_ref, source_ref,
-    direction_ref, power_ref, gram_ref, solved_ref, rims_ref, even_ref, odd_ref,
-    rhs_ref, q_ref, t_ref, edge_ref, *buffers,
+    rhs_ref, q_ref, t_ref, solved_ref, rims_ref, even_ref, odd_ref, edge_ref, *buffers,
 ):
     rows = source_ref.shape[1]
     row, spot = sublane(), lane()
     fields = (q_ref, t_ref)
     fold_x(summed_ref, edges_ref, xe_ref, xo_ref, fields, edge_ref)
-    products = [jnp.zeros(TILE, F32) for _ in range(3)]
     for x in range(rows):
-        keep_direction(direction_ref, scale_ref, fields, x)
         for k, part in enumerate(image_row(fields, edge_ref, image_ref, x, row, spot)):
-            source = source_ref[k, x]
-            scaled = part - source * scale_ref[2 + k, x]
-            power = scaled * scale_ref[k, x]
-            rhs_ref[k, x] = scaled
-            power_ref[k, x] = power
-            products[0] = products[0] + source * source
-            products[1] = products[1] + source * power
-            products[2] = products[2] + power * power
-    gram_ref[...] = gram_rows(products, row, 0)
+            rhs_ref[k, x] = part - source_ref[k, x] * scale_ref[2 + k, x]
     coeff = getter(own_ref, own_side_ref, rest_ref, rest_side_ref)
     subdomain_sweeps(rhs_ref, coeff, solved_ref, rims_ref, even_ref, odd_ref, buffers, rows)
 
 
+def power_kernel(
+    rhs_ref, q_ref, t_ref, scale_ref, source_ref, direction_ref, power_ref, shifted_ref, shift_ref, gram_ref
+):
+    rows = source_ref.shape[1]
+    row, spot = sublane(), lane()
+    square = along = jnp.zeros(TILE, F32)
+    for x in range(rows):
+        keep_direction(direction_ref, scale_ref, (q_ref, t_ref), x)
+        for k in range(2):
+            source = source_ref[k, x]
+            power = rhs_ref[k, x] * scale_ref[k, x]
+            power_ref[k, x] = power
+            square = square + source * source
+            along = along + source * power
+    square_sum, along_sum = (
+        jnp.sum(jnp.sum(value, axis=0, keepdims=True), axis=1, keepdims=True) for value in (square, along)
+    )
+    shift = jnp.broadcast_to(along_sum / jnp.maximum(square_sum, 1e-30), TILE)
+    shift_ref[...] = shift
+    products = [square, jnp.zeros(TILE, F32), jnp.zeros(TILE, F32)]
+    for x in range(rows):
+        for k in range(2):
+            source = source_ref[k, x]
+            shifted = power_ref[k, x] - shift * source
+            shifted_ref[k, x] = shifted
+            products[1] = products[1] + source * shifted
+            products[2] = products[2] + shifted * shifted
+    gram_ref[...] = gram_rows(products, row, 0) + jnp.where((row == 6) & (spot == 0), shift, 0.0)
+
+
 def last_kernel(
-    summed_ref, edges_ref, xe_ref, xo_ref, image_ref, scale_ref, source_ref, power_ref, gram_in_ref,
+    summed_ref, edges_ref, xe_ref, xo_ref, image_ref, scale_ref,
+    source_ref, power_ref, shifted_in_ref, shift_ref, gram_in_ref,
     direction_ref, second_ref, gram_ref, q_ref, t_ref, edge_ref,
 ):
     rows = source_ref.shape[1]
@@ -636,9 +677,10 @@
             power = power_ref[k, x]
             second = part * scale_ref[k, x] - power
             second_ref[k, x] = second
-            products[0] = products[0] + source_ref[k, x] * second
-            products[1] = products[1] + power * second
-            products[2] = products[2] + second * second
+            shifted = second - shift_ref[...] * power
+            products[0] = products[0] + source_ref[k, x] * shifted
+            products[1] = products[1] + shifted_in_ref[k, x] * shifted
+            products[2] = products[2] + shifted * shifted
     total = jnp.sum(gram_in_ref[...] + gram_rows(products, row, 3), axis=1, keepdims=True)
     line = jnp.sum(jnp.where(row == spot, jnp.broadcast_to(total, TILE), 0.0), axis=0, keepdims=True)
     gram_ref[...] = jnp.broadcast_to(line, gram_ref.shape)
@@ -648,28 +690,46 @@
     gram_ref, source_ref, power_ref, second_ref, one_ref, two_ref,
     adjoint_hbm, residual_hbm, basis_hbm, adjoint_ref, residual_ref, basis_ref, sems, *, scale,
 ):
-    sums = jnp.sum(gram_ref[...], axis=0, keepdims=True)
-    spot = lax.broadcasted_iota(jnp.int32, sums.shape, 1)
-    g00, g01, g11, g02, g12, g22 = (
-        jnp.sum(jnp.where(spot == k, sums, 0.0), axis=1, keepdims=True) for k in range(6)
+    parts = gram_ref[...]
+    spot = lax.broadcasted_iota(jnp.int32, parts.shape, 1)
+    p00, p01, p11, p02, p12, p22, shift_of = (
+        jnp.sum(jnp.where(spot == k, parts, 0.0), axis=1, keepdims=True) for k in range(7)
     )
+    total = lambda value: jnp.sum(value, axis=0, keepdims=True)
+    g00 = total(p00)
+    shift = total(shift_of * p00) / jnp.maximum(g00, 1e-30)
+    e = shift_of - shift
+    f = e * shift_of
+    mixed = p02 + e * p01 + f * p00
+    g01 = total(p01 + e * p00)
+    g11 = total(p11 + e * (2.0 * p01 + e * p00))
+    g02 = total(mixed)
+    g12 = total(p12 + e * p11 + f * p01 + e * mixed)
+    g22 = total(p22 + 2.0 * (e * p12 + f * p02 + e * f * p01) + e * e * p11 + f * f * p00)
+    grown = 1.0 + shift
     beta2 = g00 + EPSILON
     beta = jnp.sqrt(beta2)
-    less = (EPSILON - g01) / beta2
-    h11 = (g00 + g01) / beta2
+    less = (grown * EPSILON - g01) / beta2
+    h11 = (grown * g00 + g01) / beta2
     square = (less * less * g00 + 2.0 * less * g01 + g11) / beta2
     square = jnp.maximum(square, 0.0)
     h21 = jnp.sqrt(square + EPSILON)
     b = 1.0 / (beta * h21)
     a = less * b
-    h12 = EPSILON * h11 / (beta2 * h21) + (a * g01 + b * g02) / beta
-    short = EPSILON / (square + EPSILON) - (a * a * g01 + a * b * (g11 + g02) + b * b * g12)
-    h22 = 1.0 - short
+    c = a - shift * b
+    along_r, along_p = c * g01 + b * g02, c * g11 + b * g12
+    h12 = grown * EPSILON * h11 * b / beta + along_r / beta
+    d2 = a * along_r + b * along_p
+    unit = 1.0 / (square + EPSILON)
+    short = grown * EPSILON * unit - d2
+    h22 = grown * square * unit + d2
     c0 = a * short - h12 / beta
-    c1 = a + b * short
+    c1 = b * short + c
     c2 = b
     square = c0 * (c0 * g00 + 2.0 * (c1 * g01 + c2 * g02)) + c1 * (c1 * g11 + 2.0 * c2 * g12) + c2 * c2 * g22
     h32 = jnp.sqrt(jnp.maximum(square, 0.0) + EPSILON)
+    a = c
+    c0, c1 = c0 - shift * c1, c1 - shift * c2
     n0, n1, n2 = h21 * h32, -h11 * h32, h11 * h22 - h12 * h21
     factor = beta * n0 / (n0 * n0 + n1 * n1 + n2 * n2)
     f0, f1, f2 = factor * n0, factor * n1, factor * n2
@@ -742,7 +802,7 @@
         first_pack_kernel,
         [(4, *own), own, x_slab, x_slab, slab, slab],
         [soil_props.shape, (4, *own), pltpu.VMEM(own, jnp.int32), pltpu.VMEM((SUB, rows), jnp.int32)]
-        + [pltpu.SemaphoreType.DMA((4,))],
+        + [pltpu.SemaphoreType.DMA((7,))],
         name="first_pack",
         inside=pltpu.HBM,
     )(*(pltpu.with_memory_space_constraint(x, pltpu.HBM) for x in (soil_props, storage, soil_ids, bc_mask.T)))
@@ -776,19 +836,22 @@
     summed, edges, even, odd = call(fold_y_kernel, fold_shapes, name="fold_y")(solved, edges, ye, yo)
     xe, xo = exchange("gx", even, odd)
     halo = [(rows + 2, *TILE)] * 2 + [(4, count, *TILE)]
-    one, power, gram, solved, edges, even, odd = call(
+    rhs, q, t, solved, edges, even, odd = call(
         step_kernel,
-        [(2, *own), (2, *own), TILE] + solved_shapes,
-        [(2, *own)] + halo + buffers,
+        [(2, *own), halo[0], halo[0]] + solved_shapes,
+        halo[2:] + buffers,
         name="second_solve",
     )(summed, edges, xe, xo, *coeffs, image, scales, adjoint_source)
+    one, power, shifted, shift, gram = call(power_kernel, [(2, *own)] * 3 + [TILE, TILE], name="first_power")(
+        rhs, q, t, scales, adjoint_source
+    )
 
     ye, yo = exchange("gy", even, odd)
     summed, edges, even, odd = call(fold_y_kernel, fold_shapes, name="fold_y")(solved, edges, ye, yo)
     xe, xo = exchange("gx", even, odd)
     two, second, gram = call(
         last_kernel, [(2, *own), (2, *own), (devices, LANE)], halo, name="last_image"
-    )(summed, edges, xe, xo, image, scales, adjoint_source, power, gram)
+    )(summed, edges, xe, xo, image, scales, adjoint_source, power, shifted, shift, gram)
     gram = lax.all_to_all(gram, ("gx", "gy"), 0, 0, tiled=True)
     return tuple(
         call(

time: 49.1 us -> 49.1 us (level)
    pallas_call x9 -> x10, Pallas kernels: 5.61 us -> 5.78 us  [run(): pl.pallas_call(kernel, out_shape=[jax.ShapeDtypeStruct(shape, F32) for sh...]
  transfers between devices with their start and end apart: 14 -> 14, of which waited for: 6 -> 6; matrix products, arithmetic and copies ran while one was open for 0% -> 0% of each run, Pallas kernels for 1% -> 2%
where the time goes in v7:
time: 49.1 us; the launch traced here: 48.9 us
  starting transfers between devices  18.8 us (38%)
  waiting for transfers between devices  11.9 us (24%)
  blocking collectives  11.7 us (24%)
  Pallas kernels  5.78 us (12%)
  between operations  0.74 us (2%)
    all_to_all x1, blocking collectives, shards(): gram = lax.all_to_all(gram, ('gx', 'gy'), 0, 0, tiled=True)  11.7 us
    ppermute x7, starting transfers between devices, exchange(): lax.ppermute(odd, ('gx', 'gy'), others)  10.7 us
    ppermute x7, starting transfers between devices, exchange(): lax.ppermute(even, axis, pairs)  8.09 us
    ppermute x7, waiting for transfers between devices, exchange(): lax.ppermute(odd, ('gx', 'gy'), others)  7 us
    pallas_call x10, Pallas kernels, run(): pl.pallas_call(kernel, out_shape=[jax.ShapeDtypeStruct(shape, F32) for sh...  5.78 us
    ppermute x7, waiting for transfers between devices, exchange(): lax.ppermute(even, axis, pairs)  4.9 us
  transfers between devices with their start and end apart: 14, of which 6 were waited for; matrix products, arithmetic and copies ran while one was open for 0% of the time, Pallas kernels for 2%

profile of v7, /device:TPU:0, one launch (start us, length us, event | category | flops | bytes accessed | tf_op | source)
XLA Modules:
  0.0 48.9 jit_solution(16612087419455519455)
XLA Ops:
  0.6 1.3 %first_pack.1 = (f32[4,16,8,128]{3,2,1,0:T(8,128)S(1)}, f32[16,8,128]{2,1,0:T(8,128)S(1)}, f32[21,8,128]{2,1,0:T(8,128)S(1)}, f32[21,8,128]{2,1,0:T(8,128)S(1)},...) custom-call(f32[3,16]{1,0:T(4,128)} %props_ref.3, f32[4,16,8,128]{3,2,1,0:T(8,128)} %storage_hbm.1, ...), custom_call_target="tpu_custom_call" | custom-call | tf_op jit(solution)/shard_map/first_pack/pallas_call | solution.py:762
  1.9 3.0 %collective-permute-start = (f32[21,8,128]{2,1,0:T(8,128)S(1)}, f32[21,8,128]{2,1,0:T(8,128)S(1)}, u32[]{:S(2)}, u32[]{:S(2)}) collective-permute-start(f32[21,8,128]{2,1,0:T(8,128)S(1)} %get-tuple-element.48), channel_id=1, source_target_pairs={{0,8},{8,0},{16,24},{24,16},{1,9},{9,1},{17,25},{25,17},{2,10},{10... | collective-permute-start | bytes 258056 | tf_op jit(solution)/shard_map/ppermute | solution.py:790
  4.9 0.0 collective-permute-start.1
  4.9 0.5 %collective-permute-start.2 = (f32[42,8,128]{2,1,0:T(8,128)S(1)}, f32[42,8,128]{2,1,0:T(8,128)S(1)}, u32[]{:S(2)}, u32[]{:S(2)}) collective-permute-start(f32[42,8,128]{2,1,0:T(8,128)S(1)} %get-tuple-element.50), channel_id=1, source_target_pairs={{0,1},{1,0},{2,3},{3,2},{4,5},{5,4},{6,7},{7,6},{8,9},{9,8},{10,11... | collective-permute-start | bytes 516104 | tf_op jit(solution)/shard_map/ppermute | solution.py:790
  5.4 1.1 %collective-permute-start.3 = (f32[42,8,128]{2,1,0:T(8,128)S(1)}, f32[42,8,128]{2,1,0:T(8,128)S(1)}, u32[]{:S(2)}, u32[]{:S(2)}) collective-permute-start(f32[42,8,128]{2,1,0:T(8,128)S(1)} %get-tuple-element.51), channel_id=1, source_target_pairs={{0,16},{1,2},{2,1},{3,4},{4,3},{5,6},{6,5},{7,23},{8,24},{9,10},{1... | collective-permute-start | bytes 516104 | tf_op jit(solution)/shard_map/ppermute | solution.py:790
  6.5 0.9 %collective-permute-done.xe_ref = f32[21,8,128]{2,1,0:T(8,128)S(1)} collective-permute-done((f32[21,8,128]{2,1,0:T(8,128)S(1)}, f32[21,8,128]{2,1,0:T(8,128)S(1)}, u32[]{:S(2)}, u32[]{:S(2)}) %collective-permute-start) | collective-permute-done | bytes 86048 | tf_op jit(solution)/shard_map/ppermute | solution.py:790
  7.4 0.0 collective-permute-done.1.xo_ref
  7.5 0.1 collective-permute-start.4
  7.6 0.0 copy-start.1
  7.6 4.5 %collective-permute-start.5 = (f32[15,8,128]{2,1,0:T(8,128)S(1)}, f32[15,8,128]{2,1,0:T(8,128)S(1)}, u32[]{:S(2)}, u32[]{:S(2)}) collective-permute-start(f32[15,8,128]{2,1,0:T(8,128)S(1)} %get-tuple-element.53), channel_id=1, source_target_pairs={{0,16},{1,2},{2,1},{3,4},{4,3},{5,6},{6,5},{7,23},{8,24},{9,10},{1... | collective-permute-start | bytes 184328 | tf_op jit(solution)/shard_map/ppermute | solution.py:790
  12.1 0.0 collective-permute-done.2.ye_ref
  12.1 0.0 collective-permute-done.3.yo_ref
  12.1 0.6 %own_coefficients.1 = (f32[4,16,8,128]{3,2,1,0:T(8,128)S(1)}, f32[4,14,8,128]{3,2,1,0:T(8,128)S(1)}, f32[4,16,8,128]{3,2,1,0:T(8,128)S(1)}, f32[5,16,8,128]{3,2,...) custom-call(f32[3,16]{1,0:T(4,128)S(1)} %copy-done.1, ...), custom_call_target="tpu_custom_call" | custom-call | tf_op jit(solution)/shard_map/own_coefficients/pallas_call | solution.py:762
  12.8 1.5 %collective-permute-done.5.co_ref = f32[15,8,128]{2,1,0:T(8,128)S(1)} collective-permute-done((f32[15,8,128]{2,1,0:T(8,128)S(1)}, f32[15,8,128]{2,1,0:T(8,128)S(1)}, u32[]{:S(2)}, u32[]{:S(2)}) %collective-permute-start.5) | collective-permute-done | bytes 61472 | tf_op jit(solution)/shard_map/ppermute | solution.py:790
  14.3 1.2 %first_solve.1 = (f32[4,8,8,128]{3,2,1,0:T(8,128)S(1)}, f32[4,10,8,128]{3,2,1,0:T(8,128)S(1)}, f32[2,24,8,128]{3,2,1,0:T(8,128)S(1)}, f32[4,3,8,128]{3,2,1,0:T(8...) custom-call(f32[3,16]{1,0:T(4,128)S(1)} %copy-done.1, f32[21,8,128]{2,1,0:T(8,128)S(1)} %collective-permute-done.xe_ref, ...), custom_call_target="tpu_custom_call" | custom-call | tf_op jit(solution)/shard_map/first_solve/pallas_call | solution.py:762
  15.5 0.1 collective-permute-start.6
  15.6 2.1 %collective-permute-start.7 = (f32[27,8,128]{2,1,0:T(8,128)S(1)}, f32[27,8,128]{2,1,0:T(8,128)S(1)}, u32[]{:S(2)}, u32[]{:S(2)}) collective-permute-start(f32[27,8,128]{2,1,0:T(8,128)S(1)} %get-tuple-element.65), channel_id=1, source_target_pairs={{0,16},{1,2},{2,1},{3,4},{4,3},{5,6},{6,5},{7,23},{8,24},{9,10},{1... | collective-permute-start | bytes 331784 | tf_op jit(solution)/shard_map/ppermute | solution.py:790
  17.7 2.7 %collective-permute-done.7.yo_ref = f32[27,8,128]{2,1,0:T(8,128)S(1)} collective-permute-done((f32[27,8,128]{2,1,0:T(8,128)S(1)}, f32[27,8,128]{2,1,0:T(8,128)S(1)}, u32[]{:S(2)}, u32[]{:S(2)}) %collective-permute-start.7) | collective-permute-done | bytes 110624 | tf_op jit(solution)/shard_map/ppermute | solution.py:790
  20.5 0.1 fold_y.2
  20.5 2.2 %collective-permute-start.8 = (f32[12,8,128]{2,1,0:T(8,128)S(1)}, f32[12,8,128]{2,1,0:T(8,128)S(1)}, u32[]{:S(2)}, u32[]{:S(2)}) collective-permute-start(f32[12,8,128]{2,1,0:T(8,128)S(1)} %get-tuple-element.68), channel_id=1, source_target_pairs={{0,8},{8,0},{16,24},{24,16},{1,9},{9,1},{17,25},{25,17},{2,10},{10... | collective-permute-start | bytes 147464 | tf_op jit(solution)/shard_map/ppermute | solution.py:790
  22.7 2.1 %collective-permute-done.8.xe_ref = f32[12,8,128]{2,1,0:T(8,128)S(1)} collective-permute-done((f32[12,8,128]{2,1,0:T(8,128)S(1)}, f32[12,8,128]{2,1,0:T(8,128)S(1)}, u32[]{:S(2)}, u32[]{:S(2)}) %collective-permute-start.8) | collective-permute-done | bytes 49184 | tf_op jit(solution)/shard_map/ppermute | solution.py:790
  24.8 1.1 %second_solve.1 = (f32[2,16,8,128]{3,2,1,0:T(8,128)S(1)}, f32[18,8,128]{2,1,0:T(8,128)S(1)}, f32[18,8,128]{2,1,0:T(8,128)S(1)}, f32[2,24,8,128]{3,2,1,0:T(8,128)...) custom-call(f32[2,24,8,128]{3,2,1,0:T(8,128)S(1)} %get-tuple-element.66.summed_ref, ...), custom_call_target="tpu_custom_call" | custom-call | tf_op jit(solution)/shard_map/second_solve/pallas_call | solution.py:762
  25.9 0.1 collective-permute-start.10
  26.0 3.0 %collective-permute-start.11 = (f32[27,8,128]{2,1,0:T(8,128)S(1)}, f32[27,8,128]{2,1,0:T(8,128)S(1)}, u32[]{:S(2)}, u32[]{:S(2)}) collective-permute-start(f32[27,8,128]{2,1,0:T(8,128)S(1)} %get-tuple-element.77), channel_id=1, source_target_pairs={{0,16},{1,2},{2,1},{3,4},{4,3},{5,6},{6,5},{7,23},{8,24},{9,10},{1... | collective-permute-start | bytes 331784 | tf_op jit(solution)/shard_map/ppermute | solution.py:790
  29.0 2.7 %collective-permute-done.11.yo_ref = f32[27,8,128]{2,1,0:T(8,128)S(1)} collective-permute-done((f32[27,8,128]{2,1,0:T(8,128)S(1)}, f32[27,8,128]{2,1,0:T(8,128)S(1)}, u32[]{:S(2)}, u32[]{:S(2)}) %collective-permute-start.11) | collective-permute-done | bytes 110624 | tf_op jit(solution)/shard_map/ppermute | solution.py:790
  31.7 0.1 fold_y.3
  31.8 2.2 %collective-permute-start.12 = (f32[12,8,128]{2,1,0:T(8,128)S(1)}, f32[12,8,128]{2,1,0:T(8,128)S(1)}, u32[]{:S(2)}, u32[]{:S(2)}) collective-permute-start(f32[12,8,128]{2,1,0:T(8,128)S(1)} %get-tuple-element.80), channel_id=1, source_target_pairs={{0,8},{8,0},{16,24},{24,16},{1,9},{9,1},{17,25},{25,17},{2,10},{10... | collective-permute-start | bytes 147464 | tf_op jit(solution)/shard_map/ppermute | solution.py:790
  33.9 0.2 first_power.1
  34.1 1.9 %collective-permute-done.12.xe_ref = f32[12,8,128]{2,1,0:T(8,128)S(1)} collective-permute-done((f32[12,8,128]{2,1,0:T(8,128)S(1)}, f32[12,8,128]{2,1,0:T(8,128)S(1)}, u32[]{:S(2)}, u32[]{:S(2)}) %collective-permute-start.12) | collective-permute-done | bytes 49184 | tf_op jit(solution)/shard_map/ppermute | solution.py:790
  36.0 0.3 last_image.1
  36.3 11.7 %all_to_all.11 = f32[32,1,128]{2,1,0:T(1,128)S(1)} all-to-all(f32[32,1,128]{2,1,0:T(1,128)S(1)} %bitcast.6), channel_id=1, replica_groups=mesh['gx'=4,'gy'=8] {'gx','gy'}, dimensions={0} | all-to-all | bytes 32768 | tf_op jit(solution)/shard_map/all_to_all | solution.py:855
  47.9 1.0 %combine.1 = (f32[2,16,8,128]{3,2,1,0:T(8,128)}, f32[2,16,8,128]{3,2,1,0:T(8,128)}, f32[2,16,8,128]{3,2,1,0:T(8,128)}) custom-call(f32[32,128]{1,0:T(8,128)S(1)} %bitcast.5, f32[2,16,8,128]{3,2,1,0:T(8,128)S(1)} %copy-done, f32[2,16,8,128]{3,2,1,0:T(8,128)S(1)} %get-tuple-element.85.power_ref, f32[2,16,8,128]{3,2,1,0:T(8,128)S(1)} %get-tuple-element.90.second_ref, ...), custom_call_target="tpu_custom_call" | custom-call | tf_op jit(solution)/shard_map/combine/pallas_call | solution.py:762
  (11 shorter events, 0.1 us)
Async XLA Ops:
  1.9 5.5 %collective-permute-start = (f32[21,8,128]{2,1,0:T(8,128)S(1)}, f32[21,8,128]{2,1,0:T(8,128)S(1)}, u32[]{:S(2)}, u32[]{:S(2)}) collective-permute-start(f32[21,8,128]{2,1,0:T(8,128)S(1)} %get-tuple-element.48), channel_id=1, source_target_pairs={{0,8},{8,0},{16,24},{24,16},{1,9},{9,1},{17,25},{25,17},{2,10},{10... | collective-permute-start | bytes 258056 | tf_op jit(solution)/shard_map/ppermute | solution.py:790
  4.9 2.5 %collective-permute-start.1 = (f32[21,8,128]{2,1,0:T(8,128)S(1)}, f32[21,8,128]{2,1,0:T(8,128)S(1)}, u32[]{:S(2)}, u32[]{:S(2)}) collective-permute-start(f32[21,8,128]{2,1,0:T(8,128)S(1)} %get-tuple-element.49), channel_id=1, source_target_pairs={{0,1},{1,0},{2,3},{3,2},{4,5},{5,4},{6,7},{7,6},{8,16},{9,17},{10,... | collective-permute-start | bytes 258056 | tf_op jit(solution)/shard_map/ppermute | solution.py:790
  4.9 7.2 %collective-permute-start.2 = (f32[42,8,128]{2,1,0:T(8,128)S(1)}, f32[42,8,128]{2,1,0:T(8,128)S(1)}, u32[]{:S(2)}, u32[]{:S(2)}) collective-permute-start(f32[42,8,128]{2,1,0:T(8,128)S(1)} %get-tuple-element.50), channel_id=1, source_target_pairs={{0,1},{1,0},{2,3},{3,2},{4,5},{5,4},{6,7},{7,6},{8,9},{9,8},{10,11... | collective-permute-start | bytes 516104 | tf_op jit(solution)/shard_map/ppermute | solution.py:790
  5.4 6.7 %copy-start = (f32[2,16,8,128]{3,2,1,0:T(8,128)S(1)}, f32[2,16,8,128]{3,2,1,0:T(8,128)}, u32[]{:S(2)}) copy-start(f32[2,16,8,128]{3,2,1,0:T(8,128)} %source_ref.9) | copy-start | bytes 393220
  5.4 6.7 %collective-permute-start.3 = (f32[42,8,128]{2,1,0:T(8,128)S(1)}, f32[42,8,128]{2,1,0:T(8,128)S(1)}, u32[]{:S(2)}, u32[]{:S(2)}) collective-permute-start(f32[42,8,128]{2,1,0:T(8,128)S(1)} %get-tuple-element.51), channel_id=1, source_target_pairs={{0,16},{1,2},{2,1},{3,4},{4,3},{5,6},{6,5},{7,23},{8,24},{9,10},{1... | collective-permute-start | bytes 516104 | tf_op jit(solution)/shard_map/ppermute | solution.py:790
  7.5 5.3 %collective-permute-start.4 = (f32[15,8,128]{2,1,0:T(8,128)S(1)}, f32[15,8,128]{2,1,0:T(8,128)S(1)}, u32[]{:S(2)}, u32[]{:S(2)}) collective-permute-start(f32[15,8,128]{2,1,0:T(8,128)S(1)} %get-tuple-element.52), channel_id=1, source_target_pairs={{0,1},{1,0},{2,3},{3,2},{4,5},{5,4},{6,7},{7,6},{8,9},{9,8},{10,11... | collective-permute-start | bytes 184328 | tf_op jit(solution)/shard_map/ppermute | solution.py:790
  7.6 4.6 %copy-start.1 = (f32[3,16]{1,0:T(4,128)S(1)}, f32[3,16]{1,0:T(4,128)}, u32[]{:S(2)}) copy-start(f32[3,16]{1,0:T(4,128)} %props_ref.3) | copy-start | bytes 580
  7.6 6.7 %collective-permute-start.5 = (f32[15,8,128]{2,1,0:T(8,128)S(1)}, f32[15,8,128]{2,1,0:T(8,128)S(1)}, u32[]{:S(2)}, u32[]{:S(2)}) collective-permute-start(f32[15,8,128]{2,1,0:T(8,128)S(1)} %get-tuple-element.53), channel_id=1, source_target_pairs={{0,16},{1,2},{2,1},{3,4},{4,3},{5,6},{6,5},{7,23},{8,24},{9,10},{1... | collective-permute-start | bytes 184328 | tf_op jit(solution)/shard_map/ppermute | solution.py:790
  15.5 2.2 %collective-permute-start.6 = (f32[27,8,128]{2,1,0:T(8,128)S(1)}, f32[27,8,128]{2,1,0:T(8,128)S(1)}, u32[]{:S(2)}, u32[]{:S(2)}) collective-permute-start(f32[27,8,128]{2,1,0:T(8,128)S(1)} %get-tuple-element.64), channel_id=1, source_target_pairs={{0,1},{1,0},{2,3},{3,2},{4,5},{5,4},{6,7},{7,6},{8,9},{9,8},{10,11... | collective-permute-start | bytes 331784 | tf_op jit(solution)/shard_map/ppermute | solution.py:790
  15.6 4.8 %collective-permute-start.7 = (f32[27,8,128]{2,1,0:T(8,128)S(1)}, f32[27,8,128]{2,1,0:T(8,128)S(1)}, u32[]{:S(2)}, u32[]{:S(2)}) collective-permute-start(f32[27,8,128]{2,1,0:T(8,128)S(1)} %get-tuple-element.65), channel_id=1, source_target_pairs={{0,16},{1,2},{2,1},{3,4},{4,3},{5,6},{6,5},{7,23},{8,24},{9,10},{1... | collective-permute-start | bytes 331784 | tf_op jit(solution)/shard_map/ppermute | solution.py:790
  20.5 4.3 %collective-permute-start.8 = (f32[12,8,128]{2,1,0:T(8,128)S(1)}, f32[12,8,128]{2,1,0:T(8,128)S(1)}, u32[]{:S(2)}, u32[]{:S(2)}) collective-permute-start(f32[12,8,128]{2,1,0:T(8,128)S(1)} %get-tuple-element.68), channel_id=1, source_target_pairs={{0,8},{8,0},{16,24},{24,16},{1,9},{9,1},{17,25},{25,17},{2,10},{10... | collective-permute-start | bytes 147464 | tf_op jit(solution)/shard_map/ppermute | solution.py:790
  22.7 2.1 %collective-permute-start.9 = (f32[12,8,128]{2,1,0:T(8,128)S(1)}, f32[12,8,128]{2,1,0:T(8,128)S(1)}, u32[]{:S(2)}, u32[]{:S(2)}) collective-permute-start(f32[12,8,128]{2,1,0:T(8,128)S(1)} %get-tuple-element.69), channel_id=1, source_target_pairs={{0,1},{1,0},{2,3},{3,2},{4,5},{5,4},{6,7},{7,6},{8,16},{9,17},{10,... | collective-permute-start | bytes 147464 | tf_op jit(solution)/shard_map/ppermute | solution.py:790
  25.9 3.1 %collective-permute-start.10 = (f32[27,8,128]{2,1,0:T(8,128)S(1)}, f32[27,8,128]{2,1,0:T(8,128)S(1)}, u32[]{:S(2)}, u32[]{:S(2)}) collective-permute-start(f32[27,8,128]{2,1,0:T(8,128)S(1)} %get-tuple-element.76), channel_id=1, source_target_pairs={{0,1},{1,0},{2,3},{3,2},{4,5},{5,4},{6,7},{7,6},{8,9},{9,8},{10,11... | collective-permute-start | bytes 331784 | tf_op jit(solution)/shard_map/ppermute | solution.py:790
  26.0 5.7 %collective-permute-start.11 = (f32[27,8,128]{2,1,0:T(8,128)S(1)}, f32[27,8,128]{2,1,0:T(8,128)S(1)}, u32[]{:S(2)}, u32[]{:S(2)}) collective-permute-start(f32[27,8,128]{2,1,0:T(8,128)S(1)} %get-tuple-element.77), channel_id=1, source_target_pairs={{0,16},{1,2},{2,1},{3,4},{4,3},{5,6},{6,5},{7,23},{8,24},{9,10},{1... | collective-permute-start | bytes 331784 | tf_op jit(solution)/shard_map/ppermute | solution.py:790
  31.8 4.2 %collective-permute-start.12 = (f32[12,8,128]{2,1,0:T(8,128)S(1)}, f32[12,8,128]{2,1,0:T(8,128)S(1)}, u32[]{:S(2)}, u32[]{:S(2)}) collective-permute-start(f32[12,8,128]{2,1,0:T(8,128)S(1)} %get-tuple-element.80), channel_id=1, source_target_pairs={{0,8},{8,0},{16,24},{24,16},{1,9},{9,1},{17,25},{25,17},{2,10},{10... | collective-permute-start | bytes 147464 | tf_op jit(solution)/shard_map/ppermute | solution.py:790
  33.9 2.1 %collective-permute-start.13 = (f32[12,8,128]{2,1,0:T(8,128)S(1)}, f32[12,8,128]{2,1,0:T(8,128)S(1)}, u32[]{:S(2)}, u32[]{:S(2)}) collective-permute-start(f32[12,8,128]{2,1,0:T(8,128)S(1)} %get-tuple-element.81), channel_id=1, source_target_pairs={{0,1},{1,0},{2,3},{3,2},{4,5},{5,4},{6,7},{7,6},{8,16},{9,17},{10,... | collective-permute-start | bytes 147464 | tf_op jit(solution)/shard_map/ppermute | solution.py:790

commit v8 on v7

--- a/solution.py
+++ b/solution.py
@@ -188,62 +188,75 @@
 
 def halo_x(even_ref, odd_ref):
     first, has_low, has_high = position("gx")
-    fields = []
-    for k in range(4):
+    groups = []
+    for k in range(5):
         spots = pl.ds(k * MARGIN, MARGIN)
         low, high = from_sides(first, even_ref[spots], odd_ref[spots])
-        fields.append([low[i] for i in range(MARGIN)] + [high[i] for i in range(MARGIN)])
-    spots = pl.ds(4 * MARGIN, RIM)
-    low, high = from_sides(first, even_ref[spots], odd_ref[spots])
-    low = jnp.where(has_low, low, 0.0)
-    high = jnp.where(has_high, high, 0.0)
-    return fields, [low[i] for i in range(RIM)] + [high[i] for i in range(RIM)]
+        if k == 4:
+            low = jnp.where(has_low, low, 0.0)
+            high = jnp.where(has_high, high, 0.0)
+        groups.append([low[i] for i in range(MARGIN)] + [high[i] for i in range(MARGIN)])
+    empty = jnp.zeros(TILE, F32)
+    return groups[:4], [empty, *groups[4], empty]
+
+
+def own_row(tables, storage_ref, ids_ref, bc_ref, x, spot):
+    wire = (ids_ref[x] + 1).astype(F32)
+    kp = lookup(tables[0], wire)
+    carried = lookup(tables[2], wire)
+    held = jnp.broadcast_to(bc_ref[:, x : x + 1].astype(F32), TILE)
+    bound = jnp.where(spot == LANE - 1, 2.0 * kp * held, 0.0)
+    press = storage_ref[0, x]
+    lower = storage_ref[1, x]
+    fields = (press + bound, carried * press - storage_ref[2, x], lower, storage_ref[3, x] - carried * lower)
+    return fields, wire
 
 
 def first_pack_kernel(
     props_hbm, storage_hbm, ids_hbm, bc_hbm,
-    fields_ref, wire_ref, x_even_ref, x_odd_ref, y_even_ref, y_odd_ref,
-    props_ref, storage_ref, ids_ref, bc_ref, sems,
+    props_ref, storage_ref, ids_ref, bc_ref, even_ref, odd_ref, sems,
 ):
-    places = [(ids_hbm, ids_ref), (props_hbm, props_ref), (bc_hbm, bc_ref)]
-    places += [(storage_hbm.at[k], storage_ref.at[k]) for k in range(4)]
+    places = ((ids_hbm, ids_ref), (storage_hbm, storage_ref), (props_hbm, props_ref), (bc_hbm, bc_ref))
     copies = [pltpu.make_async_copy(src, dst, sems.at[k]) for k, (src, dst) in enumerate(places)]
     for copy in copies:
         copy.start()
     rows = ids_ref.shape[0]
     spot = lane()
+    first, _, _ = position("gx")
     for copy in copies:
         copy.wait()
     tables = wide_tables(props_ref)
+
+    ends = []
+    for start, inner, beyond in ((0, MARGIN - 1, MARGIN), (rows - MARGIN, 0, -1)):
+        values, wires = zip(*(own_row(tables, storage_ref, ids_ref, bc_ref, start + i, spot) for i in range(MARGIN)))
+        fields = [[value[k] for value in values] for k in range(4)]
+        next_wire = (ids_ref[start + beyond] + 1).astype(F32)
+        for k, table in ((0, tables[0]), (3, tables[1])):
+            face = jnp.sqrt(lookup(table, wires[inner]) * lookup(table, next_wire))
+            fields[k][inner] = fields[k][inner] + face
+        ends.append([tile for group in (*fields, wires) for tile in group])
+    for place, (low, high) in enumerate(zip(*ends)):
+        even_ref[place] = jnp.where(first, high, low)
+        odd_ref[place] = jnp.where(first, low, high)
+
+
+def own_pack_kernel(
+    props_ref, storage_ref, ids_ref, bc_ref, fields_ref, wire_ref, even_ref, odd_ref,
+):
+    rows = ids_ref.shape[0]
+    spot = lane()
+    tables = wide_tables(props_ref)
     fields = [[] for _ in range(4)]
+    wires = []
     for x in range(rows):
-        wire = (ids_ref[x] + 1).astype(F32)
+        values, wire = own_row(tables, storage_ref, ids_ref, bc_ref, x, spot)
         wire_ref[x] = wire
-        kp = lookup(tables[0], wire)
-        carried = lookup(tables[2], wire)
-        held = jnp.broadcast_to(bc_ref[:, x : x + 1].astype(F32), TILE)
-        bound = jnp.where(spot == LANE - 1, 2.0 * kp * held, 0.0)
-        press = storage_ref[0, x]
-        lower = storage_ref[1, x]
-        fields[0].append(press + bound)
-        fields[1].append(carried * press - storage_ref[2, x])
-        fields[2].append(lower)
-        fields[3].append(storage_ref[3, x] - carried * lower)
+        wires.append(wire)
         for k in range(4):
-            fields_ref[k, x] = fields[k][x]
-    first, _, _ = position("gx")
-    high, low = rows - MARGIN, 0
-    start_even = jnp.where(first, high, low)
-    start_odd = jnp.where(first, low, high)
-    wire_even = jnp.where(first, rows - RIM, 0)
-    wire_odd = jnp.where(first, 0, rows - RIM)
-    for k in range(4):
-        x_even_ref[pl.ds(k * MARGIN, MARGIN)] = fields_ref[k, pl.ds(start_even, MARGIN)]
-        x_odd_ref[pl.ds(k * MARGIN, MARGIN)] = fields_ref[k, pl.ds(start_odd, MARGIN)]
-    x_even_ref[pl.ds(4 * MARGIN, RIM)] = wire_ref[pl.ds(wire_even, RIM)]
-    x_odd_ref[pl.ds(4 * MARGIN, RIM)] = wire_ref[pl.ds(wire_odd, RIM)]
-    wire = [wire_ref[x] for x in range(rows)]
-    pack_y(fields, wire, [(wire_ref, (x,)) for x in range(rows)], y_even_ref, y_odd_ref)
+            fields_ref[k, x] = values[k]
+            fields[k].append(values[k])
+    pack_y(fields, wires, [(wire_ref, (x,)) for x in range(rows)], even_ref, odd_ref)
 
 
 def corner_pack_kernel(xe_ref, xo_ref, even_ref, odd_ref, wire_ref):
@@ -761,7 +774,9 @@
     def run(*args):
         return pl.pallas_call(
             kernel,
-            out_shape=[jax.ShapeDtypeStruct(shape, F32) for shape in outs],
+            out_shape=[
+                jax.ShapeDtypeStruct(*(spec if isinstance(spec[0], tuple) else (spec, F32))) for spec in outs
+            ],
             in_specs=[pl.BlockSpec(memory_space=inside)] * len(args),
             out_specs=[pl.BlockSpec(memory_space=outside)] * len(outs),
             scratch_shapes=[pltpu.VMEM(spec, F32) if isinstance(spec, tuple) else spec for spec in scratch],
@@ -796,17 +811,18 @@
     devices = lax.axis_size("gx") * lax.axis_size("gy")
     cells = 2.0 * rows * soil_ids.shape[1] * depth * devices
     own = (rows, *TILE)
-    x_slab = (4 * MARGIN + RIM, *TILE)
-    slab = y_slab(rows, rows, rows)
-    fields, wire, x_even, x_odd, y_even, y_odd = call(
+    x_slab = (5 * MARGIN, *TILE)
+    held = (SUB, rows)
+    *raw, x_even, x_odd = call(
         first_pack_kernel,
-        [(4, *own), own, x_slab, x_slab, slab, slab],
-        [soil_props.shape, (4, *own), pltpu.VMEM(own, jnp.int32), pltpu.VMEM((SUB, rows), jnp.int32)]
-        + [pltpu.SemaphoreType.DMA((7,))],
+        [soil_props.shape, (4, *own), (own, jnp.int32), (held, jnp.int32), x_slab, x_slab],
+        [pltpu.SemaphoreType.DMA((4,))],
         name="first_pack",
         inside=pltpu.HBM,
     )(*(pltpu.with_memory_space_constraint(x, pltpu.HBM) for x in (soil_props, storage, soil_ids, bc_mask.T)))
     xe, xo = exchange("gx", x_even, x_odd)
+    slab = y_slab(rows, rows, rows)
+    fields, wire, y_even, y_odd = call(own_pack_kernel, [(4, *own), own, slab, slab], name="own_pack")(*raw)
     ye, yo = exchange("gy", y_even, y_odd)
     slab = y_slab(5, 8, 2)
     weight = pl.CostEstimate(flops=10**11, bytes_accessed=10**9, transcendentals=0)

time: 49.1 us -> 48.8 us (level)
    pallas_call x10 -> x11, Pallas kernels: 5.78 us -> 5.89 us  [run(): pl.pallas_call(kernel, out_shape=[jax.ShapeDtypeStruct(*(spec if isinstan...]
where the time goes in v8:
time: 48.8 us; the launch traced here: 48.6 us
  starting transfers between devices  18.7 us (38%)
  waiting for transfers between devices  11.7 us (24%)
  blocking collectives  11.6 us (24%)
  Pallas kernels  5.89 us (12%)
  between operations  0.74 us (2%)
    all_to_all x1, blocking collectives, shards(): gram = lax.all_to_all(gram, ('gx', 'gy'), 0, 0, tiled=True)  11.6 us
    ppermute x7, starting transfers between devices, exchange(): lax.ppermute(odd, ('gx', 'gy'), others)  10.9 us
    ppermute x7, starting transfers between devices, exchange(): lax.ppermute(even, axis, pairs)  7.83 us
    ppermute x7, waiting for transfers between devices, exchange(): lax.ppermute(odd, ('gx', 'gy'), others)  7.01 us
    pallas_call x11, Pallas kernels, run(): pl.pallas_call(kernel, out_shape=[jax.ShapeDtypeStruct(*(spec if isinstan...  5.89 us
    ppermute x7, waiting for transfers between devices, exchange(): lax.ppermute(even, axis, pairs)  4.66 us
  transfers between devices with their start and end apart: 14, of which 6 were waited for; matrix products, arithmetic and copies ran while one was open for 0% of the time, Pallas kernels for 2%

profile of v8, /device:TPU:0, one launch (start us, length us, event | category | flops | bytes accessed | tf_op | source)
XLA Modules:
  0.0 48.6 jit_solution(13482279073798454191)
XLA Ops:
  0.6 1.2 %first_pack.1 = (f32[3,16]{1,0:T(4,128)S(1)}, f32[4,16,8,128]{3,2,1,0:T(8,128)S(1)}, s32[16,8,128]{2,1,0:T(8,128)S(1)}, s32[8,16]{1,0:T(8,128)S(1)}, f32[20,8,12...) custom-call(f32[3,16]{1,0:T(4,128)} %props_ref.3, f32[4,16,8,128]{3,2,1,0:T(8,128)} %storage_hbm.1, s32[16,8,128]{2,1,0:T(8,128)} %ids_hbm.1, ...), custom_call_target="tpu_custom_call" | custom-call | tf_op jit(solution)/shard_map/first_pack/pallas_call | solution.py:775
  1.8 3.0 %collective-permute-start = (f32[20,8,128]{2,1,0:T(8,128)S(1)}, f32[20,8,128]{2,1,0:T(8,128)S(1)}, u32[]{:S(2)}, u32[]{:S(2)}) collective-permute-start(f32[20,8,128]{2,1,0:T(8,128)S(1)} %get-tuple-element.52), channel_id=1, source_target_pairs={{0,8},{8,0},{16,24},{24,16},{1,9},{9,1},{17,25},{25,17},{2,10},{10... | collective-permute-start | bytes 245768 | tf_op jit(solution)/shard_map/ppermute | solution.py:805
  4.8 0.0 collective-permute-start.1
  4.8 0.2 own_pack.1
  5.0 0.6 %collective-permute-start.2 = (f32[42,8,128]{2,1,0:T(8,128)S(1)}, f32[42,8,128]{2,1,0:T(8,128)S(1)}, u32[]{:S(2)}, u32[]{:S(2)}) collective-permute-start(f32[42,8,128]{2,1,0:T(8,128)S(1)} %get-tuple-element.58), channel_id=1, source_target_pairs={{0,1},{1,0},{2,3},{3,2},{4,5},{5,4},{6,7},{7,6},{8,9},{9,8},{10,11... | collective-permute-start | bytes 516104 | tf_op jit(solution)/shard_map/ppermute | solution.py:805
  5.6 1.1 %collective-permute-start.3 = (f32[42,8,128]{2,1,0:T(8,128)S(1)}, f32[42,8,128]{2,1,0:T(8,128)S(1)}, u32[]{:S(2)}, u32[]{:S(2)}) collective-permute-start(f32[42,8,128]{2,1,0:T(8,128)S(1)} %get-tuple-element.59), channel_id=1, source_target_pairs={{0,16},{1,2},{2,1},{3,4},{4,3},{5,6},{6,5},{7,23},{8,24},{9,10},{1... | collective-permute-start | bytes 516104 | tf_op jit(solution)/shard_map/ppermute | solution.py:805
  6.7 0.6 %collective-permute-done.xe_ref = f32[20,8,128]{2,1,0:T(8,128)S(1)} collective-permute-done((f32[20,8,128]{2,1,0:T(8,128)S(1)}, f32[20,8,128]{2,1,0:T(8,128)S(1)}, u32[]{:S(2)}, u32[]{:S(2)}) %collective-permute-start) | collective-permute-done | bytes 81952 | tf_op jit(solution)/shard_map/ppermute | solution.py:805
  7.3 0.0 collective-permute-done.1.xo_ref
  7.3 0.1 collective-permute-start.4
  7.4 4.6 %collective-permute-start.5 = (f32[15,8,128]{2,1,0:T(8,128)S(1)}, f32[15,8,128]{2,1,0:T(8,128)S(1)}, u32[]{:S(2)}, u32[]{:S(2)}) collective-permute-start(f32[15,8,128]{2,1,0:T(8,128)S(1)} %get-tuple-element.61), channel_id=1, source_target_pairs={{0,16},{1,2},{2,1},{3,4},{4,3},{5,6},{6,5},{7,23},{8,24},{9,10},{1... | collective-permute-start | bytes 184328 | tf_op jit(solution)/shard_map/ppermute | solution.py:805
  12.0 0.0 collective-permute-done.2.ye_ref
  12.0 0.0 collective-permute-done.3.yo_ref
  12.0 0.6 %own_coefficients.1 = (f32[4,16,8,128]{3,2,1,0:T(8,128)S(1)}, f32[4,14,8,128]{3,2,1,0:T(8,128)S(1)}, f32[4,16,8,128]{3,2,1,0:T(8,128)S(1)}, f32[5,16,8,128]{3,2,...) custom-call(f32[3,16]{1,0:T(4,128)S(1)} %copy-done.1, ...), custom_call_target="tpu_custom_call" | custom-call | tf_op jit(solution)/shard_map/own_coefficients/pallas_call | solution.py:775
  12.6 1.5 %collective-permute-done.5.co_ref = f32[15,8,128]{2,1,0:T(8,128)S(1)} collective-permute-done((f32[15,8,128]{2,1,0:T(8,128)S(1)}, f32[15,8,128]{2,1,0:T(8,128)S(1)}, u32[]{:S(2)}, u32[]{:S(2)}) %collective-permute-start.5) | collective-permute-done | bytes 61472 | tf_op jit(solution)/shard_map/ppermute | solution.py:805
  14.2 1.2 %first_solve.1 = (f32[4,8,8,128]{3,2,1,0:T(8,128)S(1)}, f32[4,10,8,128]{3,2,1,0:T(8,128)S(1)}, f32[2,24,8,128]{3,2,1,0:T(8,128)S(1)}, f32[4,3,8,128]{3,2,1,0:T(8...) custom-call(f32[3,16]{1,0:T(4,128)S(1)} %copy-done.1, f32[20,8,128]{2,1,0:T(8,128)S(1)} %collective-permute-done.xe_ref, ...), custom_call_target="tpu_custom_call" | custom-call | tf_op jit(solution)/shard_map/first_solve/pallas_call | solution.py:775
  15.4 0.1 collective-permute-start.6
  15.5 2.1 %collective-permute-start.7 = (f32[27,8,128]{2,1,0:T(8,128)S(1)}, f32[27,8,128]{2,1,0:T(8,128)S(1)}, u32[]{:S(2)}, u32[]{:S(2)}) collective-permute-start(f32[27,8,128]{2,1,0:T(8,128)S(1)} %get-tuple-element.73), channel_id=1, source_target_pairs={{0,16},{1,2},{2,1},{3,4},{4,3},{5,6},{6,5},{7,23},{8,24},{9,10},{1... | collective-permute-start | bytes 331784 | tf_op jit(solution)/shard_map/ppermute | solution.py:805
  17.6 2.7 %collective-permute-done.7.yo_ref = f32[27,8,128]{2,1,0:T(8,128)S(1)} collective-permute-done((f32[27,8,128]{2,1,0:T(8,128)S(1)}, f32[27,8,128]{2,1,0:T(8,128)S(1)}, u32[]{:S(2)}, u32[]{:S(2)}) %collective-permute-start.7) | collective-permute-done | bytes 110624 | tf_op jit(solution)/shard_map/ppermute | solution.py:805
  20.4 0.1 fold_y.2
  20.4 2.0 %collective-permute-start.8 = (f32[12,8,128]{2,1,0:T(8,128)S(1)}, f32[12,8,128]{2,1,0:T(8,128)S(1)}, u32[]{:S(2)}, u32[]{:S(2)}) collective-permute-start(f32[12,8,128]{2,1,0:T(8,128)S(1)} %get-tuple-element.76), channel_id=1, source_target_pairs={{0,8},{8,0},{16,24},{24,16},{1,9},{9,1},{17,25},{25,17},{2,10},{10... | collective-permute-start | bytes 147464 | tf_op jit(solution)/shard_map/ppermute | solution.py:805
  22.4 2.1 %collective-permute-done.8.xe_ref = f32[12,8,128]{2,1,0:T(8,128)S(1)} collective-permute-done((f32[12,8,128]{2,1,0:T(8,128)S(1)}, f32[12,8,128]{2,1,0:T(8,128)S(1)}, u32[]{:S(2)}, u32[]{:S(2)}) %collective-permute-start.8) | collective-permute-done | bytes 49184 | tf_op jit(solution)/shard_map/ppermute | solution.py:805
  24.6 1.1 %second_solve.1 = (f32[2,16,8,128]{3,2,1,0:T(8,128)S(1)}, f32[18,8,128]{2,1,0:T(8,128)S(1)}, f32[18,8,128]{2,1,0:T(8,128)S(1)}, f32[2,24,8,128]{3,2,1,0:T(8,128)...) custom-call(f32[2,24,8,128]{3,2,1,0:T(8,128)S(1)} %get-tuple-element.74.summed_ref, ...), custom_call_target="tpu_custom_call" | custom-call | tf_op jit(solution)/shard_map/second_solve/pallas_call | solution.py:775
  25.7 0.1 collective-permute-start.10
  25.8 3.1 %collective-permute-start.11 = (f32[27,8,128]{2,1,0:T(8,128)S(1)}, f32[27,8,128]{2,1,0:T(8,128)S(1)}, u32[]{:S(2)}, u32[]{:S(2)}) collective-permute-start(f32[27,8,128]{2,1,0:T(8,128)S(1)} %get-tuple-element.85), channel_id=1, source_target_pairs={{0,16},{1,2},{2,1},{3,4},{4,3},{5,6},{6,5},{7,23},{8,24},{9,10},{1... | collective-permute-start | bytes 331784 | tf_op jit(solution)/shard_map/ppermute | solution.py:805
  28.8 2.7 %collective-permute-done.11.yo_ref = f32[27,8,128]{2,1,0:T(8,128)S(1)} collective-permute-done((f32[27,8,128]{2,1,0:T(8,128)S(1)}, f32[27,8,128]{2,1,0:T(8,128)S(1)}, u32[]{:S(2)}, u32[]{:S(2)}) %collective-permute-start.11) | collective-permute-done | bytes 110624 | tf_op jit(solution)/shard_map/ppermute | solution.py:805
  31.6 0.1 fold_y.3
  31.6 2.0 %collective-permute-start.12 = (f32[12,8,128]{2,1,0:T(8,128)S(1)}, f32[12,8,128]{2,1,0:T(8,128)S(1)}, u32[]{:S(2)}, u32[]{:S(2)}) collective-permute-start(f32[12,8,128]{2,1,0:T(8,128)S(1)} %get-tuple-element.88), channel_id=1, source_target_pairs={{0,8},{8,0},{16,24},{24,16},{1,9},{9,1},{17,25},{25,17},{2,10},{10... | collective-permute-start | bytes 147464 | tf_op jit(solution)/shard_map/ppermute | solution.py:805
  33.6 0.2 first_power.1
  33.8 2.0 %collective-permute-done.12.xe_ref = f32[12,8,128]{2,1,0:T(8,128)S(1)} collective-permute-done((f32[12,8,128]{2,1,0:T(8,128)S(1)}, f32[12,8,128]{2,1,0:T(8,128)S(1)}, u32[]{:S(2)}, u32[]{:S(2)}) %collective-permute-start.12) | collective-permute-done | bytes 49184 | tf_op jit(solution)/shard_map/ppermute | solution.py:805
  35.8 0.3 last_image.1
  36.1 11.6 %all_to_all.11 = f32[32,1,128]{2,1,0:T(1,128)S(1)} all-to-all(f32[32,1,128]{2,1,0:T(1,128)S(1)} %bitcast.6), channel_id=1, replica_groups=mesh['gx'=4,'gy'=8] {'gx','gy'}, dimensions={0} | all-to-all | bytes 32768 | tf_op jit(solution)/shard_map/all_to_all | solution.py:871
  47.7 1.0 %combine.1 = (f32[2,16,8,128]{3,2,1,0:T(8,128)}, f32[2,16,8,128]{3,2,1,0:T(8,128)}, f32[2,16,8,128]{3,2,1,0:T(8,128)}) custom-call(f32[32,128]{1,0:T(8,128)S(1)} %bitcast.5, f32[2,16,8,128]{3,2,1,0:T(8,128)S(1)} %copy-done, f32[2,16,8,128]{3,2,1,0:T(8,128)S(1)} %get-tuple-element.93.power_ref, f32[2,16,8,128]{3,2,1,0:T(8,128)S(1)} %get-tuple-element.98.second_ref, ...), custom_call_target="tpu_custom_call" | custom-call | tf_op jit(solution)/shard_map/combine/pallas_call | solution.py:775
  (12 shorter events, 0.1 us)
Async XLA Ops:
  1.8 5.4 %collective-permute-start = (f32[20,8,128]{2,1,0:T(8,128)S(1)}, f32[20,8,128]{2,1,0:T(8,128)S(1)}, u32[]{:S(2)}, u32[]{:S(2)}) collective-permute-start(f32[20,8,128]{2,1,0:T(8,128)S(1)} %get-tuple-element.52), channel_id=1, source_target_pairs={{0,8},{8,0},{16,24},{24,16},{1,9},{9,1},{17,25},{25,17},{2,10},{10... | collective-permute-start | bytes 245768 | tf_op jit(solution)/shard_map/ppermute | solution.py:805
  4.8 2.4 %collective-permute-start.1 = (f32[20,8,128]{2,1,0:T(8,128)S(1)}, f32[20,8,128]{2,1,0:T(8,128)S(1)}, u32[]{:S(2)}, u32[]{:S(2)}) collective-permute-start(f32[20,8,128]{2,1,0:T(8,128)S(1)} %get-tuple-element.53), channel_id=1, source_target_pairs={{0,1},{1,0},{2,3},{3,2},{4,5},{5,4},{6,7},{7,6},{8,16},{9,17},{10,... | collective-permute-start | bytes 245768 | tf_op jit(solution)/shard_map/ppermute | solution.py:805
  5.0 7.0 %collective-permute-start.2 = (f32[42,8,128]{2,1,0:T(8,128)S(1)}, f32[42,8,128]{2,1,0:T(8,128)S(1)}, u32[]{:S(2)}, u32[]{:S(2)}) collective-permute-start(f32[42,8,128]{2,1,0:T(8,128)S(1)} %get-tuple-element.58), channel_id=1, source_target_pairs={{0,1},{1,0},{2,3},{3,2},{4,5},{5,4},{6,7},{7,6},{8,9},{9,8},{10,11... | collective-permute-start | bytes 516104 | tf_op jit(solution)/shard_map/ppermute | solution.py:805
  5.6 6.4 %copy-start = (f32[2,16,8,128]{3,2,1,0:T(8,128)S(1)}, f32[2,16,8,128]{3,2,1,0:T(8,128)}, u32[]{:S(2)}) copy-start(f32[2,16,8,128]{3,2,1,0:T(8,128)} %source_ref.9) | copy-start | bytes 393220
  5.6 6.4 %collective-permute-start.3 = (f32[42,8,128]{2,1,0:T(8,128)S(1)}, f32[42,8,128]{2,1,0:T(8,128)S(1)}, u32[]{:S(2)}, u32[]{:S(2)}) collective-permute-start(f32[42,8,128]{2,1,0:T(8,128)S(1)} %get-tuple-element.59), channel_id=1, source_target_pairs={{0,16},{1,2},{2,1},{3,4},{4,3},{5,6},{6,5},{7,23},{8,24},{9,10},{1... | collective-permute-start | bytes 516104 | tf_op jit(solution)/shard_map/ppermute | solution.py:805
  7.3 5.3 %collective-permute-start.4 = (f32[15,8,128]{2,1,0:T(8,128)S(1)}, f32[15,8,128]{2,1,0:T(8,128)S(1)}, u32[]{:S(2)}, u32[]{:S(2)}) collective-permute-start(f32[15,8,128]{2,1,0:T(8,128)S(1)} %get-tuple-element.60), channel_id=1, source_target_pairs={{0,1},{1,0},{2,3},{3,2},{4,5},{5,4},{6,7},{7,6},{8,9},{9,8},{10,11... | collective-permute-start | bytes 184328 | tf_op jit(solution)/shard_map/ppermute | solution.py:805
  7.4 4.6 %copy-start.1 = (f32[3,16]{1,0:T(4,128)S(1)}, f32[3,16]{1,0:T(4,128)}, u32[]{:S(2)}) copy-start(f32[3,16]{1,0:T(4,128)} %props_ref.3) | copy-start | bytes 580
  7.4 6.8 %collective-permute-start.5 = (f32[15,8,128]{2,1,0:T(8,128)S(1)}, f32[15,8,128]{2,1,0:T(8,128)S(1)}, u32[]{:S(2)}, u32[]{:S(2)}) collective-permute-start(f32[15,8,128]{2,1,0:T(8,128)S(1)} %get-tuple-element.61), channel_id=1, source_target_pairs={{0,16},{1,2},{2,1},{3,4},{4,3},{5,6},{6,5},{7,23},{8,24},{9,10},{1... | collective-permute-start | bytes 184328 | tf_op jit(solution)/shard_map/ppermute | solution.py:805
  15.4 2.2 %collective-permute-start.6 = (f32[27,8,128]{2,1,0:T(8,128)S(1)}, f32[27,8,128]{2,1,0:T(8,128)S(1)}, u32[]{:S(2)}, u32[]{:S(2)}) collective-permute-start(f32[27,8,128]{2,1,0:T(8,128)S(1)} %get-tuple-element.72), channel_id=1, source_target_pairs={{0,1},{1,0},{2,3},{3,2},{4,5},{5,4},{6,7},{7,6},{8,9},{9,8},{10,11... | collective-permute-start | bytes 331784 | tf_op jit(solution)/shard_map/ppermute | solution.py:805
  15.5 4.8 %collective-permute-start.7 = (f32[27,8,128]{2,1,0:T(8,128)S(1)}, f32[27,8,128]{2,1,0:T(8,128)S(1)}, u32[]{:S(2)}, u32[]{:S(2)}) collective-permute-start(f32[27,8,128]{2,1,0:T(8,128)S(1)} %get-tuple-element.73), channel_id=1, source_target_pairs={{0,16},{1,2},{2,1},{3,4},{4,3},{5,6},{6,5},{7,23},{8,24},{9,10},{1... | collective-permute-start | bytes 331784 | tf_op jit(solution)/shard_map/ppermute | solution.py:805
  20.4 4.2 %collective-permute-start.8 = (f32[12,8,128]{2,1,0:T(8,128)S(1)}, f32[12,8,128]{2,1,0:T(8,128)S(1)}, u32[]{:S(2)}, u32[]{:S(2)}) collective-permute-start(f32[12,8,128]{2,1,0:T(8,128)S(1)} %get-tuple-element.76), channel_id=1, source_target_pairs={{0,8},{8,0},{16,24},{24,16},{1,9},{9,1},{17,25},{25,17},{2,10},{10... | collective-permute-start | bytes 147464 | tf_op jit(solution)/shard_map/ppermute | solution.py:805
  22.4 2.1 %collective-permute-start.9 = (f32[12,8,128]{2,1,0:T(8,128)S(1)}, f32[12,8,128]{2,1,0:T(8,128)S(1)}, u32[]{:S(2)}, u32[]{:S(2)}) collective-permute-start(f32[12,8,128]{2,1,0:T(8,128)S(1)} %get-tuple-element.77), channel_id=1, source_target_pairs={{0,1},{1,0},{2,3},{3,2},{4,5},{5,4},{6,7},{7,6},{8,16},{9,17},{10,... | collective-permute-start | bytes 147464 | tf_op jit(solution)/shard_map/ppermute | solution.py:805
  25.7 3.1 %collective-permute-start.10 = (f32[27,8,128]{2,1,0:T(8,128)S(1)}, f32[27,8,128]{2,1,0:T(8,128)S(1)}, u32[]{:S(2)}, u32[]{:S(2)}) collective-permute-start(f32[27,8,128]{2,1,0:T(8,128)S(1)} %get-tuple-element.84), channel_id=1, source_target_pairs={{0,1},{1,0},{2,3},{3,2},{4,5},{5,4},{6,7},{7,6},{8,9},{9,8},{10,11... | collective-permute-start | bytes 331784 | tf_op jit(solution)/shard_map/ppermute | solution.py:805
  25.8 5.8 %collective-permute-start.11 = (f32[27,8,128]{2,1,0:T(8,128)S(1)}, f32[27,8,128]{2,1,0:T(8,128)S(1)}, u32[]{:S(2)}, u32[]{:S(2)}) collective-permute-start(f32[27,8,128]{2,1,0:T(8,128)S(1)} %get-tuple-element.85), channel_id=1, source_target_pairs={{0,16},{1,2},{2,1},{3,4},{4,3},{5,6},{6,5},{7,23},{8,24},{9,10},{1... | collective-permute-start | bytes 331784 | tf_op jit(solution)/shard_map/ppermute | solution.py:805
  31.6 4.2 %collective-permute-start.12 = (f32[12,8,128]{2,1,0:T(8,128)S(1)}, f32[12,8,128]{2,1,0:T(8,128)S(1)}, u32[]{:S(2)}, u32[]{:S(2)}) collective-permute-start(f32[12,8,128]{2,1,0:T(8,128)S(1)} %get-tuple-element.88), channel_id=1, source_target_pairs={{0,8},{8,0},{16,24},{24,16},{1,9},{9,1},{17,25},{25,17},{2,10},{10... | collective-permute-start | bytes 147464 | tf_op jit(solution)/shard_map/ppermute | solution.py:805
  33.6 2.1 %collective-permute-start.13 = (f32[12,8,128]{2,1,0:T(8,128)S(1)}, f32[12,8,128]{2,1,0:T(8,128)S(1)}, u32[]{:S(2)}, u32[]{:S(2)}) collective-permute-start(f32[12,8,128]{2,1,0:T(8,128)S(1)} %get-tuple-element.89), channel_id=1, source_target_pairs={{0,1},{1,0},{2,3},{3,2},{4,5},{5,4},{6,7},{7,6},{8,16},{9,17},{10,... | collective-permute-start | bytes 147464 | tf_op jit(solution)/shard_map/ppermute | solution.py:805

commit v9 on v8

--- a/solution.py
+++ b/solution.py
@@ -132,7 +132,7 @@
     ]
 
 
-def pack_y(fields, wire, edges, even_ref, odd_ref):
+def pack_y(fields, wire, even_ref, odd_ref):
     first, _, _ = position("gy")
     even_low = (sublane() < 4) != first
     count, half = len(fields[0]), len(wire) // 2
@@ -147,15 +147,19 @@
             put(pair * count + i, fields[2 * pair][i], fields[2 * pair + 1][i])
     for j in range(half):
         put(2 * count + j, wire[j], wire[j + half])
-    rows_even, rows_odd = jnp.where(first, 3, 4), jnp.where(first, 4, 3)
-    if len(edges) % SUB:
-        last = even_ref.shape[0] - 1
-        even_ref[last] = odd_ref[last] = jnp.zeros(TILE, F32)
-    rim_rows(even_ref, odd_ref, 2 * count + half, edges, rows_even, rows_odd)
-
-
-def y_slab(count, ids, edges):
-    return (2 * count + ids // 2 + -(-edges // SUB), *TILE)
+
+
+def fold_beyond(fields, wire, tables, row):
+    out = list(fields)
+    for k, table in ((0, tables[0]), (3, tables[1])):
+        value = lookup(table, wire)
+        face = jnp.sqrt(value * jnp.where(row == 3, up_y(value), down_y(value)))
+        out[k] = out[k] + jnp.where((row == 3) | (row == 4), face, 0.0)
+    return out
+
+
+def y_slab(count, ids):
+    return (2 * count + ids // 2, *TILE)
 
 
 def unpack_fields(even_ref, odd_ref, count, i):
@@ -182,8 +186,7 @@
         low, high = sides(2 * count + j)
         one.append(jnp.where(row < 4, high, low))
         other.append(half_turn(jnp.where(row < 4, low, high)))
-    beyond = [sides(spot) for spot in range(2 * count + ids // 2, even_ref.shape[0])]
-    return one + other, beyond
+    return one + other
 
 
 def halo_x(even_ref, odd_ref):
@@ -255,17 +258,20 @@
         wires.append(wire)
         for k in range(4):
             fields_ref[k, x] = values[k]
-            fields[k].append(values[k])
-    pack_y(fields, wires, [(wire_ref, (x,)) for x in range(rows)], even_ref, odd_ref)
-
-
-def corner_pack_kernel(xe_ref, xo_ref, even_ref, odd_ref, wire_ref):
+        for k, value in enumerate(fold_beyond(values, wire, tables, sublane())):
+            fields[k].append(value)
+    pack_y(fields, wires, even_ref, odd_ref)
+
+
+def corner_pack_kernel(props_ref, xe_ref, xo_ref, even_ref, odd_ref):
     row = sublane()
+    tables = wide_tables(props_ref)
     fields, wire = halo_x(xe_ref, xo_ref)
+    for i in (MARGIN - 1, MARGIN):
+        for k, value in enumerate(fold_beyond([field[i] for field in fields], wire[i + 1], tables, row)):
+            fields[k][i] = value
     fields = [condense(field, row) for field in fields]
-    wire_ref[0], wire_ref[1] = wire[RIM - 1], wire[RIM]
-    edges = [(wire_ref, (j,)) for j in range(2)]
-    pack_y(fields, condense_wire(wire, row), edges, even_ref, odd_ref)
+    pack_y(fields, condense_wire(wire, row), even_ref, odd_ref)
 
 
 def sweep_row(load, coeff, j, row, spot, rhs, count):
@@ -404,36 +410,27 @@
     return [jnp.sqrt(jnp.maximum(table, 0.0)) for table in tables[:2]], tables[2]
 
 
-def beyond_lines(beyond_ref, g, j):
-    return tuple(
-        jnp.broadcast_to(beyond_ref[g, end, j // SUB, pl.ds(j % SUB, 1)], TILE) for end in (1, 0)
-    )
-
-
 def own_coefficients_kernel(
     props_ref, fields_ref, wire_ref, xe_ref, xo_ref, ye_ref, yo_ref, source_ref,
-    own_ref, own_side_ref, image_ref, scale_ref, rhs_ref, roots_ref, roots_side_ref, beyond_ref,
+    own_ref, own_side_ref, image_ref, scale_ref, rhs_ref, roots_ref, roots_side_ref,
 ):
     rows = wire_ref.shape[0]
     spot = lane()
     roots, carried = root_tables(props_ref)
     _, x_wire = halo_x(xe_ref, xo_ref)
-    sides, beyond = unpack_wire(ye_ref, yo_ref, rows, rows)
+    sides = unpack_wire(ye_ref, yo_ref, rows, rows)
     wire = x_wire[:RIM] + [wire_ref[x] for x in range(rows)] + x_wire[RIM:]
     for g in range(2):
         for j, value in enumerate(wire):
             roots_ref[g, j] = lookup(roots[g], value)
         for x in range(rows):
             roots_side_ref[g, x] = lookup(roots[g], sides[x])
-        for tile, ends in enumerate(beyond):
-            for end in range(2):
-                beyond_ref[g, end, tile] = lookup(roots[g], ends[end])
     for x in range(rows):
         inner = 0 < x < rows - 1
         sums = []
         for g in range(2):
             tiles = lambda j, tile: roots_side_ref[g, j - RIM] if tile else roots_ref[g, j]
-            lines = beyond_lines(beyond_ref, g, x) if inner else (None, None)
+            lines = (0.0, 0.0) if inner else (None, None)
             sums.append(diagonal(tiles, (x + RIM, *lines), spot))
         stores = [fields_ref[k, x] for k in range(4)]
         gp, gt = (roots_ref[g, x + RIM] for g in range(2))
@@ -460,9 +457,9 @@
 
 def first_solve_kernel(
     props_ref, xe_ref, xo_ref, ye_ref, yo_ref, ce_ref, co_ref,
-    own_ref, own_side_ref, rhs_ref, roots_ref, roots_side_ref, beyond_ref,
+    own_ref, own_side_ref, rhs_ref, roots_ref, roots_side_ref,
     rest_ref, rest_side_ref, solved_ref, rims_ref, even_ref, odd_ref,
-    corner_roots_ref, corner_beyond_ref, *buffers,
+    corner_roots_ref, *buffers,
 ):
     rows = own_ref.shape[1]
     wide = rows + 2 * MARGIN
@@ -470,17 +467,14 @@
     roots, _ = root_tables(props_ref)
     x_fields, x_wire = halo_x(xe_ref, xo_ref)
     row = sublane()
-    sides, beyond = unpack_wire(ce_ref, co_ref, 5, 8)
+    sides = unpack_wire(ce_ref, co_ref, 5, 8)
     sides = expand_wire(sides, row)
     corner_stores = [unpack_fields(ce_ref, co_ref, 5, i) for i in range(5)]
     corner_stores = [expand([stores[k] for stores in corner_stores], row) for k in range(4)]
-    own_sides, _ = unpack_wire(ye_ref, yo_ref, rows, rows)
+    own_sides = unpack_wire(ye_ref, yo_ref, rows, rows)
     for g in range(2):
         for j, value in enumerate(sides):
             corner_roots_ref[g, j] = lookup(roots[g], value)
-        for tile, ends in enumerate(beyond):
-            for end in range(2):
-                corner_beyond_ref[g, end, tile] = lookup(roots[g], ends[end])
     for i in list(range(RIM)) + list(range(wide - RIM, wide)):
         j, x = i + 1, i - MARGIN
         own_row = 0 <= x < rows
@@ -494,11 +488,7 @@
                     return roots_side_ref[g, j - RIM]
                 return corner_roots_ref[g, j if j < RIM else j - rows]
 
-            if own_row:
-                lines = beyond_lines(beyond_ref, g, x)
-            else:
-                lines = beyond_lines(corner_beyond_ref, g, 0 if j < RIM else 1)
-            sums.append((diagonal(tiles, (j, *lines), spot), tiles(j, 0), tiles(j, 1)))
+            sums.append((diagonal(tiles, (j, 0.0, 0.0), spot), tiles(j, 0), tiles(j, 1)))
         corner = i if i < MARGIN else i - rows
         if not own_row:
             stores = [x_fields[k][corner] for k in range(4)]
@@ -821,18 +811,18 @@
         inside=pltpu.HBM,
     )(*(pltpu.with_memory_space_constraint(x, pltpu.HBM) for x in (soil_props, storage, soil_ids, bc_mask.T)))
     xe, xo = exchange("gx", x_even, x_odd)
-    slab = y_slab(rows, rows, rows)
+    slab = y_slab(rows, rows)
     fields, wire, y_even, y_odd = call(own_pack_kernel, [(4, *own), own, slab, slab], name="own_pack")(*raw)
     ye, yo = exchange("gy", y_even, y_odd)
-    slab = y_slab(5, 8, 2)
+    slab = y_slab(5, 8)
     weight = pl.CostEstimate(flops=10**11, bytes_accessed=10**9, transcendentals=0)
-    even, odd = call(corner_pack_kernel, [slab, slab], [(2, *TILE)], name="corner_pack", cost=weight)(xe, xo)
+    even, odd = call(corner_pack_kernel, [slab, slab], name="corner_pack", cost=weight)(soil_props, xe, xo)
     ce, co = exchange("gy", even, odd)
     count = wide // SUB
-    own_coeff, own_side, image, scales, rhs, roots, roots_side, beyond = call(
+    own_coeff, own_side, image, scales, rhs, roots, roots_side = call(
         own_coefficients_kernel,
         [(4, *own), (4, rows - 2, *TILE), (4, *own), (5, *own), (2, *own)]
-        + [(2, rows + 2 * RIM, *TILE), (2, *own), (2, 2, -(-rows // SUB), *TILE)],
+        + [(2, rows + 2 * RIM, *TILE), (2, *own)],
         name="own_coefficients",
     )(soil_props, fields, wire, xe, xo, ye, yo, adjoint_source)
     buffers = [(wide + 2, 2, *TILE)] * 4
@@ -841,9 +831,9 @@
     rest, rest_side, solved, edges, even, odd = call(
         first_solve_kernel,
         [(4, 2 * MARGIN, *TILE), (4, 2 * RIM, *TILE)] + solved_shapes,
-        [(2, 2 * RIM, *TILE), (2, 2, 1, *TILE)] + buffers,
+        [(2, 2 * RIM, *TILE)] + buffers,
         name="first_solve",
-    )(soil_props, xe, xo, ye, yo, ce, co, own_coeff, own_side, rhs, roots, roots_side, beyond)
+    )(soil_props, xe, xo, ye, yo, ce, co, own_coeff, own_side, rhs, roots, roots_side)
     coeffs = (own_coeff, own_side, rest, rest_side)
 
     slab = (2 * (MARGIN + 2), *TILE)

time: 48.8 us -> 48.8 us (level)
  no operation moved by 1% of the time
where the time goes in v9:
time: 48.8 us; the launch traced here: 48.6 us
  starting transfers between devices  18.7 us (38%)
  waiting for transfers between devices  11.6 us (24%)
  blocking collectives  11.6 us (24%)
  Pallas kernels  5.94 us (12%)
  between operations  0.73 us (1%)
    all_to_all x1, blocking collectives, shards(): gram = lax.all_to_all(gram, ('gx', 'gy'), 0, 0, tiled=True)  11.6 us
    ppermute x7, starting transfers between devices, exchange(): lax.ppermute(odd, ('gx', 'gy'), others)  10.8 us
    ppermute x7, starting transfers between devices, exchange(): lax.ppermute(even, axis, pairs)  7.89 us
    ppermute x7, waiting for transfers between devices, exchange(): lax.ppermute(odd, ('gx', 'gy'), others)  7 us
    pallas_call x11, Pallas kernels, run(): pl.pallas_call(kernel, out_shape=[jax.ShapeDtypeStruct(*(spec if isinstan...  5.94 us
    ppermute x7, waiting for transfers between devices, exchange(): lax.ppermute(even, axis, pairs)  4.61 us
  transfers between devices with their start and end apart: 14, of which 6 were waited for; matrix products, arithmetic and copies ran while one was open for 0% of the time, Pallas kernels for 2%

profile of v9, /device:TPU:0, one launch (start us, length us, event | category | flops | bytes accessed | tf_op | source)
XLA Modules:
  0.0 48.6 jit_solution(844544862232740326)
XLA Ops:
  0.6 1.2 %first_pack.1 = (f32[3,16]{1,0:T(4,128)S(1)}, f32[4,16,8,128]{3,2,1,0:T(8,128)S(1)}, s32[16,8,128]{2,1,0:T(8,128)S(1)}, s32[8,16]{1,0:T(8,128)S(1)}, f32[20,8,12...) custom-call(f32[3,16]{1,0:T(4,128)} %props_ref.5, f32[4,16,8,128]{3,2,1,0:T(8,128)} %storage_hbm.1, s32[16,8,128]{2,1,0:T(8,128)} %ids_hbm.1, ...), custom_call_target="tpu_custom_call" | custom-call | tf_op jit(solution)/shard_map/first_pack/pallas_call | solution.py:765
  1.8 3.0 %collective-permute-start = (f32[20,8,128]{2,1,0:T(8,128)S(1)}, f32[20,8,128]{2,1,0:T(8,128)S(1)}, u32[]{:S(2)}, u32[]{:S(2)}) collective-permute-start(f32[20,8,128]{2,1,0:T(8,128)S(1)} %get-tuple-element.51), channel_id=1, source_target_pairs={{0,8},{8,0},{16,24},{24,16},{1,9},{9,1},{17,25},{25,17},{2,10},{10... | collective-permute-start | bytes 245768 | tf_op jit(solution)/shard_map/ppermute | solution.py:795
  4.8 0.0 collective-permute-start.1
  4.8 0.2 own_pack.1
  5.0 0.0 copy-start.1
  5.0 0.6 %collective-permute-start.2 = (f32[40,8,128]{2,1,0:T(8,128)S(1)}, f32[40,8,128]{2,1,0:T(8,128)S(1)}, u32[]{:S(2)}, u32[]{:S(2)}) collective-permute-start(f32[40,8,128]{2,1,0:T(8,128)S(1)} %get-tuple-element.57), channel_id=1, source_target_pairs={{0,1},{1,0},{2,3},{3,2},{4,5},{5,4},{6,7},{7,6},{8,9},{9,8},{10,11... | collective-permute-start | bytes 491528 | tf_op jit(solution)/shard_map/ppermute | solution.py:795
  5.6 1.1 %collective-permute-start.3 = (f32[40,8,128]{2,1,0:T(8,128)S(1)}, f32[40,8,128]{2,1,0:T(8,128)S(1)}, u32[]{:S(2)}, u32[]{:S(2)}) collective-permute-start(f32[40,8,128]{2,1,0:T(8,128)S(1)} %get-tuple-element.58), channel_id=1, source_target_pairs={{0,16},{1,2},{2,1},{3,4},{4,3},{5,6},{6,5},{7,23},{8,24},{9,10},{1... | collective-permute-start | bytes 491528 | tf_op jit(solution)/shard_map/ppermute | solution.py:795
  6.7 0.5 %collective-permute-done.xe_ref = f32[20,8,128]{2,1,0:T(8,128)S(1)} collective-permute-done((f32[20,8,128]{2,1,0:T(8,128)S(1)}, f32[20,8,128]{2,1,0:T(8,128)S(1)}, u32[]{:S(2)}, u32[]{:S(2)}) %collective-permute-start) | collective-permute-done | bytes 81952 | tf_op jit(solution)/shard_map/ppermute | solution.py:795
  7.3 0.0 collective-permute-done.1.xo_ref
  7.3 0.1 corner_pack.1
  7.4 0.1 collective-permute-start.4
  7.5 4.5 %collective-permute-start.5 = (f32[14,8,128]{2,1,0:T(8,128)S(1)}, f32[14,8,128]{2,1,0:T(8,128)S(1)}, u32[]{:S(2)}, u32[]{:S(2)}) collective-permute-start(f32[14,8,128]{2,1,0:T(8,128)S(1)} %get-tuple-element.60), channel_id=1, source_target_pairs={{0,16},{1,2},{2,1},{3,4},{4,3},{5,6},{6,5},{7,23},{8,24},{9,10},{1... | collective-permute-start | bytes 172040 | tf_op jit(solution)/shard_map/ppermute | solution.py:795
  12.0 0.6 %own_coefficients.1 = (f32[4,16,8,128]{3,2,1,0:T(8,128)S(1)}, f32[4,14,8,128]{3,2,1,0:T(8,128)S(1)}, f32[4,16,8,128]{3,2,1,0:T(8,128)S(1)}, f32[5,16,8,128]{3,2,...) custom-call(f32[3,16]{1,0:T(4,128)S(1)} %copy-done.1, ...), custom_call_target="tpu_custom_call" | custom-call | tf_op jit(solution)/shard_map/own_coefficients/pallas_call | solution.py:765
  12.6 1.5 %collective-permute-done.5.co_ref = f32[14,8,128]{2,1,0:T(8,128)S(1)} collective-permute-done((f32[14,8,128]{2,1,0:T(8,128)S(1)}, f32[14,8,128]{2,1,0:T(8,128)S(1)}, u32[]{:S(2)}, u32[]{:S(2)}) %collective-permute-start.5) | collective-permute-done | bytes 57376 | tf_op jit(solution)/shard_map/ppermute | solution.py:795
  14.2 1.2 %first_solve.1 = (f32[4,8,8,128]{3,2,1,0:T(8,128)S(1)}, f32[4,10,8,128]{3,2,1,0:T(8,128)S(1)}, f32[2,24,8,128]{3,2,1,0:T(8,128)S(1)}, f32[4,3,8,128]{3,2,1,0:T(8...) custom-call(f32[3,16]{1,0:T(4,128)S(1)} %copy-done.1, f32[20,8,128]{2,1,0:T(8,128)S(1)} %collective-permute-done.xe_ref, ...), custom_call_target="tpu_custom_call" | custom-call | tf_op jit(solution)/shard_map/first_solve/pallas_call | solution.py:765
  15.4 0.1 collective-permute-start.6
  15.5 2.1 %collective-permute-start.7 = (f32[27,8,128]{2,1,0:T(8,128)S(1)}, f32[27,8,128]{2,1,0:T(8,128)S(1)}, u32[]{:S(2)}, u32[]{:S(2)}) collective-permute-start(f32[27,8,128]{2,1,0:T(8,128)S(1)} %get-tuple-element.71), channel_id=1, source_target_pairs={{0,16},{1,2},{2,1},{3,4},{4,3},{5,6},{6,5},{7,23},{8,24},{9,10},{1... | collective-permute-start | bytes 331784 | tf_op jit(solution)/shard_map/ppermute | solution.py:795
  17.6 2.7 %collective-permute-done.7.yo_ref = f32[27,8,128]{2,1,0:T(8,128)S(1)} collective-permute-done((f32[27,8,128]{2,1,0:T(8,128)S(1)}, f32[27,8,128]{2,1,0:T(8,128)S(1)}, u32[]{:S(2)}, u32[]{:S(2)}) %collective-permute-start.7) | collective-permute-done | bytes 110624 | tf_op jit(solution)/shard_map/ppermute | solution.py:795
  20.3 0.1 fold_y.2
  20.4 2.0 %collective-permute-start.8 = (f32[12,8,128]{2,1,0:T(8,128)S(1)}, f32[12,8,128]{2,1,0:T(8,128)S(1)}, u32[]{:S(2)}, u32[]{:S(2)}) collective-permute-start(f32[12,8,128]{2,1,0:T(8,128)S(1)} %get-tuple-element.74), channel_id=1, source_target_pairs={{0,8},{8,0},{16,24},{24,16},{1,9},{9,1},{17,25},{25,17},{2,10},{10... | collective-permute-start | bytes 147464 | tf_op jit(solution)/shard_map/ppermute | solution.py:795
  22.4 2.1 %collective-permute-done.8.xe_ref = f32[12,8,128]{2,1,0:T(8,128)S(1)} collective-permute-done((f32[12,8,128]{2,1,0:T(8,128)S(1)}, f32[12,8,128]{2,1,0:T(8,128)S(1)}, u32[]{:S(2)}, u32[]{:S(2)}) %collective-permute-start.8) | collective-permute-done | bytes 49184 | tf_op jit(solution)/shard_map/ppermute | solution.py:795
  24.6 1.1 %second_solve.1 = (f32[2,16,8,128]{3,2,1,0:T(8,128)S(1)}, f32[18,8,128]{2,1,0:T(8,128)S(1)}, f32[18,8,128]{2,1,0:T(8,128)S(1)}, f32[2,24,8,128]{3,2,1,0:T(8,128)...) custom-call(f32[2,24,8,128]{3,2,1,0:T(8,128)S(1)} %get-tuple-element.72.summed_ref, ...), custom_call_target="tpu_custom_call" | custom-call | tf_op jit(solution)/shard_map/second_solve/pallas_call | solution.py:765
  25.7 0.1 collective-permute-start.10
  25.7 3.1 %collective-permute-start.11 = (f32[27,8,128]{2,1,0:T(8,128)S(1)}, f32[27,8,128]{2,1,0:T(8,128)S(1)}, u32[]{:S(2)}, u32[]{:S(2)}) collective-permute-start(f32[27,8,128]{2,1,0:T(8,128)S(1)} %get-tuple-element.83), channel_id=1, source_target_pairs={{0,16},{1,2},{2,1},{3,4},{4,3},{5,6},{6,5},{7,23},{8,24},{9,10},{1... | collective-permute-start | bytes 331784 | tf_op jit(solution)/shard_map/ppermute | solution.py:795
  28.8 2.7 %collective-permute-done.11.yo_ref = f32[27,8,128]{2,1,0:T(8,128)S(1)} collective-permute-done((f32[27,8,128]{2,1,0:T(8,128)S(1)}, f32[27,8,128]{2,1,0:T(8,128)S(1)}, u32[]{:S(2)}, u32[]{:S(2)}) %collective-permute-start.11) | collective-permute-done | bytes 110624 | tf_op jit(solution)/shard_map/ppermute | solution.py:795
  31.5 0.1 fold_y.3
  31.6 2.0 %collective-permute-start.12 = (f32[12,8,128]{2,1,0:T(8,128)S(1)}, f32[12,8,128]{2,1,0:T(8,128)S(1)}, u32[]{:S(2)}, u32[]{:S(2)}) collective-permute-start(f32[12,8,128]{2,1,0:T(8,128)S(1)} %get-tuple-element.86), channel_id=1, source_target_pairs={{0,8},{8,0},{16,24},{24,16},{1,9},{9,1},{17,25},{25,17},{2,10},{10... | collective-permute-start | bytes 147464 | tf_op jit(solution)/shard_map/ppermute | solution.py:795
  33.6 0.2 first_power.1
  33.8 2.0 %collective-permute-done.12.xe_ref = f32[12,8,128]{2,1,0:T(8,128)S(1)} collective-permute-done((f32[12,8,128]{2,1,0:T(8,128)S(1)}, f32[12,8,128]{2,1,0:T(8,128)S(1)}, u32[]{:S(2)}, u32[]{:S(2)}) %collective-permute-start.12) | collective-permute-done | bytes 49184 | tf_op jit(solution)/shard_map/ppermute | solution.py:795
  35.8 0.3 last_image.1
  36.0 11.6 %all_to_all.11 = f32[32,1,128]{2,1,0:T(1,128)S(1)} all-to-all(f32[32,1,128]{2,1,0:T(1,128)S(1)} %bitcast.6), channel_id=1, replica_groups=mesh['gx'=4,'gy'=8] {'gx','gy'}, dimensions={0} | all-to-all | bytes 32768 | tf_op jit(solution)/shard_map/all_to_all | solution.py:861
  47.7 1.0 %combine.1 = (f32[2,16,8,128]{3,2,1,0:T(8,128)}, f32[2,16,8,128]{3,2,1,0:T(8,128)}, f32[2,16,8,128]{3,2,1,0:T(8,128)}) custom-call(f32[32,128]{1,0:T(8,128)S(1)} %bitcast.5, f32[2,16,8,128]{3,2,1,0:T(8,128)S(1)} %copy-done, f32[2,16,8,128]{3,2,1,0:T(8,128)S(1)} %get-tuple-element.91.power_ref, f32[2,16,8,128]{3,2,1,0:T(8,128)S(1)} %get-tuple-element.96.second_ref, ...), custom_call_target="tpu_custom_call" | custom-call | tf_op jit(solution)/shard_map/combine/pallas_call | solution.py:765
  (12 shorter events, 0.0 us)
Async XLA Ops:
  1.8 5.4 %collective-permute-start = (f32[20,8,128]{2,1,0:T(8,128)S(1)}, f32[20,8,128]{2,1,0:T(8,128)S(1)}, u32[]{:S(2)}, u32[]{:S(2)}) collective-permute-start(f32[20,8,128]{2,1,0:T(8,128)S(1)} %get-tuple-element.51), channel_id=1, source_target_pairs={{0,8},{8,0},{16,24},{24,16},{1,9},{9,1},{17,25},{25,17},{2,10},{10... | collective-permute-start | bytes 245768 | tf_op jit(solution)/shard_map/ppermute | solution.py:795
  4.8 2.4 %collective-permute-start.1 = (f32[20,8,128]{2,1,0:T(8,128)S(1)}, f32[20,8,128]{2,1,0:T(8,128)S(1)}, u32[]{:S(2)}, u32[]{:S(2)}) collective-permute-start(f32[20,8,128]{2,1,0:T(8,128)S(1)} %get-tuple-element.52), channel_id=1, source_target_pairs={{0,1},{1,0},{2,3},{3,2},{4,5},{5,4},{6,7},{7,6},{8,16},{9,17},{10,... | collective-permute-start | bytes 245768 | tf_op jit(solution)/shard_map/ppermute | solution.py:795
  5.0 2.2 %copy-start.1 = (f32[3,16]{1,0:T(4,128)S(1)}, f32[3,16]{1,0:T(4,128)}, u32[]{:S(2)}) copy-start(f32[3,16]{1,0:T(4,128)} %props_ref.5) | copy-start | bytes 580
  5.0 7.0 %collective-permute-start.2 = (f32[40,8,128]{2,1,0:T(8,128)S(1)}, f32[40,8,128]{2,1,0:T(8,128)S(1)}, u32[]{:S(2)}, u32[]{:S(2)}) collective-permute-start(f32[40,8,128]{2,1,0:T(8,128)S(1)} %get-tuple-element.57), channel_id=1, source_target_pairs={{0,1},{1,0},{2,3},{3,2},{4,5},{5,4},{6,7},{7,6},{8,9},{9,8},{10,11... | collective-permute-start | bytes 491528 | tf_op jit(solution)/shard_map/ppermute | solution.py:795
  5.6 6.4 %copy-start = (f32[2,16,8,128]{3,2,1,0:T(8,128)S(1)}, f32[2,16,8,128]{3,2,1,0:T(8,128)}, u32[]{:S(2)}) copy-start(f32[2,16,8,128]{3,2,1,0:T(8,128)} %source_ref.9) | copy-start | bytes 393220
  5.6 6.4 %collective-permute-start.3 = (f32[40,8,128]{2,1,0:T(8,128)S(1)}, f32[40,8,128]{2,1,0:T(8,128)S(1)}, u32[]{:S(2)}, u32[]{:S(2)}) collective-permute-start(f32[40,8,128]{2,1,0:T(8,128)S(1)} %get-tuple-element.58), channel_id=1, source_target_pairs={{0,16},{1,2},{2,1},{3,4},{4,3},{5,6},{6,5},{7,23},{8,24},{9,10},{1... | collective-permute-start | bytes 491528 | tf_op jit(solution)/shard_map/ppermute | solution.py:795
  7.4 5.3 %collective-permute-start.4 = (f32[14,8,128]{2,1,0:T(8,128)S(1)}, f32[14,8,128]{2,1,0:T(8,128)S(1)}, u32[]{:S(2)}, u32[]{:S(2)}) collective-permute-start(f32[14,8,128]{2,1,0:T(8,128)S(1)} %get-tuple-element.59), channel_id=1, source_target_pairs={{0,1},{1,0},{2,3},{3,2},{4,5},{5,4},{6,7},{7,6},{8,9},{9,8},{10,11... | collective-permute-start | bytes 172040 | tf_op jit(solution)/shard_map/ppermute | solution.py:795
  7.5 6.7 %collective-permute-start.5 = (f32[14,8,128]{2,1,0:T(8,128)S(1)}, f32[14,8,128]{2,1,0:T(8,128)S(1)}, u32[]{:S(2)}, u32[]{:S(2)}) collective-permute-start(f32[14,8,128]{2,1,0:T(8,128)S(1)} %get-tuple-element.60), channel_id=1, source_target_pairs={{0,16},{1,2},{2,1},{3,4},{4,3},{5,6},{6,5},{7,23},{8,24},{9,10},{1... | collective-permute-start | bytes 172040 | tf_op jit(solution)/shard_map/ppermute | solution.py:795
  15.4 2.2 %collective-permute-start.6 = (f32[27,8,128]{2,1,0:T(8,128)S(1)}, f32[27,8,128]{2,1,0:T(8,128)S(1)}, u32[]{:S(2)}, u32[]{:S(2)}) collective-permute-start(f32[27,8,128]{2,1,0:T(8,128)S(1)} %get-tuple-element.70), channel_id=1, source_target_pairs={{0,1},{1,0},{2,3},{3,2},{4,5},{5,4},{6,7},{7,6},{8,9},{9,8},{10,11... | collective-permute-start | bytes 331784 | tf_op jit(solution)/shard_map/ppermute | solution.py:795
  15.5 4.8 %collective-permute-start.7 = (f32[27,8,128]{2,1,0:T(8,128)S(1)}, f32[27,8,128]{2,1,0:T(8,128)S(1)}, u32[]{:S(2)}, u32[]{:S(2)}) collective-permute-start(f32[27,8,128]{2,1,0:T(8,128)S(1)} %get-tuple-element.71), channel_id=1, source_target_pairs={{0,16},{1,2},{2,1},{3,4},{4,3},{5,6},{6,5},{7,23},{8,24},{9,10},{1... | collective-permute-start | bytes 331784 | tf_op jit(solution)/shard_map/ppermute | solution.py:795
  20.4 4.2 %collective-permute-start.8 = (f32[12,8,128]{2,1,0:T(8,128)S(1)}, f32[12,8,128]{2,1,0:T(8,128)S(1)}, u32[]{:S(2)}, u32[]{:S(2)}) collective-permute-start(f32[12,8,128]{2,1,0:T(8,128)S(1)} %get-tuple-element.74), channel_id=1, source_target_pairs={{0,8},{8,0},{16,24},{24,16},{1,9},{9,1},{17,25},{25,17},{2,10},{10... | collective-permute-start | bytes 147464 | tf_op jit(solution)/shard_map/ppermute | solution.py:795
  22.4 2.1 %collective-permute-start.9 = (f32[12,8,128]{2,1,0:T(8,128)S(1)}, f32[12,8,128]{2,1,0:T(8,128)S(1)}, u32[]{:S(2)}, u32[]{:S(2)}) collective-permute-start(f32[12,8,128]{2,1,0:T(8,128)S(1)} %get-tuple-element.75), channel_id=1, source_target_pairs={{0,1},{1,0},{2,3},{3,2},{4,5},{5,4},{6,7},{7,6},{8,16},{9,17},{10,... | collective-permute-start | bytes 147464 | tf_op jit(solution)/shard_map/ppermute | solution.py:795
  25.7 3.1 %collective-permute-start.10 = (f32[27,8,128]{2,1,0:T(8,128)S(1)}, f32[27,8,128]{2,1,0:T(8,128)S(1)}, u32[]{:S(2)}, u32[]{:S(2)}) collective-permute-start(f32[27,8,128]{2,1,0:T(8,128)S(1)} %get-tuple-element.82), channel_id=1, source_target_pairs={{0,1},{1,0},{2,3},{3,2},{4,5},{5,4},{6,7},{7,6},{8,9},{9,8},{10,11... | collective-permute-start | bytes 331784 | tf_op jit(solution)/shard_map/ppermute | solution.py:795
  25.7 5.8 %collective-permute-start.11 = (f32[27,8,128]{2,1,0:T(8,128)S(1)}, f32[27,8,128]{2,1,0:T(8,128)S(1)}, u32[]{:S(2)}, u32[]{:S(2)}) collective-permute-start(f32[27,8,128]{2,1,0:T(8,128)S(1)} %get-tuple-element.83), channel_id=1, source_target_pairs={{0,16},{1,2},{2,1},{3,4},{4,3},{5,6},{6,5},{7,23},{8,24},{9,10},{1... | collective-permute-start | bytes 331784 | tf_op jit(solution)/shard_map/ppermute | solution.py:795
  31.6 4.2 %collective-permute-start.12 = (f32[12,8,128]{2,1,0:T(8,128)S(1)}, f32[12,8,128]{2,1,0:T(8,128)S(1)}, u32[]{:S(2)}, u32[]{:S(2)}) collective-permute-start(f32[12,8,128]{2,1,0:T(8,128)S(1)} %get-tuple-element.86), channel_id=1, source_target_pairs={{0,8},{8,0},{16,24},{24,16},{1,9},{9,1},{17,25},{25,17},{2,10},{10... | collective-permute-start | bytes 147464 | tf_op jit(solution)/shard_map/ppermute | solution.py:795
  33.6 2.1 %collective-permute-start.13 = (f32[12,8,128]{2,1,0:T(8,128)S(1)}, f32[12,8,128]{2,1,0:T(8,128)S(1)}, u32[]{:S(2)}, u32[]{:S(2)}) collective-permute-start(f32[12,8,128]{2,1,0:T(8,128)S(1)} %get-tuple-element.87), channel_id=1, source_target_pairs={{0,1},{1,0},{2,3},{3,2},{4,5},{5,4},{6,7},{7,6},{8,16},{9,17},{10,... | collective-permute-start | bytes 147464 | tf_op jit(solution)/shard_map/ppermute | solution.py:795

commit v10 on v9

--- a/solution.py
+++ b/solution.py
@@ -745,15 +745,17 @@
     r0, r1, r2 = wide(f0 / beta + f1 * a + f2 * v0), wide(f1 * b + f2 * v1), wide(f2 * v2)
     s0, s1, s2 = wide(scale * v0), wide(scale * v1), wide(scale * v2)
     copies = []
-    for k in range(2):
-        for x in range(source_ref.shape[1]):
+    half = source_ref.shape[1] // 2
+    for k, part in ((0, 0), (0, 1), (1, 0), (1, 1)):
+        for x in range(part * half, part * half + half):
             source, power, second = source_ref[k, x], power_ref[k, x], second_ref[k, x]
             adjoint_ref[k, x] = z_one * one_ref[k, x] + z_two * two_ref[k, x]
             residual_ref[k, x] = r0 * source + r1 * power + r2 * second
             basis_ref[k, x] = s0 * source + s1 * power + s2 * second
         pairs = ((adjoint_ref, adjoint_hbm), (residual_ref, residual_hbm), (basis_ref, basis_hbm))
         for index, (src, dst) in enumerate(pairs):
-            copy = pltpu.make_async_copy(src.at[k], dst.at[k], sems.at[k, index])
+            spots = (k, pl.ds(part * half, half))
+            copy = pltpu.make_async_copy(src.at[spots], dst.at[spots], sems.at[2 * k + part, index])
             copy.start()
             copies.append(copy)
     for copy in copies:
@@ -863,7 +865,7 @@
         call(
             functools.partial(combine_kernel, scale=math.sqrt(cells)),
             [(2, *own)] * 3,
-            [(2, *own)] * 3 + [pltpu.SemaphoreType.DMA((2, 3))],
+            [(2, *own)] * 3 + [pltpu.SemaphoreType.DMA((4, 3))],
             name="combine",
             outside=pltpu.HBM,
         )(gram, adjoint_source, power, second, one, two)

time: 48.8 us -> 48.8 us (level)
  no operation moved by 1% of the time
where the time goes in v10:
time: 48.8 us; the launch traced here: 48.7 us
  starting transfers between devices  18.7 us (38%)
  waiting for transfers between devices  11.6 us (24%)
  blocking collectives  11.6 us (24%)
  Pallas kernels  5.98 us (12%)
  between operations  0.73 us (1%)
    all_to_all x1, blocking collectives, shards(): gram = lax.all_to_all(gram, ('gx', 'gy'), 0, 0, tiled=True)  11.6 us
    ppermute x7, starting transfers between devices, exchange(): lax.ppermute(odd, ('gx', 'gy'), others)  10.8 us
    ppermute x7, starting transfers between devices, exchange(): lax.ppermute(even, axis, pairs)  7.89 us
    ppermute x7, waiting for transfers between devices, exchange(): lax.ppermute(odd, ('gx', 'gy'), others)  7 us
    pallas_call x11, Pallas kernels, run(): pl.pallas_call(kernel, out_shape=[jax.ShapeDtypeStruct(*(spec if isinstan...  5.98 us
    ppermute x7, waiting for transfers between devices, exchange(): lax.ppermute(even, axis, pairs)  4.61 us
  transfers between devices with their start and end apart: 14, of which 6 were waited for; matrix products, arithmetic and copies ran while one was open for 0% of the time, Pallas kernels for 2%

profile of v10, /device:TPU:0, one launch (start us, length us, event | category | flops | bytes accessed | tf_op | source)
XLA Modules:
  0.0 48.7 jit_solution(659024947798605821)
XLA Ops:
  0.6 1.2 %first_pack.1 = (f32[3,16]{1,0:T(4,128)S(1)}, f32[4,16,8,128]{3,2,1,0:T(8,128)S(1)}, s32[16,8,128]{2,1,0:T(8,128)S(1)}, s32[8,16]{1,0:T(8,128)S(1)}, f32[20,8,12...) custom-call(f32[3,16]{1,0:T(4,128)} %props_ref.5, f32[4,16,8,128]{3,2,1,0:T(8,128)} %storage_hbm.1, s32[16,8,128]{2,1,0:T(8,128)} %ids_hbm.1, ...), custom_call_target="tpu_custom_call" | custom-call | tf_op jit(solution)/shard_map/first_pack/pallas_call | solution.py:767
  1.8 3.0 %collective-permute-start = (f32[20,8,128]{2,1,0:T(8,128)S(1)}, f32[20,8,128]{2,1,0:T(8,128)S(1)}, u32[]{:S(2)}, u32[]{:S(2)}) collective-permute-start(f32[20,8,128]{2,1,0:T(8,128)S(1)} %get-tuple-element.51), channel_id=1, source_target_pairs={{0,8},{8,0},{16,24},{24,16},{1,9},{9,1},{17,25},{25,17},{2,10},{10... | collective-permute-start | bytes 245768 | tf_op jit(solution)/shard_map/ppermute | solution.py:797
  4.8 0.0 collective-permute-start.1
  4.8 0.2 own_pack.1
  5.0 0.0 copy-start.1
  5.0 0.6 %collective-permute-start.2 = (f32[40,8,128]{2,1,0:T(8,128)S(1)}, f32[40,8,128]{2,1,0:T(8,128)S(1)}, u32[]{:S(2)}, u32[]{:S(2)}) collective-permute-start(f32[40,8,128]{2,1,0:T(8,128)S(1)} %get-tuple-element.57), channel_id=1, source_target_pairs={{0,1},{1,0},{2,3},{3,2},{4,5},{5,4},{6,7},{7,6},{8,9},{9,8},{10,11... | collective-permute-start | bytes 491528 | tf_op jit(solution)/shard_map/ppermute | solution.py:797
  5.6 1.1 %collective-permute-start.3 = (f32[40,8,128]{2,1,0:T(8,128)S(1)}, f32[40,8,128]{2,1,0:T(8,128)S(1)}, u32[]{:S(2)}, u32[]{:S(2)}) collective-permute-start(f32[40,8,128]{2,1,0:T(8,128)S(1)} %get-tuple-element.58), channel_id=1, source_target_pairs={{0,16},{1,2},{2,1},{3,4},{4,3},{5,6},{6,5},{7,23},{8,24},{9,10},{1... | collective-permute-start | bytes 491528 | tf_op jit(solution)/shard_map/ppermute | solution.py:797
  6.7 0.5 %collective-permute-done.xe_ref = f32[20,8,128]{2,1,0:T(8,128)S(1)} collective-permute-done((f32[20,8,128]{2,1,0:T(8,128)S(1)}, f32[20,8,128]{2,1,0:T(8,128)S(1)}, u32[]{:S(2)}, u32[]{:S(2)}) %collective-permute-start) | collective-permute-done | bytes 81952 | tf_op jit(solution)/shard_map/ppermute | solution.py:797
  7.3 0.0 collective-permute-done.1.xo_ref
  7.3 0.1 corner_pack.1
  7.4 0.1 collective-permute-start.4
  7.5 4.5 %collective-permute-start.5 = (f32[14,8,128]{2,1,0:T(8,128)S(1)}, f32[14,8,128]{2,1,0:T(8,128)S(1)}, u32[]{:S(2)}, u32[]{:S(2)}) collective-permute-start(f32[14,8,128]{2,1,0:T(8,128)S(1)} %get-tuple-element.60), channel_id=1, source_target_pairs={{0,16},{1,2},{2,1},{3,4},{4,3},{5,6},{6,5},{7,23},{8,24},{9,10},{1... | collective-permute-start | bytes 172040 | tf_op jit(solution)/shard_map/ppermute | solution.py:797
  12.0 0.6 %own_coefficients.1 = (f32[4,16,8,128]{3,2,1,0:T(8,128)S(1)}, f32[4,14,8,128]{3,2,1,0:T(8,128)S(1)}, f32[4,16,8,128]{3,2,1,0:T(8,128)S(1)}, f32[5,16,8,128]{3,2,...) custom-call(f32[3,16]{1,0:T(4,128)S(1)} %copy-done.1, ...), custom_call_target="tpu_custom_call" | custom-call | tf_op jit(solution)/shard_map/own_coefficients/pallas_call | solution.py:767
  12.6 1.5 %collective-permute-done.5.co_ref = f32[14,8,128]{2,1,0:T(8,128)S(1)} collective-permute-done((f32[14,8,128]{2,1,0:T(8,128)S(1)}, f32[14,8,128]{2,1,0:T(8,128)S(1)}, u32[]{:S(2)}, u32[]{:S(2)}) %collective-permute-start.5) | collective-permute-done | bytes 57376 | tf_op jit(solution)/shard_map/ppermute | solution.py:797
  14.2 1.2 %first_solve.1 = (f32[4,8,8,128]{3,2,1,0:T(8,128)S(1)}, f32[4,10,8,128]{3,2,1,0:T(8,128)S(1)}, f32[2,24,8,128]{3,2,1,0:T(8,128)S(1)}, f32[4,3,8,128]{3,2,1,0:T(8...) custom-call(f32[3,16]{1,0:T(4,128)S(1)} %copy-done.1, f32[20,8,128]{2,1,0:T(8,128)S(1)} %collective-permute-done.xe_ref, ...), custom_call_target="tpu_custom_call" | custom-call | tf_op jit(solution)/shard_map/first_solve/pallas_call | solution.py:767
  15.4 0.1 collective-permute-start.6
  15.5 2.1 %collective-permute-start.7 = (f32[27,8,128]{2,1,0:T(8,128)S(1)}, f32[27,8,128]{2,1,0:T(8,128)S(1)}, u32[]{:S(2)}, u32[]{:S(2)}) collective-permute-start(f32[27,8,128]{2,1,0:T(8,128)S(1)} %get-tuple-element.71), channel_id=1, source_target_pairs={{0,16},{1,2},{2,1},{3,4},{4,3},{5,6},{6,5},{7,23},{8,24},{9,10},{1... | collective-permute-start | bytes 331784 | tf_op jit(solution)/shard_map/ppermute | solution.py:797
  17.6 2.7 %collective-permute-done.7.yo_ref = f32[27,8,128]{2,1,0:T(8,128)S(1)} collective-permute-done((f32[27,8,128]{2,1,0:T(8,128)S(1)}, f32[27,8,128]{2,1,0:T(8,128)S(1)}, u32[]{:S(2)}, u32[]{:S(2)}) %collective-permute-start.7) | collective-permute-done | bytes 110624 | tf_op jit(solution)/shard_map/ppermute | solution.py:797
  20.3 0.1 fold_y.2
  20.4 2.0 %collective-permute-start.8 = (f32[12,8,128]{2,1,0:T(8,128)S(1)}, f32[12,8,128]{2,1,0:T(8,128)S(1)}, u32[]{:S(2)}, u32[]{:S(2)}) collective-permute-start(f32[12,8,128]{2,1,0:T(8,128)S(1)} %get-tuple-element.74), channel_id=1, source_target_pairs={{0,8},{8,0},{16,24},{24,16},{1,9},{9,1},{17,25},{25,17},{2,10},{10... | collective-permute-start | bytes 147464 | tf_op jit(solution)/shard_map/ppermute | solution.py:797
  22.4 2.1 %collective-permute-done.8.xe_ref = f32[12,8,128]{2,1,0:T(8,128)S(1)} collective-permute-done((f32[12,8,128]{2,1,0:T(8,128)S(1)}, f32[12,8,128]{2,1,0:T(8,128)S(1)}, u32[]{:S(2)}, u32[]{:S(2)}) %collective-permute-start.8) | collective-permute-done | bytes 49184 | tf_op jit(solution)/shard_map/ppermute | solution.py:797
  24.6 1.1 %second_solve.1 = (f32[2,16,8,128]{3,2,1,0:T(8,128)S(1)}, f32[18,8,128]{2,1,0:T(8,128)S(1)}, f32[18,8,128]{2,1,0:T(8,128)S(1)}, f32[2,24,8,128]{3,2,1,0:T(8,128)...) custom-call(f32[2,24,8,128]{3,2,1,0:T(8,128)S(1)} %get-tuple-element.72.summed_ref, ...), custom_call_target="tpu_custom_call" | custom-call | tf_op jit(solution)/shard_map/second_solve/pallas_call | solution.py:767
  25.7 0.1 collective-permute-start.10
  25.7 3.1 %collective-permute-start.11 = (f32[27,8,128]{2,1,0:T(8,128)S(1)}, f32[27,8,128]{2,1,0:T(8,128)S(1)}, u32[]{:S(2)}, u32[]{:S(2)}) collective-permute-start(f32[27,8,128]{2,1,0:T(8,128)S(1)} %get-tuple-element.83), channel_id=1, source_target_pairs={{0,16},{1,2},{2,1},{3,4},{4,3},{5,6},{6,5},{7,23},{8,24},{9,10},{1... | collective-permute-start | bytes 331784 | tf_op jit(solution)/shard_map/ppermute | solution.py:797
  28.8 2.7 %collective-permute-done.11.yo_ref = f32[27,8,128]{2,1,0:T(8,128)S(1)} collective-permute-done((f32[27,8,128]{2,1,0:T(8,128)S(1)}, f32[27,8,128]{2,1,0:T(8,128)S(1)}, u32[]{:S(2)}, u32[]{:S(2)}) %collective-permute-start.11) | collective-permute-done | bytes 110624 | tf_op jit(solution)/shard_map/ppermute | solution.py:797
  31.5 0.1 fold_y.3
  31.6 2.0 %collective-permute-start.12 = (f32[12,8,128]{2,1,0:T(8,128)S(1)}, f32[12,8,128]{2,1,0:T(8,128)S(1)}, u32[]{:S(2)}, u32[]{:S(2)}) collective-permute-start(f32[12,8,128]{2,1,0:T(8,128)S(1)} %get-tuple-element.86), channel_id=1, source_target_pairs={{0,8},{8,0},{16,24},{24,16},{1,9},{9,1},{17,25},{25,17},{2,10},{10... | collective-permute-start | bytes 147464 | tf_op jit(solution)/shard_map/ppermute | solution.py:797
  33.6 0.2 first_power.1
  33.8 2.0 %collective-permute-done.12.xe_ref = f32[12,8,128]{2,1,0:T(8,128)S(1)} collective-permute-done((f32[12,8,128]{2,1,0:T(8,128)S(1)}, f32[12,8,128]{2,1,0:T(8,128)S(1)}, u32[]{:S(2)}, u32[]{:S(2)}) %collective-permute-start.12) | collective-permute-done | bytes 49184 | tf_op jit(solution)/shard_map/ppermute | solution.py:797
  35.8 0.3 last_image.1
  36.0 11.6 %all_to_all.11 = f32[32,1,128]{2,1,0:T(1,128)S(1)} all-to-all(f32[32,1,128]{2,1,0:T(1,128)S(1)} %bitcast.6), channel_id=1, replica_groups=mesh['gx'=4,'gy'=8] {'gx','gy'}, dimensions={0} | all-to-all | bytes 32768 | tf_op jit(solution)/shard_map/all_to_all | solution.py:863
  47.7 1.0 %combine.1 = (f32[2,16,8,128]{3,2,1,0:T(8,128)}, f32[2,16,8,128]{3,2,1,0:T(8,128)}, f32[2,16,8,128]{3,2,1,0:T(8,128)}) custom-call(f32[32,128]{1,0:T(8,128)S(1)} %bitcast.5, f32[2,16,8,128]{3,2,1,0:T(8,128)S(1)} %copy-done, f32[2,16,8,128]{3,2,1,0:T(8,128)S(1)} %get-tuple-element.91.power_ref, f32[2,16,8,128]{3,2,1,0:T(8,128)S(1)} %get-tuple-element.96.second_ref, ...), custom_call_target="tpu_custom_call" | custom-call | tf_op jit(solution)/shard_map/combine/pallas_call | solution.py:767
  (12 shorter events, 0.0 us)
Async XLA Ops:
  1.8 5.4 %collective-permute-start = (f32[20,8,128]{2,1,0:T(8,128)S(1)}, f32[20,8,128]{2,1,0:T(8,128)S(1)}, u32[]{:S(2)}, u32[]{:S(2)}) collective-permute-start(f32[20,8,128]{2,1,0:T(8,128)S(1)} %get-tuple-element.51), channel_id=1, source_target_pairs={{0,8},{8,0},{16,24},{24,16},{1,9},{9,1},{17,25},{25,17},{2,10},{10... | collective-permute-start | bytes 245768 | tf_op jit(solution)/shard_map/ppermute | solution.py:797
  4.8 2.4 %collective-permute-start.1 = (f32[20,8,128]{2,1,0:T(8,128)S(1)}, f32[20,8,128]{2,1,0:T(8,128)S(1)}, u32[]{:S(2)}, u32[]{:S(2)}) collective-permute-start(f32[20,8,128]{2,1,0:T(8,128)S(1)} %get-tuple-element.52), channel_id=1, source_target_pairs={{0,1},{1,0},{2,3},{3,2},{4,5},{5,4},{6,7},{7,6},{8,16},{9,17},{10,... | collective-permute-start | bytes 245768 | tf_op jit(solution)/shard_map/ppermute | solution.py:797
  5.0 2.2 %copy-start.1 = (f32[3,16]{1,0:T(4,128)S(1)}, f32[3,16]{1,0:T(4,128)}, u32[]{:S(2)}) copy-start(f32[3,16]{1,0:T(4,128)} %props_ref.5) | copy-start | bytes 580
  5.0 7.0 %collective-permute-start.2 = (f32[40,8,128]{2,1,0:T(8,128)S(1)}, f32[40,8,128]{2,1,0:T(8,128)S(1)}, u32[]{:S(2)}, u32[]{:S(2)}) collective-permute-start(f32[40,8,128]{2,1,0:T(8,128)S(1)} %get-tuple-element.57), channel_id=1, source_target_pairs={{0,1},{1,0},{2,3},{3,2},{4,5},{5,4},{6,7},{7,6},{8,9},{9,8},{10,11... | collective-permute-start | bytes 491528 | tf_op jit(solution)/shard_map/ppermute | solution.py:797
  5.6 6.4 %copy-start = (f32[2,16,8,128]{3,2,1,0:T(8,128)S(1)}, f32[2,16,8,128]{3,2,1,0:T(8,128)}, u32[]{:S(2)}) copy-start(f32[2,16,8,128]{3,2,1,0:T(8,128)} %source_ref.9) | copy-start | bytes 393220
  5.6 6.4 %collective-permute-start.3 = (f32[40,8,128]{2,1,0:T(8,128)S(1)}, f32[40,8,128]{2,1,0:T(8,128)S(1)}, u32[]{:S(2)}, u32[]{:S(2)}) collective-permute-start(f32[40,8,128]{2,1,0:T(8,128)S(1)} %get-tuple-element.58), channel_id=1, source_target_pairs={{0,16},{1,2},{2,1},{3,4},{4,3},{5,6},{6,5},{7,23},{8,24},{9,10},{1... | collective-permute-start | bytes 491528 | tf_op jit(solution)/shard_map/ppermute | solution.py:797
  7.4 5.3 %collective-permute-start.4 = (f32[14,8,128]{2,1,0:T(8,128)S(1)}, f32[14,8,128]{2,1,0:T(8,128)S(1)}, u32[]{:S(2)}, u32[]{:S(2)}) collective-permute-start(f32[14,8,128]{2,1,0:T(8,128)S(1)} %get-tuple-element.59), channel_id=1, source_target_pairs={{0,1},{1,0},{2,3},{3,2},{4,5},{5,4},{6,7},{7,6},{8,9},{9,8},{10,11... | collective-permute-start | bytes 172040 | tf_op jit(solution)/shard_map/ppermute | solution.py:797
  7.5 6.7 %collective-permute-start.5 = (f32[14,8,128]{2,1,0:T(8,128)S(1)}, f32[14,8,128]{2,1,0:T(8,128)S(1)}, u32[]{:S(2)}, u32[]{:S(2)}) collective-permute-start(f32[14,8,128]{2,1,0:T(8,128)S(1)} %get-tuple-element.60), channel_id=1, source_target_pairs={{0,16},{1,2},{2,1},{3,4},{4,3},{5,6},{6,5},{7,23},{8,24},{9,10},{1... | collective-permute-start | bytes 172040 | tf_op jit(solution)/shard_map/ppermute | solution.py:797
  15.4 2.2 %collective-permute-start.6 = (f32[27,8,128]{2,1,0:T(8,128)S(1)}, f32[27,8,128]{2,1,0:T(8,128)S(1)}, u32[]{:S(2)}, u32[]{:S(2)}) collective-permute-start(f32[27,8,128]{2,1,0:T(8,128)S(1)} %get-tuple-element.70), channel_id=1, source_target_pairs={{0,1},{1,0},{2,3},{3,2},{4,5},{5,4},{6,7},{7,6},{8,9},{9,8},{10,11... | collective-permute-start | bytes 331784 | tf_op jit(solution)/shard_map/ppermute | solution.py:797
  15.5 4.8 %collective-permute-start.7 = (f32[27,8,128]{2,1,0:T(8,128)S(1)}, f32[27,8,128]{2,1,0:T(8,128)S(1)}, u32[]{:S(2)}, u32[]{:S(2)}) collective-permute-start(f32[27,8,128]{2,1,0:T(8,128)S(1)} %get-tuple-element.71), channel_id=1, source_target_pairs={{0,16},{1,2},{2,1},{3,4},{4,3},{5,6},{6,5},{7,23},{8,24},{9,10},{1... | collective-permute-start | bytes 331784 | tf_op jit(solution)/shard_map/ppermute | solution.py:797
  20.4 4.2 %collective-permute-start.8 = (f32[12,8,128]{2,1,0:T(8,128)S(1)}, f32[12,8,128]{2,1,0:T(8,128)S(1)}, u32[]{:S(2)}, u32[]{:S(2)}) collective-permute-start(f32[12,8,128]{2,1,0:T(8,128)S(1)} %get-tuple-element.74), channel_id=1, source_target_pairs={{0,8},{8,0},{16,24},{24,16},{1,9},{9,1},{17,25},{25,17},{2,10},{10... | collective-permute-start | bytes 147464 | tf_op jit(solution)/shard_map/ppermute | solution.py:797
  22.4 2.1 %collective-permute-start.9 = (f32[12,8,128]{2,1,0:T(8,128)S(1)}, f32[12,8,128]{2,1,0:T(8,128)S(1)}, u32[]{:S(2)}, u32[]{:S(2)}) collective-permute-start(f32[12,8,128]{2,1,0:T(8,128)S(1)} %get-tuple-element.75), channel_id=1, source_target_pairs={{0,1},{1,0},{2,3},{3,2},{4,5},{5,4},{6,7},{7,6},{8,16},{9,17},{10,... | collective-permute-start | bytes 147464 | tf_op jit(solution)/shard_map/ppermute | solution.py:797
  25.7 3.1 %collective-permute-start.10 = (f32[27,8,128]{2,1,0:T(8,128)S(1)}, f32[27,8,128]{2,1,0:T(8,128)S(1)}, u32[]{:S(2)}, u32[]{:S(2)}) collective-permute-start(f32[27,8,128]{2,1,0:T(8,128)S(1)} %get-tuple-element.82), channel_id=1, source_target_pairs={{0,1},{1,0},{2,3},{3,2},{4,5},{5,4},{6,7},{7,6},{8,9},{9,8},{10,11... | collective-permute-start | bytes 331784 | tf_op jit(solution)/shard_map/ppermute | solution.py:797
  25.7 5.8 %collective-permute-start.11 = (f32[27,8,128]{2,1,0:T(8,128)S(1)}, f32[27,8,128]{2,1,0:T(8,128)S(1)}, u32[]{:S(2)}, u32[]{:S(2)}) collective-permute-start(f32[27,8,128]{2,1,0:T(8,128)S(1)} %get-tuple-element.83), channel_id=1, source_target_pairs={{0,16},{1,2},{2,1},{3,4},{4,3},{5,6},{6,5},{7,23},{8,24},{9,10},{1... | collective-permute-start | bytes 331784 | tf_op jit(solution)/shard_map/ppermute | solution.py:797
  31.6 4.2 %collective-permute-start.12 = (f32[12,8,128]{2,1,0:T(8,128)S(1)}, f32[12,8,128]{2,1,0:T(8,128)S(1)}, u32[]{:S(2)}, u32[]{:S(2)}) collective-permute-start(f32[12,8,128]{2,1,0:T(8,128)S(1)} %get-tuple-element.86), channel_id=1, source_target_pairs={{0,8},{8,0},{16,24},{24,16},{1,9},{9,1},{17,25},{25,17},{2,10},{10... | collective-permute-start | bytes 147464 | tf_op jit(solution)/shard_map/ppermute | solution.py:797
  33.6 2.1 %collective-permute-start.13 = (f32[12,8,128]{2,1,0:T(8,128)S(1)}, f32[12,8,128]{2,1,0:T(8,128)S(1)}, u32[]{:S(2)}, u32[]{:S(2)}) collective-permute-start(f32[12,8,128]{2,1,0:T(8,128)S(1)} %get-tuple-element.87), channel_id=1, source_target_pairs={{0,1},{1,0},{2,3},{3,2},{4,5},{5,4},{6,7},{7,6},{8,16},{9,17},{10,... | collective-permute-start | bytes 147464 | tf_op jit(solution)/shard_map/ppermute | solution.py:797
